TPU v7x, 32 devices: a whole 2x2x4 slice. The times are simulated.
32 devices in a mesh: sec: 2 (over y), gz: 16 (over z, x, core).
Axes of the slice: x: 2, y: 2, z: 4, core: 2. Of those that a mesh axis runs over, the one named last changes fastest.
Arguments:
- velocity: float32 [2, 3, 32, 512, 256], P('sec', None, 'gz'), may hold values from -6 to 6
- eddy_viscosity: float32 [2, 32, 512, 256], P('sec', 'gz'), may hold values from 0.05 to 0.5
- turbine_mask: int32 [32, 512, 256], P('gz'), may hold values 0 or 1
- fringe_columns: int32 [64], replicated, may hold values from 0 to 511, as said below
Outputs:
- new_velocity: float32 [2, 3, 32, 512, 256], P('sec', None, 'gz')
Inputs may be any that keep to these rules, and one draw needn't show every extreme that they name: `fringe_columns`: 64 distinct streamwise column indices.
All inputs are finite; a program needn't handle non-finite values. No bound on the sum of `turbine_mask` on one device may be relied on, other than what follows from the above.
Results may differ from a plain program's by a relative error of at most 0.0003.
Values sent between devices are 32-bit elements; how exact they have to be, the bound alone decides.
No kernel may reach another device: no remote copies, remote signals or barrier semaphores. Data moves between devices by JAX's collectives and lax.ppermute only.
A program may use at most 128 MiB of HBM per device.

v0:
```python
import math

import jax
import jax.numpy as jnp
from jax import lax
from jax.sharding import PartitionSpec as P

step_size = 0.1
drag_coef = 0.75
cell_width = 4.0
highest = lax.Precision.HIGHEST


def from_behind(block, axis, distance):
    devices = range(lax.axis_size(axis))
    route = [(i - distance, i) for i in devices if i - distance in devices]
    return lax.ppermute(block, axis, route)


def with_halo(block, sides, width):
    for axis, dim in sides:
        count = lax.axis_size(axis)
        forward = [(i, i + 1) for i in range(count - 1)]
        backward = [(target, source) for source, target in forward]
        low = lax.ppermute(
            lax.slice_in_dim(block, block.shape[dim] - width, None, axis=dim), axis, forward
        )
        high = lax.ppermute(lax.slice_in_dim(block, 0, width, axis=dim), axis, backward)
        block = jnp.concatenate([low, block, high], axis=dim)
    return block


def derivative_table(length, cutoff):
    position = jnp.arange(length, dtype=jnp.int32)
    wavenumber = jnp.arange(1, cutoff + 1, dtype=jnp.int32)
    phases = position[:, None] * wavenumber[None, :] % length
    angles = 2.0 * math.pi / length * phases.astype(jnp.float32)
    sine_table = jnp.sin(angles)
    cosines = jnp.cos(angles)
    weight = (4.0 * math.pi / (length * length * cell_width) * wavenumber.astype(jnp.float32))[
        None, :
    ]
    return jnp.dot(cosines * weight, sine_table.T, precision=highest) - jnp.dot(
        sine_table * weight, cosines.T, precision=highest
    )


def real_basis(length):
    midpoint = length // 2
    row_index = jnp.arange(length, dtype=jnp.int32)
    position = jnp.arange(length, dtype=jnp.int32)
    wavenumber = jnp.where(row_index <= midpoint, row_index, row_index - midpoint)
    phases = wavenumber[:, None] * position[None, :] % length
    angles = 2.0 * math.pi / length * phases.astype(jnp.float32)
    scales = jnp.where(
        (row_index == 0) | (row_index == midpoint), math.sqrt(1.0 / length), math.sqrt(2.0 / length)
    ).astype(jnp.float32)
    shapes = jnp.where((row_index <= midpoint)[:, None], jnp.cos(angles), jnp.sin(angles))
    return scales[:, None] * shapes


def wave_square(row_index, length):
    midpoint = length // 2
    wavenumber = jnp.where(
        row_index < midpoint, row_index, jnp.where(row_index == midpoint, 0, row_index - midpoint)
    )
    scaled = 2.0 * math.pi / (length * cell_width) * wavenumber.astype(jnp.float32)
    return -(scaled * scaled)


def cosine_basis(length):
    mode_index = jnp.arange(length, dtype=jnp.int32)
    position = jnp.arange(length, dtype=jnp.int32)
    phases = mode_index[:, None] * (2 * position[None, :] + 1) % (4 * length)
    angles = math.pi / (2 * length) * phases.astype(jnp.float32)
    scales = jnp.where(mode_index == 0, math.sqrt(1.0 / length), math.sqrt(2.0 / length)).astype(
        jnp.float32
    )
    return scales[:, None] * jnp.cos(angles)


def vertical_eigen(mode_index, length):
    sines = jnp.sin(math.pi / (2 * length) * mode_index.astype(jnp.float32))
    return -4.0 * sines * sines


def column_inverse(height, length_x, length_y, first_column, column_count):
    mode_index = jnp.arange(height, dtype=jnp.int32)
    column = first_column + jnp.arange(column_count, dtype=jnp.int32)
    row_x = column // length_y
    row_y = column % length_y
    eigenvalue = (
        vertical_eigen(mode_index, height)[:, None]
        + wave_square(row_x, length_x)[None, :]
        + wave_square(row_y, length_y)[None, :]
    )
    null_x = (row_x == 0) | (row_x == length_x // 2)
    null_y = (row_y == 0) | (row_y == length_y // 2)
    null_mode = (mode_index == 0)[:, None] & (null_x & null_y)[None, :]
    return jnp.where(null_mode, 0.0, 1.0 / jnp.where(null_mode, -1.0, eigenvalue))


def horizontal(values, basis_x, basis_y):
    partial_value = jnp.einsum("ax,zxy->zay", basis_x, values, precision=highest)
    spectra = jnp.einsum("zay,by->zab", partial_value, basis_y, precision=highest)
    return spectra.reshape(values.shape[0], values.shape[1] * values.shape[2])


def horizontal_back(spectra, basis_x, basis_y):
    shaped = spectra.reshape(spectra.shape[0], basis_x.shape[0], basis_y.shape[0])
    partial_value = jnp.einsum("ax,zab->zxb", basis_x, shaped, precision=highest)
    return jnp.einsum("zxb,by->zxy", partial_value, basis_y, precision=highest)


def column_solve(source_column, basis_z, inverse):
    solved = jnp.dot(basis_z, source_column, precision=highest) * inverse
    return jnp.dot(basis_z.T, solved, precision=highest)


def inflow(current, fringe_columns, is_farm):
    columns = current[:, :, fringe_columns, :]
    arrived = from_behind(columns, "sec", 1)
    return current.at[:, :, fringe_columns, :].set(jnp.where(is_farm, arrived, columns))


def tendency(current, viscosity, drag_field, dealias_x, dealias_y):
    rounded = current.astype(jnp.bfloat16)
    grad_x = jnp.einsum("ij,czjy->cziy", dealias_x, rounded, preferred_element_type=jnp.float32)
    grad_y = jnp.einsum("czxj,ij->czxi", rounded, dealias_y, preferred_element_type=jnp.float32)
    padded = with_halo(current, (("gz", 1),), 1)
    upper_plane = padded[:, 2:]
    lower_plane = padded[:, :-2]
    grad_z = 0.5 * (upper_plane - lower_plane)
    laplace = upper_plane - 2.0 * current + lower_plane
    advection = -(current[0] * grad_x + current[1] * grad_y + current[2] * grad_z)
    return advection + viscosity * laplace - drag_field * jnp.abs(current[0]) * current


def project(current, full_x, full_y, basis_x, basis_y, basis_z, inverse, at_lid):
    depth_cells = current.shape[1]
    w_face = jnp.where(at_lid, 0.0, current[2])
    divergence = jnp.einsum("ij,zjy->ziy", full_x, current[0], precision=highest) + jnp.einsum(
        "zxj,ij->zxi", current[1], full_y, precision=highest
    )
    face_low = from_behind(w_face[depth_cells - 1 :], "gz", 1)
    beneath = jnp.concatenate([face_low, w_face[:-1]], axis=0)
    source = divergence + w_face - beneath
    source_column = lax.all_to_all(
        horizontal(source, basis_x, basis_y), "gz", split_axis=1, concat_axis=0, tiled=True
    )
    pressure_column = column_solve(source_column, basis_z, inverse)
    pressure_spectra = lax.all_to_all(
        pressure_column, "gz", split_axis=0, concat_axis=1, tiled=True
    )
    pressure = horizontal_back(pressure_spectra, basis_x, basis_y)
    pressure_high = from_behind(pressure[:1], "gz", -1)
    overhead = jnp.concatenate([pressure[1:], pressure_high], axis=0)
    lift = jnp.where(at_lid, 0.0, overhead - pressure)
    new_u = current[0] - jnp.einsum("ij,zjy->ziy", full_x, pressure, precision=highest)
    new_v = current[1] - jnp.einsum("zxj,ij->zxi", pressure, full_y, precision=highest)
    return jnp.stack([new_u, new_v, w_face - lift])


def local(velocity, eddy_viscosity, turbine_mask, fringe_columns):
    current = velocity[0]
    viscosity = eddy_viscosity[0]
    depth_cells = current.shape[1]
    length_x = current.shape[2]
    length_y = current.shape[3]
    slab_count = lax.axis_size("gz")
    height = depth_cells * slab_count
    slab_index = lax.axis_index("gz")
    is_farm = lax.axis_index("sec") == 1
    column_count = length_x * length_y // slab_count
    drag_field = jnp.where(is_farm, drag_coef, 0.0) * turbine_mask.astype(jnp.float32)
    dealias_x = derivative_table(length_x, (length_x - 1) // 3).astype(jnp.bfloat16)
    dealias_y = derivative_table(length_y, (length_y - 1) // 3).astype(jnp.bfloat16)
    full_x = derivative_table(length_x, length_x // 2 - 1)
    full_y = derivative_table(length_y, length_y // 2 - 1)
    basis_x = real_basis(length_x)
    basis_y = real_basis(length_y)
    basis_z = cosine_basis(height)
    inverse = column_inverse(height, length_x, length_y, slab_index * column_count, column_count)
    levels = slab_index * depth_cells + jnp.arange(depth_cells, dtype=jnp.int32)
    at_lid = (levels == height - 1)[:, None, None]
    tables = (full_x, full_y, basis_x, basis_y, basis_z, inverse, at_lid)
    start_state = inflow(current, fringe_columns, is_farm)
    middle = project(
        start_state
        + step_size * tendency(start_state, viscosity, drag_field, dealias_x, dealias_y),
        *tables
    )
    second_start = inflow(middle, fringe_columns, is_farm)
    final_update = 0.5 * (
        start_state
        + second_start
        + step_size * tendency(second_start, viscosity, drag_field, dealias_x, dealias_y)
    )
    return project(final_update, *tables)[None]


def solution(mesh):
    placed = (
        P("sec", None, "gz", None, None),
        P("sec", "gz", None, None),
        P("gz", None, None),
        P(),
    )
    return jax.shard_map(
        local,
        mesh=mesh,
        in_specs=placed,
        out_specs=P("sec", None, "gz", None, None),
        check_vma=False,
    )
```

profile of v0, /device:TPU:5, one launch (start us, length us, event | category | flops | bytes accessed | tf_op | source)
XLA Modules:
  0.0 445.5 jit_solution(6767717282440352493)
XLA Ops:
  0.7 4.3 copy.260
  13.9 2.6 copy.171
  16.5 5.9 %fusion.80 = f32[512,512]{1,0:T(8,128)} fusion(f32[170]{0:T(256)S(1)} %convert_multiply_fusion.2, s32[170]{0:T(256)S(1)} %iota_add_fusion.2), kind=kOutput, calls=%fused_computation.138 | convolution fusion | flops 537297920 | bytes 1049936 | tf_op jit(solution)/shard_map/dot_general | solution.py:43
  24.4 2.3 fusion.34
  26.7 7.2 %fusion.75 = f32[512,512]{1,0:T(8,128)} fusion(f32[255]{0:T(256)} %convert_multiply_fusion.1, s32[255]{0:T(256)} %iota_add_fusion.1), kind=kOutput, calls=%fused_computation.133 | convolution fusion | flops 805946880 | bytes 1050616 | tf_op jit(solution)/shard_map/dot_general | solution.py:43
  36.0 7.1 %scatter_fusion = f32[3,2,512,256]{3,1,2,0:T(2,128)S(1)} fusion(f32[3,2,512,256]{3,1,2,0:T(2,128)S(1)} %bitcast.207, s32[64]{0:T(128)S(1)} %compare_select_fusion.2, f32[64,3,2,256]{3,2,1,0:T(2,128)} %select_bitcast_fusion.1), kind=kCustom, calls=%fused_computation.2 | custom fusion | bytes 1179904 | tf_op jit(solution)/shard_map/scatter | solution.py:123
  43.1 3.9 copy.190
  47.0 4.2 fusion.262
  51.3 2.7 collective-permute-start.1
  54.0 3.0 collective-permute-start.2
  57.0 5.7 %fusion.33 = bf16[512,512,1,1]{1,0,3,2:T(8,128)(2,1)} fusion(f32[512,512]{1,0:T(8,128)S(1)} %copy-done.44, f32[170]{0:T(256)S(1)} %copy-done.32, s32[170]{0:T(256)S(1)} %copy-done.34), kind=kOutput, calls=%fused_computation.65 | convolution fusion | flops 537822208 | bytes 1574224 | tf_op jit(solution)/shard_map/dot_general | solution.py:43
  62.8 5.9 %fusion.29 = f32[512,512,1]{1,0,2:T(8,128)} fusion(f32[512,512]{1,0:T(8,128)S(1)} %copy-done.43, f32[255]{0:T(256)S(1)} %copy-done.35, s32[255]{0:T(256)S(1)} %copy-done.36), kind=kOutput, calls=%fused_computation.56 | convolution fusion | flops 806209024 | bytes 2099192 | tf_op jit(solution)/shard_map/dot_general | solution.py:43
  68.7 2.3 convert_element_type.135
  71.0 2.7 slice_bitcast_fusion.7
  73.7 2.3 copy.239
  79.1 2.3 copy.163
  84.7 5.8 %collective-permute-done.2 = f32[3,1,512,256]{2,3,1,0:T(8,128)} collective-permute-done((f32[3,1,512,256]{2,3,1,0:T(8,128)}, f32[3,1,512,256]{2,3,1,0:T(8,128)}, u32[]{:S(2)}, u32[]{:S(2)}) %collective-permute-start.2) | collective-permute-done | bytes 1572896 | tf_op jit(solution)/shard_map/ppermute | solution.py:25
  90.5 4.8 %fusion.14 = f32[3,2,512,256]{2,3,1,0:T(8,128)S(1)} fusion(f32[3,2,512,256]{2,3,1,0:T(8,128)S(1)} %copy-done.2, f32[3,2,256,512]{3,2,1,0:T(8,128)S(1)} %fusion.18, f32[3,1,512,256]{2,3,1,0:T(8,128)} %collective-permute-done.1, f32[3,1,512,256]{2,3,1,0:T(8,128)} %collective-permute-done.2, bf16[256,256,1,1]{1,0,3,2:T(8,128)(2,1)S(1)} %fusion.36, ...), kind=kOutput, calls=%fused_computation.28 | convolution fusion | flops 416808960 | bytes 19529728 | tf_op jit(solution)/shard_map/czxj,ij->czxi/dot_general | solution.py:129
  95.6 4.5 %collective-permute-start.3 = (f32[1,512,256]{1,2,0:T(8,128)S(1)}, f32[1,512,256]{1,2,0:T(8,128)S(1)}, u32[]{:S(2)}, u32[]{:S(2)}) collective-permute-start(f32[1,512,256]{1,2,0:T(8,128)S(1)} %get-tuple-element.21), channel_id=1, source_target_pairs={{0,1},{1,2},{2,3},{3,4},{4,5},{5,6},{6,7},{7,8},{8,9},{9,10},{10,1... | collective-permute-start | bytes 1572872 | tf_op jit(solution)/shard_map/ppermute | solution.py:17
  103.1 3.1 collective-permute-done.3
  106.2 6.2 %convolution_bitcast_fusion.6 = f32[2,512,256]{1,2,0:T(8,128)S(1)} fusion(f32[2,512,256]{1,2,0:T(8,128)S(1)} %fusion.28, f32[1,512,256]{1,2,0:T(8,128)S(1)} %get-tuple-element.22, f32[1,512,256]{1,2,0:T(8,128)S(1)} %collective-permute-done.3, s32[512]{0:T(512)S(1)} %copy-done.23, f32[512]{0:T(512)S(1)} %copy-done.25, pred[512]{0:T(512)(128)(4,1)S(1)} %copy-done.38), kind=kOutput, calls=%fused_computation.51 | convolution fusion | flops 1615331328 | bytes 3150336 | tf_op jit(solution)/shard_map/ax,zxy->zay/dot_general | solution.py:104
  112.4 5.7 %fusion.95 = f32[2,512,256]{2,1,0:T(8,128)} fusion(f32[2,512,256]{1,2,0:T(8,128)S(1)} %convolution_bitcast_fusion.6, s32[256]{0:T(256)S(1)} %add_select_fusion.10, f32[256]{0:T(256)S(1)} %or_select_fusion, pred[256]{0:T(512)(128)(4,1)S(1)} %iota_compare_fusion.3), kind=kOutput, calls=%fused_computation.158 | convolution fusion | flops 806354944 | bytes 2099456 | tf_op jit(solution)/shard_map/zay,by->zab/dot_general | solution.py:105
  118.1 2.4 all_to_all.52
  120.5 3.0 copy.179
  123.6 6.2 %all-to-all-start = ((f32[2,16,8192]{2,0,1:T(2,128)}), f32[2,16,8192]{2,0,1:T(2,128)}, u32[]{:S(2)}, u32[]{:S(2)}) async-start(f32[2,16,8192]{2,0,1:T(2,128)} %copy.179), calls=%async_computation | async-start | bytes 2097152 | tf_op jit(solution)/shard_map/all_to_all | solution.py:148
  132.6 20.3 %all-to-all-done = f32[2,16,8192]{2,0,1:T(2,128)} async-done(((f32[2,16,8192]{2,0,1:T(2,128)}), f32[2,16,8192]{2,0,1:T(2,128)}, u32[]{:S(2)}, u32[]{:S(2)}) %all-to-all-start) | async-done | bytes 1048608 | tf_op jit(solution)/shard_map/all_to_all | solution.py:148
  153.0 2.9 all_to_all.55
  155.9 2.5 convolution_multiply_fusion.1
  160.6 2.8 all_to_all.56
  163.4 32.3 %all_to_all.70 = f32[16,2,8192]{2,1,0:T(2,128)S(1)} all-to-all(f32[16,2,8192]{2,1,0:T(2,128)} %all_to_all.56), channel_id=1, replica_groups=mesh['sec'=2,'gz'=16] {'gz'}, dimensions={0} | all-to-all | bytes 2097152 | tf_op jit(solution)/shard_map/all_to_all | solution.py:152
  197.4 2.4 reshape.184
  199.7 7.6 %convolution_bitcast_fusion.5 = f32[2,512,256]{1,2,0:T(8,128)S(1)} fusion(f32[2,512,256]{2,1,0:T(8,128)} %reshape.184, s32[512]{0:T(512)} %add_select_fusion.9, f32[512]{0:T(512)} %fusion.178, pred[512]{0:T(512)(128)(4,1)} %iota_compare_fusion.2), kind=kOutput, calls=%fused_computation.50 | convolution fusion | flops 1614807040 | bytes 2101760 | tf_op jit(solution)/shard_map/ax,zab->zxb/dot_general | solution.py:111
  207.3 3.8 fusion.93
  211.1 2.5 copy.185
  217.3 2.4 fusion.31
  219.7 3.5 fusion.26
  223.2 2.5 collective-permute-done.4
  228.1 4.2 copy.189
  235.4 9.0 %collective-permute-done.5 = f32[3,2,64,256]{3,1,0,2:T(2,128)S(1)} collective-permute-done((f32[3,2,64,256]{3,1,0,2:T(2,128)}, f32[3,2,64,256]{3,1,0,2:T(2,128)S(1)}, u32[]{:S(2)}, u32[]{:S(2)}) %collective-permute-start.5) | collective-permute-done | bytes 393248 | tf_op jit(solution)/shard_map/ppermute | solution.py:17
  246.4 7.2 %scatter_fusion.1 = f32[3,2,512,256]{3,1,2,0:T(2,128)S(1)} fusion(f32[3,2,512,256]{3,1,2,0:T(2,128)S(1)} %copy.189, s32[64]{0:T(128)} %copy-done.22, f32[64,3,2,256]{3,2,1,0:T(2,128)} %select_bitcast_fusion), kind=kCustom, calls=%fused_computation.3 | custom fusion | bytes 1179904 | tf_op jit(solution)/shard_map/scatter | solution.py:123
  253.6 4.0 copy.191
  257.6 4.1 fusion.261
  263.7 4.0 collective-permute-start.7
  269.9 2.5 slice_bitcast_fusion.3
  284.1 18.0 %collective-permute-done.7 = f32[3,1,512,256]{2,3,1,0:T(8,128)} collective-permute-done((f32[3,1,512,256]{2,3,1,0:T(8,128)}, f32[3,1,512,256]{2,3,1,0:T(8,128)}, u32[]{:S(2)}, u32[]{:S(2)}) %collective-permute-start.7) | collective-permute-done | bytes 1572896 | tf_op jit(solution)/shard_map/ppermute | solution.py:25
  302.2 6.6 %fusion.7 = f32[3,2,512,256]{2,3,1,0:T(8,128)S(1)} fusion(f32[3,2,256,512]{3,2,1,0:T(8,128)S(1)} %fusion.15, f32[3,2,512,256]{2,3,1,0:T(8,128)} %copy.191, f32[3,1,512,256]{2,3,1,0:T(8,128)} %collective-permute-done.6, f32[3,1,512,256]{2,3,1,0:T(8,128)} %collective-permute-done.7, f32[3,2,512,256]{2,3,1,0:T(8,128)S(1)} %copy-done.3, ...), kind=kOutput, calls=%fused_computation.20 | convolution fusion | flops 418381824 | bytes 22675456 | tf_op jit(solution)/shard_map/czxj,ij->czxi/dot_general | solution.py:129
  309.1 4.8 %collective-permute-start.8 = (f32[1,512,256]{1,2,0:T(8,128)S(1)}, f32[1,512,256]{1,2,0:T(8,128)S(1)}, u32[]{:S(2)}, u32[]{:S(2)}) collective-permute-start(f32[1,512,256]{1,2,0:T(8,128)S(1)} %get-tuple-element.17), channel_id=1, source_target_pairs={{0,1},{1,2},{2,3},{3,4},{4,5},{5,6},{6,7},{7,8},{8,9},{9,10},{10,1... | collective-permute-start | bytes 1572872 | tf_op jit(solution)/shard_map/ppermute | solution.py:17
  316.9 2.9 collective-permute-done.8
  319.8 6.2 %convolution_bitcast_fusion.2 = f32[2,512,256]{1,2,0:T(8,128)S(1)} fusion(f32[2,512,256]{1,2,0:T(8,128)S(1)} %fusion.24, f32[1,512,256]{1,2,0:T(8,128)S(1)} %get-tuple-element.18, f32[1,512,256]{1,2,0:T(8,128)S(1)} %collective-permute-done.8, s32[512]{0:T(512)S(1)} %copy-done.24, f32[512]{0:T(512)S(1)} %copy-done.26, pred[512]{0:T(512)(128)(4,1)S(1)} %copy-done.39), kind=kOutput, calls=%fused_computation.43 | convolution fusion | flops 1615331328 | bytes 3150336 | tf_op jit(solution)/shard_map/ax,zxy->zay/dot_general | solution.py:104
  325.9 5.8 %fusion.91 = f32[2,512,256]{2,1,0:T(8,128)} fusion(f32[2,512,256]{1,2,0:T(8,128)S(1)} %convolution_bitcast_fusion.2, s32[256]{0:T(256)S(1)} %add_select_fusion.10, f32[256]{0:T(256)S(1)} %or_select_fusion, pred[256]{0:T(512)(128)(4,1)S(1)} %iota_compare_fusion.3), kind=kOutput, calls=%fused_computation.154 | convolution fusion | flops 806354944 | bytes 2099456 | tf_op jit(solution)/shard_map/zay,by->zab/dot_general | solution.py:105
  331.8 2.4 all_to_all.59
  336.3 35.4 %all_to_all.71 = f32[2,16,8192]{2,0,1:T(2,128)} all-to-all(f32[2,16,8192]{2,0,1:T(2,128)S(1)} %copy.209), channel_id=1, replica_groups=mesh['sec'=2,'gz'=16] {'gz'}, dimensions={1} | all-to-all | bytes 2097152 | tf_op jit(solution)/shard_map/all_to_all | solution.py:148
  371.7 2.9 all_to_all.62
  374.7 2.5 convolution_multiply_fusion
  379.2 2.9 all_to_all.63
  382.1 30.0 %all_to_all.72 = f32[16,2,8192]{2,1,0:T(2,128)S(1)} all-to-all(f32[16,2,8192]{2,1,0:T(2,128)} %all_to_all.63), channel_id=1, replica_groups=mesh['sec'=2,'gz'=16] {'gz'}, dimensions={0} | all-to-all | bytes 2097152 | tf_op jit(solution)/shard_map/all_to_all | solution.py:152
  413.7 2.4 reshape.185
  416.1 7.6 %convolution_bitcast_fusion.1 = f32[2,512,256]{1,2,0:T(8,128)S(1)} fusion(f32[2,512,256]{2,1,0:T(8,128)} %reshape.185, s32[512]{0:T(512)S(1)} %copy-done.24, f32[512]{0:T(512)S(1)} %copy-done.26, pred[512]{0:T(512)(128)(4,1)S(1)} %copy-done.39), kind=kOutput, calls=%fused_computation.42 | convolution fusion | flops 1614807040 | bytes 2101760 | tf_op jit(solution)/shard_map/ax,zab->zxb/dot_general | solution.py:111
  423.7 3.8 fusion.89
  427.5 2.6 copy.215
  433.8 2.4 fusion.30
  436.2 3.5 fusion.22
  439.7 2.5 collective-permute-done.9
  442.9 2.4 copy.218
  (157 shorter events, 70.2 us)
Async XLA Ops:
  0.7 35.3 %copy-start.22 = (s32[64]{0:T(128)}, s32[64]{0:T(128)S(1)}, u32[]{:S(2)}) copy-start(s32[64]{0:T(128)S(1)} %compare_select_fusion.2) | copy-start | bytes 772
  0.7 4.3 copy-start.21
  6.8 27.1 %collective-permute-start = (f32[3,2,64,256]{3,1,0,2:T(2,128)}, f32[3,2,64,256]{3,1,0,2:T(2,128)}, u32[]{:S(2)}, u32[]{:S(2)}) collective-permute-start(f32[3,2,64,256]{3,1,0,2:T(2,128)} %bitcast.1), channel_id=1, source_target_pairs={{0,16},{1,17},{2,18},{3,19},{4,20},{5,21},{6,22},{7,23},{8,24},{9,... | collective-permute-start | bytes 1179656 | tf_op jit(solution)/shard_map/ppermute | solution.py:17
  8.3 14.1 %copy-start.31 = (f32[170]{0:T(256)}, f32[170]{0:T(256)S(1)}, u32[]{:S(2)}) copy-start(f32[170]{0:T(256)S(1)} %convert_multiply_fusion.2) | copy-start | bytes 2044
  8.3 14.1 %copy-start.33 = (s32[170]{0:T(256)}, s32[170]{0:T(256)S(1)}, u32[]{:S(2)}) copy-start(s32[170]{0:T(256)S(1)} %iota_add_fusion.2) | copy-start | bytes 2044
  8.3 14.0 %copy-start.41 = (f32[127]{0:T(128)}, f32[127]{0:T(128)S(1)}, u32[]{:S(2)}) copy-start(f32[127]{0:T(128)S(1)} %convert_multiply_fusion.3) | copy-start | bytes 1528
  8.4 14.0 %copy-start.42 = (s32[127]{0:T(128)}, s32[127]{0:T(128)S(1)}, u32[]{:S(2)}) copy-start(s32[127]{0:T(128)S(1)} %iota_add_fusion.3) | copy-start | bytes 1528
  47.0 10.0 %copy-start.32 = (f32[170]{0:T(256)S(1)}, f32[170]{0:T(256)}, u32[]{:S(2)}) copy-start(f32[170]{0:T(256)} %copy-done.31) | copy-start | bytes 2044
  47.0 10.0 %copy-start.34 = (s32[170]{0:T(256)S(1)}, s32[170]{0:T(256)}, u32[]{:S(2)}) copy-start(s32[170]{0:T(256)} %copy-done.33) | copy-start | bytes 2044
  47.0 10.0 %copy-start.44 = (f32[512,512]{1,0:T(8,128)S(1)}, f32[512,512]{1,0:T(8,128)}, u32[]{:S(2)}) copy-start(f32[512,512]{1,0:T(8,128)} %fusion.80) | copy-start | bytes 3145732
  51.2 11.5 %copy-start.35 = (f32[255]{0:T(256)S(1)}, f32[255]{0:T(256)}, u32[]{:S(2)}) copy-start(f32[255]{0:T(256)} %convert_multiply_fusion.1) | copy-start | bytes 3064
  51.2 11.5 %copy-start.36 = (s32[255]{0:T(256)S(1)}, s32[255]{0:T(256)}, u32[]{:S(2)}) copy-start(s32[255]{0:T(256)} %iota_add_fusion.1) | copy-start | bytes 3064
  51.3 11.5 %copy-start.43 = (f32[512,512]{1,0:T(8,128)S(1)}, f32[512,512]{1,0:T(8,128)}, u32[]{:S(2)}) copy-start(f32[512,512]{1,0:T(8,128)} %fusion.75) | copy-start | bytes 3145732
  51.3 33.5 %collective-permute-start.1 = (f32[3,1,512,256]{2,3,1,0:T(8,128)}, f32[3,1,512,256]{2,3,1,0:T(8,128)}, u32[]{:S(2)}, u32[]{:S(2)}) collective-permute-start(f32[3,1,512,256]{2,3,1,0:T(8,128)} %get-tuple-element.14), channel_id=1, source_target_pairs={{1,0},{2,1},{3,2},{4,3},{5,4},{6,5},{7,6},{8,7},{9,8},{10,9},{11,1... | collective-permute-start | bytes 4718600 | tf_op jit(solution)/shard_map/ppermute | solution.py:28
  54.0 36.5 %collective-permute-start.2 = (f32[3,1,512,256]{2,3,1,0:T(8,128)}, f32[3,1,512,256]{2,3,1,0:T(8,128)}, u32[]{:S(2)}, u32[]{:S(2)}) collective-permute-start(f32[3,1,512,256]{2,3,1,0:T(8,128)} %get-tuple-element.13), channel_id=1, source_target_pairs={{0,1},{1,2},{2,3},{3,4},{4,5},{5,6},{6,7},{7,8},{8,9},{9,10},{10,1... | collective-permute-start | bytes 4718600 | tf_op jit(solution)/shard_map/ppermute | solution.py:25
  77.7 5.9 %copy-start.13 = (bf16[3,2,512,256]{3,1,2,0:T(2,128)(2,1)S(1)}, bf16[3,2,512,256]{3,1,2,0:T(2,128)(2,1)}, u32[]{:S(2)}) copy-start(bf16[3,2,512,256]{3,1,2,0:T(2,128)(2,1)} %convert_element_type.135) | copy-start | bytes 4718596
  77.7 5.9 %copy-start.16 = (bf16[512,512,1,1]{1,0,3,2:T(8,128)(2,1)S(1)}, bf16[512,512,1,1]{1,0,3,2:T(8,128)(2,1)}, u32[]{:S(2)}) copy-start(bf16[512,512,1,1]{1,0,3,2:T(8,128)(2,1)} %fusion.33) | copy-start | bytes 1572868
  83.6 6.9 %copy-start = (f32[2,512,256]{1,2,0:T(8,128)S(1)}, f32[2,512,256]{1,2,0:T(8,128)}, u32[]{:S(2)}) copy-start(f32[2,512,256]{1,2,0:T(8,128)} %copy.171) | copy-start | bytes 3145732
  83.6 6.9 %copy-start.2 = (f32[3,2,512,256]{2,3,1,0:T(8,128)S(1)}, f32[3,2,512,256]{2,3,1,0:T(8,128)}, u32[]{:S(2)}) copy-start(f32[3,2,512,256]{2,3,1,0:T(8,128)} %copy.190) | copy-start | bytes 9437188
  83.7 6.8 %copy-start.4 = (f32[1,2,512,256]{2,3,1,0:T(8,128)S(1)}, f32[1,2,512,256]{2,3,1,0:T(8,128)}, u32[]{:S(2)}) copy-start(f32[1,2,512,256]{2,3,1,0:T(8,128)} %copy.239) | copy-start | bytes 3145732
  95.3 5.9 %copy-start.5 = (f32[512,512,1]{1,0,2:T(8,128)S(1)}, f32[512,512,1]{1,0,2:T(8,128)}, u32[]{:S(2)}) copy-start(f32[512,512,1]{1,0,2:T(8,128)} %fusion.29) | copy-start | bytes 3145732
  95.6 10.6 %collective-permute-start.3 = (f32[1,512,256]{1,2,0:T(8,128)S(1)}, f32[1,512,256]{1,2,0:T(8,128)S(1)}, u32[]{:S(2)}, u32[]{:S(2)}) collective-permute-start(f32[1,512,256]{1,2,0:T(8,128)S(1)} %get-tuple-element.21), channel_id=1, source_target_pairs={{0,1},{1,2},{2,3},{3,4},{4,5},{5,6},{6,7},{7,8},{8,9},{9,10},{10,1... | collective-permute-start | bytes 1572872 | tf_op jit(solution)/shard_map/ppermute | solution.py:17
  101.2 5.0 %copy-start.23 = (s32[512]{0:T(512)S(1)}, s32[512]{0:T(512)}, u32[]{:S(2)}) copy-start(s32[512]{0:T(512)} %add_select_fusion.9) | copy-start | bytes 6148
  101.2 5.0 %copy-start.25 = (f32[512]{0:T(512)S(1)}, f32[512]{0:T(512)}, u32[]{:S(2)}) copy-start(f32[512]{0:T(512)} %fusion.178) | copy-start | bytes 6148
  101.2 5.0 %copy-start.38 = (pred[512]{0:T(512)(128)(4,1)S(1)}, pred[512]{0:T(512)(128)(4,1)}, u32[]{:S(2)}) copy-start(pred[512]{0:T(512)(128)(4,1)} %iota_compare_fusion.2) | copy-start | bytes 1540
  123.6 29.4 %all-to-all-start = ((f32[2,16,8192]{2,0,1:T(2,128)}), f32[2,16,8192]{2,0,1:T(2,128)}, u32[]{:S(2)}, u32[]{:S(2)}) async-start(f32[2,16,8192]{2,0,1:T(2,128)} %copy.179), calls=%async_computation | async-start | bytes 2097152 | tf_op jit(solution)/shard_map/all_to_all | solution.py:148
  155.9 2.5 copy-start.27
  155.9 2.5 copy-start.29
  213.7 6.0 %copy-start.6 = (f32[512,512,1]{1,0,2:T(8,128)S(1)}, f32[512,512,1]{1,0,2:T(8,128)}, u32[]{:S(2)}) copy-start(f32[512,512,1]{1,0,2:T(8,128)} %fusion.29) | copy-start | bytes 3145732
  213.7 6.0 %copy-start.10 = (f32[2,512,256]{2,1,0:T(8,128)S(1)}, f32[2,512,256]{2,1,0:T(8,128)}, u32[]{:S(2)}) copy-start(f32[2,512,256]{2,1,0:T(8,128)} %fusion.93) | copy-start | bytes 3145732
  215.1 10.6 %copy-start.15 = (f32[2,512,256]{1,2,0:T(8,128)S(1)}, f32[2,512,256]{1,2,0:T(8,128)}, u32[]{:S(2)}) copy-start(f32[2,512,256]{1,2,0:T(8,128)} %copy.185) | copy-start | bytes 3145732
  215.1 10.6 %collective-permute-start.4 = (f32[1,512,256]{1,2,0:T(8,128)S(1)}, f32[1,512,256]{1,2,0:T(8,128)S(1)}, u32[]{:S(2)}, u32[]{:S(2)}) collective-permute-start(f32[1,512,256]{1,2,0:T(8,128)S(1)} %get-tuple-element.20), channel_id=1, source_target_pairs={{1,0},{2,1},{3,2},{4,3},{5,4},{6,5},{7,6},{8,7},{9,8},{10,9},{11,1... | collective-permute-start | bytes 1572872 | tf_op jit(solution)/shard_map/ppermute | solution.py:17
  234.1 10.3 %collective-permute-start.5 = (f32[3,2,64,256]{3,1,0,2:T(2,128)}, f32[3,2,64,256]{3,1,0,2:T(2,128)S(1)}, u32[]{:S(2)}, u32[]{:S(2)}) collective-permute-start(f32[3,2,64,256]{3,1,0,2:T(2,128)} %bitcast.213), channel_id=1, source_target_pairs={{0,16},{1,17},{2,18},{3,19},{4,20},{5,21},{6,22},{7,23},{8,24},{9,... | collective-permute-start | bytes 1179656 | tf_op jit(solution)/shard_map/ppermute | solution.py:17
  261.7 22.4 %collective-permute-start.6 = (f32[3,1,512,256]{2,3,1,0:T(8,128)}, f32[3,1,512,256]{2,3,1,0:T(8,128)}, u32[]{:S(2)}, u32[]{:S(2)}) collective-permute-start(f32[3,1,512,256]{2,3,1,0:T(8,128)} %get-tuple-element.9), channel_id=1, source_target_pairs={{1,0},{2,1},{3,2},{4,3},{5,4},{6,5},{7,6},{8,7},{9,8},{10,9},{11,1... | collective-permute-start | bytes 4718600 | tf_op jit(solution)/shard_map/ppermute | solution.py:28
  263.7 38.5 %collective-permute-start.7 = (f32[3,1,512,256]{2,3,1,0:T(8,128)}, f32[3,1,512,256]{2,3,1,0:T(8,128)}, u32[]{:S(2)}, u32[]{:S(2)}) collective-permute-start(f32[3,1,512,256]{2,3,1,0:T(8,128)} %get-tuple-element.8), channel_id=1, source_target_pairs={{0,1},{1,2},{2,3},{3,4},{4,5},{5,6},{6,7},{7,8},{8,9},{9,10},{10,1... | collective-permute-start | bytes 4718600 | tf_op jit(solution)/shard_map/ppermute | solution.py:25
  276.4 5.9 %copy-start.12 = (bf16[3,2,512,256]{3,1,2,0:T(2,128)(2,1)S(1)}, bf16[3,2,512,256]{3,1,2,0:T(2,128)(2,1)}, u32[]{:S(2)}) copy-start(bf16[3,2,512,256]{3,1,2,0:T(2,128)(2,1)} %convert_element_type.153) | copy-start | bytes 4718596
  276.4 5.9 %copy-start.17 = (bf16[512,512,1,1]{1,0,3,2:T(8,128)(2,1)S(1)}, bf16[512,512,1,1]{1,0,3,2:T(8,128)(2,1)}, u32[]{:S(2)}) copy-start(bf16[512,512,1,1]{1,0,3,2:T(8,128)(2,1)} %fusion.33) | copy-start | bytes 1572868
  282.3 19.9 %copy-start.1 = (f32[2,512,256]{1,2,0:T(8,128)S(1)}, f32[2,512,256]{1,2,0:T(8,128)}, u32[]{:S(2)}) copy-start(f32[2,512,256]{1,2,0:T(8,128)} %copy.171) | copy-start | bytes 3145732
  282.3 19.9 %copy-start.3 = (f32[3,2,512,256]{2,3,1,0:T(8,128)S(1)}, f32[3,2,512,256]{2,3,1,0:T(8,128)}, u32[]{:S(2)}) copy-start(f32[3,2,512,256]{2,3,1,0:T(8,128)} %copy.190) | copy-start | bytes 9437188
  282.3 19.9 %copy-start.11 = (f32[1,2,512,256]{2,3,1,0:T(8,128)S(1)}, f32[1,2,512,256]{2,3,1,0:T(8,128)}, u32[]{:S(2)}) copy-start(f32[1,2,512,256]{2,3,1,0:T(8,128)} %copy.240) | copy-start | bytes 3145732
  308.8 6.1 %copy-start.7 = (f32[512,512,1]{1,0,2:T(8,128)S(1)}, f32[512,512,1]{1,0,2:T(8,128)}, u32[]{:S(2)}) copy-start(f32[512,512,1]{1,0,2:T(8,128)} %fusion.29) | copy-start | bytes 3145732
  309.1 10.7 %collective-permute-start.8 = (f32[1,512,256]{1,2,0:T(8,128)S(1)}, f32[1,512,256]{1,2,0:T(8,128)S(1)}, u32[]{:S(2)}, u32[]{:S(2)}) collective-permute-start(f32[1,512,256]{1,2,0:T(8,128)S(1)} %get-tuple-element.17), channel_id=1, source_target_pairs={{0,1},{1,2},{2,3},{3,4},{4,5},{5,6},{6,7},{7,8},{8,9},{9,10},{10,1... | collective-permute-start | bytes 1572872 | tf_op jit(solution)/shard_map/ppermute | solution.py:17
  315.0 4.8 %copy-start.24 = (s32[512]{0:T(512)S(1)}, s32[512]{0:T(512)}, u32[]{:S(2)}) copy-start(s32[512]{0:T(512)} %add_select_fusion.9) | copy-start | bytes 6148
  315.0 4.8 %copy-start.26 = (f32[512]{0:T(512)S(1)}, f32[512]{0:T(512)}, u32[]{:S(2)}) copy-start(f32[512]{0:T(512)} %fusion.178) | copy-start | bytes 6148
  315.0 4.8 %copy-start.39 = (pred[512]{0:T(512)(128)(4,1)S(1)}, pred[512]{0:T(512)(128)(4,1)}, u32[]{:S(2)}) copy-start(pred[512]{0:T(512)(128)(4,1)} %iota_compare_fusion.2) | copy-start | bytes 1540
  334.2 40.4 %copy-start.18 = (f32[8192]{0:T(1024)S(1)}, f32[8192]{0:T(1024)}, u32[]{:S(2)}) copy-start(f32[8192]{0:T(1024)} %get-tuple-element.23) | copy-start | bytes 98308
  334.2 40.4 %copy-start.19 = (f32[8192]{0:T(1024)S(1)}, f32[8192]{0:T(1024)}, u32[]{:S(2)}) copy-start(f32[8192]{0:T(1024)} %get-tuple-element.24) | copy-start | bytes 98308
  334.2 40.4 %copy-start.20 = (pred[8192]{0:T(1024)(128)(4,1)S(1)}, pred[8192]{0:T(1024)(128)(4,1)}, u32[]{:S(2)}) copy-start(pred[8192]{0:T(1024)(128)(4,1)} %or_and_fusion) | copy-start | bytes 24580
  334.2 40.4 %copy-start.28 = (s32[32]{0:T(128)S(1)}, s32[32]{0:T(128)}, u32[]{:S(2)}) copy-start(s32[32]{0:T(128)} %multiply_add_fusion) | copy-start | bytes 388
  334.2 40.4 %copy-start.30 = (f32[32]{0:T(128)S(1)}, f32[32]{0:T(128)}, u32[]{:S(2)}) copy-start(f32[32]{0:T(128)} %get-tuple-element.26) | copy-start | bytes 388
  334.2 40.4 %copy-start.37 = (f32[32]{0:T(128)S(1)}, f32[32]{0:T(128)}, u32[]{:S(2)}) copy-start(f32[32]{0:T(128)} %get-tuple-element.25) | copy-start | bytes 388
  334.2 40.4 %copy-start.40 = (pred[32]{0:T(512)(128)(4,1)S(1)}, pred[32]{0:T(512)(128)(4,1)}, u32[]{:S(2)}) copy-start(pred[32]{0:T(512)(128)(4,1)} %iota_compare_fusion.4) | copy-start | bytes 100
  430.1 6.1 %copy-start.8 = (f32[512,512,1]{1,0,2:T(8,128)S(1)}, f32[512,512,1]{1,0,2:T(8,128)}, u32[]{:S(2)}) copy-start(f32[512,512,1]{1,0,2:T(8,128)} %fusion.29) | copy-start | bytes 3145732
  430.1 6.1 %copy-start.9 = (f32[2,512,256]{2,1,0:T(8,128)S(1)}, f32[2,512,256]{2,1,0:T(8,128)}, u32[]{:S(2)}) copy-start(f32[2,512,256]{2,1,0:T(8,128)} %fusion.89) | copy-start | bytes 3145732
  431.5 10.6 %copy-start.14 = (f32[2,512,256]{1,2,0:T(8,128)S(1)}, f32[2,512,256]{1,2,0:T(8,128)}, u32[]{:S(2)}) copy-start(f32[2,512,256]{1,2,0:T(8,128)} %copy.215) | copy-start | bytes 3145732
  431.5 10.6 %collective-permute-start.9 = (f32[1,512,256]{1,2,0:T(8,128)S(1)}, f32[1,512,256]{1,2,0:T(8,128)S(1)}, u32[]{:S(2)}, u32[]{:S(2)}) collective-permute-start(f32[1,512,256]{1,2,0:T(8,128)S(1)} %get-tuple-element.16), channel_id=1, source_target_pairs={{1,0},{2,1},{3,2},{4,3},{5,4},{6,5},{7,6},{8,7},{9,8},{10,9},{11,1... | collective-permute-start | bytes 1572872 | tf_op jit(solution)/shard_map/ppermute | solution.py:17
where the time goes:
time: 451 us; the launch traced here: 445 us
  matrix products  119 us (26%)
  local copies, waits for them, and re-layouts  102 us (23%)
  blocking collectives  97.7 us (22%)
  waiting for transfers between devices  65 us (14%)
  starting transfers between devices  34.4 us (8%)
  other arithmetic  27 us (6%)
    all_to_all x2, blocking collectives, project(): lax.all_to_all(pressure_column, 'gz', split_axis=0, concat_axis=1, tiled=...  62.3 us
    all_to_all x1, blocking collectives, project(): lax.all_to_all(horizontal(source, basis_x, basis_y), 'gz', split_axis=1,...  35.4 us
    ppermute x2, waiting for transfers between devices, with_halo(): lax.ppermute(lax.slice_in_dim(block, block.shape[dim] - width, None, axis...  23.8 us
    scatter x4, local copies, waits for them, and re-layouts, inflow(): current.at[:, :, fringe_columns, :]  22.3 us
    all_to_all x1, waiting for transfers between devices, project(): lax.all_to_all(horizontal(source, basis_x, basis_y), 'gz', split_axis=1,...  20.3 us
    ppermute x6, waiting for transfers between devices, from_behind(): return lax.ppermute(block, axis, route)  20 us
    ppermute x6, starting transfers between devices, from_behind(): return lax.ppermute(block, axis, route)  16.5 us
    dot_general x4, matrix products, derivative_table(): jnp.dot(cosines * weight, sine_table.T, precision=highest)  16.4 us
  transfers between devices with their start and end apart: 11, of which 9 were waited for; matrix products, arithmetic and copies ran while one was open for 20% of the time, Pallas kernels for 0%

commit v1 on v0

v1 whole, which is shorter than its diff:
```python
import functools
import math

import jax
import jax.numpy as jnp
import ml_dtypes
import numpy as np
from jax import lax
from jax.experimental import pallas as pl
from jax.experimental.pallas import tpu as pltpu
from jax.sharding import Mesh
from jax.sharding import PartitionSpec as P

step_size = 0.1
drag_coef = 0.75
cell_width = 4.0
half_type = jnp.bfloat16
full_type = jnp.float32
vmem_bytes = 56 * 1024 * 1024
levels_axis = ("chip", "core")
every_axis = ("sec", "chip", "core")


def derivative_table(length, cutoff):
    offset = np.arange(length)
    wavenumber = np.arange(1, cutoff + 1)
    phases = offset[:, None] * wavenumber[None, :] % length
    waves = np.sin(2.0 * math.pi / length * phases)
    first = -(2.0 / (cell_width * length)) * (waves @ (2.0 * math.pi / length * wavenumber))
    return first[(offset[:, None] - offset[None, :]) % length]


def real_basis(length):
    midpoint = length // 2
    row = np.arange(length)
    wavenumber = np.where(row <= midpoint, row, row - midpoint)
    angles = 2.0 * math.pi / length * (wavenumber[:, None] * row[None, :] % length)
    scales = np.where((row == 0) | (row == midpoint), math.sqrt(1.0 / length), math.sqrt(2.0 / length))
    return scales[:, None] * np.where((row <= midpoint)[:, None], np.cos(angles), np.sin(angles))


def wave_square(length):
    midpoint = length // 2
    row = np.arange(length)
    wavenumber = np.where(row < midpoint, row, np.where(row == midpoint, 0, row - midpoint))
    return (2.0 * math.pi / (length * cell_width) * wavenumber) ** 2


def high_low(table):
    table = np.asarray(table, np.float32)
    high = table.astype(ml_dtypes.bfloat16)
    low = (table - high.astype(np.float32)).astype(ml_dtypes.bfloat16)
    return np.stack([high, low], axis=-3)


def build_tables(length_x, length_y):
    mid = length_x // 2
    full_x = derivative_table(length_x, length_x // 2 - 1)
    full_y = derivative_table(length_y, length_y // 2 - 1)
    basis_x = real_basis(length_x)
    basis_y = real_basis(length_y)
    left_part, right_part = full_x[:mid, :mid], full_x[:mid, mid:]
    derived = full_x @ basis_x.T
    squares = wave_square(length_x)[:, None] + wave_square(length_y)[None, :]
    decay = 2.0 * np.arcsinh(0.5 * np.sqrt(squares))
    return {
        "dealias_x": derivative_table(length_x, (length_x - 1) // 3).astype(ml_dtypes.bfloat16),
        "dealias_y": derivative_table(length_y, (length_y - 1) // 3).T.astype(ml_dtypes.bfloat16),
        "slope_x": high_low(np.stack([left_part + right_part, left_part - right_part])),
        "slope_y": high_low(full_y.T),
        "into_x": high_low(np.stack([basis_x[0::2, :mid], basis_x[1::2, :mid]])),
        "into_y": high_low(basis_y.T),
        "from_x": high_low(np.stack([basis_x[0::2, :mid].T, basis_x[1::2, :mid].T])),
        "from_y": high_low(basis_y),
        "from_slope_x": high_low(np.stack([derived[:mid, 0::2], derived[:mid, 1::2]])),
        "from_slope_y": high_low(basis_y @ full_y.T),
        "decay": np.stack([decay[0::2], decay[1::2]]).astype(np.float32),
    }


def product(one, other):
    return jnp.dot(one, other, preferred_element_type=full_type)


def halves(block):
    high = block.astype(half_type)
    return high, (block - high.astype(full_type)).astype(half_type)


def from_left(table, block):
    high, low = halves(block)
    return product(table[0], high) + product(table[0], low) + product(table[1], high)


def from_right(block, table):
    high, low = halves(block)
    return product(high, table[0]) + product(low, table[0]) + product(high, table[1])


def vmem():
    return pl.BlockSpec(memory_space=pltpu.VMEM)


def smem():
    return pl.BlockSpec(memory_space=pltpu.SMEM)


def hbm():
    return pl.BlockSpec(memory_space=pl.ANY)


def call(kernel, outs, in_specs, scratch, flops, args):
    moved = sum(math.prod(a.shape) * 4 for a in (*outs, *args))
    return pl.pallas_call(
        kernel,
        out_shape=outs,
        in_specs=in_specs,
        out_specs=tuple(vmem() for _ in outs),
        scratch_shapes=scratch,
        compiler_params=pltpu.CompilerParams(vmem_limit_bytes=vmem_bytes),
        cost_estimate=pl.CostEstimate(flops=int(flops), bytes_accessed=moved, transcendentals=0),
    )(*args)


def shaped(*dims, kind=full_type):
    return jax.ShapeDtypeStruct(dims, kind)


def insert_columns(target, columns, low, high, index, depth):
    def one(i, carry):
        row = pl.ds(index[i], 1)
        here = pl.ds(i, 1)
        for c in range(3):
            target[c, 0, row, :] = low[c, here, :]
            for z in range(depth):
                target[c, 1 + z, row, :] = columns[c, z, here, :]
            target[c, 1 + depth, row, :] = high[c, here, :]
        return carry

    lax.fori_loop(0, index.shape[0], one, 0)


def tendency_steps(state, rounded, viscosity, mask, drag, dealias_x, dealias_y, put):
    depth = state.shape[1] - 2
    length_x = state.shape[2]
    rows = length_x // 2

    def level(z, carry):
        for c in range(3):
            rounded[c] = state[c, z + 1].astype(half_type)

        def block(b, inner):
            part = pl.ds(pl.multiple_of(b * rows, rows), rows)
            u, v, w = (state[c, z + 1, part, :] for c in range(3))
            slow = drag * mask[z, part, :].astype(full_type) * jnp.abs(u)
            nu = viscosity[z, part, :]
            for c in range(3):
                center = state[c, z + 1, part, :]
                upper = state[c, z + 2, part, :]
                lower = state[c, z, part, :]
                grad_x = product(dealias_x[part, :], rounded[c])
                grad_y = product(rounded[c, part, :], dealias_y[...])
                advected = u * grad_x + v * grad_y + w * (0.5 * (upper - lower))
                change = nu * (upper - 2.0 * center + lower) - advected - slow * center
                put(c, z, part, center, change)
            return inner

        lax.fori_loop(0, length_x // rows, block, 0)
        return carry

    lax.fori_loop(0, depth, level, 0)


def folded(block, sign):
    mid = block.shape[0] // 2
    return block[:mid] + sign * block[mid:]


def source_spectra(state, parts, core, slope_x, slope_y, into_x, into_y, sources):
    depth = state.shape[1]
    for slot, out in enumerate(parts):
        half = core if slot == 0 else 1 - core
        sign = (1 - 2 * half).astype(full_type)

        def level(z, carry, half=half, sign=sign):
            w = folded(state[2, z], sign)
            below = folded(state[2, jnp.maximum(z - 1, 0)], sign)
            spread = from_left(slope_x[half], folded(state[0, z], sign))
            spread += from_right(folded(state[1, z], sign), slope_y)
            sources[z] = spread + w - jnp.where(z > 0, below, 0.0)
            return carry

        lax.fori_loop(0, depth, level, 0)
        sources[depth] = folded(state[2, depth - 1], sign)

        def transform(i, carry, half=half, out=out):
            out[i] = from_right(from_left(into_x[half], sources[i]), into_y)
            return carry

        lax.fori_loop(0, depth + 1, transform, 0)


def first_kernel(
    flags, index, velocity, low, high, columns, columns_low, columns_high, viscosity, mask,
    dealias_x, dealias_y, slope_x, slope_y, into_x, into_y,
    middle, upward, downward, mine, theirs,
    state, rounded, sources, slopes, sems,
):
    depth = middle.shape[1]
    mid = middle.shape[2] // 2
    is_farm, core, is_lid = flags[0], flags[1], flags[3]
    copies = [
        pltpu.make_async_copy(velocity, state.at[:, pl.ds(1, depth)], sems.at[0]),
        pltpu.make_async_copy(low, state.at[:, 0], sems.at[1]),
        pltpu.make_async_copy(high, state.at[:, depth + 1], sems.at[2]),
    ]
    for copy in copies:
        copy.start()
    for copy in copies:
        copy.wait()

    @pl.when(is_farm == 1)
    def _():
        insert_columns(state, columns, columns_low, columns_high, index, depth)

    drag = drag_coef * is_farm.astype(full_type)

    def put(c, z, part, center, change):
        moved = center + step_size * change
        if c == 2:
            moved = jnp.where((is_lid == 1) & (z == depth - 1), 0.0, moved)
        middle[c, z, part, :] = moved

    tendency_steps(state, rounded, viscosity, mask, drag, dealias_x, dealias_y, put)
    source_spectra(middle, (mine, theirs), core, slope_x, slope_y, into_x, into_y, sources)
    downward[0] = middle[0, 0]
    downward[1] = middle[1, 0]
    top = depth - 1
    for half in range(2):
        slopes[half] = from_left(slope_x[half], folded(middle[2, top], 1.0 - 2.0 * half))
    upward[0, :mid] = middle[0, top, :mid] + 0.5 * (slopes[0] + slopes[1])
    upward[0, mid:] = middle[0, top, mid:] + 0.5 * (slopes[0] - slopes[1])
    upward[1] = middle[1, top] + from_right(middle[2, top], slope_y)


def second_kernel(
    flags, index, extended, columns, velocity, start_columns, viscosity, mask,
    dealias_x, dealias_y, slope_x, slope_y, into_x, into_y,
    final, mine, theirs,
    state, start, rounded, sources, sems,
):
    depth = final.shape[1]
    is_farm, core, is_lid = flags[0], flags[1], flags[3]
    copies = [
        pltpu.make_async_copy(extended, state, sems.at[0]),
        pltpu.make_async_copy(velocity, start, sems.at[1]),
    ]
    for copy in copies:
        copy.start()
    for copy in copies:
        copy.wait()

    @pl.when(is_farm == 1)
    def _():
        def one(i, carry):
            row = pl.ds(index[i], 1)
            here = pl.ds(i, 1)
            for c in range(3):
                for z in range(depth + 2):
                    state[c, z, row, :] = columns[c, z, here, :]
                for z in range(depth):
                    start[c, z, row, :] = start_columns[c, z, here, :]
            return carry

        lax.fori_loop(0, index.shape[0], one, 0)

    drag = drag_coef * is_farm.astype(full_type)

    def put(c, z, part, center, change):
        moved = 0.5 * (start[c, z, part, :] + center + step_size * change)
        if c == 2:
            moved = jnp.where((is_lid == 1) & (z == depth - 1), 0.0, moved)
        final[c, z, part, :] = moved

    tendency_steps(state, rounded, viscosity, mask, drag, dealias_x, dealias_y, put)
    source_spectra(final, (mine, theirs), core, slope_x, slope_y, into_x, into_y, sources)


def chip_levels(core, mine, other, depth):
    is_low = core == 0
    low = [jnp.where(is_low, mine[i], other[i]) for i in range(depth + 1)]
    high = [jnp.where(is_low, other[i], mine[i]) for i in range(depth + 1)]
    levels = low[:depth] + [high[0] - low[depth]] + high[1:depth]
    return levels, low[depth], high[depth]


class Coefficients:
    def __init__(self, stacked, count):
        self.mu = lambda: stacked[0]
        self.phi = lambda i: stacked[1 + i]
        self.psi = lambda i: stacked[2 + count + i]
        self.flux_low = lambda i: stacked[3 + 2 * count + i]
        self.flux_high = lambda i: stacked[3 + 3 * count + i]
        self.entry = lambda: stacked[4 + 4 * count]
        self.scale = lambda: stacked[5 + 4 * count]


def gather_kernel(flags, mine, other, stacked, out, work):
    core = flags[1]
    depth = mine.shape[0] - 1
    count = 2 * depth
    tables = Coefficients(stacked, count)
    levels, _, top = chip_levels(core, mine, other, depth)
    mu = tables.mu()
    forward = tables.phi(0) * levels[0]
    for i in range(1, count):
        forward = mu * forward + tables.phi(i) * levels[i]
    work[0] = mu * forward - tables.phi(count) * top
    backward = -tables.psi(count) * top
    for i in reversed(range(count)):
        backward = tables.psi(i) * levels[i] + mu * backward
    work[1] = backward
    chips = out.shape[0]
    rows = out.shape[1] // 2
    for chip in range(chips):
        out[chip, :rows] = work[0, chip * rows : (chip + 1) * rows]
        out[chip, rows:] = work[1, chip * rows : (chip + 1) * rows]


def scan_kernel(received, ratio, out):
    chips = received.shape[0]
    rows = received.shape[1] // 2
    factor = ratio[...]
    carried = jnp.zeros_like(factor)
    for chip in range(chips):
        out[chip, :rows] = carried
        carried = factor * carried + received[chip, :rows]
    carried = jnp.zeros_like(factor)
    for chip in reversed(range(chips)):
        out[chip, rows:] = carried
        carried = factor * carried + received[chip, rows:]


def solve_kernel(flags, mine, other, stacked, scanned, own, partner, work):
    core = flags[1]
    depth = mine.shape[0] - 1
    count = 2 * depth
    tables = Coefficients(stacked, count)
    chips = scanned.shape[0]
    rows = scanned.shape[1] // 2
    for chip in range(chips):
        work[0, chip * rows : (chip + 1) * rows] = scanned[chip, :rows]
        work[1, chip * rows : (chip + 1) * rows] = scanned[chip, rows:]
    levels, between, top = chip_levels(core, mine, other, depth)
    mu = tables.mu()
    forward = [work[0] + tables.phi(0) * levels[0]]
    for i in range(1, count):
        forward.append(mu * forward[-1] + tables.phi(i) * levels[i])
    backward = [work[1] - tables.psi(count) * top]
    for i in reversed(range(1, count)):
        backward.append(tables.psi(i) * levels[i] + mu * backward[-1])
    backward.reverse()
    flux = [
        tables.flux_low(i) * forward[i] - tables.flux_high(i + 1) * backward[i]
        for i in range(count)
    ]
    under = tables.entry() * work[0] - tables.flux_high(0) * (
        tables.psi(0) * levels[0] + mu * backward[0]
    )
    pressure = [
        -tables.scale() * (tables.psi(i) * forward[i] + mu * tables.phi(i) * backward[i])
        for i in (0, depth)
    ]
    low = [pressure[0], *flux[:depth], under]
    high = [pressure[1], *flux[depth:], flux[depth - 1] - between]
    is_low = core == 0
    for i in range(depth + 2):
        own[i] = jnp.where(is_low, low[i], high[i])
        partner[i] = jnp.where(is_low, high[i], low[i])


def physical_fields(core, mine, other, from_x, from_y, from_slope_x, from_slope_y, spectra, slots, ghosts):
    depth = mine.shape[0] - 2
    pressures = depth + 2 if ghosts else depth
    first = 1 if ghosts else 0
    lifts = depth + 1 if ghosts else depth
    for half in range(2):
        chosen = [jnp.where(core == half, mine[i], other[i]) for i in range(depth + 2)]
        level = chosen[0]
        if ghosts:
            spectra[half, 0] = level - chosen[depth + 1]
        for z in range(depth):
            spectra[half, first + z] = level
            level = level + chosen[1 + z]
        if ghosts:
            spectra[half, first + depth] = level
        for z in range(lifts):
            spectra[half, pressures + z] = chosen[1 + z]

    def one(half, carry):
        def pressure(i, inner):
            block = spectra[half, i]
            slots[2 * i, half] = from_left(from_slope_x[half], from_right(block, from_y))
            slots[2 * i + 1, half] = from_left(from_x[half], from_right(block, from_slope_y))
            return inner

        lax.fori_loop(0, pressures, pressure, 0)

        def lift(i, inner):
            block = spectra[half, pressures + i]
            slots[2 * pressures + i, half] = from_left(from_x[half], from_right(block, from_y))
            return inner

        lax.fori_loop(0, lifts, lift, 0)
        return carry

    lax.fori_loop(0, 2, one, 0)


def unfolded(slots, i):
    return slots[i, 0] + slots[i, 1], slots[i, 0] - slots[i, 1]


def corrected_kernel(
    flags, mine, other, middle, from_below, from_above, slope_x, slope_y,
    from_x, from_y, from_slope_x, from_slope_y, index,
    out, columns,
    spectra, slots,
):
    core, is_floor, is_lid = flags[1], flags[2], flags[3]
    depth = middle.shape[1]
    mid = middle.shape[2] // 2
    physical_fields(
        core, mine, other, from_x, from_y, from_slope_x, from_slope_y, spectra, slots, True
    )
    pressures = depth + 2
    open_low = (1 - is_floor).astype(full_type)
    open_high = (1 - is_lid).astype(full_type)
    sides = (slice(0, mid), slice(mid, 2 * mid))
    for z in range(depth):
        for c in range(3):
            slot = 2 * (1 + z) + c if c < 2 else 2 * pressures + z
            for side, change in zip(sides, unfolded(slots, slot)):
                out[c, 1 + z, side] = middle[c, z, side] - change
    for c in range(2):
        for side, change in zip(sides, unfolded(slots, c)):
            out[c, 0, side] = open_low * (from_below[c, side] - change)
        for side, change in zip(sides, unfolded(slots, 2 * (depth + 1) + c)):
            out[c, depth + 1, side] = open_high * (from_above[c, side] - change)
    for side, change in zip(sides, unfolded(slots, 2 * pressures + depth)):
        out[2, 0, side] = -open_low * change
    for half in range(2):
        slots[0, half] = 0.5 * from_left(
            slope_x[half], folded(out[0, depth + 1], 1.0 - 2.0 * half)
        )
    for side, change in zip(sides, unfolded(slots, 0)):
        spread = change + from_right(out[1, depth + 1, side], slope_y)
        out[2, depth + 1, side] = open_high * (out[2, depth, side] - spread)

    def one(i, carry):
        row = pl.ds(index[i], 1)
        for c in range(3):
            for z in range(depth + 2):
                columns[c, z, pl.ds(i, 1), :] = out[c, z, row, :]
        return carry

    lax.fori_loop(0, index.shape[0], one, 0)


def last_kernel(
    flags, mine, other, final, from_x, from_y, from_slope_x, from_slope_y,
    out,
    spectra, slots,
):
    core = flags[1]
    depth = final.shape[1]
    mid = final.shape[2] // 2
    physical_fields(
        core, mine, other, from_x, from_y, from_slope_x, from_slope_y, spectra, slots, False
    )
    sides = (slice(0, mid), slice(mid, 2 * mid))
    for z in range(depth):
        for c in range(3):
            slot = 2 * z + c if c < 2 else 2 * depth + z
            for side, change in zip(sides, unfolded(slots, slot)):
                out[c, z, side] = final[c, z, side] - change


def coefficients(decay, first_level, count, height):
    def gap(steps):
        return -jnp.expm1(-steps * decay)

    still = decay == 0.0
    below = jnp.arange(count + 1, dtype=full_type)[:, None, None] + first_level
    mu = jnp.exp(-decay)
    safe = jnp.where(still, 1.0, gap(2.0 * height))

    def ratio(steps):
        return jnp.where(still, steps / height, gap(2.0 * steps) / safe)

    share = 1.0 / (1.0 + mu)
    phi = 1.0 + jnp.exp(-(2.0 * below + 1.0) * decay)
    psi = 1.0 + jnp.exp(-(2.0 * (height - below) - 1.0) * decay)
    flux_low = mu * share * ratio(height - 1.0 - below[:count])
    flux_high = mu * share * ratio(below)
    entry = share * ratio(height - below[:1])
    scale = jnp.where(still, 0.0, mu / (jnp.where(still, 1.0, gap(2.0)) * safe))
    return jnp.concatenate([mu[None], phi, psi, flux_low, flux_high, entry, scale[None]])


def local(velocity, eddy_viscosity, turbine_mask, fringe_columns):
    current = velocity[0]
    viscosity = eddy_viscosity[0]
    _, depth, length_x, length_y = current.shape
    mid = length_x // 2
    fringe = fringe_columns.shape[0]
    chips = lax.axis_size("chip")
    devices = 2 * chips
    height = devices * depth
    count = 2 * depth
    rows = mid // chips
    section = lax.axis_index("sec")
    chip = lax.axis_index("chip")
    core = lax.axis_index("core")
    place = 2 * chip + core
    is_farm = section == 1
    flags = jnp.stack([is_farm, core, place == 0, place == devices - 1]).astype(jnp.int32)
    tables = {name: jnp.asarray(table) for name, table in build_tables(length_x, length_y).items()}

    upward_route = [(i, i + 1) for i in range(devices - 1)]
    downward_route = [(i + 1, i) for i in range(devices - 1)]
    swap = [(0, 1), (1, 0)]

    def across(shift):
        return [
            (i, devices + i + shift) for i in range(devices) if 0 <= i + shift < devices
        ]

    low = lax.ppermute(current[:, depth - 1], levels_axis, upward_route)
    high = lax.ppermute(current[:, 0], levels_axis, downward_route)
    taken = current[:, :, fringe_columns, :]
    columns = lax.ppermute(taken, every_axis, across(0))
    columns_low = lax.ppermute(taken[:, depth - 1], every_axis, across(1))
    columns_high = lax.ppermute(taken[:, 0], every_axis, across(-1))

    decay = lax.dynamic_index_in_dim(tables["decay"], core, 0, keepdims=False)
    stacked = coefficients(decay, (chip * count).astype(full_type), count, float(height))
    ratio = jnp.exp(-float(count) * lax.dynamic_slice_in_dim(decay, chip * rows, rows, 0))

    block = length_x * length_y * 2
    spectrum = shaped(depth + 1, mid, length_y)
    solved = shaped(depth + 2, mid, length_y)
    message = shaped(chips, 2 * rows, length_y)
    tendency_tables = [tables["dealias_x"], tables["dealias_y"]]
    source_tables = [tables[n] for n in ("slope_x", "slope_y", "into_x", "into_y")]
    pressure_tables = [tables[n] for n in ("from_x", "from_y", "from_slope_x", "from_slope_y")]

    def solve(mine, theirs):
        other = lax.ppermute(theirs, "core", swap)
        (sums,) = call(
            gather_kernel, (message,), [smem(), vmem(), vmem(), vmem()],
            [pltpu.VMEM((2, mid, length_y), full_type)], 8 * count * block,
            (flags, mine, other, stacked),
        )
        sums = lax.all_to_all(sums, "chip", split_axis=0, concat_axis=0, tiled=True)
        (sums,) = call(scan_kernel, (message,), [vmem(), vmem()], [], 4 * block, (sums, ratio))
        sums = lax.all_to_all(sums, "chip", split_axis=0, concat_axis=0, tiled=True)
        own, partner = call(
            solve_kernel, (solved, solved), [smem()] + [vmem()] * 4,
            [pltpu.VMEM((2, mid, length_y), full_type)], 16 * count * block,
            (flags, mine, other, stacked, sums),
        )
        return own, lax.ppermute(partner, "core", swap)

    state_shape = (3, depth + 2, length_x, length_y)
    sources = pltpu.VMEM((depth + 1, mid, length_y), full_type)
    rounded = pltpu.VMEM((3, length_x, length_y), half_type)
    own_shape = shaped(3, depth, length_x, length_y)
    edge = shaped(2, length_x, length_y)
    tendency_flops = 3 * depth * block * (length_x + length_y)
    source_flops = 3 * depth * block * (length_x + 2 * length_y)

    middle, upward, downward, mine, theirs = call(
        first_kernel,
        (own_shape, edge, edge, spectrum, spectrum),
        [smem(), smem()] + [hbm()] * 3 + [vmem()] * 11,
        [
            pltpu.VMEM(state_shape, full_type), rounded, sources,
            pltpu.VMEM((2, mid, length_y), full_type), pltpu.SemaphoreType.DMA((3,)),
        ],
        tendency_flops + source_flops,
        (flags, fringe_columns, current, low, high, columns, columns_low, columns_high,
         viscosity, turbine_mask, *tendency_tables, *source_tables),
    )
    own, partner = solve(mine, theirs)
    from_below = lax.ppermute(upward, levels_axis, upward_route)
    from_above = lax.ppermute(downward, levels_axis, downward_route)
    fields = 3 * depth + 5
    extended, bands = call(
        corrected_kernel,
        (shaped(*state_shape), shaped(3, depth + 2, fringe, length_y)),
        [smem()] + [vmem()] * 11 + [smem()],
        [
            pltpu.VMEM((2, 2 * depth + 3, mid, length_y), full_type),
            pltpu.VMEM((fields, 2, mid, length_y), full_type),
        ],
        3 * fields * block * (length_x // 2 + length_y),
        (flags, own, partner, middle, from_below, from_above, tables["slope_x"],
         tables["slope_y"], *pressure_tables, fringe_columns),
    )
    bands = lax.ppermute(bands, "sec", [(0, 1)])
    final, mine, theirs = call(
        second_kernel,
        (own_shape, spectrum, spectrum),
        [smem(), smem(), hbm(), vmem(), hbm()] + [vmem()] * 9,
        [
            pltpu.VMEM(state_shape, full_type), pltpu.VMEM(own_shape.shape, full_type),
            rounded, sources, pltpu.SemaphoreType.DMA((2,)),
        ],
        tendency_flops + source_flops,
        (flags, fringe_columns, extended, bands, current, columns, viscosity, turbine_mask,
         *tendency_tables, *source_tables),
    )
    own, partner = solve(mine, theirs)
    fields = 3 * depth
    (new,) = call(
        last_kernel,
        (own_shape,),
        [smem()] + [vmem()] * 7,
        [
            pltpu.VMEM((2, 2 * depth, mid, length_y), full_type),
            pltpu.VMEM((fields, 2, mid, length_y), full_type),
        ],
        3 * fields * block * (length_x // 2 + length_y),
        (flags, own, partner, final, *pressure_tables),
    )
    return new[None]


def solution(mesh):
    sections, devices = mesh.devices.shape
    fine = Mesh(mesh.devices.reshape(sections, devices // 2, 2), every_axis)
    placed = (
        P("sec", None, levels_axis, None, None),
        P("sec", levels_axis, None, None),
        P(levels_axis, None, None),
        P(),
    )
    return jax.shard_map(
        local,
        mesh=fine,
        in_specs=placed,
        out_specs=P("sec", None, levels_axis, None, None),
        check_vma=False,
    )
```

time: 451 us -> 269 us (0.60); the launches traced: 445 us -> 268 us
  matrix products: 119 us -> 0 us
  Pallas kernels: 0 us -> 88.2 us
  local copies, waits for them, and re-layouts: 102 us -> 20.3 us
  blocking collectives: 97.7 us -> 37.7 us
  other arithmetic: 27 us -> 5.97 us
  waiting for transfers between devices: 65 us -> 77.2 us
    dot_general x32 -> x0, matrix products: 119 us -> none  [the longest x4 16.4 us: derivative_table(): jnp.dot(cosines * weight, sine_table.T, precision=highest)]
    pallas_call x0 -> x10, Pallas kernels: none -> 88.2 us  [call(): pl.pallas_call(kernel, out_shape=outs, in_specs=in_specs, out_specs=tuple...]
    all_to_all x3 -> x2, blocking collectives: 97.7 us -> 37.7 us  [solve(): sums = lax.all_to_all(sums, 'chip', split_axis=0, concat_axis=0, tiled=True)]
    all_to_all x10 -> x0, local copies, waits for them, and re-layouts: 24.7 us -> none  [the longest x6 15.8 us: project(): lax.all_to_all(horizontal(source, basis_x, basis_y), 'gz', split_axis=1,...]
    scatter x4 -> x0, local copies, waits for them, and re-layouts: 22.3 us -> none  [inflow(): current.at[:, :, fringe_columns, :]]
    mul x9 -> x0, local copies, waits for them, and re-layouts: 18.9 us -> none  [the longest x2 4.57 us: tendency(): current[0] * grad_x + current[1] * grad_y + current[2] * grad_z]
    ppermute x10 -> x12, waiting for transfers between devices: 44.6 us -> 56.6 us  [the longest x1 15.6 us: local(): columns_high = lax.ppermute(taken[:, 0], every_axis, across(-1))]
    all_to_all x1 -> x2, starting transfers between devices: 6.18 us -> 17.7 us  [solve(): sums = lax.all_to_all(sums, 'chip', split_axis=0, concat_axis=0, tiled=True)]
  transfers between devices with their start and end apart: 11 -> 14, of which waited for: 9 -> 9; matrix products, arithmetic and copies ran while one was open for 20% -> 3% of each run, Pallas kernels for 0% -> 2%
where the time goes in v1:
time: 269 us; the launch traced here: 268 us
  Pallas kernels  88.2 us (33%)
  waiting for transfers between devices  77.2 us (29%)
  starting transfers between devices  38.8 us (14%)
  blocking collectives  37.7 us (14%)
  local copies, waits for them, and re-layouts  20.3 us (8%)
  other arithmetic  5.97 us (2%)
    pallas_call x10, Pallas kernels, call(): pl.pallas_call(kernel, out_shape=outs, in_specs=in_specs, out_specs=tuple...  88.2 us
    all_to_all x2, blocking collectives, solve(): sums = lax.all_to_all(sums, 'chip', split_axis=0, concat_axis=0, tiled=True)  37.7 us
    all_to_all x2, waiting for transfers between devices, solve(): sums = lax.all_to_all(sums, 'chip', split_axis=0, concat_axis=0, tiled=True)  20.6 us
    all_to_all x2, starting transfers between devices, solve(): sums = lax.all_to_all(sums, 'chip', split_axis=0, concat_axis=0, tiled=True)  17.7 us
    ppermute x1, waiting for transfers between devices, local(): columns_high = lax.ppermute(taken[:, 0], every_axis, across(-1))  15.6 us
    ppermute x1, waiting for transfers between devices, local(): bands = lax.ppermute(bands, 'sec', [(0, 1)])  14.8 us
    ppermute x1, waiting for transfers between devices, local(): low = lax.ppermute(current[:, depth - 1], levels_axis, upward_route)  12.2 us
    ppermute x1, waiting for transfers between devices, local(): from_below = lax.ppermute(upward, levels_axis, upward_route)  8.24 us
  transfers between devices with their start and end apart: 14, of which 9 were waited for; matrix products, arithmetic and copies ran while one was open for 3% of the time, Pallas kernels for 2%

profile of v1, /device:TPU:5, one launch (start us, length us, event | category | flops | bytes accessed | tf_op | source)
XLA Modules:
  0.0 268.5 jit_solution(17378012418934274532)
XLA Ops:
  0.0 0.7 compare_select_fusion
  0.7 6.1 %copy.16 = f32[3,2,512,256]{3,1,2,0:T(2,128)} copy(f32[3,2,512,256]{3,2,1,0:T(8,128)} %bitcast.35) | data formatting | bytes 6291456 | tf_op jit(solution)/shard_map/squeeze | solution.py:512
  6.8 3.6 %gather_fusion = f32[64,3,2,256]{3,2,1,0:T(2,128)} fusion(f32[3,2,512,256]{3,1,2,0:T(2,128)} %copy.16, s32[1024]{0:T(1024)S(1)} %pad_clamp_fusion), kind=kCustom, calls=%fused_computation | custom fusion | bytes 786688 | tf_op jit(solution)/shard_map/gather | solution.py:541
  10.4 1.0 copy.19
  11.5 1.3 collective-permute-start.2
  12.8 1.9 slice_bitcast_fusion
  14.6 2.7 %collective-permute-start.1 = (f32[3,512,256]{2,1,0:T(8,128)}, f32[3,512,256]{2,1,0:T(8,128)}, u32[]{:S(2)}, u32[]{:S(2)}) collective-permute-start(f32[3,512,256]{2,1,0:T(8,128)} %get-tuple-element.33), channel_id=1, source_target_pairs={{1,0},{2,1},{3,2},{4,3},{5,4},{6,5},{7,6},{8,7},{9,8},{10,9},{11,1... | collective-permute-start | bytes 4718600 | tf_op jit(solution)/shard_map/ppermute | solution.py:540
  17.4 3.0 %collective-permute-start = (f32[3,512,256]{2,1,0:T(8,128)}, f32[3,512,256]{2,1,0:T(8,128)}, u32[]{:S(2)}, u32[]{:S(2)}) collective-permute-start(f32[3,512,256]{2,1,0:T(8,128)} %get-tuple-element.34), channel_id=1, source_target_pairs={{0,1},{1,2},{2,3},{3,4},{4,5},{5,6},{6,7},{7,8},{8,9},{9,10},{10,1... | collective-permute-start | bytes 4718600 | tf_op jit(solution)/shard_map/ppermute | solution.py:539
  20.4 1.3 collective-permute-start.4
  21.7 1.3 collective-permute-start.3
  23.1 1.1 fusion.14
  24.2 0.2 add_dynamic-update-slice_fusion.1
  24.4 0.2 add_dynamic-update-slice_fusion
  24.7 0.7 pad_add_fusion.flags
  25.4 0.7 broadcast_compare_fusion
  26.1 15.6 %collective-permute-done.4.columns_high = f32[3,64,256]{2,1,0:T(8,128)S(1)} collective-permute-done((f32[3,64,256]{2,1,0:T(8,128)S(1)}, f32[3,64,256]{2,1,0:T(8,128)S(1)}, u32[]{:S(2)}, u32[]{:S(2)}) %collective-permute-start.4) | collective-permute-done | bytes 196640 | tf_op jit(solution)/shard_map/ppermute | solution.py:544
  41.7 0.0 collective-permute-done.3.columns_low
  41.7 0.0 collective-permute-done.2.columns.start_columns
  41.7 0.0 collective-permute-done.1.high
  41.7 12.2 %collective-permute-done.low = f32[3,512,256]{2,1,0:T(8,128)} collective-permute-done((f32[3,512,256]{2,1,0:T(8,128)}, f32[3,512,256]{2,1,0:T(8,128)}, u32[]{:S(2)}, u32[]{:S(2)}) %collective-permute-start) | collective-permute-done | bytes 1572896 | tf_op jit(solution)/shard_map/ppermute | solution.py:539
  53.9 16.5 %shard_map.145 = (f32[3,2,512,256]{3,2,1,0:T(8,128)}, f32[2,512,256]{2,1,0:T(8,128)}, f32[2,512,256]{2,1,0:T(8,128)}, f32[3,256,256]{2,1,0:T(8,128)}, f32[3,256,256]{2,1,0:T(8,128)}) custom-call(s32[4]{0:T(128)} %pad_add_fusion.flags, s32[64]{0:T(128)} %index.5, f32[3,2,512,256]{3,2,1,0:T(8,128)} %bitcast.36, f32[3,512,256]{2,1,0:T(8,128)} %collective-permute-done.low, ...), custom_call_target="tpu_custom_call" | custom-call | flops 2818572288 | bytes 20447504 | tf_op jit(solution)/shard_map/pallas_call | solution.py:114
  70.4 0.1 collective-permute-start.5
  70.4 0.5 multiply_dynamic-update-slice_fusion.1
  71.0 0.6 multiply_dynamic-update-slice_fusion
  71.6 0.3 fusion.5
  71.9 0.3 fusion.8.stacked
  72.2 0.7 collective-permute-done.5.other
  72.9 1.7 copy-done
  74.6 0.3 copy-done.2
  74.9 4.2 %shard_map.146 = f32[8,64,256]{2,1,0:T(8,128)} custom-call(s32[4]{0:T(128)} %pad_add_fusion.flags, f32[3,256,256]{2,1,0:T(8,128)} %get-tuple-element.19.mine, f32[3,256,256]{2,1,0:T(8,128)} %copy-done.2, f32[22,256,256]{2,1,0:T(8,128)} %copy-done), custom_call_target="tpu_custom_call" | custom-call | flops 8388608 | bytes 7864336 | tf_op jit(solution)/shard_map/pallas_call | solution.py:114
  79.2 13.3 %all-to-all-start = ((f32[8,64,256]{2,1,0:T(8,128)}), f32[8,64,256]{2,1,0:T(8,128)S(1)}, u32[]{:S(2)}, u32[]{:S(2)}) async-start(f32[8,64,256]{2,1,0:T(8,128)} %shard_map.146), calls=%async_computation | async-start | bytes 1048576 | tf_op jit(solution)/shard_map/all_to_all | solution.py:565
  92.5 0.6 exponential_bitcast_fusion.ratio
  93.1 13.4 %all-to-all-done.received = f32[8,64,256]{2,1,0:T(8,128)S(1)} async-done(((f32[8,64,256]{2,1,0:T(8,128)}), f32[8,64,256]{2,1,0:T(8,128)S(1)}, u32[]{:S(2)}, u32[]{:S(2)}) %all-to-all-start) | async-done | bytes 524320 | tf_op jit(solution)/shard_map/all_to_all | solution.py:565
  106.5 0.8 copy-done.6
  107.3 1.9 shard_map.147
  109.2 4.3 %all-to-all-start.1 = ((f32[8,64,256]{2,1,0:T(8,128)}), f32[8,64,256]{2,1,0:T(8,128)S(1)}, u32[]{:S(2)}, u32[]{:S(2)}) async-start(f32[8,64,256]{2,1,0:T(8,128)} %shard_map.147), calls=%async_computation.1 | async-start | bytes 1048576 | tf_op jit(solution)/shard_map/all_to_all | solution.py:567
  113.5 4.3 %collective-permute-start.7 = (f32[2,512,256]{2,1,0:T(8,128)}, f32[2,512,256]{2,1,0:T(8,128)S(1)}, u32[]{:S(2)}, u32[]{:S(2)}) collective-permute-start(f32[2,512,256]{2,1,0:T(8,128)} %get-tuple-element.24), channel_id=1, source_target_pairs={{0,1},{1,2},{2,3},{3,4},{4,5},{5,6},{6,7},{7,8},{8,9},{9,10},{10,1... | collective-permute-start | bytes 3145736 | tf_op jit(solution)/shard_map/ppermute | solution.py:596
  117.8 2.1 collective-permute-start.8
  119.9 7.2 %all-to-all-done.1.scanned = f32[8,64,256]{2,1,0:T(8,128)S(1)} async-done(((f32[8,64,256]{2,1,0:T(8,128)}), f32[8,64,256]{2,1,0:T(8,128)S(1)}, u32[]{:S(2)}, u32[]{:S(2)}) %all-to-all-start.1) | async-done | bytes 524320 | tf_op jit(solution)/shard_map/all_to_all | solution.py:567
  127.2 0.8 copy-done.5
  128.0 5.3 %shard_map.148 = (f32[4,256,256]{2,1,0:T(8,128)}, f32[4,256,256]{2,1,0:T(8,128)}) custom-call(s32[4]{0:T(128)} %pad_add_fusion.flags, f32[3,256,256]{2,1,0:T(8,128)} %get-tuple-element.19.mine, f32[3,256,256]{2,1,0:T(8,128)} %copy-done.2, f32[22,256,256]{2,1,0:T(8,128)} %copy-done, f32[8,64,256]{2,1,0:T(8,128)} %copy-done.5), custom_call_target="tpu_custom_call" | custom-call | flops 16777216 | bytes 9961488 | tf_op jit(solution)/shard_map/pallas_call | solution.py:114
  133.3 1.9 collective-permute-start.6
  135.2 8.2 %collective-permute-done.7.from_below = f32[2,512,256]{2,1,0:T(8,128)S(1)} collective-permute-done((f32[2,512,256]{2,1,0:T(8,128)}, f32[2,512,256]{2,1,0:T(8,128)S(1)}, u32[]{:S(2)}, u32[]{:S(2)}) %collective-permute-start.7) | collective-permute-done | bytes 1048608 | tf_op jit(solution)/shard_map/ppermute | solution.py:596
  143.4 0.0 collective-permute-done.8.from_above
  143.4 0.0 collective-permute-done.6.other
  143.4 1.0 copy-done.13
  144.4 0.3 copy-done.14
  144.7 20.3 %shard_map.149 = (f32[3,4,512,256]{3,2,1,0:T(8,128)}, f32[3,4,64,256]{3,2,1,0:T(8,128)}) custom-call(s32[4]{0:T(128)} %pad_add_fusion.flags, f32[4,256,256]{2,1,0:T(8,128)} %get-tuple-element.21.mine, f32[4,256,256]{2,1,0:T(8,128)} %copy-done.14, f32[3,2,512,256]{3,2,1,0:T(8,128)} %get-tuple-element.23.middle, f32[2,512,256]{2,1,0:T(8,128)} %copy-done.13, ...), custom_call_target="tpu_custom_call" | custom-call | flops 4429185024 | bytes 19136784 | tf_op jit(solution)/shard_map/pallas_call | solution.py:114
  165.1 1.3 collective-permute-start.9
  166.4 14.8 %collective-permute-done.9.columns = f32[3,4,64,256]{3,2,1,0:T(8,128)S(1)} collective-permute-done((f32[3,4,64,256]{3,2,1,0:T(8,128)}, f32[3,4,64,256]{3,2,1,0:T(8,128)S(1)}, u32[]{:S(2)}, u32[]{:S(2)}) %collective-permute-start.9) | collective-permute-done | bytes 786464 | tf_op jit(solution)/shard_map/ppermute | solution.py:611
  181.2 0.9 copy-done.8
  182.1 17.2 %shard_map.150 = (f32[3,2,512,256]{3,2,1,0:T(8,128)}, f32[3,256,256]{2,1,0:T(8,128)}, f32[3,256,256]{2,1,0:T(8,128)}) custom-call(s32[4]{0:T(128)} %pad_add_fusion.flags, s32[64]{0:T(128)} %index.5, f32[3,4,512,256]{3,2,1,0:T(8,128)} %get-tuple-element.26.extended, f32[3,4,64,256]{3,2,1,0:T(8,128)} %copy-done.8, f32[3,2,512,256]{3,2,1,0:T(8,128)} %bitcast.37, ...), custom_call_target="tpu_custom_call" | custom-call | flops 2818572288 | bytes 21889296 | tf_op jit(solution)/shard_map/pallas_call | solution.py:114
  199.3 0.1 collective-permute-start.10
  199.4 2.5 collective-permute-done.10.other
  201.9 0.9 copy-done.3
  202.8 4.2 %shard_map.151 = f32[8,64,256]{2,1,0:T(8,128)} custom-call(s32[4]{0:T(128)} %pad_add_fusion.flags, f32[3,256,256]{2,1,0:T(8,128)} %get-tuple-element.28.mine, f32[3,256,256]{2,1,0:T(8,128)} %copy-done.3, f32[22,256,256]{2,1,0:T(8,128)} %copy-done), custom_call_target="tpu_custom_call" | custom-call | flops 8388608 | bytes 7864336 | tf_op jit(solution)/shard_map/pallas_call | solution.py:114
  207.0 19.9 %all_to_all.20.received = f32[8,64,256]{2,1,0:T(8,128)} all-to-all(f32[8,64,256]{2,1,0:T(8,128)} %shard_map.151), channel_id=1, replica_groups=mesh['sec'=2,'chip'=8,'core'=2] {'chip'}, dimensions={0} | all-to-all | bytes 1048576 | tf_op jit(solution)/shard_map/all_to_all | solution.py:565
  226.9 1.9 shard_map.152
  228.8 17.8 %all_to_all.21.scanned = f32[8,64,256]{2,1,0:T(8,128)} all-to-all(f32[8,64,256]{2,1,0:T(8,128)} %shard_map.152), channel_id=1, replica_groups=mesh['sec'=2,'chip'=8,'core'=2] {'chip'}, dimensions={0} | all-to-all | bytes 1048576 | tf_op jit(solution)/shard_map/all_to_all | solution.py:567
  246.6 5.3 %shard_map.153 = (f32[4,256,256]{2,1,0:T(8,128)}, f32[4,256,256]{2,1,0:T(8,128)}) custom-call(s32[4]{0:T(128)} %pad_add_fusion.flags, f32[3,256,256]{2,1,0:T(8,128)} %get-tuple-element.28.mine, f32[3,256,256]{2,1,0:T(8,128)} %copy-done.3, f32[22,256,256]{2,1,0:T(8,128)} %copy-done, f32[8,64,256]{2,1,0:T(8,128)} %all_to_all.21.scanned), custom_call_target="tpu_custom_call" | custom-call | flops 16777216 | bytes 9961488 | tf_op jit(solution)/shard_map/pallas_call | solution.py:114
  251.9 1.8 collective-permute-start.11
  253.7 2.5 collective-permute-done.11.other
  256.2 1.0 copy-done.7
  257.1 11.3 %shard_map.154 = f32[3,2,512,256]{3,2,1,0:T(8,128)} custom-call(s32[4]{0:T(128)} %pad_add_fusion.flags, f32[4,256,256]{2,1,0:T(8,128)} %get-tuple-element.30.mine, f32[4,256,256]{2,1,0:T(8,128)} %copy-done.7, f32[3,2,512,256]{3,2,1,0:T(8,128)} %get-tuple-element.32.final, bf16[2,2,256,256]{3,2,1,0:T(8,128)(2,1)} %constant.111.clone.from_x, ...), custom_call_target="tpu_custom_call" | custom-call | flops 2415919104 | bytes 11534352 | tf_op jit(solution)/shard_map/pallas_call | solution.py:114
  (27 shorter events, 0.1 us)
Async XLA Ops:
  0.7 12.1 %copy-start.1 = (f32[1,3,2,512,256]{4,3,2,1,0:T(8,128)S(1)}, f32[1,3,2,512,256]{4,3,2,1,0:T(8,128)}, u32[]{:S(2)}) copy-start(f32[1,3,2,512,256]{4,3,2,1,0:T(8,128)} %param.15) | copy-start | bytes 9437188
  11.5 30.2 %collective-permute-start.2 = (f32[3,2,64,256]{3,2,1,0:T(8,128)S(1)}, f32[3,2,64,256]{3,2,1,0:T(8,128)}, u32[]{:S(2)}, u32[]{:S(2)}) collective-permute-start(f32[3,2,64,256]{3,2,1,0:T(8,128)S(1)} %bitcast.41), channel_id=1, source_target_pairs={{0,16},{1,17},{2,18},{3,19},{4,20},{5,21},{6,22},{7,23},{8,24},{9,... | collective-permute-start | bytes 1179656 | tf_op jit(solution)/shard_map/ppermute | solution.py:542
  14.6 10.8 %copy-start.4 = (f32[2,256,256]{2,1,0:T(8,128)S(1)}, f32[2,256,256]{2,1,0:T(8,128)}, u32[]{:S(2)}) copy-start(f32[2,256,256]{2,1,0:T(8,128)} %constant.115.clone) | copy-start | bytes 1572868
  14.6 27.1 %collective-permute-start.1 = (f32[3,512,256]{2,1,0:T(8,128)}, f32[3,512,256]{2,1,0:T(8,128)}, u32[]{:S(2)}, u32[]{:S(2)}) collective-permute-start(f32[3,512,256]{2,1,0:T(8,128)} %get-tuple-element.33), channel_id=1, source_target_pairs={{1,0},{2,1},{3,2},{4,3},{5,4},{6,5},{7,6},{8,7},{9,8},{10,9},{11,1... | collective-permute-start | bytes 4718600 | tf_op jit(solution)/shard_map/ppermute | solution.py:540
  17.4 36.5 %collective-permute-start = (f32[3,512,256]{2,1,0:T(8,128)}, f32[3,512,256]{2,1,0:T(8,128)}, u32[]{:S(2)}, u32[]{:S(2)}) collective-permute-start(f32[3,512,256]{2,1,0:T(8,128)} %get-tuple-element.34), channel_id=1, source_target_pairs={{0,1},{1,2},{2,3},{3,4},{4,5},{5,6},{6,7},{7,8},{8,9},{9,10},{10,1... | collective-permute-start | bytes 4718600 | tf_op jit(solution)/shard_map/ppermute | solution.py:539
  20.4 21.3 %collective-permute-start.4 = (f32[3,64,256]{2,1,0:T(8,128)S(1)}, f32[3,64,256]{2,1,0:T(8,128)S(1)}, u32[]{:S(2)}, u32[]{:S(2)}) collective-permute-start(f32[3,64,256]{2,1,0:T(8,128)S(1)} %get-tuple-element.39), channel_id=1, source_target_pairs={{1,16},{2,17},{3,18},{4,19},{5,20},{6,21},{7,22},{8,23},{9,24},{10... | collective-permute-start | bytes 589832 | tf_op jit(solution)/shard_map/ppermute | solution.py:544
  21.7 20.0 %collective-permute-start.3 = (f32[3,64,256]{2,1,0:T(8,128)S(1)}, f32[3,64,256]{2,1,0:T(8,128)S(1)}, u32[]{:S(2)}, u32[]{:S(2)}) collective-permute-start(f32[3,64,256]{2,1,0:T(8,128)S(1)} %get-tuple-element.40), channel_id=1, source_target_pairs={{0,17},{1,18},{2,19},{3,20},{4,21},{5,22},{6,23},{7,24},{8,25},{9,... | collective-permute-start | bytes 589832 | tf_op jit(solution)/shard_map/ppermute | solution.py:543
  41.7 12.2 %copy-start.10 = (f32[3,64,256]{2,1,0:T(8,128)}, f32[3,64,256]{2,1,0:T(8,128)S(1)}, u32[]{:S(2)}) copy-start(f32[3,64,256]{2,1,0:T(8,128)S(1)} %collective-permute-done.4.columns_high) | copy-start | bytes 589828
  41.7 12.2 %copy-start.11 = (f32[3,64,256]{2,1,0:T(8,128)}, f32[3,64,256]{2,1,0:T(8,128)S(1)}, u32[]{:S(2)}) copy-start(f32[3,64,256]{2,1,0:T(8,128)S(1)} %collective-permute-done.3.columns_low) | copy-start | bytes 589828
  53.9 16.6 %copy-start.9 = (pred[256,256]{1,0:T(8,128)(4,1)S(1)}, pred[256,256]{1,0:T(8,128)(4,1)}, u32[]{:S(2)}) copy-start(pred[256,256]{1,0:T(8,128)(4,1)} %broadcast_compare_fusion) | copy-start | bytes 196612
  70.4 2.6 collective-permute-start.5
  72.2 2.4 copy-start
  72.9 2.0 copy-start.2
  79.2 38.6 %copy-start.12 = (f32[2,512,256]{2,1,0:T(8,128)S(1)}, f32[2,512,256]{2,1,0:T(8,128)}, u32[]{:S(2)}) copy-start(f32[2,512,256]{2,1,0:T(8,128)} %get-tuple-element.25) | copy-start | bytes 3145732
  79.2 27.4 %all-to-all-start = ((f32[8,64,256]{2,1,0:T(8,128)}), f32[8,64,256]{2,1,0:T(8,128)S(1)}, u32[]{:S(2)}, u32[]{:S(2)}) async-start(f32[8,64,256]{2,1,0:T(8,128)} %shard_map.146), calls=%async_computation | async-start | bytes 1048576 | tf_op jit(solution)/shard_map/all_to_all | solution.py:565
  106.5 0.8 copy-start.6
  109.2 17.9 %all-to-all-start.1 = ((f32[8,64,256]{2,1,0:T(8,128)}), f32[8,64,256]{2,1,0:T(8,128)S(1)}, u32[]{:S(2)}, u32[]{:S(2)}) async-start(f32[8,64,256]{2,1,0:T(8,128)} %shard_map.147), calls=%async_computation.1 | async-start | bytes 1048576 | tf_op jit(solution)/shard_map/all_to_all | solution.py:567
  113.5 29.9 %collective-permute-start.7 = (f32[2,512,256]{2,1,0:T(8,128)}, f32[2,512,256]{2,1,0:T(8,128)S(1)}, u32[]{:S(2)}, u32[]{:S(2)}) collective-permute-start(f32[2,512,256]{2,1,0:T(8,128)} %get-tuple-element.24), channel_id=1, source_target_pairs={{0,1},{1,2},{2,3},{3,4},{4,5},{5,6},{6,7},{7,8},{8,9},{9,10},{10,1... | collective-permute-start | bytes 3145736 | tf_op jit(solution)/shard_map/ppermute | solution.py:596
  117.8 25.6 %collective-permute-start.8 = (f32[2,512,256]{2,1,0:T(8,128)S(1)}, f32[2,512,256]{2,1,0:T(8,128)}, u32[]{:S(2)}, u32[]{:S(2)}) collective-permute-start(f32[2,512,256]{2,1,0:T(8,128)S(1)} %copy-done.12), channel_id=1, source_target_pairs={{1,0},{2,1},{3,2},{4,3},{5,4},{6,5},{7,6},{8,7},{9,8},{10,9},{11,1... | collective-permute-start | bytes 3145736 | tf_op jit(solution)/shard_map/ppermute | solution.py:597
  127.2 0.8 copy-start.5
  133.3 10.2 %collective-permute-start.6 = (f32[4,256,256]{2,1,0:T(8,128)}, f32[4,256,256]{2,1,0:T(8,128)S(1)}, u32[]{:S(2)}, u32[]{:S(2)}) collective-permute-start(f32[4,256,256]{2,1,0:T(8,128)} %get-tuple-element.22), channel_id=1, source_target_pairs={{0,1},{1,0},{2,3},{3,2},{4,5},{5,4},{6,7},{7,6},{8,9},{9,8},{10,11... | collective-permute-start | bytes 3145736 | tf_op jit(solution)/shard_map/ppermute | solution.py:573
  143.4 1.0 copy-start.13
  143.4 1.3 copy-start.14
  165.1 16.1 %collective-permute-start.9 = (f32[3,4,64,256]{3,2,1,0:T(8,128)}, f32[3,4,64,256]{3,2,1,0:T(8,128)S(1)}, u32[]{:S(2)}, u32[]{:S(2)}) collective-permute-start(f32[3,4,64,256]{3,2,1,0:T(8,128)} %get-tuple-element.27), channel_id=1, source_target_pairs={{0,16},{1,17},{2,18},{3,19},{4,20},{5,21},{6,22},{7,23},{8,24},{9,... | collective-permute-start | bytes 2359304 | tf_op jit(solution)/shard_map/ppermute | solution.py:611
  181.2 0.9 copy-start.8
  199.3 2.6 collective-permute-start.10
  201.9 0.9 copy-start.3
  251.9 4.3 %collective-permute-start.11 = (f32[4,256,256]{2,1,0:T(8,128)}, f32[4,256,256]{2,1,0:T(8,128)S(1)}, u32[]{:S(2)}, u32[]{:S(2)}) collective-permute-start(f32[4,256,256]{2,1,0:T(8,128)} %get-tuple-element.31), channel_id=1, source_target_pairs={{0,1},{1,0},{2,3},{3,2},{4,5},{5,4},{6,7},{7,6},{8,9},{9,8},{10,11... | collective-permute-start | bytes 3145736 | tf_op jit(solution)/shard_map/ppermute | solution.py:573
  256.2 1.0 copy-start.7

commit v2 on v1

--- a/solution.py
+++ b/solution.py
@@ -16,7 +16,7 @@
 cell_width = 4.0
 half_type = jnp.bfloat16
 full_type = jnp.float32
-vmem_bytes = 56 * 1024 * 1024
+vmem_bytes = 40 * 1024 * 1024
 levels_axis = ("chip", "core")
 every_axis = ("sec", "chip", "core")
 
@@ -126,31 +126,16 @@
     return jax.ShapeDtypeStruct(dims, kind)
 
 
-def insert_columns(target, columns, low, high, index, depth):
-    def one(i, carry):
-        row = pl.ds(index[i], 1)
-        here = pl.ds(i, 1)
-        for c in range(3):
-            target[c, 0, row, :] = low[c, here, :]
-            for z in range(depth):
-                target[c, 1 + z, row, :] = columns[c, z, here, :]
-            target[c, 1 + depth, row, :] = high[c, here, :]
-        return carry
-
-    lax.fori_loop(0, index.shape[0], one, 0)
-
-
 def tendency_steps(state, rounded, viscosity, mask, drag, dealias_x, dealias_y, put):
     depth = state.shape[1] - 2
     length_x = state.shape[2]
     rows = length_x // 2
-
-    def level(z, carry):
+    for z in range(depth):
         for c in range(3):
-            rounded[c] = state[c, z + 1].astype(half_type)
-
-        def block(b, inner):
-            part = pl.ds(pl.multiple_of(b * rows, rows), rows)
+            rounded[c, z] = state[c, z + 1].astype(half_type)
+    for z in range(depth):
+        for b in range(length_x // rows):
+            part = pl.ds(b * rows, rows)
             u, v, w = (state[c, z + 1, part, :] for c in range(3))
             slow = drag * mask[z, part, :].astype(full_type) * jnp.abs(u)
             nu = viscosity[z, part, :]
@@ -158,17 +143,11 @@
                 center = state[c, z + 1, part, :]
                 upper = state[c, z + 2, part, :]
                 lower = state[c, z, part, :]
-                grad_x = product(dealias_x[part, :], rounded[c])
-                grad_y = product(rounded[c, part, :], dealias_y[...])
+                grad_x = product(dealias_x[part, :], rounded[c, z])
+                grad_y = product(rounded[c, z, part, :], dealias_y[...])
                 advected = u * grad_x + v * grad_y + w * (0.5 * (upper - lower))
                 change = nu * (upper - 2.0 * center + lower) - advected - slow * center
                 put(c, z, part, center, change)
-            return inner
-
-        lax.fori_loop(0, length_x // rows, block, 0)
-        return carry
-
-    lax.fori_loop(0, depth, level, 0)
 
 
 def folded(block, sign):
@@ -176,43 +155,96 @@
     return block[:mid] + sign * block[mid:]
 
 
-def source_spectra(state, parts, core, slope_x, slope_y, into_x, into_y, sources):
+def source_spectra(state, parts, core, slope_x, slope_y, into_x, into_y):
     depth = state.shape[1]
     for slot, out in enumerate(parts):
         half = core if slot == 0 else 1 - core
         sign = (1 - 2 * half).astype(full_type)
-
-        def level(z, carry, half=half, sign=sign):
-            w = folded(state[2, z], sign)
-            below = folded(state[2, jnp.maximum(z - 1, 0)], sign)
-            spread = from_left(slope_x[half], folded(state[0, z], sign))
+        slope, into = slope_x[half], into_x[half]
+        lifted = [folded(state[2, z], sign) for z in range(depth)]
+        sources = []
+        for z in range(depth):
+            spread = from_left(slope, folded(state[0, z], sign))
             spread += from_right(folded(state[1, z], sign), slope_y)
-            sources[z] = spread + w - jnp.where(z > 0, below, 0.0)
+            sources.append(spread + lifted[z] - (lifted[z - 1] if z else 0.0))
+        sources.append(lifted[depth - 1])
+        for z, source in enumerate(sources):
+            out[z] = from_right(from_left(into, source), into_y)
+
+
+def prepare_kernel(index, velocity, held, low, high, columns, columns_low, columns_high, sems):
+    depth = held.shape[1]
+    copies = [
+        pltpu.make_async_copy(velocity.at[:, depth - 1], low, sems.at[0]),
+        pltpu.make_async_copy(velocity.at[:, 0], high, sems.at[1]),
+    ]
+    for copy in copies:
+        copy.start()
+
+    def one(i, carry):
+        row = pl.ds(index[i], 1)
+        here = pl.ds(i, 1)
+        for c in range(3):
+            for z in range(depth):
+                taken = held[c, z, row, :]
+                columns[c, z, here, :] = taken
+                if z == depth - 1:
+                    columns_low[c, here, :] = taken
+                if z == 0:
+                    columns_high[c, here, :] = taken
+        return carry
+
+    lax.fori_loop(0, index.shape[0], one, 0)
+    for copy in copies:
+        copy.wait()
+
+
+def inner_kernel(
+    flags, index, velocity, columns, viscosity, mask, dealias_x, dealias_y,
+    partial, weights,
+    state, rounded, sems,
+):
+    depth = partial.shape[1]
+    is_farm = flags[0]
+    copy = pltpu.make_async_copy(velocity, state.at[:, pl.ds(1, depth)], sems.at[0])
+    copy.start()
+    state[:, 0] = jnp.zeros_like(state[:, 0])
+    state[:, depth + 1] = jnp.zeros_like(state[:, 0])
+    copy.wait()
+
+    @pl.when(is_farm == 1)
+    def _():
+        def one(i, carry):
+            row = pl.ds(index[i], 1)
+            for c in range(3):
+                for z in range(depth):
+                    state[c, 1 + z, row, :] = columns[c, z, pl.ds(i, 1), :]
             return carry
 
-        lax.fori_loop(0, depth, level, 0)
-        sources[depth] = folded(state[2, depth - 1], sign)
-
-        def transform(i, carry, half=half, out=out):
-            out[i] = from_right(from_left(into_x[half], sources[i]), into_y)
-            return carry
-
-        lax.fori_loop(0, depth + 1, transform, 0)
+        lax.fori_loop(0, index.shape[0], one, 0)
+
+    drag = drag_coef * is_farm.astype(full_type)
+
+    def put(c, z, part, center, change):
+        partial[c, z, part, :] = center + step_size * change
+
+    tendency_steps(state, rounded, viscosity, mask, drag, dealias_x, dealias_y, put)
+    weights[0] = step_size * (viscosity[0] + 0.5 * state[2, 1])
+    weights[1] = step_size * (viscosity[depth - 1] - 0.5 * state[2, depth])
 
 
 def first_kernel(
-    flags, index, velocity, low, high, columns, columns_low, columns_high, viscosity, mask,
-    dealias_x, dealias_y, slope_x, slope_y, into_x, into_y,
+    flags, index, partial, weights, low, high, columns_low, columns_high,
+    slope_x, slope_y, into_x, into_y,
     middle, upward, downward, mine, theirs,
-    state, rounded, sources, slopes, sems,
+    ghosts, sems,
 ):
     depth = middle.shape[1]
     mid = middle.shape[2] // 2
     is_farm, core, is_lid = flags[0], flags[1], flags[3]
     copies = [
-        pltpu.make_async_copy(velocity, state.at[:, pl.ds(1, depth)], sems.at[0]),
-        pltpu.make_async_copy(low, state.at[:, 0], sems.at[1]),
-        pltpu.make_async_copy(high, state.at[:, depth + 1], sems.at[2]),
+        pltpu.make_async_copy(low, ghosts.at[0], sems.at[0]),
+        pltpu.make_async_copy(high, ghosts.at[1], sems.at[1]),
     ]
     for copy in copies:
         copy.start()
@@ -221,25 +253,36 @@
 
     @pl.when(is_farm == 1)
     def _():
-        insert_columns(state, columns, columns_low, columns_high, index, depth)
-
-    drag = drag_coef * is_farm.astype(full_type)
-
-    def put(c, z, part, center, change):
-        moved = center + step_size * change
-        if c == 2:
-            moved = jnp.where((is_lid == 1) & (z == depth - 1), 0.0, moved)
-        middle[c, z, part, :] = moved
-
-    tendency_steps(state, rounded, viscosity, mask, drag, dealias_x, dealias_y, put)
-    source_spectra(middle, (mine, theirs), core, slope_x, slope_y, into_x, into_y, sources)
+        def one(i, carry):
+            row = pl.ds(index[i], 1)
+            here = pl.ds(i, 1)
+            for c in range(3):
+                ghosts[0, c, row, :] = columns_low[c, here, :]
+                ghosts[1, c, row, :] = columns_high[c, here, :]
+            return carry
+
+        lax.fori_loop(0, index.shape[0], one, 0)
+
+    for c in range(3):
+        for z in range(depth):
+            moved = partial[c, z]
+            if z == 0:
+                moved += weights[0] * ghosts[0, c]
+            if z == depth - 1:
+                moved += weights[1] * ghosts[1, c]
+                if c == 2:
+                    moved = jnp.where(is_lid == 1, 0.0, moved)
+            middle[c, z] = moved
+    source_spectra(middle, (mine, theirs), core, slope_x, slope_y, into_x, into_y)
     downward[0] = middle[0, 0]
     downward[1] = middle[1, 0]
     top = depth - 1
-    for half in range(2):
-        slopes[half] = from_left(slope_x[half], folded(middle[2, top], 1.0 - 2.0 * half))
-    upward[0, :mid] = middle[0, top, :mid] + 0.5 * (slopes[0] + slopes[1])
-    upward[0, mid:] = middle[0, top, mid:] + 0.5 * (slopes[0] - slopes[1])
+    even, odd = (
+        0.5 * from_left(slope_x[half], folded(middle[2, top], 1.0 - 2.0 * half))
+        for half in range(2)
+    )
+    upward[0, :mid] = middle[0, top, :mid] + (even + odd)
+    upward[0, mid:] = middle[0, top, mid:] + (even - odd)
     upward[1] = middle[1, top] + from_right(middle[2, top], slope_y)
 
 
@@ -247,7 +290,7 @@
     flags, index, extended, columns, velocity, start_columns, viscosity, mask,
     dealias_x, dealias_y, slope_x, slope_y, into_x, into_y,
     final, mine, theirs,
-    state, start, rounded, sources, sems,
+    state, start, rounded, sems,
 ):
     depth = final.shape[1]
     is_farm, core, is_lid = flags[0], flags[1], flags[3]
@@ -283,7 +326,7 @@
         final[c, z, part, :] = moved
 
     tendency_steps(state, rounded, viscosity, mask, drag, dealias_x, dealias_y, put)
-    source_spectra(final, (mine, theirs), core, slope_x, slope_y, into_x, into_y, sources)
+    source_spectra(final, (mine, theirs), core, slope_x, slope_y, into_x, into_y)
 
 
 def chip_levels(core, mine, other, depth):
@@ -397,24 +440,14 @@
         for z in range(lifts):
             spectra[half, pressures + z] = chosen[1 + z]
 
-    def one(half, carry):
-        def pressure(i, inner):
+    for half in range(2):
+        for i in range(pressures):
             block = spectra[half, i]
             slots[2 * i, half] = from_left(from_slope_x[half], from_right(block, from_y))
             slots[2 * i + 1, half] = from_left(from_x[half], from_right(block, from_slope_y))
-            return inner
-
-        lax.fori_loop(0, pressures, pressure, 0)
-
-        def lift(i, inner):
+        for i in range(lifts):
             block = spectra[half, pressures + i]
             slots[2 * pressures + i, half] = from_left(from_x[half], from_right(block, from_y))
-            return inner
-
-        lax.fori_loop(0, lifts, lift, 0)
-        return carry
-
-    lax.fori_loop(0, 2, one, 0)
 
 
 def unfolded(slots, i):
@@ -536,12 +569,21 @@
             (i, devices + i + shift) for i in range(devices) if 0 <= i + shift < devices
         ]
 
-    low = lax.ppermute(current[:, depth - 1], levels_axis, upward_route)
-    high = lax.ppermute(current[:, 0], levels_axis, downward_route)
-    taken = current[:, :, fringe_columns, :]
-    columns = lax.ppermute(taken, every_axis, across(0))
-    columns_low = lax.ppermute(taken[:, depth - 1], every_axis, across(1))
-    columns_high = lax.ppermute(taken[:, 0], every_axis, across(-1))
+    edge_shape = shaped(3, length_x, length_y)
+    band = shaped(3, fringe, length_y)
+    low, high, columns, columns_low, columns_high = pl.pallas_call(
+        prepare_kernel,
+        out_shape=(edge_shape, edge_shape, shaped(3, depth, fringe, length_y), band, band),
+        in_specs=[smem(), hbm(), vmem()],
+        out_specs=(hbm(), hbm(), vmem(), vmem(), vmem()),
+        scratch_shapes=[pltpu.SemaphoreType.DMA((2,))],
+        compiler_params=pltpu.CompilerParams(vmem_limit_bytes=vmem_bytes),
+    )(fringe_columns, current, current)
+    low = lax.ppermute(low, levels_axis, upward_route)
+    high = lax.ppermute(high, levels_axis, downward_route)
+    columns = lax.ppermute(columns, every_axis, across(0))
+    columns_low = lax.ppermute(columns_low, every_axis, across(1))
+    columns_high = lax.ppermute(columns_high, every_axis, across(-1))
 
     decay = lax.dynamic_index_in_dim(tables["decay"], core, 0, keepdims=False)
     stacked = coefficients(decay, (chip * count).astype(full_type), count, float(height))
@@ -573,24 +615,28 @@
         return own, lax.ppermute(partner, "core", swap)
 
     state_shape = (3, depth + 2, length_x, length_y)
-    sources = pltpu.VMEM((depth + 1, mid, length_y), full_type)
-    rounded = pltpu.VMEM((3, length_x, length_y), half_type)
+    rounded = pltpu.VMEM((3, depth, length_x, length_y), half_type)
     own_shape = shaped(3, depth, length_x, length_y)
     edge = shaped(2, length_x, length_y)
     tendency_flops = 3 * depth * block * (length_x + length_y)
     source_flops = 3 * depth * block * (length_x + 2 * length_y)
 
+    partial, weights = call(
+        inner_kernel,
+        (own_shape, edge),
+        [smem(), smem(), hbm()] + [vmem()] * 5,
+        [pltpu.VMEM(state_shape, full_type), rounded, pltpu.SemaphoreType.DMA((1,))],
+        tendency_flops,
+        (flags, fringe_columns, current, columns, viscosity, turbine_mask, *tendency_tables),
+    )
     middle, upward, downward, mine, theirs = call(
         first_kernel,
         (own_shape, edge, edge, spectrum, spectrum),
-        [smem(), smem()] + [hbm()] * 3 + [vmem()] * 11,
-        [
-            pltpu.VMEM(state_shape, full_type), rounded, sources,
-            pltpu.VMEM((2, mid, length_y), full_type), pltpu.SemaphoreType.DMA((3,)),
-        ],
-        tendency_flops + source_flops,
-        (flags, fringe_columns, current, low, high, columns, columns_low, columns_high,
-         viscosity, turbine_mask, *tendency_tables, *source_tables),
+        [smem(), smem()] + [vmem()] * 2 + [hbm()] * 2 + [vmem()] * 6,
+        [pltpu.VMEM((2, 3, length_x, length_y), full_type), pltpu.SemaphoreType.DMA((2,))],
+        source_flops,
+        (flags, fringe_columns, partial, weights, low, high, columns_low, columns_high,
+         *source_tables),
     )
     own, partner = solve(mine, theirs)
     from_below = lax.ppermute(upward, levels_axis, upward_route)
@@ -615,7 +661,7 @@
         [smem(), smem(), hbm(), vmem(), hbm()] + [vmem()] * 9,
         [
             pltpu.VMEM(state_shape, full_type), pltpu.VMEM(own_shape.shape, full_type),
-            rounded, sources, pltpu.SemaphoreType.DMA((2,)),
+            rounded, pltpu.SemaphoreType.DMA((2,)),
         ],
         tendency_flops + source_flops,
         (flags, fringe_columns, extended, bands, current, columns, viscosity, turbine_mask,

time: 269 us -> 217 us (0.81)
  Pallas kernels: 88.2 us -> 54.4 us
  waiting for transfers between devices: 77.2 us -> 56 us
  other arithmetic: 5.97 us -> 14.8 us
  local copies, waits for them, and re-layouts: 20.3 us -> 16.7 us
    pallas_call x10 -> x11, Pallas kernels: 88.2 us -> 51.3 us  [call(): pl.pallas_call(kernel, out_shape=outs, in_specs=in_specs, out_specs=tuple...]
    ppermute x5, waiting for transfers between devices: 27.8 us -> 9.24 us  [the longest x1 5.19 us: local(): columns = lax.ppermute(columns, every_axis, across(0))]
    unnamed x30 -> x92, local copies, waits for them, and re-layouts: 7.66 us -> 16.7 us
    squeeze x3 -> x0, local copies, waits for them, and re-layouts: 8.01 us -> none  [the longest x1 6.13 us: local(): current = velocity[0]]
    unnamed x5, other arithmetic: 1.95 us -> 8.14 us
    gather x2 -> x0, local copies, waits for them, and re-layouts: 4.66 us -> none  [local(): taken = current[:, :, fringe_columns, :]]
    pallas_call x0 -> x1, Pallas kernels: none -> 3.04 us  [local(): pl.pallas_call(prepare_kernel, out_shape=(edge_shape, edge_shape, shaped(...]
    all_to_all x2, starting transfers between devices: 17.7 us -> 14.9 us  [solve(): sums = lax.all_to_all(sums, 'chip', split_axis=0, concat_axis=0, tiled=True)]
  transfers between devices with their start and end apart: 14 -> 14, of which waited for: 9 -> 8; matrix products, arithmetic and copies ran while one was open for 3% -> 7% of each run, Pallas kernels for 2% -> 4%
where the time goes in v2:
time: 217 us; the launch traced here: 216 us
  waiting for transfers between devices  56 us (26%)
  Pallas kernels  54.4 us (25%)
  starting transfers between devices  37 us (17%)
  blocking collectives  36.3 us (17%)
  local copies, waits for them, and re-layouts  16.7 us (8%)
  other arithmetic  14.8 us (7%)
    pallas_call x11, Pallas kernels, call(): pl.pallas_call(kernel, out_shape=outs, in_specs=in_specs, out_specs=tuple...  51.3 us
    all_to_all x2, blocking collectives, solve(): sums = lax.all_to_all(sums, 'chip', split_axis=0, concat_axis=0, tiled=True)  36.3 us
    all_to_all x2, waiting for transfers between devices, solve(): sums = lax.all_to_all(sums, 'chip', split_axis=0, concat_axis=0, tiled=True)  19.2 us
    unnamed x92, local copies, waits for them, and re-layouts  16.7 us
    ppermute x1, waiting for transfers between devices, local(): bands = lax.ppermute(bands, 'sec', [(0, 1)])  15 us
    all_to_all x2, starting transfers between devices, solve(): sums = lax.all_to_all(sums, 'chip', split_axis=0, concat_axis=0, tiled=True)  14.9 us
    unnamed x5, other arithmetic  8.14 us
    ppermute x1, waiting for transfers between devices, local(): from_below = lax.ppermute(upward, levels_axis, upward_route)  7.94 us
  transfers between devices with their start and end apart: 14, of which 8 were waited for; matrix products, arithmetic and copies ran while one was open for 7% of the time, Pallas kernels for 4%

profile of v2, /device:TPU:5, one launch (start us, length us, event | category | flops | bytes accessed | tf_op | source)
XLA Modules:
  0.0 216.3 jit_solution(5491580566600013621)
XLA Ops:
  0.0 1.9 copy-done
  1.9 0.7 copy-done.31
  2.5 3.0 %shard_map.145 = (f32[3,512,256]{2,1,0:T(8,128)}, f32[3,512,256]{2,1,0:T(8,128)}, f32[3,2,64,256]{3,2,1,0:T(8,128)}, f32[3,64,256]{2,1,0:T(8,128)}, f32[3,64,256]{2,1,0:T(8,128)}) custom-call(s32[64]{0:T(128)S(1)} %copy-done.31, f32[3,2,512,256]{3,2,1,0:T(8,128)S(1)} %bitcast.24, f32[3,2,512,256]{3,2,1,0:T(8,128)S(1)} %bitcast.25), custom_call_target="tpu_custom_call" | custom-call | tf_op jit(solution)/shard_map/pallas_call | solution.py:574
  5.6 3.9 %collective-permute-start.1 = (f32[3,512,256]{2,1,0:T(8,128)}, f32[3,512,256]{2,1,0:T(8,128)}, u32[]{:S(2)}, u32[]{:S(2)}) collective-permute-start(f32[3,512,256]{2,1,0:T(8,128)} %get-tuple-element.29), channel_id=1, source_target_pairs={{0,1},{1,2},{2,3},{3,4},{4,5},{5,6},{6,7},{7,8},{8,9},{9,10},{10,1... | collective-permute-start | bytes 4718600 | tf_op jit(solution)/shard_map/ppermute | solution.py:582
  9.6 1.9 collective-permute-start.2
  11.5 1.3 collective-permute-start.3
  12.8 1.3 collective-permute-start.4
  14.1 1.3 collective-permute-start
  15.5 1.6 broadcast_compare_fusion
  17.1 2.0 fusion.14
  19.0 0.7 copy-done.37
  19.7 1.4 add_dynamic-update-slice_fusion.1
  21.1 0.6 fusion.23
  22.4 2.3 %add_dynamic-update-slice_fusion = f32[22,256,256]{2,1,0:T(8,128)} fusion(f32[22,256,256]{2,1,0:T(8,128)} %add_dynamic-update-slice_fusion.1, f32[5]{0:T(128)S(1)} %get-tuple-element.53, f32[256,256]{1,0:T(8,128)} %copy-done.37), kind=kLoop, calls=%fused_computation.1 | loop fusion | flops 655360 | bytes 1572884
  24.7 0.1 pad_add_fusion.flags
  24.8 5.2 %collective-permute-done.columns.start_columns = f32[3,2,64,256]{3,2,1,0:T(8,128)S(1)} collective-permute-done((f32[3,2,64,256]{3,2,1,0:T(8,128)}, f32[3,2,64,256]{3,2,1,0:T(8,128)S(1)}, u32[]{:S(2)}, u32[]{:S(2)}) %collective-permute-start) | collective-permute-done | bytes 393248 | tf_op jit(solution)/shard_map/ppermute | solution.py:584
  30.0 1.2 copy-done.2
  31.2 1.2 copy-done.4
  32.4 1.0 copy-done.17
  33.5 0.9 copy-done.25
  34.4 4.0 %shard_map.146 = (f32[3,2,512,256]{3,2,1,0:T(8,128)S(1)}, f32[2,512,256]{2,1,0:T(8,128)S(1)}) custom-call(s32[4]{0:T(128)S(1)} %pad_add_fusion.flags, s32[64]{0:T(128)S(1)} %copy-done.32, f32[3,2,512,256]{3,2,1,0:T(8,128)S(1)} %bitcast.26, f32[3,2,64,256]{3,2,1,0:T(8,128)S(1)} %collective-permute-done.columns.start_columns, f32[2,512,256]{2,1,0:T(8,128)S(1)} %bitcast.28, ...), custom_call_target="tpu_custom_call" | custom-call | flops 1207959552 | bytes 11141392 | tf_op jit(solution)/shard_map/pallas_call | solution.py:114
  38.4 1.7 copy-done.6
  40.0 4.0 %collective-permute-done.1.low = f32[3,512,256]{2,1,0:T(8,128)} collective-permute-done((f32[3,512,256]{2,1,0:T(8,128)}, f32[3,512,256]{2,1,0:T(8,128)}, u32[]{:S(2)}, u32[]{:S(2)}) %collective-permute-start.1) | collective-permute-done | bytes 1572896 | tf_op jit(solution)/shard_map/ppermute | solution.py:582
  44.2 7.7 %shard_map.147 = (f32[3,2,512,256]{3,2,1,0:T(8,128)S(1)}, f32[2,512,256]{2,1,0:T(8,128)S(1)}, f32[2,512,256]{2,1,0:T(8,128)S(1)}, f32[3,256,256]{2,1,0:T(8,128)S(1)}, f32[3,256,256]{2,1,0:T(8,128)S(1)}) custom-call(s32[4]{0:T(128)S(1)} %pad_add_fusion.flags, s32[64]{0:T(128)S(1)} %copy-done.32, f32[3,2,512,256]{3,2,1,0:T(8,128)} %copy-done.6, ...), custom_call_target="tpu_custom_call" | custom-call | flops 1610612736 | bytes 17694992 | tf_op jit(solution)/shard_map/pallas_call | solution.py:114
  51.9 1.7 copy-done.33
  53.6 0.1 collective-permute-start.5
  53.7 1.8 multiply_dynamic-update-slice_fusion.1
  55.4 1.7 multiply_dynamic-update-slice_fusion
  57.2 1.0 fusion.5
  58.1 1.0 fusion.8.stacked
  59.1 2.9 %shard_map.148 = f32[8,64,256]{2,1,0:T(8,128)S(1)} custom-call(s32[4]{0:T(128)S(1)} %pad_add_fusion.flags, f32[3,256,256]{2,1,0:T(8,128)S(1)} %get-tuple-element.33.mine, f32[3,256,256]{2,1,0:T(8,128)S(1)} %collective-permute-done.5.other, f32[22,256,256]{2,1,0:T(8,128)} %fusion.8.stacked), custom_call_target="tpu_custom_call" | custom-call | flops 8388608 | bytes 7864336 | tf_op jit(solution)/shard_map/pallas_call | solution.py:114
  62.1 0.9 copy-done.9
  63.0 0.8 copy-done.11
  63.8 10.4 %all-to-all-start = ((f32[8,64,256]{2,1,0:T(8,128)}), f32[8,64,256]{2,1,0:T(8,128)}, u32[]{:S(2)}, u32[]{:S(2)}) async-start(f32[8,64,256]{2,1,0:T(8,128)} %copy-done.11), calls=%async_computation | async-start | bytes 1048576 | tf_op jit(solution)/shard_map/all_to_all | solution.py:607
  74.2 1.4 exponential_bitcast_fusion.ratio
  75.6 12.5 %all-to-all-done.received = f32[8,64,256]{2,1,0:T(8,128)} async-done(((f32[8,64,256]{2,1,0:T(8,128)}), f32[8,64,256]{2,1,0:T(8,128)}, u32[]{:S(2)}, u32[]{:S(2)}) %all-to-all-start) | async-done | bytes 524320 | tf_op jit(solution)/shard_map/all_to_all | solution.py:607
  88.1 0.8 copy-done.27
  88.9 1.1 shard_map.149
  89.9 0.8 copy-done.12
  90.8 4.5 %all-to-all-start.1 = ((f32[8,64,256]{2,1,0:T(8,128)}), f32[8,64,256]{2,1,0:T(8,128)}, u32[]{:S(2)}, u32[]{:S(2)}) async-start(f32[8,64,256]{2,1,0:T(8,128)} %copy-done.12), calls=%async_computation.1 | async-start | bytes 1048576 | tf_op jit(solution)/shard_map/all_to_all | solution.py:609
  95.3 4.7 %collective-permute-start.7 = (f32[2,512,256]{2,1,0:T(8,128)}, f32[2,512,256]{2,1,0:T(8,128)}, u32[]{:S(2)}, u32[]{:S(2)}) collective-permute-start(f32[2,512,256]{2,1,0:T(8,128)} %copy-done.36), channel_id=1, source_target_pairs={{0,1},{1,2},{2,3},{3,4},{4,5},{5,6},{6,7},{7,8},{8,9},{9,10},{10,1... | collective-permute-start | bytes 3145736 | tf_op jit(solution)/shard_map/ppermute | solution.py:642
  100.0 2.1 collective-permute-start.8
  102.1 6.7 %all-to-all-done.1.scanned = f32[8,64,256]{2,1,0:T(8,128)} async-done(((f32[8,64,256]{2,1,0:T(8,128)}), f32[8,64,256]{2,1,0:T(8,128)}, u32[]{:S(2)}, u32[]{:S(2)}) %all-to-all-start.1) | async-done | bytes 524320 | tf_op jit(solution)/shard_map/all_to_all | solution.py:609
  108.8 1.1 copy-done.8
  109.9 1.1 copy-done.10
  111.1 0.0 copy-start.29
  111.1 3.7 %shard_map.150 = (f32[4,256,256]{2,1,0:T(8,128)S(1)}, f32[4,256,256]{2,1,0:T(8,128)S(1)}) custom-call(s32[4]{0:T(128)S(1)} %pad_add_fusion.flags, f32[3,256,256]{2,1,0:T(8,128)S(1)} %copy-done.8, f32[3,256,256]{2,1,0:T(8,128)S(1)} %copy-done.10, f32[22,256,256]{2,1,0:T(8,128)} %fusion.8.stacked, f32[8,64,256]{2,1,0:T(8,128)} %all-to-all-done.1.scanned), custom_call_target="tpu_custom_call" | custom-call | flops 16777216 | bytes 9961488 | tf_op jit(solution)/shard_map/pallas_call | solution.py:114
  114.8 2.2 %collective-permute-start.6 = (f32[4,256,256]{2,1,0:T(8,128)S(1)}, f32[4,256,256]{2,1,0:T(8,128)S(1)}, u32[]{:S(2)}, u32[]{:S(2)}) collective-permute-start(f32[4,256,256]{2,1,0:T(8,128)S(1)} %get-tuple-element.36), channel_id=1, source_target_pairs={{0,1},{1,0},{2,3},{3,2},{4,5},{5,4},{6,7},{7,6},{8,9},{9,8},{10,11... | collective-permute-start | bytes 3145736 | tf_op jit(solution)/shard_map/ppermute | solution.py:615
  117.0 7.9 %collective-permute-done.7.from_below = f32[2,512,256]{2,1,0:T(8,128)} collective-permute-done((f32[2,512,256]{2,1,0:T(8,128)}, f32[2,512,256]{2,1,0:T(8,128)}, u32[]{:S(2)}, u32[]{:S(2)}) %collective-permute-start.7) | collective-permute-done | bytes 1048608 | tf_op jit(solution)/shard_map/ppermute | solution.py:642
  125.1 0.0 copy-start.16
  125.1 0.0 copy-start.18
  125.1 10.8 %shard_map.151 = (f32[3,4,512,256]{3,2,1,0:T(8,128)}, f32[3,4,64,256]{3,2,1,0:T(8,128)S(1)}) custom-call(s32[4]{0:T(128)S(1)} %pad_add_fusion.flags, f32[4,256,256]{2,1,0:T(8,128)S(1)} %get-tuple-element.35.mine, f32[4,256,256]{2,1,0:T(8,128)S(1)} %collective-permute-done.6.other, f32[3,2,512,256]{3,2,1,0:T(8,128)S(1)} %copy-done.34, ...), custom_call_target="tpu_custom_call" | custom-call | flops 4429185024 | bytes 19136784 | tf_op jit(solution)/shard_map/pallas_call | solution.py:114
  136.0 1.3 collective-permute-start.9
  137.2 15.0 %collective-permute-done.9.columns = f32[3,4,64,256]{3,2,1,0:T(8,128)S(1)} collective-permute-done((f32[3,4,64,256]{3,2,1,0:T(8,128)S(1)}, f32[3,4,64,256]{3,2,1,0:T(8,128)S(1)}, u32[]{:S(2)}, u32[]{:S(2)}) %collective-permute-start.9) | collective-permute-done | bytes 786464 | tf_op jit(solution)/shard_map/ppermute | solution.py:657
  152.3 9.5 %shard_map.152 = (f32[3,2,512,256]{3,2,1,0:T(8,128)S(1)}, f32[3,256,256]{2,1,0:T(8,128)S(1)}, f32[3,256,256]{2,1,0:T(8,128)S(1)}) custom-call(s32[4]{0:T(128)S(1)} %pad_add_fusion.flags, s32[64]{0:T(128)S(1)} %copy-done.32, f32[3,4,512,256]{3,2,1,0:T(8,128)} %get-tuple-element.40.extended, f32[3,4,64,256]{3,2,1,0:T(8,128)S(1)} %collective-permute-done.9.columns, ...), custom_call_target="tpu_custom_call" | custom-call | flops 2818572288 | bytes 21889296 | tf_op jit(solution)/shard_map/pallas_call | solution.py:114
  161.9 0.1 collective-permute-start.10
  161.9 2.3 %collective-permute-done.10.other = f32[3,256,256]{2,1,0:T(8,128)S(1)} collective-permute-done((f32[3,256,256]{2,1,0:T(8,128)S(1)}, f32[3,256,256]{2,1,0:T(8,128)S(1)}, u32[]{:S(2)}, u32[]{:S(2)}) %collective-permute-start.10) | collective-permute-done | bytes 786464 | tf_op jit(solution)/shard_map/ppermute | solution.py:601
  164.2 2.9 %shard_map.153 = f32[8,64,256]{2,1,0:T(8,128)S(1)} custom-call(s32[4]{0:T(128)S(1)} %pad_add_fusion.flags, f32[3,256,256]{2,1,0:T(8,128)S(1)} %get-tuple-element.42.mine, f32[3,256,256]{2,1,0:T(8,128)S(1)} %collective-permute-done.10.other, f32[22,256,256]{2,1,0:T(8,128)} %fusion.8.stacked), custom_call_target="tpu_custom_call" | custom-call | flops 8388608 | bytes 7864336 | tf_op jit(solution)/shard_map/pallas_call | solution.py:114
  167.2 18.5 %all_to_all.20.received = f32[8,64,256]{2,1,0:T(8,128)S(1)} all-to-all(f32[8,64,256]{2,1,0:T(8,128)S(1)} %shard_map.153), channel_id=1, replica_groups=mesh['sec'=2,'chip'=8,'core'=2] {'chip'}, dimensions={0} | all-to-all | bytes 1048576 | tf_op jit(solution)/shard_map/all_to_all | solution.py:607
  185.7 17.8 %all_to_all.21.scanned = f32[8,64,256]{2,1,0:T(8,128)S(1)} all-to-all(f32[8,64,256]{2,1,0:T(8,128)S(1)} %shard_map.154), channel_id=1, replica_groups=mesh['sec'=2,'chip'=8,'core'=2] {'chip'}, dimensions={0} | all-to-all | bytes 1048576 | tf_op jit(solution)/shard_map/all_to_all | solution.py:609
  203.5 3.4 %shard_map.155 = (f32[4,256,256]{2,1,0:T(8,128)S(1)}, f32[4,256,256]{2,1,0:T(8,128)S(1)}) custom-call(s32[4]{0:T(128)S(1)} %pad_add_fusion.flags, f32[3,256,256]{2,1,0:T(8,128)S(1)} %get-tuple-element.42.mine, f32[3,256,256]{2,1,0:T(8,128)S(1)} %collective-permute-done.10.other, f32[22,256,256]{2,1,0:T(8,128)} %fusion.8.stacked, ...), custom_call_target="tpu_custom_call" | custom-call | flops 16777216 | bytes 9961488 | tf_op jit(solution)/shard_map/pallas_call | solution.py:114
  207.0 1.9 collective-permute-start.11
  208.9 2.3 %collective-permute-done.11.other = f32[4,256,256]{2,1,0:T(8,128)S(1)} collective-permute-done((f32[4,256,256]{2,1,0:T(8,128)S(1)}, f32[4,256,256]{2,1,0:T(8,128)S(1)}, u32[]{:S(2)}, u32[]{:S(2)}) %collective-permute-start.11) | collective-permute-done | bytes 1048608 | tf_op jit(solution)/shard_map/ppermute | solution.py:615
  211.1 5.1 %shard_map.156 = f32[3,2,512,256]{3,2,1,0:T(8,128)} custom-call(s32[4]{0:T(128)S(1)} %pad_add_fusion.flags, f32[4,256,256]{2,1,0:T(8,128)S(1)} %get-tuple-element.44.mine, f32[4,256,256]{2,1,0:T(8,128)S(1)} %collective-permute-done.11.other, f32[3,2,512,256]{3,2,1,0:T(8,128)S(1)} %get-tuple-element.46.final, bf16[2,2,256,256]{3,2,1,0:T(8,128)(2,1)S(1)} %copy-done.24, ...), custom_call_target="tpu_custom_call" | custom-call | flops 2415919104 | bytes 11534352 | tf_op jit(solution)/shard_map/pallas_call | solution.py:114
  (84 shorter events, 0.2 us)
Async XLA Ops:
  0.0 1.9 copy-start
  1.9 0.7 copy-start.31
  5.6 24.4 %copy-start.1 = (f32[1,3,2,512,256]{4,3,2,1,0:T(8,128)S(1)}, f32[1,3,2,512,256]{4,3,2,1,0:T(8,128)}, u32[]{:S(2)}) copy-start(f32[1,3,2,512,256]{4,3,2,1,0:T(8,128)} %param.15) | copy-start | bytes 9437188
  5.6 24.4 %copy-start.32 = (s32[64]{0:T(128)S(1)}, s32[64]{0:T(128)}, u32[]{:S(2)}) copy-start(s32[64]{0:T(128)} %index.9) | copy-start | bytes 772
  5.6 38.5 %collective-permute-start.1 = (f32[3,512,256]{2,1,0:T(8,128)}, f32[3,512,256]{2,1,0:T(8,128)}, u32[]{:S(2)}, u32[]{:S(2)}) collective-permute-start(f32[3,512,256]{2,1,0:T(8,128)} %get-tuple-element.29), channel_id=1, source_target_pairs={{0,1},{1,2},{2,3},{3,4},{4,5},{5,6},{6,7},{7,8},{8,9},{9,10},{10,1... | collective-permute-start | bytes 4718600 | tf_op jit(solution)/shard_map/ppermute | solution.py:582
  9.6 34.5 %collective-permute-start.2 = (f32[3,512,256]{2,1,0:T(8,128)}, f32[3,512,256]{2,1,0:T(8,128)}, u32[]{:S(2)}, u32[]{:S(2)}) collective-permute-start(f32[3,512,256]{2,1,0:T(8,128)} %get-tuple-element.30), channel_id=1, source_target_pairs={{1,0},{2,1},{3,2},{4,3},{5,4},{6,5},{7,6},{8,7},{9,8},{10,9},{11,1... | collective-permute-start | bytes 4718600 | tf_op jit(solution)/shard_map/ppermute | solution.py:583
  11.5 28.5 %collective-permute-start.3 = (f32[3,64,256]{2,1,0:T(8,128)}, f32[3,64,256]{2,1,0:T(8,128)}, u32[]{:S(2)}, u32[]{:S(2)}) collective-permute-start(f32[3,64,256]{2,1,0:T(8,128)} %get-tuple-element.31), channel_id=1, source_target_pairs={{0,17},{1,18},{2,19},{3,20},{4,21},{5,22},{6,23},{7,24},{8,25},{9,... | collective-permute-start | bytes 589832 | tf_op jit(solution)/shard_map/ppermute | solution.py:585
  12.8 27.2 %collective-permute-start.4 = (f32[3,64,256]{2,1,0:T(8,128)}, f32[3,64,256]{2,1,0:T(8,128)}, u32[]{:S(2)}, u32[]{:S(2)}) collective-permute-start(f32[3,64,256]{2,1,0:T(8,128)} %get-tuple-element.32), channel_id=1, source_target_pairs={{1,16},{2,17},{3,18},{4,19},{5,20},{6,21},{7,22},{8,23},{9,24},{10... | collective-permute-start | bytes 589832 | tf_op jit(solution)/shard_map/ppermute | solution.py:586
  14.1 15.9 %collective-permute-start = (f32[3,2,64,256]{3,2,1,0:T(8,128)}, f32[3,2,64,256]{3,2,1,0:T(8,128)S(1)}, u32[]{:S(2)}, u32[]{:S(2)}) collective-permute-start(f32[3,2,64,256]{3,2,1,0:T(8,128)} %get-tuple-element.26), channel_id=1, source_target_pairs={{0,16},{1,17},{2,18},{3,19},{4,20},{5,21},{6,22},{7,23},{8,24},{9,... | collective-permute-start | bytes 1179656 | tf_op jit(solution)/shard_map/ppermute | solution.py:584
  15.4 3.6 %copy-start.45 = (f32[5,1,1]{0,2,1:T(1,128)}, f32[5,1,1]{0,2,1:T(1,128)S(1)}, u32[]{:S(2)}) copy-start(f32[5,1,1]{0,2,1:T(1,128)S(1)} %iota_add_fusion) | copy-start | bytes 64
  19.0 0.7 copy-start.37
  30.0 1.2 copy-start.2
  31.2 1.2 copy-start.4
  32.4 1.0 copy-start.17
  33.5 0.9 copy-start.25
  34.4 9.7 %copy-start.13 = (bf16[2,2,256,256]{3,2,1,0:T(8,128)(2,1)S(1)}, bf16[2,2,256,256]{3,2,1,0:T(8,128)(2,1)}, u32[]{:S(2)}) copy-start(bf16[2,2,256,256]{3,2,1,0:T(8,128)(2,1)} %constant.104.clone.slope_x) | copy-start | bytes 1572868
  34.4 9.7 %copy-start.15 = (bf16[2,2,256,256]{3,2,1,0:T(8,128)(2,1)S(1)}, bf16[2,2,256,256]{3,2,1,0:T(8,128)(2,1)}, u32[]{:S(2)}) copy-start(bf16[2,2,256,256]{3,2,1,0:T(8,128)(2,1)} %constant.106.clone.into_x) | copy-start | bytes 1572868
  34.4 9.7 %copy-start.19 = (bf16[2,256,256]{2,1,0:T(8,128)(2,1)S(1)}, bf16[2,256,256]{2,1,0:T(8,128)(2,1)}, u32[]{:S(2)}) copy-start(bf16[2,256,256]{2,1,0:T(8,128)(2,1)} %constant.105.clone.slope_y) | copy-start | bytes 786436
  34.4 9.7 %copy-start.21 = (bf16[2,256,256]{2,1,0:T(8,128)(2,1)S(1)}, bf16[2,256,256]{2,1,0:T(8,128)(2,1)}, u32[]{:S(2)}) copy-start(bf16[2,256,256]{2,1,0:T(8,128)(2,1)} %constant.107.clone.into_y) | copy-start | bytes 786436
  38.4 1.7 copy-start.6
  44.1 9.5 %copy-start.38 = (f32[256,256]{1,0:T(8,128)S(1)}, f32[256,256]{1,0:T(8,128)}, u32[]{:S(2)}) copy-start(f32[256,256]{1,0:T(8,128)} %copy-done.37) | copy-start | bytes 786436
  44.1 9.5 %copy-start.39 = (f32[256,256]{1,0:T(8,128)S(1)}, f32[256,256]{1,0:T(8,128)}, u32[]{:S(2)}) copy-start(f32[256,256]{1,0:T(8,128)} %get-tuple-element.47) | copy-start | bytes 786436
  44.1 9.5 %copy-start.40 = (f32[256,256]{1,0:T(8,128)S(1)}, f32[256,256]{1,0:T(8,128)}, u32[]{:S(2)}) copy-start(f32[256,256]{1,0:T(8,128)} %get-tuple-element.49) | copy-start | bytes 786436
  44.1 9.5 %copy-start.42 = (pred[256,256]{1,0:T(8,128)(4,1)S(1)}, pred[256,256]{1,0:T(8,128)(4,1)}, u32[]{:S(2)}) copy-start(pred[256,256]{1,0:T(8,128)(4,1)} %broadcast_compare_fusion) | copy-start | bytes 196612
  44.1 11.3 %copy-start.43 = (f32[5]{0:T(128)S(1)}, f32[5]{0:T(128)}, u32[]{:S(2)}) copy-start(f32[5]{0:T(128)} %get-tuple-element.55) | copy-start | bytes 64
  44.2 11.3 %copy-start.44 = (f32[5]{0:T(128)S(1)}, f32[5]{0:T(128)}, u32[]{:S(2)}) copy-start(f32[5]{0:T(128)} %get-tuple-element.56) | copy-start | bytes 64
  51.9 1.7 copy-start.33
  53.5 5.6 %copy-start.35 = (f32[2,512,256]{2,1,0:T(8,128)}, f32[2,512,256]{2,1,0:T(8,128)S(1)}, u32[]{:S(2)}) copy-start(f32[2,512,256]{2,1,0:T(8,128)S(1)} %get-tuple-element.39) | copy-start | bytes 3145732
  53.5 5.6 %copy-start.7 = (f32[3,256,256]{2,1,0:T(8,128)}, f32[3,256,256]{2,1,0:T(8,128)S(1)}, u32[]{:S(2)}) copy-start(f32[3,256,256]{2,1,0:T(8,128)S(1)} %get-tuple-element.33.mine) | copy-start | bytes 2359300
  53.5 5.6 %copy-start.36 = (f32[2,512,256]{2,1,0:T(8,128)}, f32[2,512,256]{2,1,0:T(8,128)S(1)}, u32[]{:S(2)}) copy-start(f32[2,512,256]{2,1,0:T(8,128)S(1)} %get-tuple-element.38) | copy-start | bytes 3145732
  53.5 3.6 %copy-start.41 = (f32[2,256,256]{2,1,0:T(8,128)S(1)}, f32[2,256,256]{2,1,0:T(8,128)}, u32[]{:S(2)}) copy-start(f32[2,256,256]{2,1,0:T(8,128)} %constant.112.clone) | copy-start | bytes 1572868
  53.6 5.6 %collective-permute-start.5 = (f32[3,256,256]{2,1,0:T(8,128)S(1)}, f32[3,256,256]{2,1,0:T(8,128)S(1)}, u32[]{:S(2)}, u32[]{:S(2)}) collective-permute-start(f32[3,256,256]{2,1,0:T(8,128)S(1)} %get-tuple-element.34), channel_id=1, source_target_pairs={{0,1},{1,0},{2,3},{3,2},{4,5},{5,4},{6,7},{7,6},{8,9},{9,8},{10,11... | collective-permute-start | bytes 2359304 | tf_op jit(solution)/shard_map/ppermute | solution.py:601
  62.1 0.9 copy-start.9
  63.0 0.8 copy-start.11
  63.8 24.3 %all-to-all-start = ((f32[8,64,256]{2,1,0:T(8,128)}), f32[8,64,256]{2,1,0:T(8,128)}, u32[]{:S(2)}, u32[]{:S(2)}) async-start(f32[8,64,256]{2,1,0:T(8,128)} %copy-done.11), calls=%async_computation | async-start | bytes 1048576 | tf_op jit(solution)/shard_map/all_to_all | solution.py:607
  88.1 0.8 copy-start.27
  89.9 0.8 copy-start.12
  90.8 18.0 %all-to-all-start.1 = ((f32[8,64,256]{2,1,0:T(8,128)}), f32[8,64,256]{2,1,0:T(8,128)}, u32[]{:S(2)}, u32[]{:S(2)}) async-start(f32[8,64,256]{2,1,0:T(8,128)} %copy-done.12), calls=%async_computation.1 | async-start | bytes 1048576 | tf_op jit(solution)/shard_map/all_to_all | solution.py:609
  95.3 29.7 %collective-permute-start.7 = (f32[2,512,256]{2,1,0:T(8,128)}, f32[2,512,256]{2,1,0:T(8,128)}, u32[]{:S(2)}, u32[]{:S(2)}) collective-permute-start(f32[2,512,256]{2,1,0:T(8,128)} %copy-done.36), channel_id=1, source_target_pairs={{0,1},{1,2},{2,3},{3,4},{4,5},{5,6},{6,7},{7,8},{8,9},{9,10},{10,1... | collective-permute-start | bytes 3145736 | tf_op jit(solution)/shard_map/ppermute | solution.py:642
  100.0 25.0 %collective-permute-start.8 = (f32[2,512,256]{2,1,0:T(8,128)}, f32[2,512,256]{2,1,0:T(8,128)}, u32[]{:S(2)}, u32[]{:S(2)}) collective-permute-start(f32[2,512,256]{2,1,0:T(8,128)} %copy-done.35), channel_id=1, source_target_pairs={{1,0},{2,1},{3,2},{4,3},{5,4},{6,5},{7,6},{8,7},{9,8},{10,9},{11,1... | collective-permute-start | bytes 3145736 | tf_op jit(solution)/shard_map/ppermute | solution.py:643
  108.8 1.1 copy-start.8
  109.9 1.1 copy-start.10
  111.0 13.9 %copy-start.14 = (bf16[2,2,256,256]{3,2,1,0:T(8,128)(2,1)S(1)}, bf16[2,2,256,256]{3,2,1,0:T(8,128)(2,1)}, u32[]{:S(2)}) copy-start(bf16[2,2,256,256]{3,2,1,0:T(8,128)(2,1)} %constant.104.clone.slope_x) | copy-start | bytes 1572868
  111.0 13.9 %copy-start.20 = (bf16[2,256,256]{2,1,0:T(8,128)(2,1)S(1)}, bf16[2,256,256]{2,1,0:T(8,128)(2,1)}, u32[]{:S(2)}) copy-start(bf16[2,256,256]{2,1,0:T(8,128)(2,1)} %constant.105.clone.slope_y) | copy-start | bytes 786436
  111.0 14.0 %copy-start.23 = (bf16[2,2,256,256]{3,2,1,0:T(8,128)(2,1)S(1)}, bf16[2,2,256,256]{3,2,1,0:T(8,128)(2,1)}, u32[]{:S(2)}) copy-start(bf16[2,2,256,256]{3,2,1,0:T(8,128)(2,1)} %constant.110.clone.from_slope_x) | copy-start | bytes 1572868
  111.1 14.0 %copy-start.24 = (bf16[2,2,256,256]{3,2,1,0:T(8,128)(2,1)S(1)}, bf16[2,2,256,256]{3,2,1,0:T(8,128)(2,1)}, u32[]{:S(2)}) copy-start(bf16[2,2,256,256]{3,2,1,0:T(8,128)(2,1)} %constant.108.clone.from_x) | copy-start | bytes 1572868
  111.1 14.0 %copy-start.29 = (bf16[2,256,256]{2,1,0:T(8,128)(2,1)S(1)}, bf16[2,256,256]{2,1,0:T(8,128)(2,1)}, u32[]{:S(2)}) copy-start(bf16[2,256,256]{2,1,0:T(8,128)(2,1)} %constant.111.clone.from_slope_y) | copy-start | bytes 786436
  111.1 14.0 %copy-start.30 = (bf16[2,256,256]{2,1,0:T(8,128)(2,1)S(1)}, bf16[2,256,256]{2,1,0:T(8,128)(2,1)}, u32[]{:S(2)}) copy-start(bf16[2,256,256]{2,1,0:T(8,128)(2,1)} %constant.109.clone.from_y) | copy-start | bytes 786436
  111.1 14.0 %copy-start.34 = (f32[3,2,512,256]{3,2,1,0:T(8,128)S(1)}, f32[3,2,512,256]{3,2,1,0:T(8,128)}, u32[]{:S(2)}) copy-start(f32[3,2,512,256]{3,2,1,0:T(8,128)} %copy-done.33) | copy-start | bytes 9437188
  114.8 10.2 %collective-permute-start.6 = (f32[4,256,256]{2,1,0:T(8,128)S(1)}, f32[4,256,256]{2,1,0:T(8,128)S(1)}, u32[]{:S(2)}, u32[]{:S(2)}) collective-permute-start(f32[4,256,256]{2,1,0:T(8,128)S(1)} %get-tuple-element.36), channel_id=1, source_target_pairs={{0,1},{1,0},{2,3},{3,2},{4,5},{5,4},{6,7},{7,6},{8,9},{9,8},{10,11... | collective-permute-start | bytes 3145736 | tf_op jit(solution)/shard_map/ppermute | solution.py:615
  125.1 27.2 %copy-start.3 = (f32[1,2,512,256]{3,2,1,0:T(8,128)S(1)}, f32[1,2,512,256]{3,2,1,0:T(8,128)}, u32[]{:S(2)}) copy-start(f32[1,2,512,256]{3,2,1,0:T(8,128)} %param.16) | copy-start | bytes 3145732
  125.1 27.2 %copy-start.5 = (s32[2,512,256]{2,1,0:T(8,128)S(1)}, s32[2,512,256]{2,1,0:T(8,128)}, u32[]{:S(2)}) copy-start(s32[2,512,256]{2,1,0:T(8,128)} %mask.3) | copy-start | bytes 3145732
  125.1 27.2 %copy-start.16 = (bf16[2,2,256,256]{3,2,1,0:T(8,128)(2,1)S(1)}, bf16[2,2,256,256]{3,2,1,0:T(8,128)(2,1)}, u32[]{:S(2)}) copy-start(bf16[2,2,256,256]{3,2,1,0:T(8,128)(2,1)} %constant.106.clone.into_x) | copy-start | bytes 1572868
  125.1 27.2 %copy-start.18 = (bf16[512,512]{1,0:T(8,128)(2,1)S(1)}, bf16[512,512]{1,0:T(8,128)(2,1)}, u32[]{:S(2)}) copy-start(bf16[512,512]{1,0:T(8,128)(2,1)} %constant.102.clone.dealias_x) | copy-start | bytes 1572868
  125.1 27.2 %copy-start.22 = (bf16[2,256,256]{2,1,0:T(8,128)(2,1)S(1)}, bf16[2,256,256]{2,1,0:T(8,128)(2,1)}, u32[]{:S(2)}) copy-start(bf16[2,256,256]{2,1,0:T(8,128)(2,1)} %constant.107.clone.into_y) | copy-start | bytes 786436
  125.1 27.2 %copy-start.26 = (bf16[256,256]{1,0:T(8,128)(2,1)S(1)}, bf16[256,256]{1,0:T(8,128)(2,1)}, u32[]{:S(2)}) copy-start(bf16[256,256]{1,0:T(8,128)(2,1)} %constant.103.clone.dealias_y) | copy-start | bytes 393220
  136.0 16.3 %collective-permute-start.9 = (f32[3,4,64,256]{3,2,1,0:T(8,128)S(1)}, f32[3,4,64,256]{3,2,1,0:T(8,128)S(1)}, u32[]{:S(2)}, u32[]{:S(2)}) collective-permute-start(f32[3,4,64,256]{3,2,1,0:T(8,128)S(1)} %get-tuple-element.41), channel_id=1, source_target_pairs={{0,16},{1,17},{2,18},{3,19},{4,20},{5,21},{6,22},{7,23},{8,24},{9,... | collective-permute-start | bytes 2359304 | tf_op jit(solution)/shard_map/ppermute | solution.py:657
  161.9 2.4 %collective-permute-start.10 = (f32[3,256,256]{2,1,0:T(8,128)S(1)}, f32[3,256,256]{2,1,0:T(8,128)S(1)}, u32[]{:S(2)}, u32[]{:S(2)}) collective-permute-start(f32[3,256,256]{2,1,0:T(8,128)S(1)} %get-tuple-element.43), channel_id=1, source_target_pairs={{0,1},{1,0},{2,3},{3,2},{4,5},{5,4},{6,7},{7,6},{8,9},{9,8},{10,11... | collective-permute-start | bytes 2359304 | tf_op jit(solution)/shard_map/ppermute | solution.py:601
  164.2 21.4 %copy-start.28 = (f32[32,256]{1,0:T(8,128)S(1)}, f32[32,256]{1,0:T(8,128)}, u32[]{:S(2)}) copy-start(f32[32,256]{1,0:T(8,128)} %exponential_bitcast_fusion.ratio) | copy-start | bytes 98308
  207.0 4.2 %collective-permute-start.11 = (f32[4,256,256]{2,1,0:T(8,128)S(1)}, f32[4,256,256]{2,1,0:T(8,128)S(1)}, u32[]{:S(2)}, u32[]{:S(2)}) collective-permute-start(f32[4,256,256]{2,1,0:T(8,128)S(1)} %get-tuple-element.45), channel_id=1, source_target_pairs={{0,1},{1,0},{2,3},{3,2},{4,5},{5,4},{6,7},{7,6},{8,9},{9,8},{10,11... | collective-permute-start | bytes 3145736 | tf_op jit(solution)/shard_map/ppermute | solution.py:615

commit v3 on v2

v3 whole, which is shorter than its diff:
```python
import functools
import math

import jax
import jax.numpy as jnp
import ml_dtypes
import numpy as np
from jax import lax
from jax.experimental import pallas as pl
from jax.experimental.pallas import tpu as pltpu
from jax.sharding import Mesh
from jax.sharding import PartitionSpec as P

step_size = 0.1
drag_coef = 0.75
cell_width = 4.0
half_type = jnp.bfloat16
full_type = jnp.float32
vmem_bytes = 26 * 1024 * 1024
levels_axis = ("chip", "core")
every_axis = ("sec", "chip", "core")


def derivative_table(length, cutoff):
    offset = np.arange(length)
    wavenumber = np.arange(1, cutoff + 1)
    phases = offset[:, None] * wavenumber[None, :] % length
    waves = np.sin(2.0 * math.pi / length * phases)
    first = -(2.0 / (cell_width * length)) * (waves @ (2.0 * math.pi / length * wavenumber))
    return first[(offset[:, None] - offset[None, :]) % length]


def real_basis(length):
    midpoint = length // 2
    row = np.arange(length)
    wavenumber = np.where(row <= midpoint, row, row - midpoint)
    angles = 2.0 * math.pi / length * (wavenumber[:, None] * row[None, :] % length)
    scales = np.where((row == 0) | (row == midpoint), math.sqrt(1.0 / length), math.sqrt(2.0 / length))
    return scales[:, None] * np.where((row <= midpoint)[:, None], np.cos(angles), np.sin(angles))


def wave_square(length):
    midpoint = length // 2
    row = np.arange(length)
    wavenumber = np.where(row < midpoint, row, np.where(row == midpoint, 0, row - midpoint))
    return (2.0 * math.pi / (length * cell_width) * wavenumber) ** 2


def high_low(table):
    table = np.asarray(table, np.float32)
    high = table.astype(ml_dtypes.bfloat16)
    low = (table - high.astype(np.float32)).astype(ml_dtypes.bfloat16)
    return np.stack([high, low], axis=-3)


def build_tables(length_x, length_y):
    mid = length_x // 2
    full_x = derivative_table(length_x, length_x // 2 - 1)
    full_y = derivative_table(length_y, length_y // 2 - 1)
    basis_x = real_basis(length_x)
    basis_y = real_basis(length_y)
    left_part, right_part = full_x[:mid, :mid], full_x[:mid, mid:]
    derived = full_x @ basis_x.T
    squares = wave_square(length_x)[:, None] + wave_square(length_y)[None, :]
    decay = 2.0 * np.arcsinh(0.5 * np.sqrt(squares))
    return {
        "dealias_x": derivative_table(length_x, (length_x - 1) // 3).astype(ml_dtypes.bfloat16),
        "dealias_y": derivative_table(length_y, (length_y - 1) // 3).T.astype(ml_dtypes.bfloat16),
        "slope_x": high_low(np.stack([left_part + right_part, left_part - right_part])),
        "slope_y": high_low(full_y.T),
        "into_x": high_low(np.stack([basis_x[0::2, :mid], basis_x[1::2, :mid]])),
        "into_y": high_low(basis_y.T),
        "from_x": high_low(np.stack([basis_x[0::2, :mid].T, basis_x[1::2, :mid].T])),
        "from_y": high_low(basis_y),
        "from_slope_x": high_low(np.stack([derived[:mid, 0::2], derived[:mid, 1::2]])),
        "from_slope_y": high_low(basis_y @ full_y.T),
        "decay": np.stack([decay[0::2], decay[1::2]]).astype(np.float32),
    }


def product(one, other):
    return jnp.dot(one, other, preferred_element_type=full_type)


def halves(block):
    high = block.astype(half_type)
    return high, (block - high.astype(full_type)).astype(half_type)


def from_left(table, block):
    high, low = halves(block)
    return product(table[0], high) + product(table[0], low) + product(table[1], high)


def from_right(block, table):
    high, low = halves(block)
    return product(high, table[0]) + product(low, table[0]) + product(high, table[1])


def vmem():
    return pl.BlockSpec(memory_space=pltpu.VMEM)


def smem():
    return pl.BlockSpec(memory_space=pltpu.SMEM)


def hbm():
    return pl.BlockSpec(memory_space=pltpu.HBM)


def call(kernel, outs, in_specs, scratch, flops, args, out_specs=None):
    moved = sum(math.prod(a.shape) * 4 for a in (*outs, *args))
    return pl.pallas_call(
        kernel,
        out_shape=outs,
        in_specs=in_specs,
        out_specs=out_specs or tuple(vmem() for _ in outs),
        scratch_shapes=scratch,
        compiler_params=pltpu.CompilerParams(vmem_limit_bytes=vmem_bytes),
        cost_estimate=pl.CostEstimate(flops=int(flops), bytes_accessed=moved, transcendentals=0),
    )(*args)


def shaped(*dims, kind=full_type):
    return jax.ShapeDtypeStruct(dims, kind)


def tendency_steps(state, rounded, viscosity, mask, drag, dealias_x, dealias_y, put):
    depth = state.shape[1] - 2
    length_x = state.shape[2]
    rows = length_x // 2
    for z in range(depth):
        for c in range(3):
            rounded[c, z] = state[c, z + 1].astype(half_type)
    for z in range(depth):
        for b in range(length_x // rows):
            part = pl.ds(b * rows, rows)
            u, v, w = (state[c, z + 1, part, :] for c in range(3))
            slow = drag * mask[z, part, :].astype(full_type) * jnp.abs(u)
            nu = viscosity[z, part, :]
            for c in range(3):
                center = state[c, z + 1, part, :]
                upper = state[c, z + 2, part, :]
                lower = state[c, z, part, :]
                grad_x = product(dealias_x[part, :], rounded[c, z])
                grad_y = product(rounded[c, z, part, :], dealias_y[...])
                advected = u * grad_x + v * grad_y + w * (0.5 * (upper - lower))
                change = nu * (upper - 2.0 * center + lower) - advected - slow * center
                put(c, z, part, center, change)


def folded(block, sign):
    mid = block.shape[0] // 2
    return block[:mid] + sign * block[mid:]


def source_spectra(state, out, half, slope_x, slope_y, into_x, into_y):
    depth = state.shape[1]
    sign = (1 - 2 * half).astype(full_type)
    slope, into = slope_x[half], into_x[half]
    lifted = [folded(state[2, z], sign) for z in range(depth)]
    sources = []
    for z in range(depth):
        spread = from_left(slope, folded(state[0, z], sign))
        spread += from_right(folded(state[1, z], sign), slope_y)
        sources.append(spread + lifted[z] - (lifted[z - 1] if z else 0.0))
    sources.append(lifted[depth - 1])
    for z, source in enumerate(sources):
        out[z] = from_right(from_left(into, source), into_y)


def edges_kernel(velocity, low, high):
    depth = velocity.shape[1]
    low[...] = velocity[:, depth - 1]
    high[...] = velocity[:, 0]


def columns_kernel(index, velocity, columns, columns_low, columns_high):
    depth = velocity.shape[1]

    def one(i, carry):
        row = pl.ds(index[i], 1)
        here = pl.ds(i, 1)
        for c in range(3):
            for z in range(depth):
                taken = velocity[c, z, row, :]
                columns[c, z, here, :] = taken
                if z == depth - 1:
                    columns_low[c, here, :] = taken
                if z == 0:
                    columns_high[c, here, :] = taken
        return carry

    lax.fori_loop(0, index.shape[0], one, 0)


def insert_rows(index, pairs):
    def one(i, carry):
        row = pl.ds(index[i], 1)
        for target, rows in pairs:
            for c in range(3):
                target[c, row, :] = rows[c, pl.ds(i, 1), :]
        return carry

    lax.fori_loop(0, index.shape[0], one, 0)


def inner_kernel(
    flags, index, velocity, columns, *refs,
):
    depth = velocity.shape[1]
    is_second = len(refs) == 12
    if is_second:
        earlier, earlier_columns, *refs, start = refs
    viscosity, mask, dealias_x, dealias_y, partial, weights, state, rounded, sems, *_ = refs
    is_farm = flags[0]
    copies = [pltpu.make_async_copy(velocity, state.at[:, pl.ds(1, depth)], sems.at[0])]
    if is_second:
        copies.append(pltpu.make_async_copy(earlier, start, sems.at[1]))
    for copy in copies:
        copy.start()
    state[:, 0] = jnp.zeros_like(state[:, 0])
    state[:, depth + 1] = jnp.zeros_like(state[:, 0])
    for copy in copies:
        copy.wait()

    @pl.when(is_farm == 1)
    def _():
        pairs = [(state.at[:, 1 + z], columns.at[:, z]) for z in range(depth)]
        if is_second:
            pairs += [(start.at[:, z], earlier_columns.at[:, z]) for z in range(depth)]
        insert_rows(index, pairs)

    drag = drag_coef * is_farm.astype(full_type)
    share = 0.5 if is_second else 1.0

    def put(c, z, part, center, change):
        moved = center + step_size * change
        if is_second:
            moved = 0.5 * (start[c, z, part, :] + moved)
        partial[c, z, part, :] = moved

    tendency_steps(state, rounded, viscosity, mask, drag, dealias_x, dealias_y, put)
    weights[0] = share * step_size * (viscosity[0] + 0.5 * state[2, 1])
    weights[1] = share * step_size * (viscosity[depth - 1] - 0.5 * state[2, depth])


def outer_kernel(
    flags, index, partial, weights, low, high, columns_low, columns_high,
    slope_x, slope_y, into_x, into_y,
    middle, theirs,
    ghosts, sems,
):
    depth = middle.shape[1]
    is_farm, core, is_lid = flags[0], flags[1], flags[3]
    copies = [
        pltpu.make_async_copy(low, ghosts.at[0], sems.at[0]),
        pltpu.make_async_copy(high, ghosts.at[1], sems.at[1]),
    ]
    for copy in copies:
        copy.start()
    for copy in copies:
        copy.wait()

    @pl.when(is_farm == 1)
    def _():
        insert_rows(index, [(ghosts.at[0], columns_low), (ghosts.at[1], columns_high)])

    for c in range(3):
        for z in range(depth):
            moved = partial[c, z]
            if z == 0:
                moved += weights[0] * ghosts[0, c]
            if z == depth - 1:
                moved += weights[1] * ghosts[1, c]
                if c == 2:
                    moved = jnp.where(is_lid == 1, 0.0, moved)
            middle[c, z] = moved
    source_spectra(middle, theirs, 1 - core, slope_x, slope_y, into_x, into_y)


def own_spectra_kernel(flags, middle, slope_x, slope_y, into_x, into_y, mine, *edges):
    depth = middle.shape[1]
    mid = middle.shape[2] // 2
    source_spectra(middle, mine, flags[1], slope_x, slope_y, into_x, into_y)
    if not edges:
        return
    upward, downward = edges
    downward[0] = middle[0, 0]
    downward[1] = middle[1, 0]
    top = depth - 1
    even, odd = (
        0.5 * from_left(slope_x[half], folded(middle[2, top], 1.0 - 2.0 * half))
        for half in range(2)
    )
    upward[0, :mid] = middle[0, top, :mid] + (even + odd)
    upward[0, mid:] = middle[0, top, mid:] + (even - odd)
    upward[1] = middle[1, top] + from_right(middle[2, top], slope_y)


def chip_levels(core, mine, other, depth):
    is_low = core == 0
    low = [jnp.where(is_low, mine[i], other[i]) for i in range(depth + 1)]
    high = [jnp.where(is_low, other[i], mine[i]) for i in range(depth + 1)]
    levels = low[:depth] + [high[0] - low[depth]] + high[1:depth]
    return levels, low[depth], high[depth]


class Coefficients:
    def __init__(self, stacked, count):
        self.mu = lambda: stacked[0]
        self.phi = lambda i: stacked[1 + i]
        self.psi = lambda i: stacked[2 + count + i]
        self.flux_low = lambda i: stacked[3 + 2 * count + i]
        self.flux_high = lambda i: stacked[3 + 3 * count + i]
        self.entry = lambda: stacked[4 + 4 * count]
        self.scale = lambda: stacked[5 + 4 * count]


def gather_kernel(flags, mine, other, stacked, out, work, packed, sems):
    core = flags[1]
    depth = mine.shape[0] - 1
    count = 2 * depth
    tables = Coefficients(stacked, count)
    levels, _, top = chip_levels(core, mine, other, depth)
    mu = tables.mu()
    forward = tables.phi(0) * levels[0]
    for i in range(1, count):
        forward = mu * forward + tables.phi(i) * levels[i]
    work[0] = mu * forward - tables.phi(count) * top
    backward = -tables.psi(count) * top
    for i in reversed(range(count)):
        backward = tables.psi(i) * levels[i] + mu * backward
    work[1] = backward
    chips = out.shape[0]
    rows = out.shape[1] // 2
    for chip in range(chips):
        packed[chip, :rows] = work[0, chip * rows : (chip + 1) * rows]
        packed[chip, rows:] = work[1, chip * rows : (chip + 1) * rows]
    copy = pltpu.make_async_copy(packed, out, sems.at[0])
    copy.start()
    copy.wait()


def scan_kernel(received, ratio, out, taken, packed, sems):
    chips = received.shape[0]
    rows = received.shape[1] // 2
    copy = pltpu.make_async_copy(received, taken, sems.at[0])
    copy.start()
    factor = ratio[...]
    copy.wait()
    carried = jnp.zeros_like(factor)
    for chip in range(chips):
        packed[chip, :rows] = carried
        carried = factor * carried + taken[chip, :rows]
    carried = jnp.zeros_like(factor)
    for chip in reversed(range(chips)):
        packed[chip, rows:] = carried
        carried = factor * carried + taken[chip, rows:]
    copy = pltpu.make_async_copy(packed, out, sems.at[1])
    copy.start()
    copy.wait()


def solve_kernel(flags, mine, other, stacked, received, own, partner, work, scanned, sems):
    core = flags[1]
    depth = mine.shape[0] - 1
    count = 2 * depth
    tables = Coefficients(stacked, count)
    chips = scanned.shape[0]
    rows = scanned.shape[1] // 2
    copy = pltpu.make_async_copy(received, scanned, sems.at[0])
    copy.start()
    copy.wait()
    for chip in range(chips):
        work[0, chip * rows : (chip + 1) * rows] = scanned[chip, :rows]
        work[1, chip * rows : (chip + 1) * rows] = scanned[chip, rows:]
    levels, between, top = chip_levels(core, mine, other, depth)
    mu = tables.mu()
    forward = [work[0] + tables.phi(0) * levels[0]]
    for i in range(1, count):
        forward.append(mu * forward[-1] + tables.phi(i) * levels[i])
    backward = [work[1] - tables.psi(count) * top]
    for i in reversed(range(1, count)):
        backward.append(tables.psi(i) * levels[i] + mu * backward[-1])
    backward.reverse()
    flux = [
        tables.flux_low(i) * forward[i] - tables.flux_high(i + 1) * backward[i]
        for i in range(count)
    ]
    under = tables.entry() * work[0] - tables.flux_high(0) * (
        tables.psi(0) * levels[0] + mu * backward[0]
    )
    pressure = [
        -tables.scale() * (tables.psi(i) * forward[i] + mu * tables.phi(i) * backward[i])
        for i in (0, depth)
    ]
    low = [pressure[0], *flux[:depth], under]
    high = [pressure[1], *flux[depth:], flux[depth - 1] - between]
    is_low = core == 0
    for i in range(own.shape[0]):
        own[i] = jnp.where(is_low, low[i], high[i])
        partner[i] = jnp.where(is_low, high[i], low[i])


def physical_half(fields, half, ghosts, from_x, from_y, from_slope_x, from_slope_y, slots):
    depth = fields.shape[0] - (2 if ghosts else 1)
    level = fields[0]
    pressures = [level - fields[depth + 1]] if ghosts else []
    for z in range(depth):
        pressures.append(level)
        level = level + fields[1 + z]
    if ghosts:
        pressures.append(level)
    for i, block in enumerate(pressures):
        slots[2 * i] = from_left(from_slope_x[half], from_right(block, from_y))
        slots[2 * i + 1] = from_left(from_x[half], from_right(block, from_slope_y))
    for i in range(fields.shape[0] - 1):
        block = from_right(fields[1 + i], from_y)
        slots[2 * len(pressures) + i] = from_left(from_x[half], block)


def own_half_kernel(flags, mine, from_x, from_y, from_slope_x, from_slope_y, slots, *, ghosts):
    physical_half(mine, flags[1], ghosts, from_x, from_y, from_slope_x, from_slope_y, slots)


def unfolded(core, mine, other, i):
    sign = (1 - 2 * core).astype(full_type)
    return mine[i] + other[i], sign * (mine[i] - other[i])


def fringe_kernel(
    flags, index, mine, other, middle, rows_x, rows_slope_x, from_y, from_slope_y,
    columns, columns_low, columns_high,
):
    core = flags[1]
    depth = middle.shape[1]
    fields = [
        [jnp.where(core == half, mine[i], other[i]) for i in range(mine.shape[0])]
        for half in range(2)
    ]
    pressure = [fields[half][0] for half in range(2)]
    for z in range(depth):
        slope = sum(from_left(rows_slope_x[half], pressure[half]) for half in range(2))
        plain = sum(from_left(rows_x[half], pressure[half]) for half in range(2))
        lift = sum(from_left(rows_x[half], fields[half][1 + z]) for half in range(2))
        columns[0, z] = from_right(slope, from_y)
        columns[1, z] = from_right(plain, from_slope_y)
        columns[2, z] = from_right(lift, from_y)
        pressure = [pressure[half] + fields[half][1 + z] for half in range(2)]

    def one(i, carry):
        row = pl.ds(index[i], 1)
        here = pl.ds(i, 1)
        for c in range(3):
            for z in range(depth):
                value = middle[c, z, row, :] - columns[c, z, here, :]
                columns[c, z, here, :] = value
                if z == depth - 1:
                    columns_low[c, here, :] = value
                if z == 0:
                    columns_high[c, here, :] = value
        return carry

    lax.fori_loop(0, index.shape[0], one, 0)


def corrected_kernel(
    flags, slots, fields, middle, from_below, from_above, slope_x, slope_y,
    from_x, from_y, from_slope_x, from_slope_y,
    out, low, high,
    others,
):
    core, is_floor, is_lid = flags[1], flags[2], flags[3]
    depth = middle.shape[1]
    mid = middle.shape[2] // 2
    physical_half(
        fields, 1 - core, True, from_x, from_y, from_slope_x, from_slope_y, others
    )
    pressures = depth + 2
    open_low = (1 - is_floor).astype(full_type)
    open_high = (1 - is_lid).astype(full_type)
    sides = (slice(0, mid), slice(mid, 2 * mid))
    for z in range(depth):
        for c in range(3):
            slot = 2 * (1 + z) + c if c < 2 else 2 * pressures + z
            for side, change in zip(sides, unfolded(core, slots, others, slot)):
                out[c, z, side] = middle[c, z, side] - change
    for c in range(2):
        for side, change in zip(sides, unfolded(core, slots, others, c)):
            low[c, side] = open_low * (from_below[c, side] - change)
        slot = 2 * (depth + 1) + c
        for side, change in zip(sides, unfolded(core, slots, others, slot)):
            high[c, side] = open_high * (from_above[c, side] - change)
    slot = 2 * pressures + depth
    for side, change in zip(sides, unfolded(core, slots, others, slot)):
        low[2, side] = -open_low * change
    even, odd = (
        0.5 * from_left(slope_x[half], folded(high[0], 1.0 - 2.0 * half)) for half in range(2)
    )
    for side, change in zip(sides, (even + odd, even - odd)):
        spread = change + from_right(high[1, side], slope_y)
        high[2, side] = open_high * (out[2, depth - 1, side] - spread)


def last_kernel(
    flags, slots, fields, final, from_x, from_y, from_slope_x, from_slope_y,
    out,
    others,
):
    core = flags[1]
    depth = final.shape[1]
    mid = final.shape[2] // 2
    physical_half(
        fields, 1 - core, False, from_x, from_y, from_slope_x, from_slope_y, others
    )
    sides = (slice(0, mid), slice(mid, 2 * mid))
    for z in range(depth):
        for c in range(3):
            slot = 2 * z + c if c < 2 else 2 * depth + z
            for side, change in zip(sides, unfolded(core, slots, others, slot)):
                out[c, z, side] = final[c, z, side] - change


def coefficients(decay, first_level, count, height):
    def gap(steps):
        return -jnp.expm1(-steps * decay)

    still = decay == 0.0
    below = jnp.arange(count + 1, dtype=full_type)[:, None, None] + first_level
    mu = jnp.exp(-decay)
    safe = jnp.where(still, 1.0, gap(2.0 * height))

    def ratio(steps):
        return jnp.where(still, steps / height, gap(2.0 * steps) / safe)

    share = 1.0 / (1.0 + mu)
    phi = 1.0 + jnp.exp(-(2.0 * below + 1.0) * decay)
    psi = 1.0 + jnp.exp(-(2.0 * (height - below) - 1.0) * decay)
    flux_low = mu * share * ratio(height - 1.0 - below[:count])
    flux_high = mu * share * ratio(below)
    entry = share * ratio(height - below[:1])
    scale = jnp.where(still, 0.0, mu / (jnp.where(still, 1.0, gap(2.0)) * safe))
    return jnp.concatenate([mu[None], phi, psi, flux_low, flux_high, entry, scale[None]])


def local(velocity, eddy_viscosity, turbine_mask, fringe_columns):
    current = velocity[0]
    viscosity = eddy_viscosity[0]
    _, depth, length_x, length_y = current.shape
    mid = length_x // 2
    fringe = fringe_columns.shape[0]
    chips = lax.axis_size("chip")
    devices = 2 * chips
    height = devices * depth
    count = 2 * depth
    rows = mid // chips
    section = lax.axis_index("sec")
    chip = lax.axis_index("chip")
    core = lax.axis_index("core")
    place = 2 * chip + core
    is_farm = section == 1
    flags = jnp.stack([is_farm, core, place == 0, place == devices - 1]).astype(jnp.int32)
    tables = {name: jnp.asarray(table) for name, table in build_tables(length_x, length_y).items()}

    upward_route = [(i, i + 1) for i in range(devices - 1)]
    downward_route = [(i + 1, i) for i in range(devices - 1)]
    swap = [(0, 1), (1, 0)]

    def across(shift):
        return [
            (i, devices + i + shift) for i in range(devices) if 0 <= i + shift < devices
        ]

    state_shape = (3, depth + 2, length_x, length_y)
    own_shape = shaped(3, depth, length_x, length_y)
    edge = shaped(2, length_x, length_y)
    whole_edge = shaped(3, length_x, length_y)
    band = shaped(3, fringe, length_y)
    bands = (shaped(3, depth, fringe, length_y), band, band)
    decay = lax.dynamic_index_in_dim(tables["decay"], core, 0, keepdims=False)
    stacked = coefficients(decay, (chip * count).astype(full_type), count, float(height))
    ratio = jnp.exp(-float(count) * lax.dynamic_slice_in_dim(decay, chip * rows, rows, 0))

    low, high = call(edges_kernel, (whole_edge, whole_edge), [vmem()], [], 0, (current,))
    low, high, held = lax.optimization_barrier((low, high, current))
    low = lax.ppermute(low, levels_axis, upward_route)
    high = lax.ppermute(high, levels_axis, downward_route)
    farm_downward = [(devices + i + 1, devices + i) for i in range(devices - 1)]

    held, stacked = lax.optimization_barrier((held, stacked))
    taken = call(columns_kernel, bands, [smem(), vmem()], [], 0, (fringe_columns, held))
    columns = lax.ppermute(taken[0], every_axis, across(0))
    columns_low = lax.ppermute(taken[1], every_axis, across(1))
    columns_high = lax.ppermute(columns[:, 0], every_axis, farm_downward)
    away = jnp.where(fringe_columns < mid, 1.0, -1.0)[:, None]
    signs = jnp.stack([jnp.ones_like(away), away])[:, None].astype(half_type)
    rows_x, rows_slope_x = (
        jnp.take(tables[name], fringe_columns % mid, axis=2) * signs
        for name in ("from_x", "from_slope_x")
    )

    block = length_x * length_y * 2
    spectrum = shaped(depth + 1, mid, length_y)
    message = shaped(chips, 2 * rows, length_y)
    tendency_tables = [tables["dealias_x"], tables["dealias_y"]]
    source_tables = [tables[n] for n in ("slope_x", "slope_y", "into_x", "into_y")]
    pressure_tables = [tables[n] for n in ("from_x", "from_y", "from_slope_x", "from_slope_y")]

    packed = pltpu.VMEM(message.shape, full_type)
    halved = pltpu.VMEM((2, mid, length_y), full_type)

    def solve(mine, other, fields, beside=()):
        (sums,) = call(
            gather_kernel, (message,), [smem(), vmem(), vmem(), vmem()],
            [halved, packed, pltpu.SemaphoreType.DMA((1,))], 8 * count * block,
            (flags, mine, other, stacked), (hbm(),),
        )
        sums = lax.all_to_all(sums, "chip", split_axis=0, concat_axis=0, tiled=True)
        (sums,) = call(
            scan_kernel, (message,), [hbm(), vmem()],
            [packed, packed, pltpu.SemaphoreType.DMA((2,))], 4 * block, (sums, ratio), (hbm(),),
        )
        sums, *beside = lax.optimization_barrier((sums, *beside))
        sums = lax.all_to_all(sums, "chip", split_axis=0, concat_axis=0, tiled=True)
        solved = shaped(fields, mid, length_y)
        own, partner = call(
            solve_kernel, (solved, solved), [smem()] + [vmem()] * 3 + [hbm()],
            [halved, packed, pltpu.SemaphoreType.DMA((1,))], 16 * count * block,
            (flags, mine, other, stacked, sums),
        )
        partner = lax.ppermute(partner, "core", swap)
        ghosts = bool(beside)
        half_fields = 3 * depth + (5 if ghosts else 0)
        (slots,) = call(
            functools.partial(own_half_kernel, ghosts=ghosts),
            (shaped(half_fields, mid, length_y),), [smem()] + [vmem()] * 5, [],
            3 * half_fields * block * (length_x // 2 + length_y) // 2,
            (flags, own, *pressure_tables),
        )
        return own, partner, slots, *beside

    rounded = pltpu.VMEM((3, depth, length_x, length_y), half_type)
    state = pltpu.VMEM(state_shape, full_type)
    tendency_flops = 3 * depth * block * (length_x + length_y)
    source_flops = 3 * depth * block * (length_x + 2 * length_y)

    ghosts = pltpu.VMEM((2, 3, length_x, length_y), full_type)
    partial, weights = call(
        inner_kernel,
        (own_shape, edge),
        [smem(), smem(), hbm()] + [vmem()] * 5,
        [state, rounded, pltpu.SemaphoreType.DMA((1,))],
        tendency_flops,
        (flags, fringe_columns, current, columns, viscosity, turbine_mask, *tendency_tables),
    )
    partial, stacked, ratio, rows_x, rows_slope_x = lax.optimization_barrier(
        (partial, stacked, ratio, rows_x, rows_slope_x)
    )

    def spectra(partial, weights, low, high, columns_low, columns_high, edges):
        middle, theirs = call(
            outer_kernel,
            (own_shape, spectrum),
            [smem(), smem()] + [vmem()] * 2 + [hbm()] * 2 + [vmem()] * 6,
            [ghosts, pltpu.SemaphoreType.DMA((2,))],
            source_flops // 2,
            (flags, fringe_columns, partial, weights, low, high, columns_low, columns_high,
             *source_tables),
        )
        other = lax.ppermute(theirs, "core", swap)
        mine, *edges = call(
            own_spectra_kernel,
            (spectrum, *edges),
            [smem()] + [vmem()] * 5,
            [],
            source_flops // 2,
            (flags, middle, *source_tables),
        )
        return middle, mine, other, *edges

    middle, mine, other, upward, downward = spectra(
        partial, weights, low, high, columns_low, columns_high, (edge, edge)
    )
    from_below = lax.ppermute(upward, levels_axis, upward_route)
    from_above = lax.ppermute(downward, levels_axis, downward_route)
    own, partner, slots, from_below, from_above = solve(
        mine, other, depth + 2, (from_below, from_above)
    )
    taken = call(
        fringe_kernel, bands, [smem(), smem()] + [vmem()] * 7, [],
        9 * depth * block * (length_x + length_y) // 8,
        (flags, fringe_columns, own, partner, middle, rows_x, rows_slope_x,
         tables["from_y"], tables["from_slope_y"]),
    )
    partner, *taken = lax.optimization_barrier((partner, *taken))
    new_columns = lax.ppermute(taken[0], every_axis, across(0))
    new_columns_low = lax.ppermute(taken[1], every_axis, across(1))
    half_fields = 3 * depth + 5
    corrected, low, high = call(
        corrected_kernel,
        (own_shape, whole_edge, whole_edge),
        [smem()] + [vmem()] * 11,
        [pltpu.VMEM((half_fields, mid, length_y), full_type)],
        3 * half_fields * block * (length_x // 2 + length_y) // 2,
        (flags, slots, partner, middle, from_below, from_above, tables["slope_x"],
         tables["slope_y"], *pressure_tables),
    )
    new_columns, corrected = lax.optimization_barrier((new_columns, corrected))
    new_columns_high = lax.ppermute(new_columns[:, 0], every_axis, farm_downward)
    partial, weights = call(
        inner_kernel,
        (own_shape, edge),
        [smem(), smem(), hbm(), vmem(), hbm()] + [vmem()] * 5,
        [state, rounded, pltpu.SemaphoreType.DMA((2,)), pltpu.VMEM(own_shape.shape, full_type)],
        tendency_flops,
        (flags, fringe_columns, corrected, new_columns, current, columns, viscosity, turbine_mask,
         *tendency_tables),
    )
    final, mine, other = spectra(
        partial, weights, low, high, new_columns_low, new_columns_high, ()
    )
    _, partner, slots = solve(mine, other, depth + 1)
    half_fields = 3 * depth
    (new,) = call(
        last_kernel,
        (own_shape,),
        [smem()] + [vmem()] * 7,
        [pltpu.VMEM((half_fields, mid, length_y), full_type)],
        3 * half_fields * block * (length_x // 2 + length_y) // 2,
        (flags, slots, partner, final, *pressure_tables),
    )
    return new[None]


def solution(mesh):
    sections, devices = mesh.devices.shape
    fine = Mesh(mesh.devices.reshape(sections, devices // 2, 2), every_axis)
    placed = (
        P("sec", None, levels_axis, None, None),
        P("sec", levels_axis, None, None),
        P(levels_axis, None, None),
        P(),
    )
    return jax.shard_map(
        local,
        mesh=fine,
        in_specs=placed,
        out_specs=P("sec", None, levels_axis, None, None),
        check_vma=False,
    )
```

time: 217 us -> 190 us (0.88)
  blocking collectives: 36.3 us -> 80.8 us
  waiting for transfers between devices: 56 us -> 12.8 us
  starting transfers between devices: 37 us -> 26.5 us
  other arithmetic: 14.8 us -> 4.43 us
  Pallas kernels: 54.4 us -> 49.7 us
  local copies, waits for them, and re-layouts: 16.7 us -> 14 us
    all_to_all x2 -> x4, blocking collectives: 36.3 us -> 80.8 us  [solve(): sums = lax.all_to_all(sums, 'chip', split_axis=0, concat_axis=0, tiled=True)]
    all_to_all x2 -> x0, waiting for transfers between devices: 19.2 us -> none  [solve(): sums = lax.all_to_all(sums, 'chip', split_axis=0, concat_axis=0, tiled=True)]
    all_to_all x2 -> x0, starting transfers between devices: 14.9 us -> none  [solve(): sums = lax.all_to_all(sums, 'chip', split_axis=0, concat_axis=0, tiled=True)]
    ppermute x8 -> x10, waiting for transfers between devices: 24.8 us -> 12 us  [the longest x1 6 us: local(): columns = lax.ppermute(taken[0], every_axis, across(0))]
    ppermute x1, waiting for transfers between devices: 7.94 us -> 0.01 us  [local(): from_below = lax.ppermute(upward, levels_axis, upward_route)]
    unnamed x92 -> x51, local copies, waits for them, and re-layouts: 16.7 us -> 8.88 us
    unnamed x5 -> x7, other arithmetic: 8.14 us -> 1.96 us
    ppermute x8 -> x10, starting transfers between devices: 9.42 us -> 14.5 us  [the longest x2 4.07 us: solve(): partner = lax.ppermute(partner, 'core', swap)]
  transfers between devices with their start and end apart: 14 -> 14, of which waited for: 8 -> 6; matrix products, arithmetic and copies ran while one was open for 7% -> 5% of each run, Pallas kernels for 4% -> 14%
where the time goes in v3:
time: 190 us; the launch traced here: 189 us
  blocking collectives  80.8 us (43%)
  Pallas kernels  49.7 us (26%)
  starting transfers between devices  26.5 us (14%)
  local copies, waits for them, and re-layouts  14 us (7%)
  waiting for transfers between devices  12.8 us (7%)
  other arithmetic  4.43 us (2%)
    all_to_all x4, blocking collectives, solve(): sums = lax.all_to_all(sums, 'chip', split_axis=0, concat_axis=0, tiled=True)  80.8 us
    pallas_call x19, Pallas kernels, call(): pl.pallas_call(kernel, out_shape=outs, in_specs=in_specs, out_specs=out_s...  49.7 us
    unnamed x51, local copies, waits for them, and re-layouts  8.88 us
    ppermute x1, waiting for transfers between devices, local(): columns = lax.ppermute(taken[0], every_axis, across(0))  6 us
    gather x2, local copies, waits for them, and re-layouts, local(): jnp.take(tables[name], fringe_columns % mid, axis=2) * signs  5.08 us
    ppermute x1, starting transfers between devices, local(): from_below = lax.ppermute(upward, levels_axis, upward_route)  4.4 us
    ppermute x2, starting transfers between devices, solve(): partner = lax.ppermute(partner, 'core', swap)  4.07 us
  transfers between devices with their start and end apart: 14, of which 6 were waited for; matrix products, arithmetic and copies ran while one was open for 5% of the time, Pallas kernels for 14%

profile of v3, /device:TPU:5, one launch (start us, length us, event | category | flops | bytes accessed | tf_op | source)
XLA Modules:
  0.0 189.0 jit_solution(211358496419568466)
XLA Ops:
  0.0 1.9 copy-done.1
  1.9 1.9 shard_map.145
  3.8 3.7 %collective-permute-start.1 = (f32[3,512,256]{2,1,0:T(8,128)}, f32[3,512,256]{2,1,0:T(8,128)}, u32[]{:S(2)}, u32[]{:S(2)}) collective-permute-start(f32[3,512,256]{2,1,0:T(8,128)} %get-tuple-element.57), channel_id=1, source_target_pairs={{0,1},{1,2},{2,3},{3,4},{4,5},{5,6},{6,7},{7,8},{8,9},{9,10},{10,1... | collective-permute-start | bytes 4718600 | tf_op jit(solution)/shard_map/ppermute | solution.py:588
  7.4 1.9 %collective-permute-start.2 = (f32[3,512,256]{2,1,0:T(8,128)}, f32[3,512,256]{2,1,0:T(8,128)}, u32[]{:S(2)}, u32[]{:S(2)}) collective-permute-start(f32[3,512,256]{2,1,0:T(8,128)} %get-tuple-element.58), channel_id=1, source_target_pairs={{1,0},{2,1},{3,2},{4,3},{5,4},{6,5},{7,6},{8,7},{9,8},{10,9},{11,1... | collective-permute-start | bytes 4718600 | tf_op jit(solution)/shard_map/ppermute | solution.py:589
  9.5 0.2 fusion.14
  9.7 0.2 add_dynamic-update-slice_fusion.1
  10.0 0.2 add_dynamic-update-slice_fusion
  10.2 0.0 copy-start.22
  10.2 0.5 multiply_dynamic-update-slice_fusion.1
  10.8 0.6 multiply_dynamic-update-slice_fusion
  11.5 0.3 fusion.5
  11.7 0.3 fusion.8.stacked
  12.0 2.5 %copy-done = f32[22,256,256]{2,1,0:T(8,128)} copy-done((f32[22,256,256]{2,1,0:T(8,128)}, f32[22,256,256]{2,1,0:T(8,128)S(1)}, u32[]{:S(2)}) %copy-start) | copy-done | bytes 5767192
  14.5 2.3 %shard_map.146 = (f32[3,2,64,256]{3,2,1,0:T(8,128)}, f32[3,64,256]{2,1,0:T(8,128)}, f32[3,64,256]{2,1,0:T(8,128)}) custom-call(s32[64]{0:T(128)S(1)} %copy-done.20, f32[3,2,512,256]{3,2,1,0:T(8,128)S(1)} %bitcast.41), custom_call_target="tpu_custom_call" | custom-call | bytes 3932416 | tf_op jit(solution)/shard_map/pallas_call | solution.py:114
  16.8 1.3 collective-permute-start.3
  18.1 1.3 collective-permute-start
  19.5 2.5 %gather_fusion.1 = bf16[64,2,2,256]{3,2,1,0:T(2,128)(2,1)} fusion(bf16[2,2,256,256]{3,1,2,0:T(2,128)(2,1)} %constant.140.clone2.1, s32[1024]{0:T(1024)S(1)} %pad_clamp_fusion), kind=kCustom, calls=%fused_computation.1.clone | custom fusion | bytes 262400 | tf_op jit(solution)/shard_map/jit(_take)/gather | solution.py:600
  22.1 2.5 %gather_fusion = bf16[64,2,2,256]{3,2,1,0:T(2,128)(2,1)} fusion(bf16[2,2,256,256]{3,1,2,0:T(2,128)(2,1)} %constant.138.clone2.1, s32[1024]{0:T(1024)S(1)} %pad_clamp_fusion), kind=kCustom, calls=%fused_computation.clone | custom fusion | bytes 262400 | tf_op jit(solution)/shard_map/jit(_take)/gather | solution.py:600
  24.6 0.8 exponential_bitcast_fusion.ratio
  25.4 1.1 bitcast_multiply_fusion
  26.5 6.0 %collective-permute-done.columns.refs_1_ = f32[3,2,64,256]{3,2,1,0:T(8,128)S(1)} collective-permute-done((f32[3,2,64,256]{3,2,1,0:T(8,128)}, f32[3,2,64,256]{3,2,1,0:T(8,128)S(1)}, u32[]{:S(2)}, u32[]{:S(2)}) %collective-permute-start) | collective-permute-done | bytes 393248 | tf_op jit(solution)/shard_map/ppermute | solution.py:594
  32.5 1.9 %collective-permute-start.4 = (f32[3,64,256]{2,1,0:T(8,128)S(1)}, f32[3,64,256]{2,1,0:T(8,128)S(1)}, u32[]{:S(2)}, u32[]{:S(2)}) collective-permute-start(f32[3,64,256]{2,1,0:T(8,128)S(1)} %slice_bitcast_fusion), channel_id=1, source_target_pairs={{17,16},{18,17},{19,18},{20,19},{21,20},{22,21},{23,22},{24,23},{2... | collective-permute-start | bytes 589832 | tf_op jit(solution)/shard_map/ppermute | solution.py:596
  34.4 0.1 pad_add_fusion.flags
  34.5 1.2 copy-done.7
  35.7 1.2 copy-done.9
  36.9 1.0 copy-done.16
  38.0 0.9 copy-done.18
  38.9 4.3 %shard_map.147 = (f32[3,2,512,256]{3,2,1,0:T(8,128)S(1)}, f32[2,512,256]{2,1,0:T(8,128)S(1)}) custom-call(s32[4]{0:T(128)S(1)} %pad_add_fusion.flags, s32[64]{0:T(128)S(1)} %copy-done.20, f32[3,2,512,256]{3,2,1,0:T(8,128)S(1)} %bitcast.42, f32[3,2,64,256]{3,2,1,0:T(8,128)S(1)} %collective-permute-done.columns.refs_1_, f32[2,512,256]{2,1,0:T(8,128)S(1)} %bitcast.44, ...), custom_call_target="tpu_custom_call" | custom-call | flops 1207959552 | bytes 11141392 | tf_op jit(solution)/shard_map/pallas_call | solution.py:114
  43.2 0.8 collective-permute-done.1.low
  44.1 6.0 %shard_map.148 = (f32[3,2,512,256]{3,2,1,0:T(8,128)S(1)}, f32[3,256,256]{2,1,0:T(8,128)S(1)}) custom-call(s32[4]{0:T(128)S(1)} %pad_add_fusion.flags, s32[64]{0:T(128)S(1)} %copy-done.20, f32[3,2,512,256]{3,2,1,0:T(8,128)S(1)} %get-tuple-element.55.partial, f32[2,512,256]{2,1,0:T(8,128)S(1)} %get-tuple-element.56.weights, ...), custom_call_target="tpu_custom_call" | custom-call | flops 805306368 | bytes 14811408 | tf_op jit(solution)/shard_map/pallas_call | solution.py:114
  50.1 0.1 collective-permute-start.5
  50.2 2.5 %shard_map.149 = (f32[3,256,256]{2,1,0:T(8,128)S(1)}, f32[2,512,256]{2,1,0:T(8,128)S(1)}, f32[2,512,256]{2,1,0:T(8,128)S(1)}) custom-call(s32[4]{0:T(128)S(1)} %pad_add_fusion.flags, f32[3,2,512,256]{3,2,1,0:T(8,128)S(1)} %get-tuple-element.60.middle, bf16[2,2,256,256]{3,2,1,0:T(8,128)(2,1)S(1)} %copy-done.3, bf16[2,256,256]{2,1,0:T(8,128)(2,1)S(1)} %copy-done.5, ...), custom_call_target="tpu_custom_call" | custom-call | flops 805306368 | bytes 9175056 | tf_op jit(solution)/shard_map/pallas_call | solution.py:114
  52.7 4.4 %collective-permute-start.6 = (f32[2,512,256]{2,1,0:T(8,128)S(1)}, f32[2,512,256]{2,1,0:T(8,128)S(1)}, u32[]{:S(2)}, u32[]{:S(2)}) collective-permute-start(f32[2,512,256]{2,1,0:T(8,128)S(1)} %get-tuple-element.65), channel_id=1, source_target_pairs={{0,1},{1,2},{2,3},{3,4},{4,5},{5,6},{6,7},{7,8},{8,9},{9,10},{10,1... | collective-permute-start | bytes 3145736 | tf_op jit(solution)/shard_map/ppermute | solution.py:686
  57.1 1.9 %collective-permute-start.7 = (f32[2,512,256]{2,1,0:T(8,128)S(1)}, f32[2,512,256]{2,1,0:T(8,128)S(1)}, u32[]{:S(2)}, u32[]{:S(2)}) collective-permute-start(f32[2,512,256]{2,1,0:T(8,128)S(1)} %get-tuple-element.66), channel_id=1, source_target_pairs={{1,0},{2,1},{3,2},{4,3},{5,4},{6,5},{7,6},{8,7},{9,8},{10,9},{11,1... | collective-permute-start | bytes 3145736 | tf_op jit(solution)/shard_map/ppermute | solution.py:687
  59.0 0.9 shard_map.150
  60.0 25.3 %all_to_all.20.received = f32[8,64,256]{2,1,0:T(8,128)S(1)} all-to-all(f32[8,64,256]{2,1,0:T(8,128)S(1)} %shard_map.150), channel_id=1, replica_groups=mesh['sec'=2,'chip'=8,'core'=2] {'chip'}, dimensions={0} | all-to-all | bytes 1048576 | tf_op jit(solution)/shard_map/all_to_all | solution.py:620
  85.3 0.1 shard_map.151
  85.4 20.5 %all_to_all.21.received = f32[8,64,256]{2,1,0:T(8,128)S(1)} all-to-all(f32[8,64,256]{2,1,0:T(8,128)S(1)} %shard_map.151), channel_id=1, replica_groups=mesh['sec'=2,'chip'=8,'core'=2] {'chip'}, dimensions={0} | all-to-all | bytes 1048576 | tf_op jit(solution)/shard_map/all_to_all | solution.py:626
  105.9 1.6 shard_map.152
  107.5 2.1 %collective-permute-start.8 = (f32[4,256,256]{2,1,0:T(8,128)S(1)}, f32[4,256,256]{2,1,0:T(8,128)S(1)}, u32[]{:S(2)}, u32[]{:S(2)}) collective-permute-start(f32[4,256,256]{2,1,0:T(8,128)S(1)} %get-tuple-element.68), channel_id=1, source_target_pairs={{0,1},{1,0},{2,3},{3,2},{4,5},{5,4},{6,7},{7,6},{8,9},{9,8},{10,11... | collective-permute-start | bytes 3145736 | tf_op jit(solution)/shard_map/ppermute | solution.py:633
  109.6 2.3 %collective-permute-done.8.other.fields = f32[4,256,256]{2,1,0:T(8,128)S(1)} collective-permute-done((f32[4,256,256]{2,1,0:T(8,128)S(1)}, f32[4,256,256]{2,1,0:T(8,128)S(1)}, u32[]{:S(2)}, u32[]{:S(2)}) %collective-permute-start.8) | collective-permute-done | bytes 1048608 | tf_op jit(solution)/shard_map/ppermute | solution.py:633
  111.9 3.7 %shard_map.153 = (f32[3,2,64,256]{3,2,1,0:T(8,128)S(1)}, f32[3,64,256]{2,1,0:T(8,128)S(1)}, f32[3,64,256]{2,1,0:T(8,128)}) custom-call(s32[4]{0:T(128)S(1)} %pad_add_fusion.flags, s32[64]{0:T(128)S(1)} %copy-done.20, f32[4,256,256]{2,1,0:T(8,128)S(1)} %get-tuple-element.69.mine, f32[4,256,256]{2,1,0:T(8,128)S(1)} %collective-permute-done.8.other.fields, ...), custom_call_target="tpu_custom_call" | custom-call | flops 452984832 | bytes 7602448 | tf_op jit(solution)/shard_map/pallas_call | solution.py:114
  115.7 1.3 collective-permute-start.9
  117.0 3.3 %shard_map.154.slots = f32[11,256,256]{2,1,0:T(8,128)S(1)} custom-call(s32[4]{0:T(128)S(1)} %pad_add_fusion.flags, f32[4,256,256]{2,1,0:T(8,128)S(1)} %get-tuple-element.69.mine, bf16[2,2,256,256]{3,2,1,0:T(8,128)(2,1)S(1)} %copy-done.14, bf16[2,256,256]{2,1,0:T(8,128)(2,1)S(1)} %copy-done.12, bf16[2,2,256,256]{3,2,1,0:T(8,128)(2,1)S(1)} %copy-done.13, ...), custom_call_target="tpu_custom_call" | custom-call | flops 2214592512 | bytes 7077904 | tf_op jit(solution)/shard_map/pallas_call | solution.py:114
  120.3 0.0 copy-start.17
  120.3 0.0 copy-start.19
  120.4 1.4 collective-permute-start.10
  121.8 3.9 %shard_map.155 = (f32[3,2,512,256]{3,2,1,0:T(8,128)S(1)}, f32[3,512,256]{2,1,0:T(8,128)S(1)}, f32[3,512,256]{2,1,0:T(8,128)S(1)}) custom-call(s32[4]{0:T(128)S(1)} %pad_add_fusion.flags, f32[11,256,256]{2,1,0:T(8,128)S(1)} %shard_map.154.slots, f32[4,256,256]{2,1,0:T(8,128)S(1)} %collective-permute-done.8.other.fields, ...), custom_call_target="tpu_custom_call" | custom-call | flops 2214592512 | bytes 20185104 | tf_op jit(solution)/shard_map/pallas_call | solution.py:114
  125.7 2.2 %collective-permute-done.9 = f32[3,2,64,256]{3,2,0,1:T(8,128)S(1)} collective-permute-done((f32[3,2,64,256]{3,2,0,1:T(8,128)S(1)}, f32[3,2,64,256]{3,2,0,1:T(8,128)S(1)}, u32[]{:S(2)}, u32[]{:S(2)}) %collective-permute-start.9) | collective-permute-done | bytes 393248 | tf_op jit(solution)/shard_map/ppermute | solution.py:698
  127.9 3.1 %collective-permute-start.11 = (f32[3,64,256]{2,1,0:T(8,128)S(1)}, f32[3,64,256]{2,1,0:T(8,128)S(1)}, u32[]{:S(2)}, u32[]{:S(2)}) collective-permute-start(f32[3,64,256]{2,1,0:T(8,128)S(1)} %slice_bitcast_fusion.1), channel_id=1, source_target_pairs={{17,16},{18,17},{19,18},{20,19},{21,20},{22,21},{23,22},{24,23},{2... | collective-permute-start | bytes 589832 | tf_op jit(solution)/shard_map/ppermute | solution.py:711
  131.1 5.0 %shard_map.156 = (f32[3,2,512,256]{3,2,1,0:T(8,128)S(1)}, f32[2,512,256]{2,1,0:T(8,128)S(1)}) custom-call(s32[4]{0:T(128)S(1)} %pad_add_fusion.flags, s32[64]{0:T(128)S(1)} %copy-done.20, f32[3,2,512,256]{3,2,1,0:T(8,128)S(1)} %get-tuple-element.79.velocity, f32[3,2,64,256]{3,2,1,0:T(8,128)S(1)} %copy.21.columns, f32[3,2,512,256]{3,2,1,0:T(8,128)S(1)} %bitcast.43, ...), custom_call_target="tpu_custom_call" | custom-call | flops 1207959552 | bytes 14680336 | tf_op jit(solution)/shard_map/pallas_call | solution.py:114
  136.2 1.4 collective-permute-done.11.columns_high
  137.6 3.4 %shard_map.157 = (f32[3,2,512,256]{3,2,1,0:T(8,128)S(1)}, f32[3,256,256]{2,1,0:T(8,128)S(1)}) custom-call(s32[4]{0:T(128)S(1)} %pad_add_fusion.flags, s32[64]{0:T(128)S(1)} %copy-done.20, f32[3,2,512,256]{3,2,1,0:T(8,128)S(1)} %get-tuple-element.81.partial, f32[2,512,256]{2,1,0:T(8,128)S(1)} %get-tuple-element.82.weights, ...), custom_call_target="tpu_custom_call" | custom-call | flops 805306368 | bytes 14811408 | tf_op jit(solution)/shard_map/pallas_call | solution.py:114
  141.0 0.1 collective-permute-start.12
  141.1 2.2 %shard_map.158.mine = f32[3,256,256]{2,1,0:T(8,128)S(1)} custom-call(s32[4]{0:T(128)S(1)} %pad_add_fusion.flags, f32[3,2,512,256]{3,2,1,0:T(8,128)S(1)} %get-tuple-element.86.middle.final, bf16[2,2,256,256]{3,2,1,0:T(8,128)(2,1)S(1)} %copy-done.3, bf16[2,256,256]{2,1,0:T(8,128)(2,1)S(1)} %copy-done.5, bf16[2,2,256,256]{3,2,1,0:T(8,128)(2,1)S(1)} %copy-done.4, ...), custom_call_target="tpu_custom_call" | custom-call | flops 805306368 | bytes 7077904 | tf_op jit(solution)/shard_map/pallas_call | solution.py:114
  143.3 0.1 collective-permute-done.12.other
  143.3 0.9 shard_map.159
  144.2 17.6 %all_to_all.22.received = f32[8,64,256]{2,1,0:T(8,128)S(1)} all-to-all(f32[8,64,256]{2,1,0:T(8,128)S(1)} %shard_map.159), channel_id=1, replica_groups=mesh['sec'=2,'chip'=8,'core'=2] {'chip'}, dimensions={0} | all-to-all | bytes 1048576 | tf_op jit(solution)/shard_map/all_to_all | solution.py:620
  161.8 0.1 shard_map.160
  162.0 17.4 %all_to_all.23.received = f32[8,64,256]{2,1,0:T(8,128)S(1)} all-to-all(f32[8,64,256]{2,1,0:T(8,128)S(1)} %shard_map.160), channel_id=1, replica_groups=mesh['sec'=2,'chip'=8,'core'=2] {'chip'}, dimensions={0} | all-to-all | bytes 1048576 | tf_op jit(solution)/shard_map/all_to_all | solution.py:626
  179.4 1.4 shard_map.161
  180.8 1.9 %collective-permute-start.13 = (f32[3,256,256]{2,1,0:T(8,128)S(1)}, f32[3,256,256]{2,1,0:T(8,128)S(1)}, u32[]{:S(2)}, u32[]{:S(2)}) collective-permute-start(f32[3,256,256]{2,1,0:T(8,128)S(1)} %get-tuple-element.89), channel_id=1, source_target_pairs={{0,1},{1,0},{2,3},{3,2},{4,5},{5,4},{6,7},{7,6},{8,9},{9,8},{10,11... | collective-permute-start | bytes 2359304 | tf_op jit(solution)/shard_map/ppermute | solution.py:633
  182.7 2.3 %shard_map.162.slots = f32[6,256,256]{2,1,0:T(8,128)S(1)} custom-call(s32[4]{0:T(128)S(1)} %pad_add_fusion.flags, f32[3,256,256]{2,1,0:T(8,128)S(1)} %get-tuple-element.88.mine, bf16[2,2,256,256]{3,2,1,0:T(8,128)(2,1)S(1)} %copy-done.14, bf16[2,256,256]{2,1,0:T(8,128)(2,1)S(1)} %copy-done.12, bf16[2,2,256,256]{3,2,1,0:T(8,128)(2,1)S(1)} %copy-done.13, ...), custom_call_target="tpu_custom_call" | custom-call | flops 1207959552 | bytes 5505040 | tf_op jit(solution)/shard_map/pallas_call | solution.py:114
  185.0 4.0 %shard_map.163 = f32[3,2,512,256]{3,2,1,0:T(8,128)} custom-call(s32[4]{0:T(128)S(1)} %pad_add_fusion.flags, f32[6,256,256]{2,1,0:T(8,128)S(1)} %shard_map.162.slots, f32[3,256,256]{2,1,0:T(8,128)S(1)} %collective-permute-done.13.fields, f32[3,2,512,256]{3,2,1,0:T(8,128)S(1)} %get-tuple-element.86.middle.final, bf16[2,2,256,256]{3,2,1,0:T(8,128)(2,1)S(1)} %copy-done.15, ...), custom_call_target="tpu_custom_call" | custom-call | flops 1207959552 | bytes 11796496 | tf_op jit(solution)/shard_map/pallas_call | solution.py:114
  (63 shorter events, 0.3 us)
Async XLA Ops:
  0.0 1.9 copy-start.1
  1.9 7.5 %copy-start.21 = (f32[2,256,256]{2,1,0:T(8,128)S(1)}, f32[2,256,256]{2,1,0:T(8,128)}, u32[]{:S(2)}) copy-start(f32[2,256,256]{2,1,0:T(8,128)} %constant.142.clone) | copy-start | bytes 1572868
  3.8 40.3 %collective-permute-start.1 = (f32[3,512,256]{2,1,0:T(8,128)}, f32[3,512,256]{2,1,0:T(8,128)}, u32[]{:S(2)}, u32[]{:S(2)}) collective-permute-start(f32[3,512,256]{2,1,0:T(8,128)} %get-tuple-element.57), channel_id=1, source_target_pairs={{0,1},{1,2},{2,3},{3,4},{4,5},{5,6},{6,7},{7,8},{8,9},{9,10},{10,1... | collective-permute-start | bytes 4718600 | tf_op jit(solution)/shard_map/ppermute | solution.py:588
  7.4 36.6 %collective-permute-start.2 = (f32[3,512,256]{2,1,0:T(8,128)}, f32[3,512,256]{2,1,0:T(8,128)}, u32[]{:S(2)}, u32[]{:S(2)}) collective-permute-start(f32[3,512,256]{2,1,0:T(8,128)} %get-tuple-element.58), channel_id=1, source_target_pairs={{1,0},{2,1},{3,2},{4,3},{5,4},{6,5},{7,6},{8,7},{9,8},{10,9},{11,1... | collective-permute-start | bytes 4718600 | tf_op jit(solution)/shard_map/ppermute | solution.py:589
  10.2 1.2 copy-start.22
  10.8 3.7 %copy-start.2 = (f32[1,3,2,512,256]{4,3,2,1,0:T(8,128)S(1)}, f32[1,3,2,512,256]{4,3,2,1,0:T(8,128)}, u32[]{:S(2)}) copy-start(f32[1,3,2,512,256]{4,3,2,1,0:T(8,128)} %param.17) | copy-start | bytes 9437188
  10.8 3.7 %copy-start.20 = (s32[64]{0:T(128)S(1)}, s32[64]{0:T(128)}, u32[]{:S(2)}) copy-start(s32[64]{0:T(128)} %index.11) | copy-start | bytes 772
  12.0 2.5 %copy-start = (f32[22,256,256]{2,1,0:T(8,128)}, f32[22,256,256]{2,1,0:T(8,128)S(1)}, u32[]{:S(2)}) copy-start(f32[22,256,256]{2,1,0:T(8,128)S(1)} %fusion.8.stacked) | copy-start | bytes 17301508
  16.8 26.4 %collective-permute-start.3 = (f32[3,64,256]{2,1,0:T(8,128)}, f32[3,64,256]{2,1,0:T(8,128)}, u32[]{:S(2)}, u32[]{:S(2)}) collective-permute-start(f32[3,64,256]{2,1,0:T(8,128)} %get-tuple-element.59), channel_id=1, source_target_pairs={{0,17},{1,18},{2,19},{3,20},{4,21},{5,22},{6,23},{7,24},{8,25},{9,... | collective-permute-start | bytes 589832 | tf_op jit(solution)/shard_map/ppermute | solution.py:595
  18.1 14.3 %collective-permute-start = (f32[3,2,64,256]{3,2,1,0:T(8,128)}, f32[3,2,64,256]{3,2,1,0:T(8,128)S(1)}, u32[]{:S(2)}, u32[]{:S(2)}) collective-permute-start(f32[3,2,64,256]{3,2,1,0:T(8,128)} %get-tuple-element.52), channel_id=1, source_target_pairs={{0,16},{1,17},{2,18},{3,19},{4,20},{5,21},{6,22},{7,23},{8,24},{9,... | collective-permute-start | bytes 1179656 | tf_op jit(solution)/shard_map/ppermute | solution.py:594
  32.5 10.7 %collective-permute-start.4 = (f32[3,64,256]{2,1,0:T(8,128)S(1)}, f32[3,64,256]{2,1,0:T(8,128)S(1)}, u32[]{:S(2)}, u32[]{:S(2)}) collective-permute-start(f32[3,64,256]{2,1,0:T(8,128)S(1)} %slice_bitcast_fusion), channel_id=1, source_target_pairs={{17,16},{18,17},{19,18},{20,19},{21,20},{22,21},{23,22},{24,23},{2... | collective-permute-start | bytes 589832 | tf_op jit(solution)/shard_map/ppermute | solution.py:596
  34.5 1.2 copy-start.7
  35.7 1.2 copy-start.9
  36.9 1.0 copy-start.16
  38.0 0.9 copy-start.18
  38.9 5.2 %copy-start.3 = (bf16[2,2,256,256]{3,2,1,0:T(8,128)(2,1)S(1)}, bf16[2,2,256,256]{3,2,1,0:T(8,128)(2,1)}, u32[]{:S(2)}) copy-start(bf16[2,2,256,256]{3,2,1,0:T(8,128)(2,1)} %constant.134.clone.slope_x) | copy-start | bytes 1572868
  38.9 5.2 %copy-start.4 = (bf16[2,2,256,256]{3,2,1,0:T(8,128)(2,1)S(1)}, bf16[2,2,256,256]{3,2,1,0:T(8,128)(2,1)}, u32[]{:S(2)}) copy-start(bf16[2,2,256,256]{3,2,1,0:T(8,128)(2,1)} %constant.136.clone.into_x) | copy-start | bytes 1572868
  38.9 5.2 %copy-start.5 = (bf16[2,256,256]{2,1,0:T(8,128)(2,1)S(1)}, bf16[2,256,256]{2,1,0:T(8,128)(2,1)}, u32[]{:S(2)}) copy-start(bf16[2,256,256]{2,1,0:T(8,128)(2,1)} %constant.135.clone.slope_y) | copy-start | bytes 786436
  38.9 5.2 %copy-start.6 = (bf16[2,256,256]{2,1,0:T(8,128)(2,1)S(1)}, bf16[2,256,256]{2,1,0:T(8,128)(2,1)}, u32[]{:S(2)}) copy-start(bf16[2,256,256]{2,1,0:T(8,128)(2,1)} %constant.137.clone.into_y) | copy-start | bytes 786436
  44.1 15.0 %slice-start = ((s8[5767168]{0:T(1024)(128)(4,1)}), s8[4194304]{0:T(1024)(128)(4,1)S(1)}, s32[]{:S(2)}) async-start(s8[5767168]{0:T(1024)(128)(4,1)} %bitcast.38), calls=%async_computation.4 | async-start | bytes 8388608
  44.1 14.9 %slice-start.1 = ((s8[5767168]{0:T(1024)(128)(4,1)}), s8[1572864]{0:T(1024)(128)(4,1)S(1)}, s32[]{:S(2)}) async-start(s8[5767168]{0:T(1024)(128)(4,1)} %bitcast.38), calls=%async_computation.5 | async-start | bytes 3145728
  50.1 8.9 %collective-permute-start.5 = (f32[3,256,256]{2,1,0:T(8,128)S(1)}, f32[3,256,256]{2,1,0:T(8,128)S(1)}, u32[]{:S(2)}, u32[]{:S(2)}) collective-permute-start(f32[3,256,256]{2,1,0:T(8,128)S(1)} %get-tuple-element.62), channel_id=1, source_target_pairs={{0,1},{1,0},{2,3},{3,2},{4,5},{5,4},{6,7},{7,6},{8,9},{9,8},{10,11... | collective-permute-start | bytes 2359304 | tf_op jit(solution)/shard_map/ppermute | solution.py:672
  52.7 32.7 %collective-permute-start.6 = (f32[2,512,256]{2,1,0:T(8,128)S(1)}, f32[2,512,256]{2,1,0:T(8,128)S(1)}, u32[]{:S(2)}, u32[]{:S(2)}) collective-permute-start(f32[2,512,256]{2,1,0:T(8,128)S(1)} %get-tuple-element.65), channel_id=1, source_target_pairs={{0,1},{1,2},{2,3},{3,4},{4,5},{5,6},{6,7},{7,8},{8,9},{9,10},{10,1... | collective-permute-start | bytes 3145736 | tf_op jit(solution)/shard_map/ppermute | solution.py:686
  57.1 28.3 %collective-permute-start.7 = (f32[2,512,256]{2,1,0:T(8,128)S(1)}, f32[2,512,256]{2,1,0:T(8,128)S(1)}, u32[]{:S(2)}, u32[]{:S(2)}) collective-permute-start(f32[2,512,256]{2,1,0:T(8,128)S(1)} %get-tuple-element.66), channel_id=1, source_target_pairs={{1,0},{2,1},{3,2},{4,3},{5,4},{6,5},{7,6},{8,7},{9,8},{10,9},{11,1... | collective-permute-start | bytes 3145736 | tf_op jit(solution)/shard_map/ppermute | solution.py:687
  105.9 6.0 %copy-start.11 = (bf16[2,256,256]{2,1,0:T(8,128)(2,1)S(1)}, bf16[2,256,256]{2,1,0:T(8,128)(2,1)}, u32[]{:S(2)}) copy-start(bf16[2,256,256]{2,1,0:T(8,128)(2,1)} %constant.141.clone.from_slope_y) | copy-start | bytes 786436
  105.9 6.0 %copy-start.12 = (bf16[2,256,256]{2,1,0:T(8,128)(2,1)S(1)}, bf16[2,256,256]{2,1,0:T(8,128)(2,1)}, u32[]{:S(2)}) copy-start(bf16[2,256,256]{2,1,0:T(8,128)(2,1)} %constant.139.clone.from_y) | copy-start | bytes 786436
  107.5 4.4 %collective-permute-start.8 = (f32[4,256,256]{2,1,0:T(8,128)S(1)}, f32[4,256,256]{2,1,0:T(8,128)S(1)}, u32[]{:S(2)}, u32[]{:S(2)}) collective-permute-start(f32[4,256,256]{2,1,0:T(8,128)S(1)} %get-tuple-element.68), channel_id=1, source_target_pairs={{0,1},{1,0},{2,3},{3,2},{4,5},{5,4},{6,7},{7,6},{8,9},{9,8},{10,11... | collective-permute-start | bytes 3145736 | tf_op jit(solution)/shard_map/ppermute | solution.py:633
  111.9 5.1 %copy-start.13 = (bf16[2,2,256,256]{3,2,1,0:T(8,128)(2,1)S(1)}, bf16[2,2,256,256]{3,2,1,0:T(8,128)(2,1)}, u32[]{:S(2)}) copy-start(bf16[2,2,256,256]{3,2,1,0:T(8,128)(2,1)} %constant.140.clone.from_slope_x) | copy-start | bytes 1572868
  111.9 5.1 %copy-start.14 = (bf16[2,2,256,256]{3,2,1,0:T(8,128)(2,1)S(1)}, bf16[2,2,256,256]{3,2,1,0:T(8,128)(2,1)}, u32[]{:S(2)}) copy-start(bf16[2,2,256,256]{3,2,1,0:T(8,128)(2,1)} %constant.138.clone.from_x) | copy-start | bytes 1572868
  115.7 12.2 %collective-permute-start.9 = (f32[3,2,64,256]{3,2,0,1:T(8,128)S(1)}, f32[3,2,64,256]{3,2,0,1:T(8,128)S(1)}, u32[]{:S(2)}, u32[]{:S(2)}) collective-permute-start(f32[3,2,64,256]{3,2,0,1:T(8,128)S(1)} %copy.20), channel_id=1, source_target_pairs={{0,16},{1,17},{2,18},{3,19},{4,20},{5,21},{6,22},{7,23},{8,24},{9,... | collective-permute-start | bytes 1179656 | tf_op jit(solution)/shard_map/ppermute | solution.py:698
  120.3 10.8 %copy-start.17 = (bf16[512,512]{1,0:T(8,128)(2,1)S(1)}, bf16[512,512]{1,0:T(8,128)(2,1)}, u32[]{:S(2)}) copy-start(bf16[512,512]{1,0:T(8,128)(2,1)} %constant.132.clone.refs_2_.refs_4_) | copy-start | bytes 1572868
  120.3 10.8 %copy-start.19 = (bf16[256,256]{1,0:T(8,128)(2,1)S(1)}, bf16[256,256]{1,0:T(8,128)(2,1)}, u32[]{:S(2)}) copy-start(bf16[256,256]{1,0:T(8,128)(2,1)} %constant.133.clone.refs_3_.refs_5_) | copy-start | bytes 393220
  120.4 15.8 %collective-permute-start.10 = (f32[3,64,256]{2,1,0:T(8,128)S(1)}, f32[3,64,256]{2,1,0:T(8,128)S(1)}, u32[]{:S(2)}, u32[]{:S(2)}) collective-permute-start(f32[3,64,256]{2,1,0:T(8,128)S(1)} %get-tuple-element.85), channel_id=1, source_target_pairs={{0,17},{1,18},{2,19},{3,20},{4,21},{5,22},{6,23},{7,24},{8,25},{9,... | collective-permute-start | bytes 589832 | tf_op jit(solution)/shard_map/ppermute | solution.py:699
  121.8 9.3 %copy-start.10 = (s32[2,512,256]{2,1,0:T(8,128)S(1)}, s32[2,512,256]{2,1,0:T(8,128)}, u32[]{:S(2)}) copy-start(s32[2,512,256]{2,1,0:T(8,128)} %refs_3_.2) | copy-start | bytes 3145732
  125.7 5.4 %copy-start.8 = (f32[1,2,512,256]{3,2,1,0:T(8,128)S(1)}, f32[1,2,512,256]{3,2,1,0:T(8,128)}, u32[]{:S(2)}) copy-start(f32[1,2,512,256]{3,2,1,0:T(8,128)} %param.18) | copy-start | bytes 3145732
  127.9 9.6 %collective-permute-start.11 = (f32[3,64,256]{2,1,0:T(8,128)S(1)}, f32[3,64,256]{2,1,0:T(8,128)S(1)}, u32[]{:S(2)}, u32[]{:S(2)}) collective-permute-start(f32[3,64,256]{2,1,0:T(8,128)S(1)} %slice_bitcast_fusion.1), channel_id=1, source_target_pairs={{17,16},{18,17},{19,18},{20,19},{21,20},{22,21},{23,22},{24,23},{2... | collective-permute-start | bytes 589832 | tf_op jit(solution)/shard_map/ppermute | solution.py:711
  141.0 2.4 %collective-permute-start.12 = (f32[3,256,256]{2,1,0:T(8,128)S(1)}, f32[3,256,256]{2,1,0:T(8,128)S(1)}, u32[]{:S(2)}, u32[]{:S(2)}) collective-permute-start(f32[3,256,256]{2,1,0:T(8,128)S(1)} %get-tuple-element.87), channel_id=1, source_target_pairs={{0,1},{1,0},{2,3},{3,2},{4,5},{5,4},{6,7},{7,6},{8,9},{9,8},{10,11... | collective-permute-start | bytes 2359304 | tf_op jit(solution)/shard_map/ppermute | solution.py:672
  180.8 4.2 %collective-permute-start.13 = (f32[3,256,256]{2,1,0:T(8,128)S(1)}, f32[3,256,256]{2,1,0:T(8,128)S(1)}, u32[]{:S(2)}, u32[]{:S(2)}) collective-permute-start(f32[3,256,256]{2,1,0:T(8,128)S(1)} %get-tuple-element.89), channel_id=1, source_target_pairs={{0,1},{1,0},{2,3},{3,2},{4,5},{5,4},{6,7},{7,6},{8,9},{9,8},{10,11... | collective-permute-start | bytes 2359304 | tf_op jit(solution)/shard_map/ppermute | solution.py:633
  182.7 2.3 %copy-start.15 = (bf16[2,2,256,256]{3,2,1,0:T(8,128)(2,1)S(1)}, bf16[2,2,256,256]{3,2,1,0:T(8,128)(2,1)}, u32[]{:S(2)}) copy-start(bf16[2,2,256,256]{3,2,1,0:T(8,128)(2,1)} %constant.138.clone.from_x) | copy-start | bytes 1572868

commit v4 on v3

--- a/solution.py
+++ b/solution.py
@@ -127,26 +127,30 @@
 
 
 def tendency_steps(state, rounded, viscosity, mask, drag, dealias_x, dealias_y, put):
-    depth = state.shape[1] - 2
+    depth = state.shape[1]
     length_x = state.shape[2]
     rows = length_x // 2
     for z in range(depth):
         for c in range(3):
-            rounded[c, z] = state[c, z + 1].astype(half_type)
+            rounded[c, z] = state[c, z].astype(half_type)
     for z in range(depth):
         for b in range(length_x // rows):
             part = pl.ds(b * rows, rows)
-            u, v, w = (state[c, z + 1, part, :] for c in range(3))
+            u, v, w = (state[c, z, part, :] for c in range(3))
             slow = drag * mask[z, part, :].astype(full_type) * jnp.abs(u)
             nu = viscosity[z, part, :]
+            still = 2.0 * nu + slow
+            rising = nu - 0.5 * w if z < depth - 1 else None
+            sinking = nu + 0.5 * w if z > 0 else None
             for c in range(3):
-                center = state[c, z + 1, part, :]
-                upper = state[c, z + 2, part, :]
-                lower = state[c, z, part, :]
+                center = state[c, z, part, :]
                 grad_x = product(dealias_x[part, :], rounded[c, z])
                 grad_y = product(rounded[c, z, part, :], dealias_y[...])
-                advected = u * grad_x + v * grad_y + w * (0.5 * (upper - lower))
-                change = nu * (upper - 2.0 * center + lower) - advected - slow * center
+                change = -(u * grad_x + v * grad_y + still * center)
+                if rising is not None:
+                    change += rising * state[c, z + 1, part, :]
+                if sinking is not None:
+                    change += sinking * state[c, z - 1, part, :]
                 put(c, z, part, center, change)
 
 
@@ -192,7 +196,7 @@
                     columns_high[c, here, :] = taken
         return carry
 
-    lax.fori_loop(0, index.shape[0], one, 0)
+    lax.fori_loop(0, index.shape[0], one, 0, unroll=8)
 
 
 def insert_rows(index, pairs):
@@ -203,80 +207,66 @@
                 target[c, row, :] = rows[c, pl.ds(i, 1), :]
         return carry
 
-    lax.fori_loop(0, index.shape[0], one, 0)
-
-
-def inner_kernel(
-    flags, index, velocity, columns, *refs,
-):
-    depth = velocity.shape[1]
-    is_second = len(refs) == 12
-    if is_second:
-        earlier, earlier_columns, *refs, start = refs
-    viscosity, mask, dealias_x, dealias_y, partial, weights, state, rounded, sems, *_ = refs
+    lax.fori_loop(0, index.shape[0], one, 0, unroll=8)
+
+
+def inner_kernel(flags, index, given, columns, viscosity, mask, dealias_x, dealias_y, *refs):
+    depth = given.shape[1]
+    earlier = refs[0] if len(refs) == 5 else None
+    partial, weights, state, rounded = refs[-4:]
     is_farm = flags[0]
-    copies = [pltpu.make_async_copy(velocity, state.at[:, pl.ds(1, depth)], sems.at[0])]
-    if is_second:
-        copies.append(pltpu.make_async_copy(earlier, start, sems.at[1]))
-    for copy in copies:
-        copy.start()
-    state[:, 0] = jnp.zeros_like(state[:, 0])
-    state[:, depth + 1] = jnp.zeros_like(state[:, 0])
-    for copy in copies:
-        copy.wait()
+    state[...] = given[...]
 
     @pl.when(is_farm == 1)
     def _():
-        pairs = [(state.at[:, 1 + z], columns.at[:, z]) for z in range(depth)]
-        if is_second:
-            pairs += [(start.at[:, z], earlier_columns.at[:, z]) for z in range(depth)]
-        insert_rows(index, pairs)
+        insert_rows(index, [(state.at[:, z], columns.at[:, z]) for z in range(depth)])
 
     drag = drag_coef * is_farm.astype(full_type)
-    share = 0.5 if is_second else 1.0
+    share = 1.0 if earlier is None else 0.5
 
     def put(c, z, part, center, change):
         moved = center + step_size * change
-        if is_second:
-            moved = 0.5 * (start[c, z, part, :] + moved)
+        if earlier is not None:
+            moved = 0.5 * (earlier[c, z, part, :] + moved)
         partial[c, z, part, :] = moved
 
     tendency_steps(state, rounded, viscosity, mask, drag, dealias_x, dealias_y, put)
-    weights[0] = share * step_size * (viscosity[0] + 0.5 * state[2, 1])
-    weights[1] = share * step_size * (viscosity[depth - 1] - 0.5 * state[2, depth])
+    weights[0] = share * step_size * (viscosity[0] + 0.5 * state[2, 0])
+    weights[1] = share * step_size * (viscosity[depth - 1] - 0.5 * state[2, depth - 1])
 
 
 def outer_kernel(
     flags, index, partial, weights, low, high, columns_low, columns_high,
     slope_x, slope_y, into_x, into_y,
     middle, theirs,
-    ghosts, sems,
 ):
     depth = middle.shape[1]
     is_farm, core, is_lid = flags[0], flags[1], flags[3]
-    copies = [
-        pltpu.make_async_copy(low, ghosts.at[0], sems.at[0]),
-        pltpu.make_async_copy(high, ghosts.at[1], sems.at[1]),
-    ]
-    for copy in copies:
-        copy.start()
-    for copy in copies:
-        copy.wait()
-
-    @pl.when(is_farm == 1)
-    def _():
-        insert_rows(index, [(ghosts.at[0], columns_low), (ghosts.at[1], columns_high)])
-
     for c in range(3):
         for z in range(depth):
             moved = partial[c, z]
             if z == 0:
-                moved += weights[0] * ghosts[0, c]
+                moved += weights[0] * low[c]
             if z == depth - 1:
-                moved += weights[1] * ghosts[1, c]
+                moved += weights[1] * high[c]
                 if c == 2:
                     moved = jnp.where(is_lid == 1, 0.0, moved)
             middle[c, z] = moved
+
+    @pl.when(is_farm == 1)
+    def _():
+        def one(i, carry):
+            row = pl.ds(index[i], 1)
+            here = pl.ds(i, 1)
+            for c in range(3):
+                lag = columns_low[c, here, :] - low[c, row, :]
+                middle[c, 0, row, :] += weights[0, row, :] * lag
+                lag = columns_high[c, here, :] - high[c, row, :]
+                middle[c, depth - 1, row, :] += weights[1, row, :] * lag
+            return carry
+
+        lax.fori_loop(0, index.shape[0], one, 0, unroll=8)
+
     source_spectra(middle, theirs, 1 - core, slope_x, slope_y, into_x, into_y)
 
 
@@ -436,19 +426,32 @@
 ):
     core = flags[1]
     depth = middle.shape[1]
-    fields = [
-        [jnp.where(core == half, mine[i], other[i]) for i in range(mine.shape[0])]
-        for half in range(2)
-    ]
-    pressure = [fields[half][0] for half in range(2)]
+    count = rows_x.shape[2]
+    slopes = [0.0] * depth
+    plains = [0.0] * depth
+    lifts = [0.0] * depth
+    for half in range(2):
+        fields = [jnp.where(core == half, mine[i], other[i]) for i in range(1 + depth)]
+        single = jnp.concatenate([rows_x[half, 0], rows_x[half, 1]])
+        both = jnp.concatenate([rows_slope_x[half, 0], single, rows_slope_x[half, 1]])
+        level = fields[0]
+        for z in range(depth):
+            high, low = halves(level)
+            by_high = product(both, high)
+            by_low = product(both[: 2 * count], low)
+            slopes[z] += by_high[:count] + by_high[3 * count :] + by_low[:count]
+            plains[z] += by_high[count : 2 * count] + by_high[2 * count : 3 * count]
+            plains[z] += by_low[count:]
+            high, low = halves(fields[1 + z])
+            by_high = product(single, high)
+            lifts[z] += by_high[:count] + by_high[count:] + product(single[:count], low)
+            level = level + fields[1 + z]
+    through = from_right(jnp.concatenate(slopes + lifts), from_y)
+    across = from_right(jnp.concatenate(plains), from_slope_y)
     for z in range(depth):
-        slope = sum(from_left(rows_slope_x[half], pressure[half]) for half in range(2))
-        plain = sum(from_left(rows_x[half], pressure[half]) for half in range(2))
-        lift = sum(from_left(rows_x[half], fields[half][1 + z]) for half in range(2))
-        columns[0, z] = from_right(slope, from_y)
-        columns[1, z] = from_right(plain, from_slope_y)
-        columns[2, z] = from_right(lift, from_y)
-        pressure = [pressure[half] + fields[half][1 + z] for half in range(2)]
+        columns[0, z] = through[z * count : (z + 1) * count]
+        columns[1, z] = across[z * count : (z + 1) * count]
+        columns[2, z] = through[(depth + z) * count : (depth + z + 1) * count]
 
     def one(i, carry):
         row = pl.ds(index[i], 1)
@@ -463,42 +466,54 @@
                     columns_high[c, here, :] = value
         return carry
 
-    lax.fori_loop(0, index.shape[0], one, 0)
+    lax.fori_loop(0, index.shape[0], one, 0, unroll=8)
 
 
 def corrected_kernel(
-    flags, slots, fields, middle, from_below, from_above, slope_x, slope_y,
-    from_x, from_y, from_slope_x, from_slope_y,
-    out, low, high,
+    flags, slots, fields, middle, from_x, from_y, from_slope_x, from_slope_y,
+    out, low_change, high_change,
     others,
 ):
-    core, is_floor, is_lid = flags[1], flags[2], flags[3]
+    core = flags[1]
     depth = middle.shape[1]
     mid = middle.shape[2] // 2
     physical_half(
         fields, 1 - core, True, from_x, from_y, from_slope_x, from_slope_y, others
     )
     pressures = depth + 2
-    open_low = (1 - is_floor).astype(full_type)
-    open_high = (1 - is_lid).astype(full_type)
     sides = (slice(0, mid), slice(mid, 2 * mid))
     for z in range(depth):
         for c in range(3):
             slot = 2 * (1 + z) + c if c < 2 else 2 * pressures + z
             for side, change in zip(sides, unfolded(core, slots, others, slot)):
                 out[c, z, side] = middle[c, z, side] - change
+    for c in range(3):
+        slot = c if c < 2 else 2 * pressures + depth
+        for side, change in zip(sides, unfolded(core, slots, others, slot)):
+            low_change[c, side] = change
     for c in range(2):
-        for side, change in zip(sides, unfolded(core, slots, others, c)):
-            low[c, side] = open_low * (from_below[c, side] - change)
         slot = 2 * (depth + 1) + c
         for side, change in zip(sides, unfolded(core, slots, others, slot)):
-            high[c, side] = open_high * (from_above[c, side] - change)
-    slot = 2 * pressures + depth
-    for side, change in zip(sides, unfolded(core, slots, others, slot)):
-        low[2, side] = -open_low * change
+            high_change[c, side] = change
+
+
+def ghost_kernel(
+    flags, out, low_change, high_change, from_below, from_above, slope_x, slope_y,
+    low, high,
+):
+    is_floor, is_lid = flags[2], flags[3]
+    depth = out.shape[1]
+    mid = out.shape[2] // 2
+    open_low = (1 - is_floor).astype(full_type)
+    open_high = (1 - is_lid).astype(full_type)
+    for c in range(2):
+        low[c] = open_low * (from_below[c] - low_change[c])
+        high[c] = open_high * (from_above[c] - high_change[c])
+    low[2] = -open_low * low_change[2]
     even, odd = (
         0.5 * from_left(slope_x[half], folded(high[0], 1.0 - 2.0 * half)) for half in range(2)
     )
+    sides = (slice(0, mid), slice(mid, 2 * mid))
     for side, change in zip(sides, (even + odd, even - odd)):
         spread = change + from_right(high[1, side], slope_y)
         high[2, side] = open_high * (out[2, depth - 1, side] - spread)
@@ -590,10 +605,8 @@
     farm_downward = [(devices + i + 1, devices + i) for i in range(devices - 1)]
 
     held, stacked = lax.optimization_barrier((held, stacked))
-    taken = call(columns_kernel, bands, [smem(), vmem()], [], 0, (fringe_columns, held))
+    taken = [*call(columns_kernel, bands, [smem(), vmem()], [], 0, (fringe_columns, held))]
     columns = lax.ppermute(taken[0], every_axis, across(0))
-    columns_low = lax.ppermute(taken[1], every_axis, across(1))
-    columns_high = lax.ppermute(columns[:, 0], every_axis, farm_downward)
     away = jnp.where(fringe_columns < mid, 1.0, -1.0)[:, None]
     signs = jnp.stack([jnp.ones_like(away), away])[:, None].astype(half_type)
     rows_x, rows_slope_x = (
@@ -601,6 +614,9 @@
         for name in ("from_x", "from_slope_x")
     )
 
+    rows_x, taken[1] = lax.optimization_barrier((rows_x, taken[1]))
+    columns_low = lax.ppermute(taken[1], every_axis, across(1))
+    columns_high = lax.ppermute(columns[:, 0], every_axis, farm_downward)
     block = length_x * length_y * 2
     spectrum = shaped(depth + 1, mid, length_y)
     message = shaped(chips, 2 * rows, length_y)
@@ -622,7 +638,6 @@
             scan_kernel, (message,), [hbm(), vmem()],
             [packed, packed, pltpu.SemaphoreType.DMA((2,))], 4 * block, (sums, ratio), (hbm(),),
         )
-        sums, *beside = lax.optimization_barrier((sums, *beside))
         sums = lax.all_to_all(sums, "chip", split_axis=0, concat_axis=0, tiled=True)
         solved = shaped(fields, mid, length_y)
         own, partner = call(
@@ -630,6 +645,7 @@
             [halved, packed, pltpu.SemaphoreType.DMA((1,))], 16 * count * block,
             (flags, mine, other, stacked, sums),
         )
+        own, *beside = lax.optimization_barrier((own, *beside))
         partner = lax.ppermute(partner, "core", swap)
         ghosts = bool(beside)
         half_fields = 3 * depth + (5 if ghosts else 0)
@@ -646,15 +662,19 @@
     tendency_flops = 3 * depth * block * (length_x + length_y)
     source_flops = 3 * depth * block * (length_x + 2 * length_y)
 
-    ghosts = pltpu.VMEM((2, 3, length_x, length_y), full_type)
-    partial, weights = call(
-        inner_kernel,
-        (own_shape, edge),
-        [smem(), smem(), hbm()] + [vmem()] * 5,
-        [state, rounded, pltpu.SemaphoreType.DMA((1,))],
-        tendency_flops,
-        (flags, fringe_columns, current, columns, viscosity, turbine_mask, *tendency_tables),
-    )
+    def inner(state, columns, earlier):
+        kept = () if earlier else (own_shape,)
+        return call(
+            inner_kernel,
+            (own_shape, edge, *kept),
+            [smem(), smem()] + [vmem()] * (6 + len(earlier)),
+            ([pltpu.VMEM(own_shape.shape, full_type)] if earlier else []) + [rounded],
+            tendency_flops,
+            (flags, fringe_columns, state, columns, viscosity, turbine_mask, *tendency_tables,
+             *earlier),
+        )
+
+    partial, weights, start = inner(current, columns, ())
     partial, stacked, ratio, rows_x, rows_slope_x = lax.optimization_barrier(
         (partial, stacked, ratio, rows_x, rows_slope_x)
     )
@@ -663,8 +683,8 @@
         middle, theirs = call(
             outer_kernel,
             (own_shape, spectrum),
-            [smem(), smem()] + [vmem()] * 2 + [hbm()] * 2 + [vmem()] * 6,
-            [ghosts, pltpu.SemaphoreType.DMA((2,))],
+            [smem(), smem()] + [vmem()] * 10,
+            [],
             source_flops // 2,
             (flags, fringe_columns, partial, weights, low, high, columns_low, columns_high,
              *source_tables),
@@ -683,11 +703,9 @@
     middle, mine, other, upward, downward = spectra(
         partial, weights, low, high, columns_low, columns_high, (edge, edge)
     )
+    own, partner, slots, upward, downward = solve(mine, other, depth + 2, (upward, downward))
     from_below = lax.ppermute(upward, levels_axis, upward_route)
     from_above = lax.ppermute(downward, levels_axis, downward_route)
-    own, partner, slots, from_below, from_above = solve(
-        mine, other, depth + 2, (from_below, from_above)
-    )
     taken = call(
         fringe_kernel, bands, [smem(), smem()] + [vmem()] * 7, [],
         9 * depth * block * (length_x + length_y) // 8,
@@ -696,27 +714,26 @@
     )
     partner, *taken = lax.optimization_barrier((partner, *taken))
     new_columns = lax.ppermute(taken[0], every_axis, across(0))
+    slots, *taken[1:] = lax.optimization_barrier((slots, *taken[1:]))
     new_columns_low = lax.ppermute(taken[1], every_axis, across(1))
+    new_columns_high = lax.ppermute(taken[2], every_axis, across(-1))
     half_fields = 3 * depth + 5
-    corrected, low, high = call(
+    corrected, low_change, high_change = call(
         corrected_kernel,
-        (own_shape, whole_edge, whole_edge),
-        [smem()] + [vmem()] * 11,
+        (own_shape, whole_edge, edge),
+        [smem()] + [vmem()] * 7,
         [pltpu.VMEM((half_fields, mid, length_y), full_type)],
         3 * half_fields * block * (length_x // 2 + length_y) // 2,
-        (flags, slots, partner, middle, from_below, from_above, tables["slope_x"],
-         tables["slope_y"], *pressure_tables),
+        (flags, slots, partner, middle, *pressure_tables),
     )
     new_columns, corrected = lax.optimization_barrier((new_columns, corrected))
-    new_columns_high = lax.ppermute(new_columns[:, 0], every_axis, farm_downward)
-    partial, weights = call(
-        inner_kernel,
-        (own_shape, edge),
-        [smem(), smem(), hbm(), vmem(), hbm()] + [vmem()] * 5,
-        [state, rounded, pltpu.SemaphoreType.DMA((2,)), pltpu.VMEM(own_shape.shape, full_type)],
-        tendency_flops,
-        (flags, fringe_columns, corrected, new_columns, current, columns, viscosity, turbine_mask,
-         *tendency_tables),
+    partial, weights = inner(corrected, new_columns, (start,))
+    partial, from_below, from_above = lax.optimization_barrier((partial, from_below, from_above))
+    low, high = call(
+        ghost_kernel, (whole_edge, whole_edge), [smem()] + [vmem()] * 7, [],
+        3 * block * (length_x // 2 + length_y),
+        (flags, corrected, low_change, high_change, from_below, from_above, tables["slope_x"],
+         tables["slope_y"]),
     )
     final, mine, other = spectra(
         partial, weights, low, high, new_columns_low, new_columns_high, ()

time: 190 us -> 176 us (0.926)
  blocking collectives: 80.8 us -> 73.7 us
  starting transfers between devices: 26.5 us -> 23.6 us
  Pallas kernels: 49.7 us -> 47.1 us
    all_to_all x4, blocking collectives: 80.8 us -> 73.7 us  [solve(): sums = lax.all_to_all(sums, 'chip', split_axis=0, concat_axis=0, tiled=True)]
    ppermute x1, waiting for transfers between devices: 6 us -> 3.15 us  [local(): columns = lax.ppermute(taken[0], every_axis, across(0))]
    pallas_call x19 -> x20, Pallas kernels: 49.7 us -> 47.1 us  [call(): pl.pallas_call(kernel, out_shape=outs, in_specs=in_specs, out_specs=out_s...]
    ppermute x1, waiting for transfers between devices: 0.82 us -> 3.48 us  [local(): low = lax.ppermute(low, levels_axis, upward_route)]
    ppermute x2, waiting for transfers between devices: 2.29 us -> 0.01 us  [solve(): partner = lax.ppermute(partner, 'core', swap)]
    unnamed x51 -> x47, local copies, waits for them, and re-layouts: 8.88 us -> 6.75 us
  transfers between devices with their start and end apart: 14 -> 14, of which waited for: 6 -> 5; matrix products, arithmetic and copies ran while one was open for 5% -> 7% of each run, Pallas kernels for 14% -> 16%
where the time goes in v4:
time: 176 us; the launch traced here: 175 us
  blocking collectives  73.7 us (42%)
  Pallas kernels  47.1 us (27%)
  starting transfers between devices  23.6 us (13%)
  local copies, waits for them, and re-layouts  14.6 us (8%)
  waiting for transfers between devices  11.3 us (6%)
  other arithmetic  4.52 us (3%)
    all_to_all x4, blocking collectives, solve(): sums = lax.all_to_all(sums, 'chip', split_axis=0, concat_axis=0, tiled=True)  73.7 us
    pallas_call x20, Pallas kernels, call(): pl.pallas_call(kernel, out_shape=outs, in_specs=in_specs, out_specs=out_s...  47.1 us
    unnamed x47, local copies, waits for them, and re-layouts  6.75 us
    gather x2, local copies, waits for them, and re-layouts, local(): jnp.take(tables[name], fringe_columns % mid, axis=2) * signs  5.11 us
    ppermute x1, waiting for transfers between devices, local(): new_columns = lax.ppermute(taken[0], every_axis, across(0))  4.03 us
    ppermute x2, starting transfers between devices, solve(): partner = lax.ppermute(partner, 'core', swap)  3.88 us
    ppermute x1, starting transfers between devices, local(): low = lax.ppermute(low, levels_axis, upward_route)  3.67 us
  transfers between devices with their start and end apart: 14, of which 5 were waited for; matrix products, arithmetic and copies ran while one was open for 7% of the time, Pallas kernels for 16%

profile of v4, /device:TPU:5, one launch (start us, length us, event | category | flops | bytes accessed | tf_op | source)
XLA Modules:
  0.0 175.5 jit_solution(6485930091127357619)
XLA Ops:
  0.0 1.9 %copy-done.1 = f32[1,3,2,512,256]{4,3,2,1,0:T(8,128)S(1)} copy-done((f32[1,3,2,512,256]{4,3,2,1,0:T(8,128)S(1)}, f32[1,3,2,512,256]{4,3,2,1,0:T(8,128)}, u32[]{:S(2)}) %copy-start.1) | copy-done | bytes 3145752
  1.9 1.9 %shard_map.145 = (f32[3,512,256]{2,1,0:T(8,128)}, f32[3,512,256]{2,1,0:T(8,128)}) custom-call(f32[3,2,512,256]{3,2,1,0:T(8,128)S(1)} %bitcast.38), custom_call_target="tpu_custom_call" | custom-call | bytes 6291456 | tf_op jit(solution)/shard_map/pallas_call | solution.py:114
  3.8 3.7 %collective-permute-start.1 = (f32[3,512,256]{2,1,0:T(8,128)}, f32[3,512,256]{2,1,0:T(8,128)}, u32[]{:S(2)}, u32[]{:S(2)}) collective-permute-start(f32[3,512,256]{2,1,0:T(8,128)} %get-tuple-element.72), channel_id=1, source_target_pairs={{0,1},{1,2},{2,3},{3,4},{4,5},{5,6},{6,7},{7,8},{8,9},{9,10},{10,1... | collective-permute-start | bytes 4718600 | tf_op jit(solution)/shard_map/ppermute | solution.py:603
  7.4 1.9 %collective-permute-start.2 = (f32[3,512,256]{2,1,0:T(8,128)}, f32[3,512,256]{2,1,0:T(8,128)}, u32[]{:S(2)}, u32[]{:S(2)}) collective-permute-start(f32[3,512,256]{2,1,0:T(8,128)} %get-tuple-element.73), channel_id=1, source_target_pairs={{1,0},{2,1},{3,2},{4,3},{5,4},{6,5},{7,6},{8,7},{9,8},{10,9},{11,1... | collective-permute-start | bytes 4718600 | tf_op jit(solution)/shard_map/ppermute | solution.py:604
  9.5 0.2 fusion.14
  9.7 0.2 add_dynamic-update-slice_fusion.1
  9.9 0.2 add_dynamic-update-slice_fusion
  10.2 0.0 copy-start.20
  10.2 0.5 multiply_dynamic-update-slice_fusion.1
  10.8 0.6 multiply_dynamic-update-slice_fusion
  11.4 0.3 fusion.5
  11.7 0.3 fusion.8.stacked
  12.0 2.5 %copy-done = f32[22,256,256]{2,1,0:T(8,128)} copy-done((f32[22,256,256]{2,1,0:T(8,128)}, f32[22,256,256]{2,1,0:T(8,128)S(1)}, u32[]{:S(2)}) %copy-start) | copy-done | bytes 5767192
  14.5 1.8 %shard_map.146 = (f32[3,2,64,256]{3,2,1,0:T(8,128)S(1)}, f32[3,64,256]{2,1,0:T(8,128)S(1)}, f32[3,64,256]{2,1,0:T(8,128)}) custom-call(s32[64]{0:T(128)S(1)} %copy-done.17, f32[3,2,512,256]{3,2,1,0:T(8,128)S(1)} %bitcast.39), custom_call_target="tpu_custom_call" | custom-call | bytes 3932416 | tf_op jit(solution)/shard_map/pallas_call | solution.py:114
  16.3 0.8 copy.18
  17.1 0.0 copy-done.18
  17.1 1.3 collective-permute-start
  18.5 2.6 %gather_fusion.1 = bf16[64,2,2,256]{3,2,1,0:T(2,128)(2,1)} fusion(bf16[2,2,256,256]{3,1,2,0:T(2,128)(2,1)} %constant.140.clone2.1, s32[1024]{0:T(1024)S(1)} %pad_clamp_fusion), kind=kCustom, calls=%fused_computation.1.clone | custom fusion | bytes 262400 | tf_op jit(solution)/shard_map/jit(_take)/gather | solution.py:613
  21.0 2.5 %gather_fusion = bf16[64,2,2,256]{3,2,1,0:T(2,128)(2,1)} fusion(bf16[2,2,256,256]{3,1,2,0:T(2,128)(2,1)} %constant.138.clone2.1, s32[1024]{0:T(1024)S(1)} %pad_clamp_fusion), kind=kCustom, calls=%fused_computation.clone | custom fusion | bytes 262400 | tf_op jit(solution)/shard_map/jit(_take)/gather | solution.py:613
  23.6 1.1 bitcast_multiply_fusion
  24.6 1.3 collective-permute-start.3
  26.0 0.9 exponential_bitcast_fusion.ratio
  26.9 3.2 %collective-permute-done = f32[3,2,64,256]{3,2,0,1:T(8,128)} collective-permute-done((f32[3,2,64,256]{3,2,0,1:T(8,128)}, f32[3,2,64,256]{3,2,0,1:T(8,128)}, u32[]{:S(2)}, u32[]{:S(2)}) %collective-permute-start) | collective-permute-done | bytes 393248 | tf_op jit(solution)/shard_map/ppermute | solution.py:609
  30.0 0.9 slice_bitcast_fusion
  31.0 2.3 %collective-permute-start.4 = (f32[3,64,256]{2,1,0:T(8,128)S(1)}, f32[3,64,256]{2,1,0:T(8,128)S(1)}, u32[]{:S(2)}, u32[]{:S(2)}) collective-permute-start(f32[3,64,256]{2,1,0:T(8,128)S(1)} %slice_bitcast_fusion), channel_id=1, source_target_pairs={{17,16},{18,17},{19,18},{20,19},{21,20},{22,21},{23,22},{24,23},{2... | collective-permute-start | bytes 589832 | tf_op jit(solution)/shard_map/ppermute | solution.py:619
  33.3 0.1 pad_add_fusion.flags
  33.4 1.0 copy.19.columns
  34.4 1.2 copy-done.8
  35.6 1.0 copy-done.14
  36.7 3.8 %shard_map.147 = (f32[3,2,512,256]{3,2,1,0:T(8,128)S(1)}, f32[2,512,256]{2,1,0:T(8,128)S(1)}, f32[3,2,512,256]{3,2,1,0:T(8,128)S(1)}) custom-call(s32[4]{0:T(128)S(1)} %pad_add_fusion.flags, s32[64]{0:T(128)S(1)} %copy-done.17, f32[3,2,512,256]{3,2,1,0:T(8,128)S(1)} %bitcast.40, f32[3,2,64,256]{3,2,1,0:T(8,128)S(1)} %copy.19.columns, ...), custom_call_target="tpu_custom_call" | custom-call | flops 1207959552 | bytes 14287120 | tf_op jit(solution)/shard_map/pallas_call | solution.py:114
  40.6 3.5 %collective-permute-done.1.low = f32[3,512,256]{2,1,0:T(8,128)} collective-permute-done((f32[3,512,256]{2,1,0:T(8,128)}, f32[3,512,256]{2,1,0:T(8,128)}, u32[]{:S(2)}, u32[]{:S(2)}) %collective-permute-start.1) | collective-permute-done | bytes 1572896 | tf_op jit(solution)/shard_map/ppermute | solution.py:603
  44.1 5.0 %shard_map.148 = (f32[3,2,512,256]{3,2,1,0:T(8,128)S(1)}, f32[3,256,256]{2,1,0:T(8,128)S(1)}) custom-call(s32[4]{0:T(128)S(1)} %pad_add_fusion.flags, s32[64]{0:T(128)S(1)} %copy-done.17, f32[3,2,512,256]{3,2,1,0:T(8,128)S(1)} %get-tuple-element.70.partial, f32[2,512,256]{2,1,0:T(8,128)S(1)} %get-tuple-element.71.weights, ...), custom_call_target="tpu_custom_call" | custom-call | flops 805306368 | bytes 14811408 | tf_op jit(solution)/shard_map/pallas_call | solution.py:114
  49.1 0.1 collective-permute-start.5
  49.2 3.5 %shard_map.149 = (f32[3,256,256]{2,1,0:T(8,128)S(1)}, f32[2,512,256]{2,1,0:T(8,128)}, f32[2,512,256]{2,1,0:T(8,128)S(1)}) custom-call(s32[4]{0:T(128)S(1)} %pad_add_fusion.flags, f32[3,2,512,256]{3,2,1,0:T(8,128)S(1)} %get-tuple-element.75.middle, bf16[2,2,256,256]{3,2,1,0:T(8,128)(2,1)S(1)} %copy-done.3, bf16[2,256,256]{2,1,0:T(8,128)(2,1)S(1)} %copy-done.5, ...), custom_call_target="tpu_custom_call" | custom-call | flops 805306368 | bytes 9175056 | tf_op jit(solution)/shard_map/pallas_call | solution.py:114
  52.7 0.9 shard_map.150
  53.6 19.6 %all_to_all.20.received = f32[8,64,256]{2,1,0:T(8,128)S(1)} all-to-all(f32[8,64,256]{2,1,0:T(8,128)S(1)} %shard_map.150), channel_id=1, replica_groups=mesh['sec'=2,'chip'=8,'core'=2] {'chip'}, dimensions={0} | all-to-all | bytes 1048576 | tf_op jit(solution)/shard_map/all_to_all | solution.py:636
  73.2 0.1 shard_map.151
  73.3 17.4 %all_to_all.21.received = f32[8,64,256]{2,1,0:T(8,128)S(1)} all-to-all(f32[8,64,256]{2,1,0:T(8,128)S(1)} %shard_map.151), channel_id=1, replica_groups=mesh['sec'=2,'chip'=8,'core'=2] {'chip'}, dimensions={0} | all-to-all | bytes 1048576 | tf_op jit(solution)/shard_map/all_to_all | solution.py:641
  90.8 1.6 shard_map.152
  92.4 1.9 %collective-permute-start.6 = (f32[4,256,256]{2,1,0:T(8,128)S(1)}, f32[4,256,256]{2,1,0:T(8,128)S(1)}, u32[]{:S(2)}, u32[]{:S(2)}) collective-permute-start(f32[4,256,256]{2,1,0:T(8,128)S(1)} %get-tuple-element.80), channel_id=1, source_target_pairs={{0,1},{1,0},{2,3},{3,2},{4,5},{5,4},{6,7},{7,6},{8,9},{9,8},{10,11... | collective-permute-start | bytes 3145736 | tf_op jit(solution)/shard_map/ppermute | solution.py:649
  94.3 3.2 %collective-permute-start.8 = (f32[2,512,256]{2,1,0:T(8,128)}, f32[2,512,256]{2,1,0:T(8,128)S(1)}, u32[]{:S(2)}, u32[]{:S(2)}) collective-permute-start(f32[2,512,256]{2,1,0:T(8,128)} %get-tuple-element.100), channel_id=1, source_target_pairs={{0,1},{1,2},{2,3},{3,4},{4,5},{5,6},{6,7},{7,8},{8,9},{9,10},{10,1... | collective-permute-start | bytes 3145736 | tf_op jit(solution)/shard_map/ppermute | solution.py:707
  97.5 1.9 %collective-permute-start.9 = (f32[2,512,256]{2,1,0:T(8,128)S(1)}, f32[2,512,256]{2,1,0:T(8,128)S(1)}, u32[]{:S(2)}, u32[]{:S(2)}) collective-permute-start(f32[2,512,256]{2,1,0:T(8,128)S(1)} %get-tuple-element.101), channel_id=1, source_target_pairs={{1,0},{2,1},{3,2},{4,3},{5,4},{6,5},{7,6},{8,7},{9,8},{10,9},{11,1... | collective-permute-start | bytes 3145736 | tf_op jit(solution)/shard_map/ppermute | solution.py:708
  99.5 2.1 %shard_map.153 = (f32[3,2,64,256]{3,2,1,0:T(8,128)S(1)}, f32[3,64,256]{2,1,0:T(8,128)S(1)}, f32[3,64,256]{2,1,0:T(8,128)S(1)}) custom-call(s32[4]{0:T(128)S(1)} %pad_add_fusion.flags, s32[64]{0:T(128)S(1)} %copy-done.17, f32[4,256,256]{2,1,0:T(8,128)S(1)} %get-tuple-element.84.mine, f32[4,256,256]{2,1,0:T(8,128)S(1)} %collective-permute-done.6.other.fields, ...), custom_call_target="tpu_custom_call" | custom-call | flops 452984832 | bytes 7602448 | tf_op jit(solution)/shard_map/pallas_call | solution.py:114
  101.6 1.3 collective-permute-start.7
  102.9 3.3 %shard_map.154.slots = f32[11,256,256]{2,1,0:T(8,128)S(1)} custom-call(s32[4]{0:T(128)S(1)} %pad_add_fusion.flags, f32[4,256,256]{2,1,0:T(8,128)S(1)} %get-tuple-element.84.mine, bf16[2,2,256,256]{3,2,1,0:T(8,128)(2,1)S(1)} %copy-done.13, bf16[2,256,256]{2,1,0:T(8,128)(2,1)S(1)} %copy-done.11, bf16[2,2,256,256]{3,2,1,0:T(8,128)(2,1)S(1)} %copy-done.12, ...), custom_call_target="tpu_custom_call" | custom-call | flops 2214592512 | bytes 7077904 | tf_op jit(solution)/shard_map/pallas_call | solution.py:114
  106.2 1.4 collective-permute-start.10
  107.7 1.3 collective-permute-start.11
  109.0 3.4 %shard_map.155 = (f32[3,2,512,256]{3,2,1,0:T(8,128)S(1)}, f32[3,512,256]{2,1,0:T(8,128)S(1)}, f32[2,512,256]{2,1,0:T(8,128)S(1)}) custom-call(s32[4]{0:T(128)S(1)} %pad_add_fusion.flags, f32[11,256,256]{2,1,0:T(8,128)S(1)} %shard_map.154.slots, f32[4,256,256]{2,1,0:T(8,128)S(1)} %collective-permute-done.6.other.fields, ...), custom_call_target="tpu_custom_call" | custom-call | flops 2214592512 | bytes 15990800 | tf_op jit(solution)/shard_map/pallas_call | solution.py:114
  112.3 4.0 %collective-permute-done.7.columns = f32[3,2,64,256]{3,2,1,0:T(8,128)S(1)} collective-permute-done((f32[3,2,64,256]{3,2,1,0:T(8,128)S(1)}, f32[3,2,64,256]{3,2,1,0:T(8,128)S(1)}, u32[]{:S(2)}, u32[]{:S(2)}) %collective-permute-start.7) | collective-permute-done | bytes 393248 | tf_op jit(solution)/shard_map/ppermute | solution.py:716
  116.4 3.8 %shard_map.156 = (f32[3,2,512,256]{3,2,1,0:T(8,128)S(1)}, f32[2,512,256]{2,1,0:T(8,128)S(1)}) custom-call(s32[4]{0:T(128)S(1)} %pad_add_fusion.flags, s32[64]{0:T(128)S(1)} %copy-done.17, f32[3,2,512,256]{3,2,1,0:T(8,128)S(1)} %get-tuple-element.96.given.out, f32[3,2,64,256]{3,2,1,0:T(8,128)S(1)} %collective-permute-done.7.columns, ...), custom_call_target="tpu_custom_call" | custom-call | flops 1207959552 | bytes 14287120 | tf_op jit(solution)/shard_map/pallas_call | solution.py:114
  120.2 0.6 collective-permute-done.8.from_below
  120.8 1.5 shard_map.157
  122.3 3.6 %shard_map.158 = (f32[3,2,512,256]{3,2,1,0:T(8,128)S(1)}, f32[3,256,256]{2,1,0:T(8,128)S(1)}) custom-call(s32[4]{0:T(128)S(1)} %pad_add_fusion.flags, s32[64]{0:T(128)S(1)} %copy-done.17, f32[3,2,512,256]{3,2,1,0:T(8,128)S(1)} %get-tuple-element.102.partial, f32[2,512,256]{2,1,0:T(8,128)S(1)} %get-tuple-element.103.weights, ...), custom_call_target="tpu_custom_call" | custom-call | flops 805306368 | bytes 14811408 | tf_op jit(solution)/shard_map/pallas_call | solution.py:114
  125.8 0.1 collective-permute-start.12
  125.9 2.2 %shard_map.159.mine = f32[3,256,256]{2,1,0:T(8,128)S(1)} custom-call(s32[4]{0:T(128)S(1)} %pad_add_fusion.flags, f32[3,2,512,256]{3,2,1,0:T(8,128)S(1)} %get-tuple-element.112.middle.final, bf16[2,2,256,256]{3,2,1,0:T(8,128)(2,1)S(1)} %copy-done.3, bf16[2,256,256]{2,1,0:T(8,128)(2,1)S(1)} %copy-done.5, bf16[2,2,256,256]{3,2,1,0:T(8,128)(2,1)S(1)} %copy-done.4, ...), custom_call_target="tpu_custom_call" | custom-call | flops 805306368 | bytes 7077904 | tf_op jit(solution)/shard_map/pallas_call | solution.py:114
  128.1 0.1 collective-permute-done.12.other
  128.2 0.9 shard_map.160
  129.1 19.2 %all_to_all.22.received = f32[8,64,256]{2,1,0:T(8,128)S(1)} all-to-all(f32[8,64,256]{2,1,0:T(8,128)S(1)} %shard_map.160), channel_id=1, replica_groups=mesh['sec'=2,'chip'=8,'core'=2] {'chip'}, dimensions={0} | all-to-all | bytes 1048576 | tf_op jit(solution)/shard_map/all_to_all | solution.py:636
  148.3 0.1 shard_map.161
  148.5 17.4 %all_to_all.23.received = f32[8,64,256]{2,1,0:T(8,128)S(1)} all-to-all(f32[8,64,256]{2,1,0:T(8,128)S(1)} %shard_map.161), channel_id=1, replica_groups=mesh['sec'=2,'chip'=8,'core'=2] {'chip'}, dimensions={0} | all-to-all | bytes 1048576 | tf_op jit(solution)/shard_map/all_to_all | solution.py:641
  165.9 1.4 shard_map.162
  167.3 1.9 %collective-permute-start.13 = (f32[3,256,256]{2,1,0:T(8,128)S(1)}, f32[3,256,256]{2,1,0:T(8,128)S(1)}, u32[]{:S(2)}, u32[]{:S(2)}) collective-permute-start(f32[3,256,256]{2,1,0:T(8,128)S(1)} %get-tuple-element.115), channel_id=1, source_target_pairs={{0,1},{1,0},{2,3},{3,2},{4,5},{5,4},{6,7},{7,6},{8,9},{9,8},{10,11... | collective-permute-start | bytes 2359304 | tf_op jit(solution)/shard_map/ppermute | solution.py:649
  169.2 2.3 %shard_map.163.slots = f32[6,256,256]{2,1,0:T(8,128)S(1)} custom-call(s32[4]{0:T(128)S(1)} %pad_add_fusion.flags, f32[3,256,256]{2,1,0:T(8,128)S(1)} %get-tuple-element.114.mine, bf16[2,2,256,256]{3,2,1,0:T(8,128)(2,1)S(1)} %copy-done.13, bf16[2,256,256]{2,1,0:T(8,128)(2,1)S(1)} %copy-done.11, bf16[2,2,256,256]{3,2,1,0:T(8,128)(2,1)S(1)} %copy-done.12, ...), custom_call_target="tpu_custom_call" | custom-call | flops 1207959552 | bytes 5505040 | tf_op jit(solution)/shard_map/pallas_call | solution.py:114
  171.5 4.0 %shard_map.164 = f32[3,2,512,256]{3,2,1,0:T(8,128)} custom-call(s32[4]{0:T(128)S(1)} %pad_add_fusion.flags, f32[6,256,256]{2,1,0:T(8,128)S(1)} %shard_map.163.slots, f32[3,256,256]{2,1,0:T(8,128)S(1)} %collective-permute-done.13.fields, f32[3,2,512,256]{3,2,1,0:T(8,128)S(1)} %get-tuple-element.112.middle.final, bf16[2,2,256,256]{3,2,1,0:T(8,128)(2,1)S(1)} %copy-done.13, ...), custom_call_target="tpu_custom_call" | custom-call | flops 1207959552 | bytes 11796496 | tf_op jit(solution)/shard_map/pallas_call | solution.py:114
  (59 shorter events, 0.2 us)
Async XLA Ops:
  0.0 1.9 %copy-start.1 = (f32[1,3,2,512,256]{4,3,2,1,0:T(8,128)S(1)}, f32[1,3,2,512,256]{4,3,2,1,0:T(8,128)}, u32[]{:S(2)}) copy-start(f32[1,3,2,512,256]{4,3,2,1,0:T(8,128)} %param.17) | copy-start | bytes 9437188
  1.9 7.5 %copy-start.19 = (f32[2,256,256]{2,1,0:T(8,128)S(1)}, f32[2,256,256]{2,1,0:T(8,128)}, u32[]{:S(2)}) copy-start(f32[2,256,256]{2,1,0:T(8,128)} %constant.142.clone) | copy-start | bytes 1572868
  3.8 40.3 %collective-permute-start.1 = (f32[3,512,256]{2,1,0:T(8,128)}, f32[3,512,256]{2,1,0:T(8,128)}, u32[]{:S(2)}, u32[]{:S(2)}) collective-permute-start(f32[3,512,256]{2,1,0:T(8,128)} %get-tuple-element.72), channel_id=1, source_target_pairs={{0,1},{1,2},{2,3},{3,4},{4,5},{5,6},{6,7},{7,8},{8,9},{9,10},{10,1... | collective-permute-start | bytes 4718600 | tf_op jit(solution)/shard_map/ppermute | solution.py:603
  7.4 36.6 %collective-permute-start.2 = (f32[3,512,256]{2,1,0:T(8,128)}, f32[3,512,256]{2,1,0:T(8,128)}, u32[]{:S(2)}, u32[]{:S(2)}) collective-permute-start(f32[3,512,256]{2,1,0:T(8,128)} %get-tuple-element.73), channel_id=1, source_target_pairs={{1,0},{2,1},{3,2},{4,3},{5,4},{6,5},{7,6},{8,7},{9,8},{10,9},{11,1... | collective-permute-start | bytes 4718600 | tf_op jit(solution)/shard_map/ppermute | solution.py:604
  10.2 1.2 copy-start.20
  10.8 3.7 %copy-start.2 = (f32[1,3,2,512,256]{4,3,2,1,0:T(8,128)S(1)}, f32[1,3,2,512,256]{4,3,2,1,0:T(8,128)}, u32[]{:S(2)}) copy-start(f32[1,3,2,512,256]{4,3,2,1,0:T(8,128)} %param.17) | copy-start | bytes 9437188
  10.8 3.7 %copy-start.17 = (s32[64]{0:T(128)S(1)}, s32[64]{0:T(128)}, u32[]{:S(2)}) copy-start(s32[64]{0:T(128)} %index.11) | copy-start | bytes 772
  12.0 2.5 %copy-start = (f32[22,256,256]{2,1,0:T(8,128)}, f32[22,256,256]{2,1,0:T(8,128)S(1)}, u32[]{:S(2)}) copy-start(f32[22,256,256]{2,1,0:T(8,128)S(1)} %fusion.8.stacked) | copy-start | bytes 17301508
  16.3 0.8 copy-start.18
  16.3 18.1 %copy-start.16 = (bf16[256,256]{1,0:T(8,128)(2,1)S(1)}, bf16[256,256]{1,0:T(8,128)(2,1)}, u32[]{:S(2)}) copy-start(bf16[256,256]{1,0:T(8,128)(2,1)} %constant.133.clone.dealias_y) | copy-start | bytes 393220
  17.1 12.9 %collective-permute-start = (f32[3,2,64,256]{3,2,0,1:T(8,128)}, f32[3,2,64,256]{3,2,0,1:T(8,128)}, u32[]{:S(2)}, u32[]{:S(2)}) collective-permute-start(f32[3,2,64,256]{3,2,0,1:T(8,128)} %copy.18), channel_id=1, source_target_pairs={{0,16},{1,17},{2,18},{3,19},{4,20},{5,21},{6,22},{7,23},{8,24},{9,... | collective-permute-start | bytes 1179656 | tf_op jit(solution)/shard_map/ppermute | solution.py:609
  24.6 15.9 %collective-permute-start.3 = (f32[3,64,256]{2,1,0:T(8,128)}, f32[3,64,256]{2,1,0:T(8,128)}, u32[]{:S(2)}, u32[]{:S(2)}) collective-permute-start(f32[3,64,256]{2,1,0:T(8,128)} %copy-done.18), channel_id=1, source_target_pairs={{0,17},{1,18},{2,19},{3,20},{4,21},{5,22},{6,23},{7,24},{8,25},{9,... | collective-permute-start | bytes 589832 | tf_op jit(solution)/shard_map/ppermute | solution.py:618
  26.0 8.4 %copy-start.7 = (f32[1,2,512,256]{3,2,1,0:T(8,128)S(1)}, f32[1,2,512,256]{3,2,1,0:T(8,128)}, u32[]{:S(2)}) copy-start(f32[1,2,512,256]{3,2,1,0:T(8,128)} %param.18) | copy-start | bytes 3145732
  31.0 9.6 %collective-permute-start.4 = (f32[3,64,256]{2,1,0:T(8,128)S(1)}, f32[3,64,256]{2,1,0:T(8,128)S(1)}, u32[]{:S(2)}, u32[]{:S(2)}) collective-permute-start(f32[3,64,256]{2,1,0:T(8,128)S(1)} %slice_bitcast_fusion), channel_id=1, source_target_pairs={{17,16},{18,17},{19,18},{20,19},{21,20},{22,21},{23,22},{24,23},{2... | collective-permute-start | bytes 589832 | tf_op jit(solution)/shard_map/ppermute | solution.py:619
  34.4 1.2 copy-start.8
  35.6 1.0 copy-start.14
  36.7 7.4 %copy-start.3 = (bf16[2,2,256,256]{3,2,1,0:T(8,128)(2,1)S(1)}, bf16[2,2,256,256]{3,2,1,0:T(8,128)(2,1)}, u32[]{:S(2)}) copy-start(bf16[2,2,256,256]{3,2,1,0:T(8,128)(2,1)} %constant.134.clone.slope_x) | copy-start | bytes 1572868
  36.7 7.4 %copy-start.4 = (bf16[2,2,256,256]{3,2,1,0:T(8,128)(2,1)S(1)}, bf16[2,2,256,256]{3,2,1,0:T(8,128)(2,1)}, u32[]{:S(2)}) copy-start(bf16[2,2,256,256]{3,2,1,0:T(8,128)(2,1)} %constant.136.clone.into_x) | copy-start | bytes 1572868
  36.7 7.4 %copy-start.5 = (bf16[2,256,256]{2,1,0:T(8,128)(2,1)S(1)}, bf16[2,256,256]{2,1,0:T(8,128)(2,1)}, u32[]{:S(2)}) copy-start(bf16[2,256,256]{2,1,0:T(8,128)(2,1)} %constant.135.clone.slope_y) | copy-start | bytes 786436
  36.7 7.4 %copy-start.6 = (bf16[2,256,256]{2,1,0:T(8,128)(2,1)S(1)}, bf16[2,256,256]{2,1,0:T(8,128)(2,1)}, u32[]{:S(2)}) copy-start(bf16[2,256,256]{2,1,0:T(8,128)(2,1)} %constant.137.clone.into_y) | copy-start | bytes 786436
  36.7 16.0 %slice-start = ((s8[5767168]{0:T(1024)(128)(4,1)}), s8[4194304]{0:T(1024)(128)(4,1)S(1)}, s32[]{:S(2)}) async-start(s8[5767168]{0:T(1024)(128)(4,1)} %bitcast.36), calls=%async_computation.4 | async-start | bytes 8388608
  44.1 8.6 %slice-start.1 = ((s8[5767168]{0:T(1024)(128)(4,1)}), s8[1572864]{0:T(1024)(128)(4,1)S(1)}, s32[]{:S(2)}) async-start(s8[5767168]{0:T(1024)(128)(4,1)} %bitcast.36), calls=%async_computation.5 | async-start | bytes 3145728
  49.1 3.5 %collective-permute-start.5 = (f32[3,256,256]{2,1,0:T(8,128)S(1)}, f32[3,256,256]{2,1,0:T(8,128)S(1)}, u32[]{:S(2)}, u32[]{:S(2)}) collective-permute-start(f32[3,256,256]{2,1,0:T(8,128)S(1)} %get-tuple-element.77), channel_id=1, source_target_pairs={{0,1},{1,0},{2,3},{3,2},{4,5},{5,4},{6,7},{7,6},{8,9},{9,8},{10,11... | collective-permute-start | bytes 2359304 | tf_op jit(solution)/shard_map/ppermute | solution.py:692
  90.8 8.7 %copy-start.10 = (bf16[2,256,256]{2,1,0:T(8,128)(2,1)S(1)}, bf16[2,256,256]{2,1,0:T(8,128)(2,1)}, u32[]{:S(2)}) copy-start(bf16[2,256,256]{2,1,0:T(8,128)(2,1)} %constant.141.clone.from_slope_y) | copy-start | bytes 786436
  90.8 8.7 %copy-start.11 = (bf16[2,256,256]{2,1,0:T(8,128)(2,1)S(1)}, bf16[2,256,256]{2,1,0:T(8,128)(2,1)}, u32[]{:S(2)}) copy-start(bf16[2,256,256]{2,1,0:T(8,128)(2,1)} %constant.139.clone.from_y) | copy-start | bytes 786436
  92.4 7.1 %collective-permute-start.6 = (f32[4,256,256]{2,1,0:T(8,128)S(1)}, f32[4,256,256]{2,1,0:T(8,128)S(1)}, u32[]{:S(2)}, u32[]{:S(2)}) collective-permute-start(f32[4,256,256]{2,1,0:T(8,128)S(1)} %get-tuple-element.80), channel_id=1, source_target_pairs={{0,1},{1,0},{2,3},{3,2},{4,5},{5,4},{6,7},{7,6},{8,9},{9,8},{10,11... | collective-permute-start | bytes 3145736 | tf_op jit(solution)/shard_map/ppermute | solution.py:649
  94.3 8.6 %copy-start.12 = (bf16[2,2,256,256]{3,2,1,0:T(8,128)(2,1)S(1)}, bf16[2,2,256,256]{3,2,1,0:T(8,128)(2,1)}, u32[]{:S(2)}) copy-start(bf16[2,2,256,256]{3,2,1,0:T(8,128)(2,1)} %constant.140.clone.from_slope_x) | copy-start | bytes 1572868
  94.3 8.6 %copy-start.13 = (bf16[2,2,256,256]{3,2,1,0:T(8,128)(2,1)S(1)}, bf16[2,2,256,256]{3,2,1,0:T(8,128)(2,1)}, u32[]{:S(2)}) copy-start(bf16[2,2,256,256]{3,2,1,0:T(8,128)(2,1)} %constant.138.clone.from_x) | copy-start | bytes 1572868
  94.3 26.5 %collective-permute-start.8 = (f32[2,512,256]{2,1,0:T(8,128)}, f32[2,512,256]{2,1,0:T(8,128)S(1)}, u32[]{:S(2)}, u32[]{:S(2)}) collective-permute-start(f32[2,512,256]{2,1,0:T(8,128)} %get-tuple-element.100), channel_id=1, source_target_pairs={{0,1},{1,2},{2,3},{3,4},{4,5},{5,6},{6,7},{7,8},{8,9},{9,10},{10,1... | collective-permute-start | bytes 3145736 | tf_op jit(solution)/shard_map/ppermute | solution.py:707
  97.5 23.3 %collective-permute-start.9 = (f32[2,512,256]{2,1,0:T(8,128)S(1)}, f32[2,512,256]{2,1,0:T(8,128)S(1)}, u32[]{:S(2)}, u32[]{:S(2)}) collective-permute-start(f32[2,512,256]{2,1,0:T(8,128)S(1)} %get-tuple-element.101), channel_id=1, source_target_pairs={{1,0},{2,1},{3,2},{4,3},{5,4},{6,5},{7,6},{8,7},{9,8},{10,9},{11,1... | collective-permute-start | bytes 3145736 | tf_op jit(solution)/shard_map/ppermute | solution.py:708
  101.6 14.8 %collective-permute-start.7 = (f32[3,2,64,256]{3,2,1,0:T(8,128)S(1)}, f32[3,2,64,256]{3,2,1,0:T(8,128)S(1)}, u32[]{:S(2)}, u32[]{:S(2)}) collective-permute-start(f32[3,2,64,256]{3,2,1,0:T(8,128)S(1)} %get-tuple-element.90), channel_id=1, source_target_pairs={{0,16},{1,17},{2,18},{3,19},{4,20},{5,21},{6,22},{7,23},{8,24},{9,... | collective-permute-start | bytes 1179656 | tf_op jit(solution)/shard_map/ppermute | solution.py:716
  106.2 10.2 %copy-start.9 = (s32[2,512,256]{2,1,0:T(8,128)S(1)}, s32[2,512,256]{2,1,0:T(8,128)}, u32[]{:S(2)}) copy-start(s32[2,512,256]{2,1,0:T(8,128)} %mask.3) | copy-start | bytes 3145732
  106.2 10.2 %copy-start.15 = (bf16[512,512]{1,0:T(8,128)(2,1)S(1)}, bf16[512,512]{1,0:T(8,128)(2,1)}, u32[]{:S(2)}) copy-start(bf16[512,512]{1,0:T(8,128)(2,1)} %constant.132.clone.dealias_x) | copy-start | bytes 1572868
  106.2 16.0 %collective-permute-start.10 = (f32[3,64,256]{2,1,0:T(8,128)S(1)}, f32[3,64,256]{2,1,0:T(8,128)S(1)}, u32[]{:S(2)}, u32[]{:S(2)}) collective-permute-start(f32[3,64,256]{2,1,0:T(8,128)S(1)} %get-tuple-element.110), channel_id=1, source_target_pairs={{0,17},{1,18},{2,19},{3,20},{4,21},{5,22},{6,23},{7,24},{8,25},{9,... | collective-permute-start | bytes 589832 | tf_op jit(solution)/shard_map/ppermute | solution.py:718
  107.7 14.6 %collective-permute-start.11 = (f32[3,64,256]{2,1,0:T(8,128)S(1)}, f32[3,64,256]{2,1,0:T(8,128)S(1)}, u32[]{:S(2)}, u32[]{:S(2)}) collective-permute-start(f32[3,64,256]{2,1,0:T(8,128)S(1)} %get-tuple-element.111), channel_id=1, source_target_pairs={{1,16},{2,17},{3,18},{4,19},{5,20},{6,21},{7,22},{8,23},{9,24},{10... | collective-permute-start | bytes 589832 | tf_op jit(solution)/shard_map/ppermute | solution.py:719
  125.8 2.4 %collective-permute-start.12 = (f32[3,256,256]{2,1,0:T(8,128)S(1)}, f32[3,256,256]{2,1,0:T(8,128)S(1)}, u32[]{:S(2)}, u32[]{:S(2)}) collective-permute-start(f32[3,256,256]{2,1,0:T(8,128)S(1)} %get-tuple-element.113), channel_id=1, source_target_pairs={{0,1},{1,0},{2,3},{3,2},{4,5},{5,4},{6,7},{7,6},{8,9},{9,8},{10,11... | collective-permute-start | bytes 2359304 | tf_op jit(solution)/shard_map/ppermute | solution.py:692
  167.3 4.2 %collective-permute-start.13 = (f32[3,256,256]{2,1,0:T(8,128)S(1)}, f32[3,256,256]{2,1,0:T(8,128)S(1)}, u32[]{:S(2)}, u32[]{:S(2)}) collective-permute-start(f32[3,256,256]{2,1,0:T(8,128)S(1)} %get-tuple-element.115), channel_id=1, source_target_pairs={{0,1},{1,0},{2,3},{3,2},{4,5},{5,4},{6,7},{7,6},{8,9},{9,8},{10,11... | collective-permute-start | bytes 2359304 | tf_op jit(solution)/shard_map/ppermute | solution.py:649

commit v5 on v4

--- a/solution.py
+++ b/solution.py
@@ -235,13 +235,11 @@
     weights[1] = share * step_size * (viscosity[depth - 1] - 0.5 * state[2, depth - 1])
 
 
-def outer_kernel(
-    flags, index, partial, weights, low, high, columns_low, columns_high,
-    slope_x, slope_y, into_x, into_y,
-    middle, theirs,
+def add_ghosts(
+    flags, index, partial, weights, low, high, columns_low, columns_high, middle,
 ):
     depth = middle.shape[1]
-    is_farm, core, is_lid = flags[0], flags[1], flags[3]
+    is_farm, is_lid = flags[0], flags[3]
     for c in range(3):
         for z in range(depth):
             moved = partial[c, z]
@@ -267,7 +265,34 @@
 
         lax.fori_loop(0, index.shape[0], one, 0, unroll=8)
 
-    source_spectra(middle, theirs, 1 - core, slope_x, slope_y, into_x, into_y)
+
+def outer_kernel(
+    flags, index, partial, weights, low, high, columns_low, columns_high,
+    slope_x, slope_y, into_x, into_y,
+    middle, theirs, downward,
+):
+    add_ghosts(
+        flags, index, partial, weights, low, high, columns_low, columns_high, middle
+    )
+    downward[0] = middle[0, 0]
+    downward[1] = middle[1, 0]
+    source_spectra(middle, theirs, 1 - flags[1], slope_x, slope_y, into_x, into_y)
+
+
+def second_outer_kernel(
+    flags, index, partial, weights, low_change, high_change, columns_low, columns_high,
+    slope_x, slope_y, into_x, into_y, corrected, from_below, from_above,
+    middle, theirs,
+    low, high,
+):
+    ghost_levels(
+        flags, corrected, low_change, high_change, from_below, from_above, slope_x, slope_y,
+        low, high,
+    )
+    add_ghosts(
+        flags, index, partial, weights, low, high, columns_low, columns_high, middle
+    )
+    source_spectra(middle, theirs, 1 - flags[1], slope_x, slope_y, into_x, into_y)
 
 
 def own_spectra_kernel(flags, middle, slope_x, slope_y, into_x, into_y, mine, *edges):
@@ -276,9 +301,7 @@
     source_spectra(middle, mine, flags[1], slope_x, slope_y, into_x, into_y)
     if not edges:
         return
-    upward, downward = edges
-    downward[0] = middle[0, 0]
-    downward[1] = middle[1, 0]
+    (upward,) = edges
     top = depth - 1
     even, odd = (
         0.5 * from_left(slope_x[half], folded(middle[2, top], 1.0 - 2.0 * half))
@@ -497,7 +520,7 @@
             high_change[c, side] = change
 
 
-def ghost_kernel(
+def ghost_levels(
     flags, out, low_change, high_change, from_below, from_above, slope_x, slope_y,
     low, high,
 ):
@@ -638,6 +661,10 @@
             scan_kernel, (message,), [hbm(), vmem()],
             [packed, packed, pltpu.SemaphoreType.DMA((2,))], 4 * block, (sums, ratio), (hbm(),),
         )
+        if beside:
+            upward, from_above = beside
+            sums, from_above = lax.optimization_barrier((sums, from_above))
+            beside = (upward, from_above)
         sums = lax.all_to_all(sums, "chip", split_axis=0, concat_axis=0, tiled=True)
         solved = shaped(fields, mid, length_y)
         own, partner = call(
@@ -679,33 +706,33 @@
         (partial, stacked, ratio, rows_x, rows_slope_x)
     )
 
-    def spectra(partial, weights, low, high, columns_low, columns_high, edges):
-        middle, theirs = call(
-            outer_kernel,
-            (own_shape, spectrum),
-            [smem(), smem()] + [vmem()] * 10,
-            [],
+    def spectra(partial, weights, low, high, columns_low, columns_high, more=()):
+        middle, theirs, *downward = call(
+            second_outer_kernel if more else outer_kernel,
+            (own_shape, spectrum) if more else (own_shape, spectrum, edge),
+            [smem(), smem()] + [vmem()] * (10 + len(more)),
+            [pltpu.VMEM(whole_edge.shape, full_type)] * 2 if more else [],
             source_flops // 2,
             (flags, fringe_columns, partial, weights, low, high, columns_low, columns_high,
-             *source_tables),
+             *source_tables, *more),
         )
         other = lax.ppermute(theirs, "core", swap)
-        mine, *edges = call(
+        mine, *upward = call(
             own_spectra_kernel,
-            (spectrum, *edges),
+            (spectrum,) if more else (spectrum, edge),
             [smem()] + [vmem()] * 5,
             [],
             source_flops // 2,
             (flags, middle, *source_tables),
         )
-        return middle, mine, other, *edges
+        return middle, mine, other, *upward, *downward
 
     middle, mine, other, upward, downward = spectra(
-        partial, weights, low, high, columns_low, columns_high, (edge, edge)
-    )
-    own, partner, slots, upward, downward = solve(mine, other, depth + 2, (upward, downward))
+        partial, weights, low, high, columns_low, columns_high
+    )
+    from_above = lax.ppermute(downward, levels_axis, downward_route)
+    own, partner, slots, upward, from_above = solve(mine, other, depth + 2, (upward, from_above))
     from_below = lax.ppermute(upward, levels_axis, upward_route)
-    from_above = lax.ppermute(downward, levels_axis, downward_route)
     taken = call(
         fringe_kernel, bands, [smem(), smem()] + [vmem()] * 7, [],
         9 * depth * block * (length_x + length_y) // 8,
@@ -714,7 +741,6 @@
     )
     partner, *taken = lax.optimization_barrier((partner, *taken))
     new_columns = lax.ppermute(taken[0], every_axis, across(0))
-    slots, *taken[1:] = lax.optimization_barrier((slots, *taken[1:]))
     new_columns_low = lax.ppermute(taken[1], every_axis, across(1))
     new_columns_high = lax.ppermute(taken[2], every_axis, across(-1))
     half_fields = 3 * depth + 5
@@ -729,14 +755,9 @@
     new_columns, corrected = lax.optimization_barrier((new_columns, corrected))
     partial, weights = inner(corrected, new_columns, (start,))
     partial, from_below, from_above = lax.optimization_barrier((partial, from_below, from_above))
-    low, high = call(
-        ghost_kernel, (whole_edge, whole_edge), [smem()] + [vmem()] * 7, [],
-        3 * block * (length_x // 2 + length_y),
-        (flags, corrected, low_change, high_change, from_below, from_above, tables["slope_x"],
-         tables["slope_y"]),
-    )
     final, mine, other = spectra(
-        partial, weights, low, high, new_columns_low, new_columns_high, ()
+        partial, weights, low_change, high_change, new_columns_low, new_columns_high,
+        (corrected, from_below, from_above),
     )
     _, partner, slots = solve(mine, other, depth + 1)
     half_fields = 3 * depth

time: 176 us -> 175 us (level)
  blocking collectives: 73.7 us -> 68.5 us
  starting transfers between devices: 23.6 us -> 28.6 us
    all_to_all x4, blocking collectives: 73.7 us -> 68.5 us  [solve(): sums = lax.all_to_all(sums, 'chip', split_axis=0, concat_axis=0, tiled=True)]
    ppermute x2, starting transfers between devices: 3.88 us -> 8.14 us  [solve(): partner = lax.ppermute(partner, 'core', swap)]
    pallas_call x20 -> x19, Pallas kernels: 47.1 us -> 45.7 us  [call(): pl.pallas_call(kernel, out_shape=outs, in_specs=in_specs, out_specs=out_s...]
    unnamed x47 -> x49, local copies, waits for them, and re-layouts: 6.75 us -> 7.97 us
  transfers between devices with their start and end apart: 14 -> 14, of which waited for: 5 -> 4; matrix products, arithmetic and copies ran while one was open for 7% -> 7% of each run, Pallas kernels for 16% -> 15%
where the time goes in v5:
time: 175 us; the launch traced here: 174 us
  blocking collectives  68.5 us (39%)
  Pallas kernels  45.7 us (26%)
  starting transfers between devices  28.6 us (16%)
  local copies, waits for them, and re-layouts  15.9 us (9%)
  waiting for transfers between devices  10.2 us (6%)
  other arithmetic  4.44 us (3%)
    all_to_all x4, blocking collectives, solve(): sums = lax.all_to_all(sums, 'chip', split_axis=0, concat_axis=0, tiled=True)  68.5 us
    pallas_call x19, Pallas kernels, call(): pl.pallas_call(kernel, out_shape=outs, in_specs=in_specs, out_specs=out_s...  45.7 us
    ppermute x2, starting transfers between devices, solve(): partner = lax.ppermute(partner, 'core', swap)  8.14 us
    unnamed x49, local copies, waits for them, and re-layouts  7.97 us
    gather x2, local copies, waits for them, and re-layouts, local(): jnp.take(tables[name], fringe_columns % mid, axis=2) * signs  5.11 us
    ppermute x1, waiting for transfers between devices, local(): new_columns = lax.ppermute(taken[0], every_axis, across(0))  4.34 us
    ppermute x1, starting transfers between devices, local(): low = lax.ppermute(low, levels_axis, upward_route)  3.67 us
  transfers between devices with their start and end apart: 14, of which 4 were waited for; matrix products, arithmetic and copies ran while one was open for 7% of the time, Pallas kernels for 15%

profile of v5, /device:TPU:5, one launch (start us, length us, event | category | flops | bytes accessed | tf_op | source)
XLA Modules:
  0.0 174.0 jit_solution(12993619671027012044)
XLA Ops:
  0.0 1.9 %copy-done.1 = f32[1,3,2,512,256]{4,3,2,1,0:T(8,128)S(1)} copy-done((f32[1,3,2,512,256]{4,3,2,1,0:T(8,128)S(1)}, f32[1,3,2,512,256]{4,3,2,1,0:T(8,128)}, u32[]{:S(2)}) %copy-start.1) | copy-done | bytes 3145752
  1.9 1.9 %shard_map.145 = (f32[3,512,256]{2,1,0:T(8,128)}, f32[3,512,256]{2,1,0:T(8,128)}) custom-call(f32[3,2,512,256]{3,2,1,0:T(8,128)S(1)} %bitcast.38), custom_call_target="tpu_custom_call" | custom-call | bytes 6291456 | tf_op jit(solution)/shard_map/pallas_call | solution.py:114
  3.8 3.7 %collective-permute-start.1 = (f32[3,512,256]{2,1,0:T(8,128)}, f32[3,512,256]{2,1,0:T(8,128)}, u32[]{:S(2)}, u32[]{:S(2)}) collective-permute-start(f32[3,512,256]{2,1,0:T(8,128)} %get-tuple-element.69), channel_id=1, source_target_pairs={{0,1},{1,2},{2,3},{3,4},{4,5},{5,6},{6,7},{7,8},{8,9},{9,10},{10,1... | collective-permute-start | bytes 4718600 | tf_op jit(solution)/shard_map/ppermute | solution.py:626
  7.4 1.9 %collective-permute-start.2 = (f32[3,512,256]{2,1,0:T(8,128)}, f32[3,512,256]{2,1,0:T(8,128)}, u32[]{:S(2)}, u32[]{:S(2)}) collective-permute-start(f32[3,512,256]{2,1,0:T(8,128)} %get-tuple-element.70), channel_id=1, source_target_pairs={{1,0},{2,1},{3,2},{4,3},{5,4},{6,5},{7,6},{8,7},{9,8},{10,9},{11,1... | collective-permute-start | bytes 4718600 | tf_op jit(solution)/shard_map/ppermute | solution.py:627
  9.5 0.2 fusion.14
  9.7 0.2 add_dynamic-update-slice_fusion.1
  9.9 0.0 copy-start.21
  10.0 0.2 add_dynamic-update-slice_fusion
  10.2 0.5 multiply_dynamic-update-slice_fusion.1
  10.8 0.6 multiply_dynamic-update-slice_fusion
  11.4 0.3 fusion.5
  11.7 0.3 fusion.8.stacked
  12.0 2.5 %copy-done = f32[22,256,256]{2,1,0:T(8,128)} copy-done((f32[22,256,256]{2,1,0:T(8,128)}, f32[22,256,256]{2,1,0:T(8,128)S(1)}, u32[]{:S(2)}) %copy-start) | copy-done | bytes 5767192
  14.5 1.8 %shard_map.146 = (f32[3,2,64,256]{3,2,1,0:T(8,128)S(1)}, f32[3,64,256]{2,1,0:T(8,128)S(1)}, f32[3,64,256]{2,1,0:T(8,128)}) custom-call(s32[64]{0:T(128)S(1)} %copy-done.18, f32[3,2,512,256]{3,2,1,0:T(8,128)S(1)} %bitcast.39), custom_call_target="tpu_custom_call" | custom-call | bytes 3932416 | tf_op jit(solution)/shard_map/pallas_call | solution.py:114
  16.3 0.8 copy.18
  17.1 1.3 collective-permute-start
  18.5 2.6 %gather_fusion.1 = bf16[64,2,2,256]{3,2,1,0:T(2,128)(2,1)} fusion(bf16[2,2,256,256]{3,1,2,0:T(2,128)(2,1)} %constant.140.clone2.1, s32[1024]{0:T(1024)S(1)} %pad_clamp_fusion), kind=kCustom, calls=%fused_computation.1.clone | custom fusion | bytes 262400 | tf_op jit(solution)/shard_map/jit(_take)/gather | solution.py:636
  21.0 2.5 %gather_fusion = bf16[64,2,2,256]{3,2,1,0:T(2,128)(2,1)} fusion(bf16[2,2,256,256]{3,1,2,0:T(2,128)(2,1)} %constant.138.clone2.1, s32[1024]{0:T(1024)S(1)} %pad_clamp_fusion), kind=kCustom, calls=%fused_computation.clone | custom fusion | bytes 262400 | tf_op jit(solution)/shard_map/jit(_take)/gather | solution.py:636
  23.6 1.1 bitcast_multiply_fusion
  24.7 1.3 collective-permute-start.3
  26.0 0.8 exponential_bitcast_fusion.ratio
  26.8 3.2 %collective-permute-done = f32[3,2,64,256]{3,2,0,1:T(8,128)} collective-permute-done((f32[3,2,64,256]{3,2,0,1:T(8,128)}, f32[3,2,64,256]{3,2,0,1:T(8,128)}, u32[]{:S(2)}, u32[]{:S(2)}) %collective-permute-start) | collective-permute-done | bytes 393248 | tf_op jit(solution)/shard_map/ppermute | solution.py:632
  30.0 0.9 slice_bitcast_fusion
  31.0 2.3 %collective-permute-start.4 = (f32[3,64,256]{2,1,0:T(8,128)S(1)}, f32[3,64,256]{2,1,0:T(8,128)S(1)}, u32[]{:S(2)}, u32[]{:S(2)}) collective-permute-start(f32[3,64,256]{2,1,0:T(8,128)S(1)} %slice_bitcast_fusion), channel_id=1, source_target_pairs={{17,16},{18,17},{19,18},{20,19},{21,20},{22,21},{23,22},{24,23},{2... | collective-permute-start | bytes 589832 | tf_op jit(solution)/shard_map/ppermute | solution.py:642
  33.3 0.1 pad_add_fusion.flags
  33.4 1.0 copy.19.columns
  34.4 0.0 copy-start.7
  34.4 1.2 copy-done.7
  35.6 1.2 copy-done.9
  36.9 1.0 copy-done.15
  37.9 3.8 %shard_map.147 = (f32[3,2,512,256]{3,2,1,0:T(8,128)S(1)}, f32[2,512,256]{2,1,0:T(8,128)S(1)}, f32[3,2,512,256]{3,2,1,0:T(8,128)S(1)}) custom-call(s32[4]{0:T(128)S(1)} %pad_add_fusion.flags, s32[64]{0:T(128)S(1)} %copy-done.18, f32[3,2,512,256]{3,2,1,0:T(8,128)S(1)} %bitcast.40, f32[3,2,64,256]{3,2,1,0:T(8,128)S(1)} %copy.19.columns, ...), custom_call_target="tpu_custom_call" | custom-call | flops 1207959552 | bytes 14287120 | tf_op jit(solution)/shard_map/pallas_call | solution.py:114
  41.8 2.2 %collective-permute-done.1.low = f32[3,512,256]{2,1,0:T(8,128)} collective-permute-done((f32[3,512,256]{2,1,0:T(8,128)}, f32[3,512,256]{2,1,0:T(8,128)}, u32[]{:S(2)}, u32[]{:S(2)}) %collective-permute-start.1) | collective-permute-done | bytes 1572896 | tf_op jit(solution)/shard_map/ppermute | solution.py:626
  44.1 5.2 %shard_map.148 = (f32[3,2,512,256]{3,2,1,0:T(8,128)S(1)}, f32[3,256,256]{2,1,0:T(8,128)S(1)}, f32[2,512,256]{2,1,0:T(8,128)S(1)}) custom-call(s32[4]{0:T(128)S(1)} %pad_add_fusion.flags, s32[64]{0:T(128)S(1)} %copy-done.18, f32[3,2,512,256]{3,2,1,0:T(8,128)S(1)} %get-tuple-element.67.partial, f32[2,512,256]{2,1,0:T(8,128)S(1)} %get-tuple-element.68.weights, ...), custom_call_target="tpu_custom_call" | custom-call | flops 805306368 | bytes 15859984 | tf_op jit(solution)/shard_map/pallas_call | solution.py:114
  49.3 0.1 collective-permute-start.5
  49.4 2.4 %collective-permute-start.6 = (f32[2,512,256]{2,1,0:T(8,128)S(1)}, f32[2,512,256]{2,1,0:T(8,128)S(1)}, u32[]{:S(2)}, u32[]{:S(2)}) collective-permute-start(f32[2,512,256]{2,1,0:T(8,128)S(1)} %get-tuple-element.77), channel_id=1, source_target_pairs={{1,0},{2,1},{3,2},{4,3},{5,4},{6,5},{7,6},{8,7},{9,8},{10,9},{11,1... | collective-permute-start | bytes 3145736 | tf_op jit(solution)/shard_map/ppermute | solution.py:733
  51.8 2.5 %shard_map.149 = (f32[3,256,256]{2,1,0:T(8,128)S(1)}, f32[2,512,256]{2,1,0:T(8,128)S(1)}) custom-call(s32[4]{0:T(128)S(1)} %pad_add_fusion.flags, f32[3,2,512,256]{3,2,1,0:T(8,128)S(1)} %get-tuple-element.72.middle, bf16[2,2,256,256]{3,2,1,0:T(8,128)(2,1)S(1)} %copy-done.4, bf16[2,256,256]{2,1,0:T(8,128)(2,1)S(1)} %copy-done.6, ...), custom_call_target="tpu_custom_call" | custom-call | flops 805306368 | bytes 8126480 | tf_op jit(solution)/shard_map/pallas_call | solution.py:114
  54.3 0.9 shard_map.150
  55.2 17.8 %all_to_all.20.received = f32[8,64,256]{2,1,0:T(8,128)S(1)} all-to-all(f32[8,64,256]{2,1,0:T(8,128)S(1)} %shard_map.150), channel_id=1, replica_groups=mesh['sec'=2,'chip'=8,'core'=2] {'chip'}, dimensions={0} | all-to-all | bytes 1048576 | tf_op jit(solution)/shard_map/all_to_all | solution.py:659
  73.0 0.1 shard_map.151
  73.1 14.8 %all_to_all.21.received = f32[8,64,256]{2,1,0:T(8,128)S(1)} all-to-all(f32[8,64,256]{2,1,0:T(8,128)S(1)} %shard_map.151), channel_id=1, replica_groups=mesh['sec'=2,'chip'=8,'core'=2] {'chip'}, dimensions={0} | all-to-all | bytes 1048576 | tf_op jit(solution)/shard_map/all_to_all | solution.py:668
  87.9 1.6 shard_map.152
  89.5 6.3 %collective-permute-start.7 = (f32[4,256,256]{2,1,0:T(8,128)S(1)}, f32[4,256,256]{2,1,0:T(8,128)S(1)}, u32[]{:S(2)}, u32[]{:S(2)}) collective-permute-start(f32[4,256,256]{2,1,0:T(8,128)S(1)} %get-tuple-element.79), channel_id=1, source_target_pairs={{0,1},{1,0},{2,3},{3,2},{4,5},{5,4},{6,7},{7,6},{8,9},{9,8},{10,11... | collective-permute-start | bytes 3145736 | tf_op jit(solution)/shard_map/ppermute | solution.py:676
  95.8 3.1 %collective-permute-start.9 = (f32[2,512,256]{2,1,0:T(8,128)S(1)}, f32[2,512,256]{2,1,0:T(8,128)S(1)}, u32[]{:S(2)}, u32[]{:S(2)}) collective-permute-start(f32[2,512,256]{2,1,0:T(8,128)S(1)} %get-tuple-element.96), channel_id=1, source_target_pairs={{0,1},{1,2},{2,3},{3,4},{4,5},{5,6},{6,7},{7,8},{8,9},{9,10},{10,1... | collective-permute-start | bytes 3145736 | tf_op jit(solution)/shard_map/ppermute | solution.py:735
  98.9 2.1 %shard_map.153 = (f32[3,2,64,256]{3,2,1,0:T(8,128)S(1)}, f32[3,64,256]{2,1,0:T(8,128)S(1)}, f32[3,64,256]{2,1,0:T(8,128)S(1)}) custom-call(s32[4]{0:T(128)S(1)} %pad_add_fusion.flags, s32[64]{0:T(128)S(1)} %copy-done.18, f32[4,256,256]{2,1,0:T(8,128)S(1)} %get-tuple-element.83.mine, f32[4,256,256]{2,1,0:T(8,128)S(1)} %collective-permute-done.7.other.fields, ...), custom_call_target="tpu_custom_call" | custom-call | flops 452984832 | bytes 7602448 | tf_op jit(solution)/shard_map/pallas_call | solution.py:114
  101.0 1.3 collective-permute-start.8
  102.4 3.3 %shard_map.154.slots = f32[11,256,256]{2,1,0:T(8,128)S(1)} custom-call(s32[4]{0:T(128)S(1)} %pad_add_fusion.flags, f32[4,256,256]{2,1,0:T(8,128)S(1)} %get-tuple-element.83.mine, bf16[2,2,256,256]{3,2,1,0:T(8,128)(2,1)S(1)} %copy-done.14, bf16[2,256,256]{2,1,0:T(8,128)(2,1)S(1)} %copy-done.12, bf16[2,2,256,256]{3,2,1,0:T(8,128)(2,1)S(1)} %copy-done.13, ...), custom_call_target="tpu_custom_call" | custom-call | flops 2214592512 | bytes 7077904 | tf_op jit(solution)/shard_map/pallas_call | solution.py:114
  105.7 0.0 copy-start.16
  105.7 1.4 collective-permute-start.10
  107.2 1.3 collective-permute-start.11
  108.5 3.4 %shard_map.155 = (f32[3,2,512,256]{3,2,1,0:T(8,128)S(1)}, f32[3,512,256]{2,1,0:T(8,128)S(1)}, f32[2,512,256]{2,1,0:T(8,128)S(1)}) custom-call(s32[4]{0:T(128)S(1)} %pad_add_fusion.flags, f32[11,256,256]{2,1,0:T(8,128)S(1)} %shard_map.154.slots, f32[4,256,256]{2,1,0:T(8,128)S(1)} %collective-permute-done.7.other.fields, ...), custom_call_target="tpu_custom_call" | custom-call | flops 2214592512 | bytes 15990800 | tf_op jit(solution)/shard_map/pallas_call | solution.py:114
  111.8 4.3 %collective-permute-done.8.columns = f32[3,2,64,256]{3,2,1,0:T(8,128)S(1)} collective-permute-done((f32[3,2,64,256]{3,2,1,0:T(8,128)S(1)}, f32[3,2,64,256]{3,2,1,0:T(8,128)S(1)}, u32[]{:S(2)}, u32[]{:S(2)}) %collective-permute-start.8) | collective-permute-done | bytes 393248 | tf_op jit(solution)/shard_map/ppermute | solution.py:743
  116.2 3.8 %shard_map.156 = (f32[3,2,512,256]{3,2,1,0:T(8,128)S(1)}, f32[2,512,256]{2,1,0:T(8,128)S(1)}) custom-call(s32[4]{0:T(128)S(1)} %pad_add_fusion.flags, s32[64]{0:T(128)S(1)} %copy-done.18, f32[3,2,512,256]{3,2,1,0:T(8,128)S(1)} %get-tuple-element.92.given.corrected, f32[3,2,64,256]{3,2,1,0:T(8,128)S(1)} %collective-permute-done.8.columns, ...), custom_call_target="tpu_custom_call" | custom-call | flops 1207959552 | bytes 14287120 | tf_op jit(solution)/shard_map/pallas_call | solution.py:114
  120.0 0.4 collective-permute-done.10.columns_low
  120.4 4.5 %shard_map.157 = (f32[3,2,512,256]{3,2,1,0:T(8,128)S(1)}, f32[3,256,256]{2,1,0:T(8,128)S(1)}) custom-call(s32[4]{0:T(128)S(1)} %pad_add_fusion.flags, s32[64]{0:T(128)S(1)} %copy-done.18, f32[3,2,512,256]{3,2,1,0:T(8,128)S(1)} %get-tuple-element.98.partial, f32[2,512,256]{2,1,0:T(8,128)S(1)} %get-tuple-element.99.weights, ...), custom_call_target="tpu_custom_call" | custom-call | flops 805306368 | bytes 19530000 | tf_op jit(solution)/shard_map/pallas_call | solution.py:114
  124.9 0.5 collective-permute-start.12
  125.3 2.2 %shard_map.158.mine = f32[3,256,256]{2,1,0:T(8,128)S(1)} custom-call(s32[4]{0:T(128)S(1)} %pad_add_fusion.flags, f32[3,2,512,256]{3,2,1,0:T(8,128)S(1)} %get-tuple-element.106.middle.final, bf16[2,2,256,256]{3,2,1,0:T(8,128)(2,1)S(1)} %copy-done.4, bf16[2,256,256]{2,1,0:T(8,128)(2,1)S(1)} %copy-done.6, bf16[2,2,256,256]{3,2,1,0:T(8,128)(2,1)S(1)} %copy-done.3, ...), custom_call_target="tpu_custom_call" | custom-call | flops 805306368 | bytes 7077904 | tf_op jit(solution)/shard_map/pallas_call | solution.py:114
  127.5 0.9 shard_map.159
  128.5 18.4 %all_to_all.22.received = f32[8,64,256]{2,1,0:T(8,128)S(1)} all-to-all(f32[8,64,256]{2,1,0:T(8,128)S(1)} %shard_map.159), channel_id=1, replica_groups=mesh['sec'=2,'chip'=8,'core'=2] {'chip'}, dimensions={0} | all-to-all | bytes 1048576 | tf_op jit(solution)/shard_map/all_to_all | solution.py:659
  146.9 0.1 shard_map.160
  147.0 17.5 %all_to_all.23.received = f32[8,64,256]{2,1,0:T(8,128)S(1)} all-to-all(f32[8,64,256]{2,1,0:T(8,128)S(1)} %shard_map.160), channel_id=1, replica_groups=mesh['sec'=2,'chip'=8,'core'=2] {'chip'}, dimensions={0} | all-to-all | bytes 1048576 | tf_op jit(solution)/shard_map/all_to_all | solution.py:668
  164.5 1.4 shard_map.161
  165.9 1.8 %collective-permute-start.13 = (f32[3,256,256]{2,1,0:T(8,128)S(1)}, f32[3,256,256]{2,1,0:T(8,128)S(1)}, u32[]{:S(2)}, u32[]{:S(2)}) collective-permute-start(f32[3,256,256]{2,1,0:T(8,128)S(1)} %get-tuple-element.109), channel_id=1, source_target_pairs={{0,1},{1,0},{2,3},{3,2},{4,5},{5,4},{6,7},{7,6},{8,9},{9,8},{10,11... | collective-permute-start | bytes 2359304 | tf_op jit(solution)/shard_map/ppermute | solution.py:676
  167.7 2.3 %shard_map.162.slots = f32[6,256,256]{2,1,0:T(8,128)S(1)} custom-call(s32[4]{0:T(128)S(1)} %pad_add_fusion.flags, f32[3,256,256]{2,1,0:T(8,128)S(1)} %get-tuple-element.108.mine, bf16[2,2,256,256]{3,2,1,0:T(8,128)(2,1)S(1)} %copy-done.14, bf16[2,256,256]{2,1,0:T(8,128)(2,1)S(1)} %copy-done.12, bf16[2,2,256,256]{3,2,1,0:T(8,128)(2,1)S(1)} %copy-done.13, ...), custom_call_target="tpu_custom_call" | custom-call | flops 1207959552 | bytes 5505040 | tf_op jit(solution)/shard_map/pallas_call | solution.py:114
  170.0 4.0 %shard_map.163 = f32[3,2,512,256]{3,2,1,0:T(8,128)} custom-call(s32[4]{0:T(128)S(1)} %pad_add_fusion.flags, f32[6,256,256]{2,1,0:T(8,128)S(1)} %shard_map.162.slots, f32[3,256,256]{2,1,0:T(8,128)S(1)} %collective-permute-done.13.fields, f32[3,2,512,256]{3,2,1,0:T(8,128)S(1)} %get-tuple-element.106.middle.final, bf16[2,2,256,256]{3,2,1,0:T(8,128)(2,1)S(1)} %copy-done.14, ...), custom_call_target="tpu_custom_call" | custom-call | flops 1207959552 | bytes 11796496 | tf_op jit(solution)/shard_map/pallas_call | solution.py:114
  (60 shorter events, 0.2 us)
Async XLA Ops:
  0.0 1.9 %copy-start.1 = (f32[1,3,2,512,256]{4,3,2,1,0:T(8,128)S(1)}, f32[1,3,2,512,256]{4,3,2,1,0:T(8,128)}, u32[]{:S(2)}) copy-start(f32[1,3,2,512,256]{4,3,2,1,0:T(8,128)} %param.17) | copy-start | bytes 9437188
  1.9 7.5 %copy-start.20 = (f32[2,256,256]{2,1,0:T(8,128)S(1)}, f32[2,256,256]{2,1,0:T(8,128)}, u32[]{:S(2)}) copy-start(f32[2,256,256]{2,1,0:T(8,128)} %constant.142.clone) | copy-start | bytes 1572868
  3.8 40.3 %collective-permute-start.1 = (f32[3,512,256]{2,1,0:T(8,128)}, f32[3,512,256]{2,1,0:T(8,128)}, u32[]{:S(2)}, u32[]{:S(2)}) collective-permute-start(f32[3,512,256]{2,1,0:T(8,128)} %get-tuple-element.69), channel_id=1, source_target_pairs={{0,1},{1,2},{2,3},{3,4},{4,5},{5,6},{6,7},{7,8},{8,9},{9,10},{10,1... | collective-permute-start | bytes 4718600 | tf_op jit(solution)/shard_map/ppermute | solution.py:626
  7.4 36.6 %collective-permute-start.2 = (f32[3,512,256]{2,1,0:T(8,128)}, f32[3,512,256]{2,1,0:T(8,128)}, u32[]{:S(2)}, u32[]{:S(2)}) collective-permute-start(f32[3,512,256]{2,1,0:T(8,128)} %get-tuple-element.70), channel_id=1, source_target_pairs={{1,0},{2,1},{3,2},{4,3},{5,4},{6,5},{7,6},{8,7},{9,8},{10,9},{11,1... | collective-permute-start | bytes 4718600 | tf_op jit(solution)/shard_map/ppermute | solution.py:627
  9.9 1.5 copy-start.21
  10.2 4.3 %copy-start.2 = (f32[1,3,2,512,256]{4,3,2,1,0:T(8,128)S(1)}, f32[1,3,2,512,256]{4,3,2,1,0:T(8,128)}, u32[]{:S(2)}) copy-start(f32[1,3,2,512,256]{4,3,2,1,0:T(8,128)} %param.17) | copy-start | bytes 9437188
  10.2 4.3 %copy-start.18 = (s32[64]{0:T(128)S(1)}, s32[64]{0:T(128)}, u32[]{:S(2)}) copy-start(s32[64]{0:T(128)} %index.11) | copy-start | bytes 772
  12.0 2.5 %copy-start = (f32[22,256,256]{2,1,0:T(8,128)}, f32[22,256,256]{2,1,0:T(8,128)S(1)}, u32[]{:S(2)}) copy-start(f32[22,256,256]{2,1,0:T(8,128)S(1)} %fusion.8.stacked) | copy-start | bytes 17301508
  14.5 19.9 %copy-start.17 = (bf16[256,256]{1,0:T(8,128)(2,1)S(1)}, bf16[256,256]{1,0:T(8,128)(2,1)}, u32[]{:S(2)}) copy-start(bf16[256,256]{1,0:T(8,128)(2,1)} %constant.133.clone.dealias_y) | copy-start | bytes 393220
  16.3 7.3 %copy-start.19 = (f32[3,64,256]{2,1,0:T(8,128)}, f32[3,64,256]{2,1,0:T(8,128)S(1)}, u32[]{:S(2)}) copy-start(f32[3,64,256]{2,1,0:T(8,128)S(1)} %get-tuple-element.71) | copy-start | bytes 589828
  17.1 12.9 %collective-permute-start = (f32[3,2,64,256]{3,2,0,1:T(8,128)}, f32[3,2,64,256]{3,2,0,1:T(8,128)}, u32[]{:S(2)}, u32[]{:S(2)}) collective-permute-start(f32[3,2,64,256]{3,2,0,1:T(8,128)} %copy.18), channel_id=1, source_target_pairs={{0,16},{1,17},{2,18},{3,19},{4,20},{5,21},{6,22},{7,23},{8,24},{9,... | collective-permute-start | bytes 1179656 | tf_op jit(solution)/shard_map/ppermute | solution.py:632
  24.7 17.1 %collective-permute-start.3 = (f32[3,64,256]{2,1,0:T(8,128)}, f32[3,64,256]{2,1,0:T(8,128)}, u32[]{:S(2)}, u32[]{:S(2)}) collective-permute-start(f32[3,64,256]{2,1,0:T(8,128)} %copy-done.19), channel_id=1, source_target_pairs={{0,17},{1,18},{2,19},{3,20},{4,21},{5,22},{6,23},{7,24},{8,25},{9,... | collective-permute-start | bytes 589832 | tf_op jit(solution)/shard_map/ppermute | solution.py:641
  31.0 10.8 %collective-permute-start.4 = (f32[3,64,256]{2,1,0:T(8,128)S(1)}, f32[3,64,256]{2,1,0:T(8,128)S(1)}, u32[]{:S(2)}, u32[]{:S(2)}) collective-permute-start(f32[3,64,256]{2,1,0:T(8,128)S(1)} %slice_bitcast_fusion), channel_id=1, source_target_pairs={{17,16},{18,17},{19,18},{20,19},{21,20},{22,21},{23,22},{24,23},{2... | collective-permute-start | bytes 589832 | tf_op jit(solution)/shard_map/ppermute | solution.py:642
  34.4 1.2 copy-start.7
  35.6 1.2 copy-start.9
  36.9 1.0 copy-start.15
  37.9 6.1 %copy-start.3 = (bf16[2,2,256,256]{3,2,1,0:T(8,128)(2,1)S(1)}, bf16[2,2,256,256]{3,2,1,0:T(8,128)(2,1)}, u32[]{:S(2)}) copy-start(bf16[2,2,256,256]{3,2,1,0:T(8,128)(2,1)} %constant.136.clone.into_x) | copy-start | bytes 1572868
  37.9 6.1 %copy-start.4 = (bf16[2,2,256,256]{3,2,1,0:T(8,128)(2,1)S(1)}, bf16[2,2,256,256]{3,2,1,0:T(8,128)(2,1)}, u32[]{:S(2)}) copy-start(bf16[2,2,256,256]{3,2,1,0:T(8,128)(2,1)} %constant.134.clone.slope_x) | copy-start | bytes 1572868
  37.9 6.1 %copy-start.5 = (bf16[2,256,256]{2,1,0:T(8,128)(2,1)S(1)}, bf16[2,256,256]{2,1,0:T(8,128)(2,1)}, u32[]{:S(2)}) copy-start(bf16[2,256,256]{2,1,0:T(8,128)(2,1)} %constant.137.clone.into_y) | copy-start | bytes 786436
  37.9 6.2 %copy-start.6 = (bf16[2,256,256]{2,1,0:T(8,128)(2,1)S(1)}, bf16[2,256,256]{2,1,0:T(8,128)(2,1)}, u32[]{:S(2)}) copy-start(bf16[2,256,256]{2,1,0:T(8,128)(2,1)} %constant.135.clone.slope_y) | copy-start | bytes 786436
  44.0 10.2 %slice-start = ((s8[5767168]{0:T(1024)(128)(4,1)}), s8[4194304]{0:T(1024)(128)(4,1)S(1)}, s32[]{:S(2)}) async-start(s8[5767168]{0:T(1024)(128)(4,1)} %bitcast.36), calls=%async_computation.4 | async-start | bytes 8388608
  44.1 10.2 %slice-start.1 = ((s8[5767168]{0:T(1024)(128)(4,1)}), s8[1572864]{0:T(1024)(128)(4,1)S(1)}, s32[]{:S(2)}) async-start(s8[5767168]{0:T(1024)(128)(4,1)} %bitcast.36), calls=%async_computation.5 | async-start | bytes 3145728
  49.3 5.0 %collective-permute-start.5 = (f32[3,256,256]{2,1,0:T(8,128)S(1)}, f32[3,256,256]{2,1,0:T(8,128)S(1)}, u32[]{:S(2)}, u32[]{:S(2)}) collective-permute-start(f32[3,256,256]{2,1,0:T(8,128)S(1)} %get-tuple-element.74), channel_id=1, source_target_pairs={{0,1},{1,0},{2,3},{3,2},{4,5},{5,4},{6,7},{7,6},{8,9},{9,8},{10,11... | collective-permute-start | bytes 2359304 | tf_op jit(solution)/shard_map/ppermute | solution.py:719
  49.4 23.8 %collective-permute-start.6 = (f32[2,512,256]{2,1,0:T(8,128)S(1)}, f32[2,512,256]{2,1,0:T(8,128)S(1)}, u32[]{:S(2)}, u32[]{:S(2)}) collective-permute-start(f32[2,512,256]{2,1,0:T(8,128)S(1)} %get-tuple-element.77), channel_id=1, source_target_pairs={{1,0},{2,1},{3,2},{4,3},{5,4},{6,5},{7,6},{8,7},{9,8},{10,9},{11,1... | collective-permute-start | bytes 3145736 | tf_op jit(solution)/shard_map/ppermute | solution.py:733
  87.9 11.0 %copy-start.11 = (bf16[2,256,256]{2,1,0:T(8,128)(2,1)S(1)}, bf16[2,256,256]{2,1,0:T(8,128)(2,1)}, u32[]{:S(2)}) copy-start(bf16[2,256,256]{2,1,0:T(8,128)(2,1)} %constant.141.clone.from_slope_y) | copy-start | bytes 786436
  87.9 11.0 %copy-start.12 = (bf16[2,256,256]{2,1,0:T(8,128)(2,1)S(1)}, bf16[2,256,256]{2,1,0:T(8,128)(2,1)}, u32[]{:S(2)}) copy-start(bf16[2,256,256]{2,1,0:T(8,128)(2,1)} %constant.139.clone.from_y) | copy-start | bytes 786436
  89.5 9.4 %collective-permute-start.7 = (f32[4,256,256]{2,1,0:T(8,128)S(1)}, f32[4,256,256]{2,1,0:T(8,128)S(1)}, u32[]{:S(2)}, u32[]{:S(2)}) collective-permute-start(f32[4,256,256]{2,1,0:T(8,128)S(1)} %get-tuple-element.79), channel_id=1, source_target_pairs={{0,1},{1,0},{2,3},{3,2},{4,5},{5,4},{6,7},{7,6},{8,9},{9,8},{10,11... | collective-permute-start | bytes 3145736 | tf_op jit(solution)/shard_map/ppermute | solution.py:676
  95.8 6.6 %copy-start.13 = (bf16[2,2,256,256]{3,2,1,0:T(8,128)(2,1)S(1)}, bf16[2,2,256,256]{3,2,1,0:T(8,128)(2,1)}, u32[]{:S(2)}) copy-start(bf16[2,2,256,256]{3,2,1,0:T(8,128)(2,1)} %constant.140.clone.from_slope_x) | copy-start | bytes 1572868
  95.8 6.6 %copy-start.14 = (bf16[2,2,256,256]{3,2,1,0:T(8,128)(2,1)S(1)}, bf16[2,2,256,256]{3,2,1,0:T(8,128)(2,1)}, u32[]{:S(2)}) copy-start(bf16[2,2,256,256]{3,2,1,0:T(8,128)(2,1)} %constant.138.clone.from_x) | copy-start | bytes 1572868
  95.8 24.2 %collective-permute-start.9 = (f32[2,512,256]{2,1,0:T(8,128)S(1)}, f32[2,512,256]{2,1,0:T(8,128)S(1)}, u32[]{:S(2)}, u32[]{:S(2)}) collective-permute-start(f32[2,512,256]{2,1,0:T(8,128)S(1)} %get-tuple-element.96), channel_id=1, source_target_pairs={{0,1},{1,2},{2,3},{3,4},{4,5},{5,6},{6,7},{7,8},{8,9},{9,10},{10,1... | collective-permute-start | bytes 3145736 | tf_op jit(solution)/shard_map/ppermute | solution.py:735
  101.0 15.1 %collective-permute-start.8 = (f32[3,2,64,256]{3,2,1,0:T(8,128)S(1)}, f32[3,2,64,256]{3,2,1,0:T(8,128)S(1)}, u32[]{:S(2)}, u32[]{:S(2)}) collective-permute-start(f32[3,2,64,256]{3,2,1,0:T(8,128)S(1)} %get-tuple-element.89), channel_id=1, source_target_pairs={{0,16},{1,17},{2,18},{3,19},{4,20},{5,21},{6,22},{7,23},{8,24},{9,... | collective-permute-start | bytes 1179656 | tf_op jit(solution)/shard_map/ppermute | solution.py:743
  105.7 10.5 %copy-start.8 = (f32[1,2,512,256]{3,2,1,0:T(8,128)S(1)}, f32[1,2,512,256]{3,2,1,0:T(8,128)}, u32[]{:S(2)}) copy-start(f32[1,2,512,256]{3,2,1,0:T(8,128)} %param.18) | copy-start | bytes 3145732
  105.7 10.5 %copy-start.10 = (s32[2,512,256]{2,1,0:T(8,128)S(1)}, s32[2,512,256]{2,1,0:T(8,128)}, u32[]{:S(2)}) copy-start(s32[2,512,256]{2,1,0:T(8,128)} %mask.3) | copy-start | bytes 3145732
  105.7 10.5 %copy-start.16 = (bf16[512,512]{1,0:T(8,128)(2,1)S(1)}, bf16[512,512]{1,0:T(8,128)(2,1)}, u32[]{:S(2)}) copy-start(bf16[512,512]{1,0:T(8,128)(2,1)} %constant.132.clone.dealias_x) | copy-start | bytes 1572868
  105.7 14.7 %collective-permute-start.10 = (f32[3,64,256]{2,1,0:T(8,128)S(1)}, f32[3,64,256]{2,1,0:T(8,128)S(1)}, u32[]{:S(2)}, u32[]{:S(2)}) collective-permute-start(f32[3,64,256]{2,1,0:T(8,128)S(1)} %get-tuple-element.102), channel_id=1, source_target_pairs={{0,17},{1,18},{2,19},{3,20},{4,21},{5,22},{6,23},{7,24},{8,25},{9,... | collective-permute-start | bytes 589832 | tf_op jit(solution)/shard_map/ppermute | solution.py:744
  107.2 13.2 %collective-permute-start.11 = (f32[3,64,256]{2,1,0:T(8,128)S(1)}, f32[3,64,256]{2,1,0:T(8,128)S(1)}, u32[]{:S(2)}, u32[]{:S(2)}) collective-permute-start(f32[3,64,256]{2,1,0:T(8,128)S(1)} %get-tuple-element.103), channel_id=1, source_target_pairs={{1,16},{2,17},{3,18},{4,19},{5,20},{6,21},{7,22},{8,23},{9,24},{10... | collective-permute-start | bytes 589832 | tf_op jit(solution)/shard_map/ppermute | solution.py:745
  124.9 2.7 %collective-permute-start.12 = (f32[3,256,256]{2,1,0:T(8,128)S(1)}, f32[3,256,256]{2,1,0:T(8,128)S(1)}, u32[]{:S(2)}, u32[]{:S(2)}) collective-permute-start(f32[3,256,256]{2,1,0:T(8,128)S(1)} %get-tuple-element.107), channel_id=1, source_target_pairs={{0,1},{1,0},{2,3},{3,2},{4,5},{5,4},{6,7},{7,6},{8,9},{9,8},{10,11... | collective-permute-start | bytes 2359304 | tf_op jit(solution)/shard_map/ppermute | solution.py:719
  165.9 4.1 %collective-permute-start.13 = (f32[3,256,256]{2,1,0:T(8,128)S(1)}, f32[3,256,256]{2,1,0:T(8,128)S(1)}, u32[]{:S(2)}, u32[]{:S(2)}) collective-permute-start(f32[3,256,256]{2,1,0:T(8,128)S(1)} %get-tuple-element.109), channel_id=1, source_target_pairs={{0,1},{1,0},{2,3},{3,2},{4,5},{5,4},{6,7},{7,6},{8,9},{9,8},{10,11... | collective-permute-start | bytes 2359304 | tf_op jit(solution)/shard_map/ppermute | solution.py:676

commit v6 on v5

--- a/solution.py
+++ b/solution.py
@@ -545,20 +545,30 @@
 def last_kernel(
     flags, slots, fields, final, from_x, from_y, from_slope_x, from_slope_y,
     out,
-    others,
+    held, sems,
 ):
     core = flags[1]
     depth = final.shape[1]
     mid = final.shape[2] // 2
-    physical_half(
-        fields, 1 - core, False, from_x, from_y, from_slope_x, from_slope_y, others
-    )
-    sides = (slice(0, mid), slice(mid, 2 * mid))
+    half = 1 - core
+    sign = (1 - 2 * core).astype(full_type)
+    level = fields[0]
+    copies = []
     for z in range(depth):
-        for c in range(3):
-            slot = 2 * z + c if c < 2 else 2 * depth + z
-            for side, change in zip(sides, unfolded(core, slots, others, slot)):
-                out[c, z, side] = final[c, z, side] - change
+        lift = fields[1 + z]
+        for c, (block, left, right) in enumerate(
+            ((level, from_slope_x, from_y), (level, from_x, from_slope_y), (lift, from_x, from_y))
+        ):
+            other = from_left(left[half], from_right(block, right))
+            mine = slots[2 * z + c if c < 2 else 2 * depth + z]
+            held[c, z, :mid] = final[c, z, :mid] - (mine + other)
+            held[c, z, mid:] = final[c, z, mid:] - sign * (mine - other)
+            copy = pltpu.make_async_copy(held.at[c, z], out.at[c, z], sems.at[3 * z + c])
+            copy.start()
+            copies.append(copy)
+        level = level + lift
+    for copy in copies:
+        copy.wait()
 
 
 def coefficients(decay, first_level, count, height):
@@ -765,9 +775,10 @@
         last_kernel,
         (own_shape,),
         [smem()] + [vmem()] * 7,
-        [pltpu.VMEM((half_fields, mid, length_y), full_type)],
+        [pltpu.VMEM(own_shape.shape, full_type), pltpu.SemaphoreType.DMA((half_fields,))],
         3 * half_fields * block * (length_x // 2 + length_y) // 2,
         (flags, slots, partner, final, *pressure_tables),
+        (hbm(),),
     )
     return new[None]
 

time: 175 us -> 174 us (level)
  no operation moved by 1% of the time
where the time goes in v6:
time: 174 us; the launch traced here: 173 us
  blocking collectives  68.5 us (39%)
  Pallas kernels  44.8 us (26%)
  starting transfers between devices  28.6 us (16%)
  local copies, waits for them, and re-layouts  15.9 us (9%)
  waiting for transfers between devices  10.2 us (6%)
  other arithmetic  4.44 us (3%)
    all_to_all x4, blocking collectives, solve(): sums = lax.all_to_all(sums, 'chip', split_axis=0, concat_axis=0, tiled=True)  68.5 us
    pallas_call x19, Pallas kernels, call(): pl.pallas_call(kernel, out_shape=outs, in_specs=in_specs, out_specs=out_s...  44.8 us
    ppermute x2, starting transfers between devices, solve(): partner = lax.ppermute(partner, 'core', swap)  8.13 us
    unnamed x49, local copies, waits for them, and re-layouts  7.97 us
    gather x2, local copies, waits for them, and re-layouts, local(): jnp.take(tables[name], fringe_columns % mid, axis=2) * signs  5.12 us
    ppermute x1, waiting for transfers between devices, local(): new_columns = lax.ppermute(taken[0], every_axis, across(0))  4.34 us
    ppermute x1, starting transfers between devices, local(): low = lax.ppermute(low, levels_axis, upward_route)  3.67 us
  transfers between devices with their start and end apart: 14, of which 4 were waited for; matrix products, arithmetic and copies ran while one was open for 7% of the time, Pallas kernels for 15%

profile of v6, /device:TPU:5, one launch (start us, length us, event | category | flops | bytes accessed | tf_op | source)
XLA Modules:
  0.0 173.3 jit_solution(12469166095383893610)
XLA Ops:
  0.0 1.9 %copy-done.1 = f32[1,3,2,512,256]{4,3,2,1,0:T(8,128)S(1)} copy-done((f32[1,3,2,512,256]{4,3,2,1,0:T(8,128)S(1)}, f32[1,3,2,512,256]{4,3,2,1,0:T(8,128)}, u32[]{:S(2)}) %copy-start.1) | copy-done | bytes 3145752
  1.9 1.9 %shard_map.145 = (f32[3,512,256]{2,1,0:T(8,128)}, f32[3,512,256]{2,1,0:T(8,128)}) custom-call(f32[3,2,512,256]{3,2,1,0:T(8,128)S(1)} %bitcast.38), custom_call_target="tpu_custom_call" | custom-call | bytes 6291456 | tf_op jit(solution)/shard_map/pallas_call | solution.py:114
  3.8 3.7 %collective-permute-start.1 = (f32[3,512,256]{2,1,0:T(8,128)}, f32[3,512,256]{2,1,0:T(8,128)}, u32[]{:S(2)}, u32[]{:S(2)}) collective-permute-start(f32[3,512,256]{2,1,0:T(8,128)} %get-tuple-element.69), channel_id=1, source_target_pairs={{0,1},{1,2},{2,3},{3,4},{4,5},{5,6},{6,7},{7,8},{8,9},{9,10},{10,1... | collective-permute-start | bytes 4718600 | tf_op jit(solution)/shard_map/ppermute | solution.py:636
  7.4 1.9 %collective-permute-start.2 = (f32[3,512,256]{2,1,0:T(8,128)}, f32[3,512,256]{2,1,0:T(8,128)}, u32[]{:S(2)}, u32[]{:S(2)}) collective-permute-start(f32[3,512,256]{2,1,0:T(8,128)} %get-tuple-element.70), channel_id=1, source_target_pairs={{1,0},{2,1},{3,2},{4,3},{5,4},{6,5},{7,6},{8,7},{9,8},{10,9},{11,1... | collective-permute-start | bytes 4718600 | tf_op jit(solution)/shard_map/ppermute | solution.py:637
  9.5 0.2 fusion.14
  9.7 0.2 add_dynamic-update-slice_fusion.1
  9.9 0.0 copy-start.21
  10.0 0.2 add_dynamic-update-slice_fusion
  10.2 0.0 copy-start.2
  10.2 0.5 multiply_dynamic-update-slice_fusion.1
  10.8 0.6 multiply_dynamic-update-slice_fusion
  11.4 0.3 fusion.5
  11.7 0.3 fusion.8.stacked
  12.0 2.5 %copy-done = f32[22,256,256]{2,1,0:T(8,128)} copy-done((f32[22,256,256]{2,1,0:T(8,128)}, f32[22,256,256]{2,1,0:T(8,128)S(1)}, u32[]{:S(2)}) %copy-start) | copy-done | bytes 5767192
  14.5 1.8 %shard_map.146 = (f32[3,2,64,256]{3,2,1,0:T(8,128)S(1)}, f32[3,64,256]{2,1,0:T(8,128)S(1)}, f32[3,64,256]{2,1,0:T(8,128)}) custom-call(s32[64]{0:T(128)S(1)} %copy-done.18, f32[3,2,512,256]{3,2,1,0:T(8,128)S(1)} %bitcast.39), custom_call_target="tpu_custom_call" | custom-call | bytes 3932416 | tf_op jit(solution)/shard_map/pallas_call | solution.py:114
  16.3 0.8 copy.18
  17.1 1.3 collective-permute-start
  18.5 2.6 %gather_fusion.1 = bf16[64,2,2,256]{3,2,1,0:T(2,128)(2,1)} fusion(bf16[2,2,256,256]{3,1,2,0:T(2,128)(2,1)} %constant.140.clone2.1, s32[1024]{0:T(1024)S(1)} %pad_clamp_fusion), kind=kCustom, calls=%fused_computation.1.clone | custom fusion | bytes 262400 | tf_op jit(solution)/shard_map/jit(_take)/gather | solution.py:646
  21.1 2.5 %gather_fusion = bf16[64,2,2,256]{3,2,1,0:T(2,128)(2,1)} fusion(bf16[2,2,256,256]{3,1,2,0:T(2,128)(2,1)} %constant.138.clone2.1, s32[1024]{0:T(1024)S(1)} %pad_clamp_fusion), kind=kCustom, calls=%fused_computation.clone | custom fusion | bytes 262400 | tf_op jit(solution)/shard_map/jit(_take)/gather | solution.py:646
  23.6 1.1 bitcast_multiply_fusion
  24.7 1.3 collective-permute-start.3
  26.0 0.8 exponential_bitcast_fusion.ratio
  26.8 3.2 %collective-permute-done = f32[3,2,64,256]{3,2,0,1:T(8,128)} collective-permute-done((f32[3,2,64,256]{3,2,0,1:T(8,128)}, f32[3,2,64,256]{3,2,0,1:T(8,128)}, u32[]{:S(2)}, u32[]{:S(2)}) %collective-permute-start) | collective-permute-done | bytes 393248 | tf_op jit(solution)/shard_map/ppermute | solution.py:642
  30.0 0.9 slice_bitcast_fusion
  31.0 2.3 %collective-permute-start.4 = (f32[3,64,256]{2,1,0:T(8,128)S(1)}, f32[3,64,256]{2,1,0:T(8,128)S(1)}, u32[]{:S(2)}, u32[]{:S(2)}) collective-permute-start(f32[3,64,256]{2,1,0:T(8,128)S(1)} %slice_bitcast_fusion), channel_id=1, source_target_pairs={{17,16},{18,17},{19,18},{20,19},{21,20},{22,21},{23,22},{24,23},{2... | collective-permute-start | bytes 589832 | tf_op jit(solution)/shard_map/ppermute | solution.py:652
  33.3 0.1 pad_add_fusion.flags
  33.4 1.0 copy.19.columns
  34.4 1.2 copy-done.7
  35.6 1.2 copy-done.9
  36.9 1.0 copy-done.15
  37.9 3.8 %shard_map.147 = (f32[3,2,512,256]{3,2,1,0:T(8,128)S(1)}, f32[2,512,256]{2,1,0:T(8,128)S(1)}, f32[3,2,512,256]{3,2,1,0:T(8,128)S(1)}) custom-call(s32[4]{0:T(128)S(1)} %pad_add_fusion.flags, s32[64]{0:T(128)S(1)} %copy-done.18, f32[3,2,512,256]{3,2,1,0:T(8,128)S(1)} %bitcast.40, f32[3,2,64,256]{3,2,1,0:T(8,128)S(1)} %copy.19.columns, ...), custom_call_target="tpu_custom_call" | custom-call | flops 1207959552 | bytes 14287120 | tf_op jit(solution)/shard_map/pallas_call | solution.py:114
  41.8 2.2 %collective-permute-done.1.low = f32[3,512,256]{2,1,0:T(8,128)} collective-permute-done((f32[3,512,256]{2,1,0:T(8,128)}, f32[3,512,256]{2,1,0:T(8,128)}, u32[]{:S(2)}, u32[]{:S(2)}) %collective-permute-start.1) | collective-permute-done | bytes 1572896 | tf_op jit(solution)/shard_map/ppermute | solution.py:636
  44.1 5.2 %shard_map.148 = (f32[3,2,512,256]{3,2,1,0:T(8,128)S(1)}, f32[3,256,256]{2,1,0:T(8,128)S(1)}, f32[2,512,256]{2,1,0:T(8,128)S(1)}) custom-call(s32[4]{0:T(128)S(1)} %pad_add_fusion.flags, s32[64]{0:T(128)S(1)} %copy-done.18, f32[3,2,512,256]{3,2,1,0:T(8,128)S(1)} %get-tuple-element.67.partial, f32[2,512,256]{2,1,0:T(8,128)S(1)} %get-tuple-element.68.weights, ...), custom_call_target="tpu_custom_call" | custom-call | flops 805306368 | bytes 15859984 | tf_op jit(solution)/shard_map/pallas_call | solution.py:114
  49.3 0.1 collective-permute-start.5
  49.4 2.4 %collective-permute-start.6 = (f32[2,512,256]{2,1,0:T(8,128)S(1)}, f32[2,512,256]{2,1,0:T(8,128)S(1)}, u32[]{:S(2)}, u32[]{:S(2)}) collective-permute-start(f32[2,512,256]{2,1,0:T(8,128)S(1)} %get-tuple-element.77), channel_id=1, source_target_pairs={{1,0},{2,1},{3,2},{4,3},{5,4},{6,5},{7,6},{8,7},{9,8},{10,9},{11,1... | collective-permute-start | bytes 3145736 | tf_op jit(solution)/shard_map/ppermute | solution.py:743
  51.8 2.5 %shard_map.149 = (f32[3,256,256]{2,1,0:T(8,128)S(1)}, f32[2,512,256]{2,1,0:T(8,128)S(1)}) custom-call(s32[4]{0:T(128)S(1)} %pad_add_fusion.flags, f32[3,2,512,256]{3,2,1,0:T(8,128)S(1)} %get-tuple-element.72.middle, bf16[2,2,256,256]{3,2,1,0:T(8,128)(2,1)S(1)} %copy-done.4, bf16[2,256,256]{2,1,0:T(8,128)(2,1)S(1)} %copy-done.6, ...), custom_call_target="tpu_custom_call" | custom-call | flops 805306368 | bytes 8126480 | tf_op jit(solution)/shard_map/pallas_call | solution.py:114
  54.3 0.9 shard_map.150
  55.2 17.8 %all_to_all.20.received = f32[8,64,256]{2,1,0:T(8,128)S(1)} all-to-all(f32[8,64,256]{2,1,0:T(8,128)S(1)} %shard_map.150), channel_id=1, replica_groups=mesh['sec'=2,'chip'=8,'core'=2] {'chip'}, dimensions={0} | all-to-all | bytes 1048576 | tf_op jit(solution)/shard_map/all_to_all | solution.py:669
  73.0 0.1 shard_map.151
  73.1 14.8 %all_to_all.21.received = f32[8,64,256]{2,1,0:T(8,128)S(1)} all-to-all(f32[8,64,256]{2,1,0:T(8,128)S(1)} %shard_map.151), channel_id=1, replica_groups=mesh['sec'=2,'chip'=8,'core'=2] {'chip'}, dimensions={0} | all-to-all | bytes 1048576 | tf_op jit(solution)/shard_map/all_to_all | solution.py:678
  87.9 1.6 shard_map.152
  89.5 6.3 %collective-permute-start.7 = (f32[4,256,256]{2,1,0:T(8,128)S(1)}, f32[4,256,256]{2,1,0:T(8,128)S(1)}, u32[]{:S(2)}, u32[]{:S(2)}) collective-permute-start(f32[4,256,256]{2,1,0:T(8,128)S(1)} %get-tuple-element.79), channel_id=1, source_target_pairs={{0,1},{1,0},{2,3},{3,2},{4,5},{5,4},{6,7},{7,6},{8,9},{9,8},{10,11... | collective-permute-start | bytes 3145736 | tf_op jit(solution)/shard_map/ppermute | solution.py:686
  95.8 3.1 %collective-permute-start.9 = (f32[2,512,256]{2,1,0:T(8,128)S(1)}, f32[2,512,256]{2,1,0:T(8,128)S(1)}, u32[]{:S(2)}, u32[]{:S(2)}) collective-permute-start(f32[2,512,256]{2,1,0:T(8,128)S(1)} %get-tuple-element.96), channel_id=1, source_target_pairs={{0,1},{1,2},{2,3},{3,4},{4,5},{5,6},{6,7},{7,8},{8,9},{9,10},{10,1... | collective-permute-start | bytes 3145736 | tf_op jit(solution)/shard_map/ppermute | solution.py:745
  98.9 2.1 %shard_map.153 = (f32[3,2,64,256]{3,2,1,0:T(8,128)S(1)}, f32[3,64,256]{2,1,0:T(8,128)S(1)}, f32[3,64,256]{2,1,0:T(8,128)S(1)}) custom-call(s32[4]{0:T(128)S(1)} %pad_add_fusion.flags, s32[64]{0:T(128)S(1)} %copy-done.18, f32[4,256,256]{2,1,0:T(8,128)S(1)} %get-tuple-element.83.mine, f32[4,256,256]{2,1,0:T(8,128)S(1)} %collective-permute-done.7.other.fields, ...), custom_call_target="tpu_custom_call" | custom-call | flops 452984832 | bytes 7602448 | tf_op jit(solution)/shard_map/pallas_call | solution.py:114
  101.0 1.3 collective-permute-start.8
  102.4 3.3 %shard_map.154.slots = f32[11,256,256]{2,1,0:T(8,128)S(1)} custom-call(s32[4]{0:T(128)S(1)} %pad_add_fusion.flags, f32[4,256,256]{2,1,0:T(8,128)S(1)} %get-tuple-element.83.mine, bf16[2,2,256,256]{3,2,1,0:T(8,128)(2,1)S(1)} %copy-done.14, bf16[2,256,256]{2,1,0:T(8,128)(2,1)S(1)} %copy-done.12, bf16[2,2,256,256]{3,2,1,0:T(8,128)(2,1)S(1)} %copy-done.13, ...), custom_call_target="tpu_custom_call" | custom-call | flops 2214592512 | bytes 7077904 | tf_op jit(solution)/shard_map/pallas_call | solution.py:114
  105.7 0.0 copy-start.16
  105.7 1.4 collective-permute-start.10
  107.2 1.3 collective-permute-start.11
  108.5 3.4 %shard_map.155 = (f32[3,2,512,256]{3,2,1,0:T(8,128)S(1)}, f32[3,512,256]{2,1,0:T(8,128)S(1)}, f32[2,512,256]{2,1,0:T(8,128)S(1)}) custom-call(s32[4]{0:T(128)S(1)} %pad_add_fusion.flags, f32[11,256,256]{2,1,0:T(8,128)S(1)} %shard_map.154.slots, f32[4,256,256]{2,1,0:T(8,128)S(1)} %collective-permute-done.7.other.fields, ...), custom_call_target="tpu_custom_call" | custom-call | flops 2214592512 | bytes 15990800 | tf_op jit(solution)/shard_map/pallas_call | solution.py:114
  111.8 4.3 %collective-permute-done.8.columns = f32[3,2,64,256]{3,2,1,0:T(8,128)S(1)} collective-permute-done((f32[3,2,64,256]{3,2,1,0:T(8,128)S(1)}, f32[3,2,64,256]{3,2,1,0:T(8,128)S(1)}, u32[]{:S(2)}, u32[]{:S(2)}) %collective-permute-start.8) | collective-permute-done | bytes 393248 | tf_op jit(solution)/shard_map/ppermute | solution.py:753
  116.2 3.8 %shard_map.156 = (f32[3,2,512,256]{3,2,1,0:T(8,128)S(1)}, f32[2,512,256]{2,1,0:T(8,128)S(1)}) custom-call(s32[4]{0:T(128)S(1)} %pad_add_fusion.flags, s32[64]{0:T(128)S(1)} %copy-done.18, f32[3,2,512,256]{3,2,1,0:T(8,128)S(1)} %get-tuple-element.92.given.corrected, f32[3,2,64,256]{3,2,1,0:T(8,128)S(1)} %collective-permute-done.8.columns, ...), custom_call_target="tpu_custom_call" | custom-call | flops 1207959552 | bytes 14287120 | tf_op jit(solution)/shard_map/pallas_call | solution.py:114
  120.0 0.3 collective-permute-done.10.columns_low
  120.4 4.5 %shard_map.157 = (f32[3,2,512,256]{3,2,1,0:T(8,128)S(1)}, f32[3,256,256]{2,1,0:T(8,128)S(1)}) custom-call(s32[4]{0:T(128)S(1)} %pad_add_fusion.flags, s32[64]{0:T(128)S(1)} %copy-done.18, f32[3,2,512,256]{3,2,1,0:T(8,128)S(1)} %get-tuple-element.98.partial, f32[2,512,256]{2,1,0:T(8,128)S(1)} %get-tuple-element.99.weights, ...), custom_call_target="tpu_custom_call" | custom-call | flops 805306368 | bytes 19530000 | tf_op jit(solution)/shard_map/pallas_call | solution.py:114
  124.9 0.5 collective-permute-start.12
  125.3 2.2 %shard_map.158.mine = f32[3,256,256]{2,1,0:T(8,128)S(1)} custom-call(s32[4]{0:T(128)S(1)} %pad_add_fusion.flags, f32[3,2,512,256]{3,2,1,0:T(8,128)S(1)} %get-tuple-element.106.middle.final, bf16[2,2,256,256]{3,2,1,0:T(8,128)(2,1)S(1)} %copy-done.4, bf16[2,256,256]{2,1,0:T(8,128)(2,1)S(1)} %copy-done.6, bf16[2,2,256,256]{3,2,1,0:T(8,128)(2,1)S(1)} %copy-done.3, ...), custom_call_target="tpu_custom_call" | custom-call | flops 805306368 | bytes 7077904 | tf_op jit(solution)/shard_map/pallas_call | solution.py:114
  127.5 0.9 shard_map.159
  128.5 18.4 %all_to_all.22.received = f32[8,64,256]{2,1,0:T(8,128)S(1)} all-to-all(f32[8,64,256]{2,1,0:T(8,128)S(1)} %shard_map.159), channel_id=1, replica_groups=mesh['sec'=2,'chip'=8,'core'=2] {'chip'}, dimensions={0} | all-to-all | bytes 1048576 | tf_op jit(solution)/shard_map/all_to_all | solution.py:669
  146.9 0.1 shard_map.160
  147.0 17.5 %all_to_all.23.received = f32[8,64,256]{2,1,0:T(8,128)S(1)} all-to-all(f32[8,64,256]{2,1,0:T(8,128)S(1)} %shard_map.160), channel_id=1, replica_groups=mesh['sec'=2,'chip'=8,'core'=2] {'chip'}, dimensions={0} | all-to-all | bytes 1048576 | tf_op jit(solution)/shard_map/all_to_all | solution.py:678
  164.5 1.4 shard_map.161
  165.9 1.8 %collective-permute-start.13 = (f32[3,256,256]{2,1,0:T(8,128)S(1)}, f32[3,256,256]{2,1,0:T(8,128)S(1)}, u32[]{:S(2)}, u32[]{:S(2)}) collective-permute-start(f32[3,256,256]{2,1,0:T(8,128)S(1)} %get-tuple-element.109), channel_id=1, source_target_pairs={{0,1},{1,0},{2,3},{3,2},{4,5},{5,4},{6,7},{7,6},{8,9},{9,8},{10,11... | collective-permute-start | bytes 2359304 | tf_op jit(solution)/shard_map/ppermute | solution.py:686
  167.8 2.3 %shard_map.162.slots = f32[6,256,256]{2,1,0:T(8,128)S(1)} custom-call(s32[4]{0:T(128)S(1)} %pad_add_fusion.flags, f32[3,256,256]{2,1,0:T(8,128)S(1)} %get-tuple-element.108.mine, bf16[2,2,256,256]{3,2,1,0:T(8,128)(2,1)S(1)} %copy-done.14, bf16[2,256,256]{2,1,0:T(8,128)(2,1)S(1)} %copy-done.12, bf16[2,2,256,256]{3,2,1,0:T(8,128)(2,1)S(1)} %copy-done.13, ...), custom_call_target="tpu_custom_call" | custom-call | flops 1207959552 | bytes 5505040 | tf_op jit(solution)/shard_map/pallas_call | solution.py:114
  170.0 3.1 %shard_map.163 = f32[3,2,512,256]{3,2,1,0:T(8,128)} custom-call(s32[4]{0:T(128)S(1)} %pad_add_fusion.flags, f32[6,256,256]{2,1,0:T(8,128)S(1)} %shard_map.162.slots, f32[3,256,256]{2,1,0:T(8,128)S(1)} %collective-permute-done.13.fields, f32[3,2,512,256]{3,2,1,0:T(8,128)S(1)} %get-tuple-element.106.middle.final, bf16[2,2,256,256]{3,2,1,0:T(8,128)(2,1)S(1)} %copy-done.14, ...), custom_call_target="tpu_custom_call" | custom-call | flops 1207959552 | bytes 11796496 | tf_op jit(solution)/shard_map/pallas_call | solution.py:114
  (60 shorter events, 0.2 us)
Async XLA Ops:
  0.0 1.9 %copy-start.1 = (f32[1,3,2,512,256]{4,3,2,1,0:T(8,128)S(1)}, f32[1,3,2,512,256]{4,3,2,1,0:T(8,128)}, u32[]{:S(2)}) copy-start(f32[1,3,2,512,256]{4,3,2,1,0:T(8,128)} %param.17) | copy-start | bytes 9437188
  1.9 7.5 %copy-start.20 = (f32[2,256,256]{2,1,0:T(8,128)S(1)}, f32[2,256,256]{2,1,0:T(8,128)}, u32[]{:S(2)}) copy-start(f32[2,256,256]{2,1,0:T(8,128)} %constant.142.clone) | copy-start | bytes 1572868
  3.8 40.3 %collective-permute-start.1 = (f32[3,512,256]{2,1,0:T(8,128)}, f32[3,512,256]{2,1,0:T(8,128)}, u32[]{:S(2)}, u32[]{:S(2)}) collective-permute-start(f32[3,512,256]{2,1,0:T(8,128)} %get-tuple-element.69), channel_id=1, source_target_pairs={{0,1},{1,2},{2,3},{3,4},{4,5},{5,6},{6,7},{7,8},{8,9},{9,10},{10,1... | collective-permute-start | bytes 4718600 | tf_op jit(solution)/shard_map/ppermute | solution.py:636
  7.4 36.6 %collective-permute-start.2 = (f32[3,512,256]{2,1,0:T(8,128)}, f32[3,512,256]{2,1,0:T(8,128)}, u32[]{:S(2)}, u32[]{:S(2)}) collective-permute-start(f32[3,512,256]{2,1,0:T(8,128)} %get-tuple-element.70), channel_id=1, source_target_pairs={{1,0},{2,1},{3,2},{4,3},{5,4},{6,5},{7,6},{8,7},{9,8},{10,9},{11,1... | collective-permute-start | bytes 4718600 | tf_op jit(solution)/shard_map/ppermute | solution.py:637
  9.9 1.5 copy-start.21
  10.2 4.3 %copy-start.2 = (f32[1,3,2,512,256]{4,3,2,1,0:T(8,128)S(1)}, f32[1,3,2,512,256]{4,3,2,1,0:T(8,128)}, u32[]{:S(2)}) copy-start(f32[1,3,2,512,256]{4,3,2,1,0:T(8,128)} %param.17) | copy-start | bytes 9437188
  10.2 4.3 %copy-start.18 = (s32[64]{0:T(128)S(1)}, s32[64]{0:T(128)}, u32[]{:S(2)}) copy-start(s32[64]{0:T(128)} %index.11) | copy-start | bytes 772
  12.0 2.5 %copy-start = (f32[22,256,256]{2,1,0:T(8,128)}, f32[22,256,256]{2,1,0:T(8,128)S(1)}, u32[]{:S(2)}) copy-start(f32[22,256,256]{2,1,0:T(8,128)S(1)} %fusion.8.stacked) | copy-start | bytes 17301508
  14.5 19.9 %copy-start.17 = (bf16[256,256]{1,0:T(8,128)(2,1)S(1)}, bf16[256,256]{1,0:T(8,128)(2,1)}, u32[]{:S(2)}) copy-start(bf16[256,256]{1,0:T(8,128)(2,1)} %constant.133.clone.dealias_y) | copy-start | bytes 393220
  16.3 7.3 %copy-start.19 = (f32[3,64,256]{2,1,0:T(8,128)}, f32[3,64,256]{2,1,0:T(8,128)S(1)}, u32[]{:S(2)}) copy-start(f32[3,64,256]{2,1,0:T(8,128)S(1)} %get-tuple-element.71) | copy-start | bytes 589828
  17.1 12.9 %collective-permute-start = (f32[3,2,64,256]{3,2,0,1:T(8,128)}, f32[3,2,64,256]{3,2,0,1:T(8,128)}, u32[]{:S(2)}, u32[]{:S(2)}) collective-permute-start(f32[3,2,64,256]{3,2,0,1:T(8,128)} %copy.18), channel_id=1, source_target_pairs={{0,16},{1,17},{2,18},{3,19},{4,20},{5,21},{6,22},{7,23},{8,24},{9,... | collective-permute-start | bytes 1179656 | tf_op jit(solution)/shard_map/ppermute | solution.py:642
  24.7 17.1 %collective-permute-start.3 = (f32[3,64,256]{2,1,0:T(8,128)}, f32[3,64,256]{2,1,0:T(8,128)}, u32[]{:S(2)}, u32[]{:S(2)}) collective-permute-start(f32[3,64,256]{2,1,0:T(8,128)} %copy-done.19), channel_id=1, source_target_pairs={{0,17},{1,18},{2,19},{3,20},{4,21},{5,22},{6,23},{7,24},{8,25},{9,... | collective-permute-start | bytes 589832 | tf_op jit(solution)/shard_map/ppermute | solution.py:651
  31.0 10.8 %collective-permute-start.4 = (f32[3,64,256]{2,1,0:T(8,128)S(1)}, f32[3,64,256]{2,1,0:T(8,128)S(1)}, u32[]{:S(2)}, u32[]{:S(2)}) collective-permute-start(f32[3,64,256]{2,1,0:T(8,128)S(1)} %slice_bitcast_fusion), channel_id=1, source_target_pairs={{17,16},{18,17},{19,18},{20,19},{21,20},{22,21},{23,22},{24,23},{2... | collective-permute-start | bytes 589832 | tf_op jit(solution)/shard_map/ppermute | solution.py:652
  34.4 1.2 copy-start.7
  35.6 1.2 copy-start.9
  36.9 1.0 copy-start.15
  37.9 6.1 %copy-start.3 = (bf16[2,2,256,256]{3,2,1,0:T(8,128)(2,1)S(1)}, bf16[2,2,256,256]{3,2,1,0:T(8,128)(2,1)}, u32[]{:S(2)}) copy-start(bf16[2,2,256,256]{3,2,1,0:T(8,128)(2,1)} %constant.136.clone.into_x) | copy-start | bytes 1572868
  37.9 6.1 %copy-start.4 = (bf16[2,2,256,256]{3,2,1,0:T(8,128)(2,1)S(1)}, bf16[2,2,256,256]{3,2,1,0:T(8,128)(2,1)}, u32[]{:S(2)}) copy-start(bf16[2,2,256,256]{3,2,1,0:T(8,128)(2,1)} %constant.134.clone.slope_x) | copy-start | bytes 1572868
  37.9 6.1 %copy-start.5 = (bf16[2,256,256]{2,1,0:T(8,128)(2,1)S(1)}, bf16[2,256,256]{2,1,0:T(8,128)(2,1)}, u32[]{:S(2)}) copy-start(bf16[2,256,256]{2,1,0:T(8,128)(2,1)} %constant.137.clone.into_y) | copy-start | bytes 786436
  37.9 6.2 %copy-start.6 = (bf16[2,256,256]{2,1,0:T(8,128)(2,1)S(1)}, bf16[2,256,256]{2,1,0:T(8,128)(2,1)}, u32[]{:S(2)}) copy-start(bf16[2,256,256]{2,1,0:T(8,128)(2,1)} %constant.135.clone.slope_y) | copy-start | bytes 786436
  44.0 10.2 %slice-start = ((s8[5767168]{0:T(1024)(128)(4,1)}), s8[4194304]{0:T(1024)(128)(4,1)S(1)}, s32[]{:S(2)}) async-start(s8[5767168]{0:T(1024)(128)(4,1)} %bitcast.36), calls=%async_computation.4 | async-start | bytes 8388608
  44.1 10.2 %slice-start.1 = ((s8[5767168]{0:T(1024)(128)(4,1)}), s8[1572864]{0:T(1024)(128)(4,1)S(1)}, s32[]{:S(2)}) async-start(s8[5767168]{0:T(1024)(128)(4,1)} %bitcast.36), calls=%async_computation.5 | async-start | bytes 3145728
  49.3 5.0 %collective-permute-start.5 = (f32[3,256,256]{2,1,0:T(8,128)S(1)}, f32[3,256,256]{2,1,0:T(8,128)S(1)}, u32[]{:S(2)}, u32[]{:S(2)}) collective-permute-start(f32[3,256,256]{2,1,0:T(8,128)S(1)} %get-tuple-element.74), channel_id=1, source_target_pairs={{0,1},{1,0},{2,3},{3,2},{4,5},{5,4},{6,7},{7,6},{8,9},{9,8},{10,11... | collective-permute-start | bytes 2359304 | tf_op jit(solution)/shard_map/ppermute | solution.py:729
  49.4 23.8 %collective-permute-start.6 = (f32[2,512,256]{2,1,0:T(8,128)S(1)}, f32[2,512,256]{2,1,0:T(8,128)S(1)}, u32[]{:S(2)}, u32[]{:S(2)}) collective-permute-start(f32[2,512,256]{2,1,0:T(8,128)S(1)} %get-tuple-element.77), channel_id=1, source_target_pairs={{1,0},{2,1},{3,2},{4,3},{5,4},{6,5},{7,6},{8,7},{9,8},{10,9},{11,1... | collective-permute-start | bytes 3145736 | tf_op jit(solution)/shard_map/ppermute | solution.py:743
  87.9 11.0 %copy-start.11 = (bf16[2,256,256]{2,1,0:T(8,128)(2,1)S(1)}, bf16[2,256,256]{2,1,0:T(8,128)(2,1)}, u32[]{:S(2)}) copy-start(bf16[2,256,256]{2,1,0:T(8,128)(2,1)} %constant.141.clone.from_slope_y) | copy-start | bytes 786436
  87.9 11.0 %copy-start.12 = (bf16[2,256,256]{2,1,0:T(8,128)(2,1)S(1)}, bf16[2,256,256]{2,1,0:T(8,128)(2,1)}, u32[]{:S(2)}) copy-start(bf16[2,256,256]{2,1,0:T(8,128)(2,1)} %constant.139.clone.from_y) | copy-start | bytes 786436
  89.5 9.4 %collective-permute-start.7 = (f32[4,256,256]{2,1,0:T(8,128)S(1)}, f32[4,256,256]{2,1,0:T(8,128)S(1)}, u32[]{:S(2)}, u32[]{:S(2)}) collective-permute-start(f32[4,256,256]{2,1,0:T(8,128)S(1)} %get-tuple-element.79), channel_id=1, source_target_pairs={{0,1},{1,0},{2,3},{3,2},{4,5},{5,4},{6,7},{7,6},{8,9},{9,8},{10,11... | collective-permute-start | bytes 3145736 | tf_op jit(solution)/shard_map/ppermute | solution.py:686
  95.8 6.6 %copy-start.13 = (bf16[2,2,256,256]{3,2,1,0:T(8,128)(2,1)S(1)}, bf16[2,2,256,256]{3,2,1,0:T(8,128)(2,1)}, u32[]{:S(2)}) copy-start(bf16[2,2,256,256]{3,2,1,0:T(8,128)(2,1)} %constant.140.clone.from_slope_x) | copy-start | bytes 1572868
  95.8 6.6 %copy-start.14 = (bf16[2,2,256,256]{3,2,1,0:T(8,128)(2,1)S(1)}, bf16[2,2,256,256]{3,2,1,0:T(8,128)(2,1)}, u32[]{:S(2)}) copy-start(bf16[2,2,256,256]{3,2,1,0:T(8,128)(2,1)} %constant.138.clone.from_x) | copy-start | bytes 1572868
  95.8 24.2 %collective-permute-start.9 = (f32[2,512,256]{2,1,0:T(8,128)S(1)}, f32[2,512,256]{2,1,0:T(8,128)S(1)}, u32[]{:S(2)}, u32[]{:S(2)}) collective-permute-start(f32[2,512,256]{2,1,0:T(8,128)S(1)} %get-tuple-element.96), channel_id=1, source_target_pairs={{0,1},{1,2},{2,3},{3,4},{4,5},{5,6},{6,7},{7,8},{8,9},{9,10},{10,1... | collective-permute-start | bytes 3145736 | tf_op jit(solution)/shard_map/ppermute | solution.py:745
  101.0 15.1 %collective-permute-start.8 = (f32[3,2,64,256]{3,2,1,0:T(8,128)S(1)}, f32[3,2,64,256]{3,2,1,0:T(8,128)S(1)}, u32[]{:S(2)}, u32[]{:S(2)}) collective-permute-start(f32[3,2,64,256]{3,2,1,0:T(8,128)S(1)} %get-tuple-element.89), channel_id=1, source_target_pairs={{0,16},{1,17},{2,18},{3,19},{4,20},{5,21},{6,22},{7,23},{8,24},{9,... | collective-permute-start | bytes 1179656 | tf_op jit(solution)/shard_map/ppermute | solution.py:753
  105.7 10.5 %copy-start.8 = (f32[1,2,512,256]{3,2,1,0:T(8,128)S(1)}, f32[1,2,512,256]{3,2,1,0:T(8,128)}, u32[]{:S(2)}) copy-start(f32[1,2,512,256]{3,2,1,0:T(8,128)} %param.18) | copy-start | bytes 3145732
  105.7 10.5 %copy-start.10 = (s32[2,512,256]{2,1,0:T(8,128)S(1)}, s32[2,512,256]{2,1,0:T(8,128)}, u32[]{:S(2)}) copy-start(s32[2,512,256]{2,1,0:T(8,128)} %mask.3) | copy-start | bytes 3145732
  105.7 10.5 %copy-start.16 = (bf16[512,512]{1,0:T(8,128)(2,1)S(1)}, bf16[512,512]{1,0:T(8,128)(2,1)}, u32[]{:S(2)}) copy-start(bf16[512,512]{1,0:T(8,128)(2,1)} %constant.132.clone.dealias_x) | copy-start | bytes 1572868
  105.7 14.7 %collective-permute-start.10 = (f32[3,64,256]{2,1,0:T(8,128)S(1)}, f32[3,64,256]{2,1,0:T(8,128)S(1)}, u32[]{:S(2)}, u32[]{:S(2)}) collective-permute-start(f32[3,64,256]{2,1,0:T(8,128)S(1)} %get-tuple-element.102), channel_id=1, source_target_pairs={{0,17},{1,18},{2,19},{3,20},{4,21},{5,22},{6,23},{7,24},{8,25},{9,... | collective-permute-start | bytes 589832 | tf_op jit(solution)/shard_map/ppermute | solution.py:754
  107.2 13.2 %collective-permute-start.11 = (f32[3,64,256]{2,1,0:T(8,128)S(1)}, f32[3,64,256]{2,1,0:T(8,128)S(1)}, u32[]{:S(2)}, u32[]{:S(2)}) collective-permute-start(f32[3,64,256]{2,1,0:T(8,128)S(1)} %get-tuple-element.103), channel_id=1, source_target_pairs={{1,16},{2,17},{3,18},{4,19},{5,20},{6,21},{7,22},{8,23},{9,24},{10... | collective-permute-start | bytes 589832 | tf_op jit(solution)/shard_map/ppermute | solution.py:755
  124.9 2.7 %collective-permute-start.12 = (f32[3,256,256]{2,1,0:T(8,128)S(1)}, f32[3,256,256]{2,1,0:T(8,128)S(1)}, u32[]{:S(2)}, u32[]{:S(2)}) collective-permute-start(f32[3,256,256]{2,1,0:T(8,128)S(1)} %get-tuple-element.107), channel_id=1, source_target_pairs={{0,1},{1,0},{2,3},{3,2},{4,5},{5,4},{6,7},{7,6},{8,9},{9,8},{10,11... | collective-permute-start | bytes 2359304 | tf_op jit(solution)/shard_map/ppermute | solution.py:729
  165.9 4.1 %collective-permute-start.13 = (f32[3,256,256]{2,1,0:T(8,128)S(1)}, f32[3,256,256]{2,1,0:T(8,128)S(1)}, u32[]{:S(2)}, u32[]{:S(2)}) collective-permute-start(f32[3,256,256]{2,1,0:T(8,128)S(1)} %get-tuple-element.109), channel_id=1, source_target_pairs={{0,1},{1,0},{2,3},{3,2},{4,5},{5,4},{6,7},{7,6},{8,9},{9,8},{10,11... | collective-permute-start | bytes 2359304 | tf_op jit(solution)/shard_map/ppermute | solution.py:686

commit v7 on v6

--- a/solution.py
+++ b/solution.py
@@ -110,7 +110,7 @@
 
 
 def call(kernel, outs, in_specs, scratch, flops, args, out_specs=None):
-    moved = sum(math.prod(a.shape) * 4 for a in (*outs, *args))
+    moved = sum(math.prod(a.shape) * 4 for a in (*outs, *args)) if flops else 0
     return pl.pallas_call(
         kernel,
         out_shape=outs,
@@ -689,7 +689,7 @@
         (slots,) = call(
             functools.partial(own_half_kernel, ghosts=ghosts),
             (shaped(half_fields, mid, length_y),), [smem()] + [vmem()] * 5, [],
-            3 * half_fields * block * (length_x // 2 + length_y) // 2,
+            0,
             (flags, own, *pressure_tables),
         )
         return own, partner, slots, *beside
@@ -759,7 +759,7 @@
         (own_shape, whole_edge, edge),
         [smem()] + [vmem()] * 7,
         [pltpu.VMEM((half_fields, mid, length_y), full_type)],
-        3 * half_fields * block * (length_x // 2 + length_y) // 2,
+        0,
         (flags, slots, partner, middle, *pressure_tables),
     )
     new_columns, corrected = lax.optimization_barrier((new_columns, corrected))

time: 174 us -> 174 us (level)
    unnamed x49 -> x51, local copies, waits for them, and re-layouts: 7.97 us -> 7.97 us
where the time goes in v7:
time: 174 us; the launch traced here: 173 us
  blocking collectives  68.5 us (39%)
  Pallas kernels  44.8 us (26%)
  starting transfers between devices  28.4 us (16%)
  local copies, waits for them, and re-layouts  15.2 us (9%)
  waiting for transfers between devices  10.5 us (6%)
  other arithmetic  5.03 us (3%)
    all_to_all x4, blocking collectives, solve(): sums = lax.all_to_all(sums, 'chip', split_axis=0, concat_axis=0, tiled=True)  68.5 us
    pallas_call x19, Pallas kernels, call(): pl.pallas_call(kernel, out_shape=outs, in_specs=in_specs, out_specs=out_s...  44.8 us
    ppermute x2, starting transfers between devices, solve(): partner = lax.ppermute(partner, 'core', swap)  8.13 us
    unnamed x51, local copies, waits for them, and re-layouts  7.97 us
    gather x2, local copies, waits for them, and re-layouts, local(): jnp.take(tables[name], fringe_columns % mid, axis=2) * signs  4.47 us
    ppermute x1, waiting for transfers between devices, local(): new_columns = lax.ppermute(taken[0], every_axis, across(0))  4.45 us
    ppermute x1, starting transfers between devices, local(): low = lax.ppermute(low, levels_axis, upward_route)  3.67 us
  transfers between devices with their start and end apart: 14, of which 4 were waited for; matrix products, arithmetic and copies ran while one was open for 7% of the time, Pallas kernels for 15%

profile of v7, /device:TPU:5, one launch (start us, length us, event | category | flops | bytes accessed | tf_op | source)
XLA Modules:
  0.0 173.4 jit_solution(4264376534165041834)
XLA Ops:
  0.0 1.9 %copy-done.1 = f32[1,3,2,512,256]{4,3,2,1,0:T(8,128)S(1)} copy-done((f32[1,3,2,512,256]{4,3,2,1,0:T(8,128)S(1)}, f32[1,3,2,512,256]{4,3,2,1,0:T(8,128)}, u32[]{:S(2)}) %copy-start.1) | copy-done | bytes 3145752
  1.9 1.9 %shard_map.145 = (f32[3,512,256]{2,1,0:T(8,128)}, f32[3,512,256]{2,1,0:T(8,128)}) custom-call(f32[3,2,512,256]{3,2,1,0:T(8,128)S(1)} %bitcast.38), custom_call_target="tpu_custom_call" | custom-call | tf_op jit(solution)/shard_map/pallas_call | solution.py:114
  3.8 3.7 %collective-permute-start.1 = (f32[3,512,256]{2,1,0:T(8,128)}, f32[3,512,256]{2,1,0:T(8,128)}, u32[]{:S(2)}, u32[]{:S(2)}) collective-permute-start(f32[3,512,256]{2,1,0:T(8,128)} %get-tuple-element.69), channel_id=1, source_target_pairs={{0,1},{1,2},{2,3},{3,4},{4,5},{5,6},{6,7},{7,8},{8,9},{9,10},{10,1... | collective-permute-start | bytes 4718600 | tf_op jit(solution)/shard_map/ppermute | solution.py:636
  7.4 1.9 %collective-permute-start.2 = (f32[3,512,256]{2,1,0:T(8,128)}, f32[3,512,256]{2,1,0:T(8,128)}, u32[]{:S(2)}, u32[]{:S(2)}) collective-permute-start(f32[3,512,256]{2,1,0:T(8,128)} %get-tuple-element.70), channel_id=1, source_target_pairs={{1,0},{2,1},{3,2},{4,3},{5,4},{6,5},{7,6},{8,7},{9,8},{10,9},{11,1... | collective-permute-start | bytes 4718600 | tf_op jit(solution)/shard_map/ppermute | solution.py:637
  9.5 0.2 fusion.14
  9.7 0.2 add_dynamic-update-slice_fusion.1
  10.0 0.0 copy-start.22
  10.0 0.2 add_dynamic-update-slice_fusion
  10.2 0.5 multiply_dynamic-update-slice_fusion.1
  10.8 0.6 multiply_dynamic-update-slice_fusion
  11.5 0.3 fusion.5
  11.7 0.3 fusion.8.stacked
  12.0 2.5 %copy-done = f32[22,256,256]{2,1,0:T(8,128)} copy-done((f32[22,256,256]{2,1,0:T(8,128)}, f32[22,256,256]{2,1,0:T(8,128)S(1)}, u32[]{:S(2)}) %copy-start) | copy-done | bytes 5767192
  14.5 1.8 %shard_map.146 = (f32[3,2,64,256]{3,2,1,0:T(8,128)S(1)}, f32[3,64,256]{2,1,0:T(8,128)S(1)}, f32[3,64,256]{2,1,0:T(8,128)}) custom-call(s32[64]{0:T(128)S(1)} %copy-done.19, f32[3,2,512,256]{3,2,1,0:T(8,128)S(1)} %bitcast.39), custom_call_target="tpu_custom_call" | custom-call | tf_op jit(solution)/shard_map/pallas_call | solution.py:114
  16.3 0.8 copy.18
  17.1 1.3 collective-permute-start
  18.5 1.9 %gather_fusion.1 = bf16[64,2,2,256]{3,2,1,0:T(2,128)(2,1)S(1)} fusion(bf16[2,2,256,256]{3,1,2,0:T(2,128)(2,1)} %constant.140.clone2.1, s32[1024]{0:T(1024)S(1)} %pad_clamp_fusion), kind=kCustom, calls=%fused_computation.1.clone | custom fusion | bytes 262400 | tf_op jit(solution)/shard_map/jit(_take)/gather | solution.py:646
  20.4 2.6 %gather_fusion = bf16[64,2,2,256]{3,2,1,0:T(2,128)(2,1)} fusion(bf16[2,2,256,256]{3,1,2,0:T(2,128)(2,1)} %constant.138.clone2.1, s32[1024]{0:T(1024)S(1)} %pad_clamp_fusion), kind=kCustom, calls=%fused_computation.clone | custom fusion | bytes 262400 | tf_op jit(solution)/shard_map/jit(_take)/gather | solution.py:646
  22.9 1.6 bitcast_multiply_fusion
  24.6 1.3 collective-permute-start.3
  25.9 0.8 exponential_bitcast_fusion.ratio
  26.7 3.4 %collective-permute-done = f32[3,2,64,256]{3,2,0,1:T(8,128)} collective-permute-done((f32[3,2,64,256]{3,2,0,1:T(8,128)}, f32[3,2,64,256]{3,2,0,1:T(8,128)}, u32[]{:S(2)}, u32[]{:S(2)}) %collective-permute-start) | collective-permute-done | bytes 393248 | tf_op jit(solution)/shard_map/ppermute | solution.py:642
  30.2 0.9 slice_bitcast_fusion
  31.1 2.2 %collective-permute-start.4 = (f32[3,64,256]{2,1,0:T(8,128)S(1)}, f32[3,64,256]{2,1,0:T(8,128)S(1)}, u32[]{:S(2)}, u32[]{:S(2)}) collective-permute-start(f32[3,64,256]{2,1,0:T(8,128)S(1)} %slice_bitcast_fusion), channel_id=1, source_target_pairs={{17,16},{18,17},{19,18},{20,19},{21,20},{22,21},{23,22},{24,23},{2... | collective-permute-start | bytes 589832 | tf_op jit(solution)/shard_map/ppermute | solution.py:652
  33.4 0.1 pad_add_fusion.flags
  33.4 1.0 copy.19.columns
  34.5 0.0 copy-start.11
  34.5 1.2 copy-done.11
  35.7 1.2 copy-done.13
  36.9 1.0 copy-done.15
  38.0 3.8 %shard_map.147 = (f32[3,2,512,256]{3,2,1,0:T(8,128)S(1)}, f32[2,512,256]{2,1,0:T(8,128)S(1)}, f32[3,2,512,256]{3,2,1,0:T(8,128)S(1)}) custom-call(s32[4]{0:T(128)S(1)} %pad_add_fusion.flags, s32[64]{0:T(128)S(1)} %copy-done.19, f32[3,2,512,256]{3,2,1,0:T(8,128)S(1)} %bitcast.40, f32[3,2,64,256]{3,2,1,0:T(8,128)S(1)} %copy.19.columns, ...), custom_call_target="tpu_custom_call" | custom-call | flops 1207959552 | bytes 14287120 | tf_op jit(solution)/shard_map/pallas_call | solution.py:114
  41.9 2.2 %collective-permute-done.1.low = f32[3,512,256]{2,1,0:T(8,128)} collective-permute-done((f32[3,512,256]{2,1,0:T(8,128)}, f32[3,512,256]{2,1,0:T(8,128)}, u32[]{:S(2)}, u32[]{:S(2)}) %collective-permute-start.1) | collective-permute-done | bytes 1572896 | tf_op jit(solution)/shard_map/ppermute | solution.py:636
  44.1 5.2 %shard_map.148 = (f32[3,2,512,256]{3,2,1,0:T(8,128)S(1)}, f32[3,256,256]{2,1,0:T(8,128)S(1)}, f32[2,512,256]{2,1,0:T(8,128)S(1)}) custom-call(s32[4]{0:T(128)S(1)} %pad_add_fusion.flags, s32[64]{0:T(128)S(1)} %copy-done.19, f32[3,2,512,256]{3,2,1,0:T(8,128)S(1)} %get-tuple-element.67.partial, f32[2,512,256]{2,1,0:T(8,128)S(1)} %get-tuple-element.68.weights, ...), custom_call_target="tpu_custom_call" | custom-call | flops 805306368 | bytes 15859984 | tf_op jit(solution)/shard_map/pallas_call | solution.py:114
  49.3 0.1 collective-permute-start.5
  49.4 2.4 %collective-permute-start.6 = (f32[2,512,256]{2,1,0:T(8,128)S(1)}, f32[2,512,256]{2,1,0:T(8,128)S(1)}, u32[]{:S(2)}, u32[]{:S(2)}) collective-permute-start(f32[2,512,256]{2,1,0:T(8,128)S(1)} %get-tuple-element.77), channel_id=1, source_target_pairs={{1,0},{2,1},{3,2},{4,3},{5,4},{6,5},{7,6},{8,7},{9,8},{10,9},{11,1... | collective-permute-start | bytes 3145736 | tf_op jit(solution)/shard_map/ppermute | solution.py:743
  51.8 2.5 %shard_map.149 = (f32[3,256,256]{2,1,0:T(8,128)S(1)}, f32[2,512,256]{2,1,0:T(8,128)S(1)}) custom-call(s32[4]{0:T(128)S(1)} %pad_add_fusion.flags, f32[3,2,512,256]{3,2,1,0:T(8,128)S(1)} %get-tuple-element.72.middle, bf16[2,2,256,256]{3,2,1,0:T(8,128)(2,1)S(1)} %copy-done.6, bf16[2,256,256]{2,1,0:T(8,128)(2,1)S(1)} %copy-done.10, ...), custom_call_target="tpu_custom_call" | custom-call | flops 805306368 | bytes 8126480 | tf_op jit(solution)/shard_map/pallas_call | solution.py:114
  54.3 0.9 shard_map.150
  55.2 17.8 %all_to_all.20.received = f32[8,64,256]{2,1,0:T(8,128)S(1)} all-to-all(f32[8,64,256]{2,1,0:T(8,128)S(1)} %shard_map.150), channel_id=1, replica_groups=mesh['sec'=2,'chip'=8,'core'=2] {'chip'}, dimensions={0} | all-to-all | bytes 1048576 | tf_op jit(solution)/shard_map/all_to_all | solution.py:669
  73.0 0.1 shard_map.151
  73.1 14.8 %all_to_all.21.received = f32[8,64,256]{2,1,0:T(8,128)S(1)} all-to-all(f32[8,64,256]{2,1,0:T(8,128)S(1)} %shard_map.151), channel_id=1, replica_groups=mesh['sec'=2,'chip'=8,'core'=2] {'chip'}, dimensions={0} | all-to-all | bytes 1048576 | tf_op jit(solution)/shard_map/all_to_all | solution.py:678
  87.9 1.6 shard_map.152
  89.5 6.3 %collective-permute-start.7 = (f32[4,256,256]{2,1,0:T(8,128)S(1)}, f32[4,256,256]{2,1,0:T(8,128)S(1)}, u32[]{:S(2)}, u32[]{:S(2)}) collective-permute-start(f32[4,256,256]{2,1,0:T(8,128)S(1)} %get-tuple-element.79), channel_id=1, source_target_pairs={{0,1},{1,0},{2,3},{3,2},{4,5},{5,4},{6,7},{7,6},{8,9},{9,8},{10,11... | collective-permute-start | bytes 3145736 | tf_op jit(solution)/shard_map/ppermute | solution.py:686
  95.8 3.1 %collective-permute-start.9 = (f32[2,512,256]{2,1,0:T(8,128)S(1)}, f32[2,512,256]{2,1,0:T(8,128)S(1)}, u32[]{:S(2)}, u32[]{:S(2)}) collective-permute-start(f32[2,512,256]{2,1,0:T(8,128)S(1)} %get-tuple-element.96), channel_id=1, source_target_pairs={{0,1},{1,2},{2,3},{3,4},{4,5},{5,6},{6,7},{7,8},{8,9},{9,10},{10,1... | collective-permute-start | bytes 3145736 | tf_op jit(solution)/shard_map/ppermute | solution.py:745
  98.9 2.1 %shard_map.153 = (f32[3,2,64,256]{3,2,1,0:T(8,128)S(1)}, f32[3,64,256]{2,1,0:T(8,128)S(1)}, f32[3,64,256]{2,1,0:T(8,128)S(1)}) custom-call(s32[4]{0:T(128)S(1)} %pad_add_fusion.flags, s32[64]{0:T(128)S(1)} %copy-done.19, f32[4,256,256]{2,1,0:T(8,128)S(1)} %get-tuple-element.83.mine, f32[4,256,256]{2,1,0:T(8,128)S(1)} %collective-permute-done.7.other.fields, ...), custom_call_target="tpu_custom_call" | custom-call | flops 452984832 | bytes 7602448 | tf_op jit(solution)/shard_map/pallas_call | solution.py:114
  101.1 1.3 collective-permute-start.8
  102.4 1.3 collective-permute-start.10
  103.7 1.3 collective-permute-start.11
  105.0 3.3 %shard_map.154.slots = f32[11,256,256]{2,1,0:T(8,128)S(1)} custom-call(s32[4]{0:T(128)S(1)} %pad_add_fusion.flags, f32[4,256,256]{2,1,0:T(8,128)S(1)} %get-tuple-element.83.mine, bf16[2,2,256,256]{3,2,1,0:T(8,128)(2,1)S(1)} %copy-done.4, bf16[2,256,256]{2,1,0:T(8,128)(2,1)S(1)} %copy-done.8, bf16[2,2,256,256]{3,2,1,0:T(8,128)(2,1)S(1)} %copy-done.3, ...), custom_call_target="tpu_custom_call" | custom-call | tf_op jit(solution)/shard_map/pallas_call | solution.py:114
  108.3 0.0 copy-start.16
  108.3 3.4 %shard_map.155 = (f32[3,2,512,256]{3,2,1,0:T(8,128)S(1)}, f32[3,512,256]{2,1,0:T(8,128)S(1)}, f32[2,512,256]{2,1,0:T(8,128)S(1)}) custom-call(s32[4]{0:T(128)S(1)} %pad_add_fusion.flags, f32[11,256,256]{2,1,0:T(8,128)S(1)} %shard_map.154.slots, f32[4,256,256]{2,1,0:T(8,128)S(1)} %collective-permute-done.7.other.fields, ...), custom_call_target="tpu_custom_call" | custom-call | tf_op jit(solution)/shard_map/pallas_call | solution.py:114
  111.7 4.4 %collective-permute-done.8.columns = f32[3,2,64,256]{3,2,1,0:T(8,128)S(1)} collective-permute-done((f32[3,2,64,256]{3,2,1,0:T(8,128)S(1)}, f32[3,2,64,256]{3,2,1,0:T(8,128)S(1)}, u32[]{:S(2)}, u32[]{:S(2)}) %collective-permute-start.8) | collective-permute-done | bytes 393248 | tf_op jit(solution)/shard_map/ppermute | solution.py:753
  116.2 3.8 %shard_map.156 = (f32[3,2,512,256]{3,2,1,0:T(8,128)S(1)}, f32[2,512,256]{2,1,0:T(8,128)S(1)}) custom-call(s32[4]{0:T(128)S(1)} %pad_add_fusion.flags, s32[64]{0:T(128)S(1)} %copy-done.19, f32[3,2,512,256]{3,2,1,0:T(8,128)S(1)} %get-tuple-element.92.given.corrected, f32[3,2,64,256]{3,2,1,0:T(8,128)S(1)} %collective-permute-done.8.columns, ...), custom_call_target="tpu_custom_call" | custom-call | flops 1207959552 | bytes 14287120 | tf_op jit(solution)/shard_map/pallas_call | solution.py:114
  120.0 0.4 collective-permute-done.10.columns_low
  120.4 4.5 %shard_map.157 = (f32[3,2,512,256]{3,2,1,0:T(8,128)S(1)}, f32[3,256,256]{2,1,0:T(8,128)S(1)}) custom-call(s32[4]{0:T(128)S(1)} %pad_add_fusion.flags, s32[64]{0:T(128)S(1)} %copy-done.19, f32[3,2,512,256]{3,2,1,0:T(8,128)S(1)} %get-tuple-element.98.partial, f32[2,512,256]{2,1,0:T(8,128)S(1)} %get-tuple-element.99.weights, ...), custom_call_target="tpu_custom_call" | custom-call | flops 805306368 | bytes 19530000 | tf_op jit(solution)/shard_map/pallas_call | solution.py:114
  124.9 0.5 collective-permute-start.12
  125.4 2.2 %shard_map.158.mine = f32[3,256,256]{2,1,0:T(8,128)S(1)} custom-call(s32[4]{0:T(128)S(1)} %pad_add_fusion.flags, f32[3,2,512,256]{3,2,1,0:T(8,128)S(1)} %get-tuple-element.106.middle.final, bf16[2,2,256,256]{3,2,1,0:T(8,128)(2,1)S(1)} %copy-done.6, bf16[2,256,256]{2,1,0:T(8,128)(2,1)S(1)} %copy-done.10, bf16[2,2,256,256]{3,2,1,0:T(8,128)(2,1)S(1)} %copy-done.5, ...), custom_call_target="tpu_custom_call" | custom-call | flops 805306368 | bytes 7077904 | tf_op jit(solution)/shard_map/pallas_call | solution.py:114
  127.6 0.9 shard_map.159
  128.5 18.4 %all_to_all.22.received = f32[8,64,256]{2,1,0:T(8,128)S(1)} all-to-all(f32[8,64,256]{2,1,0:T(8,128)S(1)} %shard_map.159), channel_id=1, replica_groups=mesh['sec'=2,'chip'=8,'core'=2] {'chip'}, dimensions={0} | all-to-all | bytes 1048576 | tf_op jit(solution)/shard_map/all_to_all | solution.py:669
  146.9 0.1 shard_map.160
  147.0 17.5 %all_to_all.23.received = f32[8,64,256]{2,1,0:T(8,128)S(1)} all-to-all(f32[8,64,256]{2,1,0:T(8,128)S(1)} %shard_map.160), channel_id=1, replica_groups=mesh['sec'=2,'chip'=8,'core'=2] {'chip'}, dimensions={0} | all-to-all | bytes 1048576 | tf_op jit(solution)/shard_map/all_to_all | solution.py:678
  164.6 1.4 shard_map.161
  166.0 1.8 %collective-permute-start.13 = (f32[3,256,256]{2,1,0:T(8,128)S(1)}, f32[3,256,256]{2,1,0:T(8,128)S(1)}, u32[]{:S(2)}, u32[]{:S(2)}) collective-permute-start(f32[3,256,256]{2,1,0:T(8,128)S(1)} %get-tuple-element.109), channel_id=1, source_target_pairs={{0,1},{1,0},{2,3},{3,2},{4,5},{5,4},{6,7},{7,6},{8,9},{9,8},{10,11... | collective-permute-start | bytes 2359304 | tf_op jit(solution)/shard_map/ppermute | solution.py:686
  167.8 2.3 %shard_map.162.slots = f32[6,256,256]{2,1,0:T(8,128)S(1)} custom-call(s32[4]{0:T(128)S(1)} %pad_add_fusion.flags, f32[3,256,256]{2,1,0:T(8,128)S(1)} %get-tuple-element.108.mine, bf16[2,2,256,256]{3,2,1,0:T(8,128)(2,1)S(1)} %copy-done.4, bf16[2,256,256]{2,1,0:T(8,128)(2,1)S(1)} %copy-done.8, bf16[2,2,256,256]{3,2,1,0:T(8,128)(2,1)S(1)} %copy-done.3, ...), custom_call_target="tpu_custom_call" | custom-call | tf_op jit(solution)/shard_map/pallas_call | solution.py:114
  170.0 3.1 %shard_map.163 = f32[3,2,512,256]{3,2,1,0:T(8,128)} custom-call(s32[4]{0:T(128)S(1)} %pad_add_fusion.flags, f32[6,256,256]{2,1,0:T(8,128)S(1)} %shard_map.162.slots, f32[3,256,256]{2,1,0:T(8,128)S(1)} %collective-permute-done.13.fields, f32[3,2,512,256]{3,2,1,0:T(8,128)S(1)} %get-tuple-element.106.middle.final, bf16[2,2,256,256]{3,2,1,0:T(8,128)(2,1)S(1)} %copy-done.4, ...), custom_call_target="tpu_custom_call" | custom-call | flops 1207959552 | bytes 11796496 | tf_op jit(solution)/shard_map/pallas_call | solution.py:114
  (62 shorter events, 0.2 us)
Async XLA Ops:
  0.0 1.9 %copy-start.1 = (f32[1,3,2,512,256]{4,3,2,1,0:T(8,128)S(1)}, f32[1,3,2,512,256]{4,3,2,1,0:T(8,128)}, u32[]{:S(2)}) copy-start(f32[1,3,2,512,256]{4,3,2,1,0:T(8,128)} %param.17) | copy-start | bytes 9437188
  1.9 7.5 %copy-start.21 = (f32[2,256,256]{2,1,0:T(8,128)S(1)}, f32[2,256,256]{2,1,0:T(8,128)}, u32[]{:S(2)}) copy-start(f32[2,256,256]{2,1,0:T(8,128)} %constant.142.clone) | copy-start | bytes 1572868
  3.8 40.3 %collective-permute-start.1 = (f32[3,512,256]{2,1,0:T(8,128)}, f32[3,512,256]{2,1,0:T(8,128)}, u32[]{:S(2)}, u32[]{:S(2)}) collective-permute-start(f32[3,512,256]{2,1,0:T(8,128)} %get-tuple-element.69), channel_id=1, source_target_pairs={{0,1},{1,2},{2,3},{3,4},{4,5},{5,6},{6,7},{7,8},{8,9},{9,10},{10,1... | collective-permute-start | bytes 4718600 | tf_op jit(solution)/shard_map/ppermute | solution.py:636
  7.4 36.6 %collective-permute-start.2 = (f32[3,512,256]{2,1,0:T(8,128)}, f32[3,512,256]{2,1,0:T(8,128)}, u32[]{:S(2)}, u32[]{:S(2)}) collective-permute-start(f32[3,512,256]{2,1,0:T(8,128)} %get-tuple-element.70), channel_id=1, source_target_pairs={{1,0},{2,1},{3,2},{4,3},{5,4},{6,5},{7,6},{8,7},{9,8},{10,9},{11,1... | collective-permute-start | bytes 4718600 | tf_op jit(solution)/shard_map/ppermute | solution.py:637
  10.0 1.5 copy-start.22
  10.2 4.3 %copy-start.2 = (f32[1,3,2,512,256]{4,3,2,1,0:T(8,128)S(1)}, f32[1,3,2,512,256]{4,3,2,1,0:T(8,128)}, u32[]{:S(2)}) copy-start(f32[1,3,2,512,256]{4,3,2,1,0:T(8,128)} %param.17) | copy-start | bytes 9437188
  10.2 4.3 %copy-start.19 = (s32[64]{0:T(128)S(1)}, s32[64]{0:T(128)}, u32[]{:S(2)}) copy-start(s32[64]{0:T(128)} %index.11) | copy-start | bytes 772
  12.0 2.5 %copy-start = (f32[22,256,256]{2,1,0:T(8,128)}, f32[22,256,256]{2,1,0:T(8,128)S(1)}, u32[]{:S(2)}) copy-start(f32[22,256,256]{2,1,0:T(8,128)S(1)} %fusion.8.stacked) | copy-start | bytes 17301508
  14.5 20.0 %copy-start.17 = (bf16[256,256]{1,0:T(8,128)(2,1)S(1)}, bf16[256,256]{1,0:T(8,128)(2,1)}, u32[]{:S(2)}) copy-start(bf16[256,256]{1,0:T(8,128)(2,1)} %constant.133.clone.dealias_y) | copy-start | bytes 393220
  16.3 0.8 copy-start.20
  17.1 13.0 %collective-permute-start = (f32[3,2,64,256]{3,2,0,1:T(8,128)}, f32[3,2,64,256]{3,2,0,1:T(8,128)}, u32[]{:S(2)}, u32[]{:S(2)}) collective-permute-start(f32[3,2,64,256]{3,2,0,1:T(8,128)} %copy.18), channel_id=1, source_target_pairs={{0,16},{1,17},{2,18},{3,19},{4,20},{5,21},{6,22},{7,23},{8,24},{9,... | collective-permute-start | bytes 1179656 | tf_op jit(solution)/shard_map/ppermute | solution.py:642
  24.6 17.2 %collective-permute-start.3 = (f32[3,64,256]{2,1,0:T(8,128)}, f32[3,64,256]{2,1,0:T(8,128)}, u32[]{:S(2)}, u32[]{:S(2)}) collective-permute-start(f32[3,64,256]{2,1,0:T(8,128)} %copy-done.20), channel_id=1, source_target_pairs={{0,17},{1,18},{2,19},{3,20},{4,21},{5,22},{6,23},{7,24},{8,25},{9,... | collective-permute-start | bytes 589832 | tf_op jit(solution)/shard_map/ppermute | solution.py:651
  31.1 10.7 %collective-permute-start.4 = (f32[3,64,256]{2,1,0:T(8,128)S(1)}, f32[3,64,256]{2,1,0:T(8,128)S(1)}, u32[]{:S(2)}, u32[]{:S(2)}) collective-permute-start(f32[3,64,256]{2,1,0:T(8,128)S(1)} %slice_bitcast_fusion), channel_id=1, source_target_pairs={{17,16},{18,17},{19,18},{20,19},{21,20},{22,21},{23,22},{24,23},{2... | collective-permute-start | bytes 589832 | tf_op jit(solution)/shard_map/ppermute | solution.py:652
  34.5 1.2 copy-start.11
  35.7 1.2 copy-start.13
  36.9 1.0 copy-start.15
  38.0 6.1 %copy-start.5 = (bf16[2,2,256,256]{3,2,1,0:T(8,128)(2,1)S(1)}, bf16[2,2,256,256]{3,2,1,0:T(8,128)(2,1)}, u32[]{:S(2)}) copy-start(bf16[2,2,256,256]{3,2,1,0:T(8,128)(2,1)} %constant.136.clone.into_x) | copy-start | bytes 1572868
  38.0 6.1 %copy-start.6 = (bf16[2,2,256,256]{3,2,1,0:T(8,128)(2,1)S(1)}, bf16[2,2,256,256]{3,2,1,0:T(8,128)(2,1)}, u32[]{:S(2)}) copy-start(bf16[2,2,256,256]{3,2,1,0:T(8,128)(2,1)} %constant.134.clone.slope_x) | copy-start | bytes 1572868
  38.0 6.1 %copy-start.9 = (bf16[2,256,256]{2,1,0:T(8,128)(2,1)S(1)}, bf16[2,256,256]{2,1,0:T(8,128)(2,1)}, u32[]{:S(2)}) copy-start(bf16[2,256,256]{2,1,0:T(8,128)(2,1)} %constant.137.clone.into_y) | copy-start | bytes 786436
  38.0 6.1 %copy-start.10 = (bf16[2,256,256]{2,1,0:T(8,128)(2,1)S(1)}, bf16[2,256,256]{2,1,0:T(8,128)(2,1)}, u32[]{:S(2)}) copy-start(bf16[2,256,256]{2,1,0:T(8,128)(2,1)} %constant.135.clone.slope_y) | copy-start | bytes 786436
  44.1 10.2 %slice-start = ((s8[5767168]{0:T(1024)(128)(4,1)}), s8[4194304]{0:T(1024)(128)(4,1)S(1)}, s32[]{:S(2)}) async-start(s8[5767168]{0:T(1024)(128)(4,1)} %bitcast.36), calls=%async_computation.4 | async-start | bytes 8388608
  44.1 10.2 %slice-start.1 = ((s8[5767168]{0:T(1024)(128)(4,1)}), s8[1572864]{0:T(1024)(128)(4,1)S(1)}, s32[]{:S(2)}) async-start(s8[5767168]{0:T(1024)(128)(4,1)} %bitcast.36), calls=%async_computation.5 | async-start | bytes 3145728
  49.3 5.0 %collective-permute-start.5 = (f32[3,256,256]{2,1,0:T(8,128)S(1)}, f32[3,256,256]{2,1,0:T(8,128)S(1)}, u32[]{:S(2)}, u32[]{:S(2)}) collective-permute-start(f32[3,256,256]{2,1,0:T(8,128)S(1)} %get-tuple-element.74), channel_id=1, source_target_pairs={{0,1},{1,0},{2,3},{3,2},{4,5},{5,4},{6,7},{7,6},{8,9},{9,8},{10,11... | collective-permute-start | bytes 2359304 | tf_op jit(solution)/shard_map/ppermute | solution.py:729
  49.4 23.8 %collective-permute-start.6 = (f32[2,512,256]{2,1,0:T(8,128)S(1)}, f32[2,512,256]{2,1,0:T(8,128)S(1)}, u32[]{:S(2)}, u32[]{:S(2)}) collective-permute-start(f32[2,512,256]{2,1,0:T(8,128)S(1)} %get-tuple-element.77), channel_id=1, source_target_pairs={{1,0},{2,1},{3,2},{4,3},{5,4},{6,5},{7,6},{8,7},{9,8},{10,9},{11,1... | collective-permute-start | bytes 3145736 | tf_op jit(solution)/shard_map/ppermute | solution.py:743
  87.9 11.0 %copy-start.7 = (bf16[2,256,256]{2,1,0:T(8,128)(2,1)S(1)}, bf16[2,256,256]{2,1,0:T(8,128)(2,1)}, u32[]{:S(2)}) copy-start(bf16[2,256,256]{2,1,0:T(8,128)(2,1)} %constant.141.clone.from_slope_y) | copy-start | bytes 786436
  87.9 11.0 %copy-start.8 = (bf16[2,256,256]{2,1,0:T(8,128)(2,1)S(1)}, bf16[2,256,256]{2,1,0:T(8,128)(2,1)}, u32[]{:S(2)}) copy-start(bf16[2,256,256]{2,1,0:T(8,128)(2,1)} %constant.139.clone.from_y) | copy-start | bytes 786436
  87.9 11.0 %copy-start.18 = (bf16[2,2,64,256]{3,2,1,0:T(8,128)(2,1)S(1)}, bf16[2,2,64,256]{3,2,1,0:T(8,128)(2,1)}, u32[]{:S(2)}) copy-start(bf16[2,2,64,256]{3,2,1,0:T(8,128)(2,1)} %get-tuple-element.84.rows_x) | copy-start | bytes 393220
  89.5 9.4 %collective-permute-start.7 = (f32[4,256,256]{2,1,0:T(8,128)S(1)}, f32[4,256,256]{2,1,0:T(8,128)S(1)}, u32[]{:S(2)}, u32[]{:S(2)}) collective-permute-start(f32[4,256,256]{2,1,0:T(8,128)S(1)} %get-tuple-element.79), channel_id=1, source_target_pairs={{0,1},{1,0},{2,3},{3,2},{4,5},{5,4},{6,7},{7,6},{8,9},{9,8},{10,11... | collective-permute-start | bytes 3145736 | tf_op jit(solution)/shard_map/ppermute | solution.py:686
  95.8 9.2 %copy-start.3 = (bf16[2,2,256,256]{3,2,1,0:T(8,128)(2,1)S(1)}, bf16[2,2,256,256]{3,2,1,0:T(8,128)(2,1)}, u32[]{:S(2)}) copy-start(bf16[2,2,256,256]{3,2,1,0:T(8,128)(2,1)} %constant.140.clone.from_slope_x) | copy-start | bytes 1572868
  95.8 9.2 %copy-start.4 = (bf16[2,2,256,256]{3,2,1,0:T(8,128)(2,1)S(1)}, bf16[2,2,256,256]{3,2,1,0:T(8,128)(2,1)}, u32[]{:S(2)}) copy-start(bf16[2,2,256,256]{3,2,1,0:T(8,128)(2,1)} %constant.138.clone.from_x) | copy-start | bytes 1572868
  95.8 24.2 %collective-permute-start.9 = (f32[2,512,256]{2,1,0:T(8,128)S(1)}, f32[2,512,256]{2,1,0:T(8,128)S(1)}, u32[]{:S(2)}, u32[]{:S(2)}) collective-permute-start(f32[2,512,256]{2,1,0:T(8,128)S(1)} %get-tuple-element.96), channel_id=1, source_target_pairs={{0,1},{1,2},{2,3},{3,4},{4,5},{5,6},{6,7},{7,8},{8,9},{9,10},{10,1... | collective-permute-start | bytes 3145736 | tf_op jit(solution)/shard_map/ppermute | solution.py:745
  101.1 15.1 %collective-permute-start.8 = (f32[3,2,64,256]{3,2,1,0:T(8,128)S(1)}, f32[3,2,64,256]{3,2,1,0:T(8,128)S(1)}, u32[]{:S(2)}, u32[]{:S(2)}) collective-permute-start(f32[3,2,64,256]{3,2,1,0:T(8,128)S(1)} %get-tuple-element.89), channel_id=1, source_target_pairs={{0,16},{1,17},{2,18},{3,19},{4,20},{5,21},{6,22},{7,23},{8,24},{9,... | collective-permute-start | bytes 1179656 | tf_op jit(solution)/shard_map/ppermute | solution.py:753
  102.4 18.0 %collective-permute-start.10 = (f32[3,64,256]{2,1,0:T(8,128)S(1)}, f32[3,64,256]{2,1,0:T(8,128)S(1)}, u32[]{:S(2)}, u32[]{:S(2)}) collective-permute-start(f32[3,64,256]{2,1,0:T(8,128)S(1)} %get-tuple-element.102), channel_id=1, source_target_pairs={{0,17},{1,18},{2,19},{3,20},{4,21},{5,22},{6,23},{7,24},{8,25},{9,... | collective-permute-start | bytes 589832 | tf_op jit(solution)/shard_map/ppermute | solution.py:754
  103.7 16.7 %collective-permute-start.11 = (f32[3,64,256]{2,1,0:T(8,128)S(1)}, f32[3,64,256]{2,1,0:T(8,128)S(1)}, u32[]{:S(2)}, u32[]{:S(2)}) collective-permute-start(f32[3,64,256]{2,1,0:T(8,128)S(1)} %get-tuple-element.103), channel_id=1, source_target_pairs={{1,16},{2,17},{3,18},{4,19},{5,20},{6,21},{7,22},{8,23},{9,24},{10... | collective-permute-start | bytes 589832 | tf_op jit(solution)/shard_map/ppermute | solution.py:755
  108.3 7.9 %copy-start.12 = (f32[1,2,512,256]{3,2,1,0:T(8,128)S(1)}, f32[1,2,512,256]{3,2,1,0:T(8,128)}, u32[]{:S(2)}) copy-start(f32[1,2,512,256]{3,2,1,0:T(8,128)} %param.18) | copy-start | bytes 3145732
  108.3 7.8 %copy-start.14 = (s32[2,512,256]{2,1,0:T(8,128)S(1)}, s32[2,512,256]{2,1,0:T(8,128)}, u32[]{:S(2)}) copy-start(s32[2,512,256]{2,1,0:T(8,128)} %mask.3) | copy-start | bytes 3145732
  108.3 7.8 %copy-start.16 = (bf16[512,512]{1,0:T(8,128)(2,1)S(1)}, bf16[512,512]{1,0:T(8,128)(2,1)}, u32[]{:S(2)}) copy-start(bf16[512,512]{1,0:T(8,128)(2,1)} %constant.132.clone.dealias_x) | copy-start | bytes 1572868
  124.9 2.7 %collective-permute-start.12 = (f32[3,256,256]{2,1,0:T(8,128)S(1)}, f32[3,256,256]{2,1,0:T(8,128)S(1)}, u32[]{:S(2)}, u32[]{:S(2)}) collective-permute-start(f32[3,256,256]{2,1,0:T(8,128)S(1)} %get-tuple-element.107), channel_id=1, source_target_pairs={{0,1},{1,0},{2,3},{3,2},{4,5},{5,4},{6,7},{7,6},{8,9},{9,8},{10,11... | collective-permute-start | bytes 2359304 | tf_op jit(solution)/shard_map/ppermute | solution.py:729
  166.0 4.1 %collective-permute-start.13 = (f32[3,256,256]{2,1,0:T(8,128)S(1)}, f32[3,256,256]{2,1,0:T(8,128)S(1)}, u32[]{:S(2)}, u32[]{:S(2)}) collective-permute-start(f32[3,256,256]{2,1,0:T(8,128)S(1)} %get-tuple-element.109), channel_id=1, source_target_pairs={{0,1},{1,0},{2,3},{3,2},{4,5},{5,4},{6,7},{7,6},{8,9},{9,8},{10,11... | collective-permute-start | bytes 2359304 | tf_op jit(solution)/shard_map/ppermute | solution.py:686
